TPU v7x, 32 devices: a whole 2x2x4 slice. The times are simulated.
32 devices in a mesh: grp: 4 (over y, x), seq: 8 (over z, core).
Axes of the slice: x: 2, y: 2, z: 4, core: 2. Of those that a mesh axis runs over, the one named last changes fastest.
Arguments:
- points: bfloat16 [16384, 512], P(('grp', 'seq')), may hold values from -6 to 6
- pattern_first: int32 [256, 3], P(('grp', 'seq')), may hold values from 0 to 63, as said below
- pattern_second: int32 [256, 3], P(('grp', 'seq')), may hold values from 0 to 7
- destination: int32 [16384], P(('grp', 'seq')), may hold values from 0 to 16383, as said below
- norm_gains: float32 [4, 512], replicated, may hold values from 0.1 to 1.9
- w_qkv: bfloat16 [2, 512, 1536], replicated
- w_proj: bfloat16 [2, 512, 512], replicated, may hold values from -0.25 to 0.25
- w_up: bfloat16 [2, 512, 2048], replicated, may hold values from -0.25 to 0.25
- w_down: bfloat16 [2, 2048, 512], replicated, may hold values from -0.125 to 0.125
- w_head: bfloat16 [3, 512], replicated, may hold values from -0.25 to 0.25
Outputs:
- features: bfloat16 [16384, 512], P(('grp', 'seq'))
- normals: float32 [3, 16384], P(None, ('grp', 'seq'))
Inputs may be any that keep to these rules, and one draw needn't show every extreme that they name: `pattern_first`: the 24 entries of the patches of one device name at most 4 patches (repeats counted) lying on any one device of the group, and exactly 4 on some device. `destination`: a permutation of the positions; the 512 points of one device place at most 32 points in any one block of 512 consecutive positions of the second order, and exactly 32 in some block for every device.
All inputs are finite; a program needn't handle non-finite values.
Results may differ from a plain program's by a relative error of at most 0.024.
Values may be sent and summed in bfloat16 or wider, within the bound.
No kernel may reach another device: no remote copies, remote signals or barrier semaphores. Data moves between devices by JAX's collectives and lax.ppermute only.
A program may use at most 128 MiB of HBM per device.

v0:
```python
import jax
import jax.numpy as jnp
from jax import lax
from jax.sharding import PartitionSpec as P

HEADS = 8
PATCH = 64


def layer_norm(rows, gains):
    values = rows.astype(jnp.float32)
    average = jnp.mean(values, axis=-1, keepdims=True)
    spread = jnp.mean((values - average) ** 2, axis=-1, keepdims=True)
    return ((values - average) * lax.rsqrt(spread + 1e-05) * gains).astype(jnp.bfloat16)


def attend(queries, key_rows, value_rows):
    count = key_rows.shape[0]
    channels = queries.shape[1]
    head_dim = channels // HEADS
    qh = queries.reshape(count, PATCH, HEADS, head_dim)
    kh = key_rows.reshape(count, -1, HEADS, head_dim)
    vh = value_rows.reshape(count, -1, HEADS, head_dim)
    scores = jnp.einsum(
        "nqhd,nkhd->nhqk", qh, kh, preferred_element_type=jnp.float32
    ) * head_dim ** (-0.5)
    probs = jax.nn.softmax(scores, axis=-1).astype(jnp.bfloat16)
    mixed = jnp.einsum("nhqk,nkhd->nqhd", probs, vh, preferred_element_type=jnp.float32)
    return mixed.reshape(count * PATCH, channels).astype(jnp.bfloat16)


def finish(rows, attended, section, norm_gains, w_proj, w_up, w_down):
    first = (
        rows.astype(jnp.float32)
        + jnp.dot(attended, w_proj[section], preferred_element_type=jnp.float32)
    ).astype(jnp.bfloat16)
    hidden = layer_norm(first, norm_gains[2 * section + 1])
    upper = jnp.dot(hidden, w_up[section], preferred_element_type=jnp.float32)
    act = jax.nn.gelu(upper, approximate=False).astype(jnp.bfloat16)
    return (
        first.astype(jnp.float32)
        + jnp.dot(act, w_down[section], preferred_element_type=jnp.float32)
    ).astype(jnp.bfloat16)


def shards(
    points,
    pattern_first,
    pattern_second,
    destination,
    norm_gains,
    w_qkv,
    w_proj,
    w_up,
    w_down,
    w_head,
):
    rows_here, channels = points.shape
    patches = rows_here // PATCH
    normed = layer_norm(points, norm_gains[0])
    proj = jnp.dot(normed, w_qkv[0], preferred_element_type=jnp.float32)
    queries = proj[:, :channels].astype(jnp.bfloat16)
    key_flat = proj[:, channels : 2 * channels].astype(jnp.bfloat16)
    value_flat = proj[:, 2 * channels :].astype(jnp.bfloat16)
    key_own = key_flat.reshape(patches, PATCH, channels)
    value_own = value_flat.reshape(patches, PATCH, channels)
    key_group, value_group = (
        lax.all_gather(key_flat, "seq", axis=0, tiled=True),
        lax.all_gather(value_flat, "seq", axis=0, tiled=True),
    )
    key_chosen = key_group.reshape(-1, PATCH, channels)[pattern_first]
    value_chosen = value_group.reshape(-1, PATCH, channels)[pattern_first]
    key_rows = jnp.concatenate([key_own[:, None], key_chosen], axis=1).reshape(
        patches, -1, channels
    )
    value_rows = jnp.concatenate([value_own[:, None], value_chosen], axis=1).reshape(
        patches, -1, channels
    )
    first = finish(
        points, attend(queries, key_rows, value_rows), 0, norm_gains, w_proj, w_up, w_down
    )
    group_count = lax.axis_size("grp")
    shard_count = lax.axis_size("seq")
    devices = group_count * shard_count
    capacity = 2 * rows_here // devices
    slot_total = devices * capacity
    target = destination // rows_here
    place_at = destination % rows_here
    onehot_dev = (target[:, None] == jnp.arange(devices, dtype=jnp.int32)[None, :]).astype(
        jnp.int32
    )
    earlier = jnp.cumsum(onehot_dev, axis=0) - onehot_dev
    send_rank = jnp.sum(earlier * onehot_dev, axis=1)
    slot_index = target * capacity + send_rank
    row_ids = jnp.arange(rows_here, dtype=jnp.int32)
    slot_ids = jnp.arange(slot_total, dtype=jnp.int32)
    match_send = (slot_index[None, :] == slot_ids[:, None]).astype(jnp.int32)
    filled = jnp.sum(match_send, axis=1)
    source_row = jnp.sum(match_send * row_ids[None, :], axis=1)
    outgoing = first[source_row].reshape(devices, capacity, channels)
    out_places = jnp.where(filled > 0, place_at[source_row], -1).reshape(devices, capacity)
    incoming, in_places = (
        lax.all_to_all(outgoing, ("grp", "seq"), split_axis=0, concat_axis=0, tiled=True),
        lax.all_to_all(out_places, ("grp", "seq"), split_axis=0, concat_axis=0, tiled=True),
    )
    incoming = incoming.reshape(-1, channels)
    in_places = in_places.reshape(-1)
    match_recv = (in_places[None, :] == row_ids[:, None]).astype(jnp.int32)
    pick_slot = jnp.sum(match_recv * slot_ids[None, :], axis=1)
    second = incoming[pick_slot]
    normed_two = layer_norm(second, norm_gains[2])
    proj_two = jnp.dot(normed_two, w_qkv[1], preferred_element_type=jnp.float32)
    queries_two = proj_two[:, :channels].astype(jnp.bfloat16)
    key_two = (
        proj_two[:, channels : 2 * channels].astype(jnp.bfloat16).reshape(patches, PATCH, channels)
    )
    value_two = proj_two[:, 2 * channels :].astype(jnp.bfloat16).reshape(patches, PATCH, channels)
    key_rows_two = jnp.concatenate([key_two[:, None], key_two[pattern_second]], axis=1).reshape(
        patches, -1, channels
    )
    value_rows_two = jnp.concatenate(
        [value_two[:, None], value_two[pattern_second]], axis=1
    ).reshape(patches, -1, channels)
    features = finish(
        second,
        attend(queries_two, key_rows_two, value_rows_two),
        1,
        norm_gains,
        w_proj,
        w_up,
        w_down,
    )
    normals = lax.dot_general(
        w_head, features, (((1,), (1,)), ((), ())), preferred_element_type=jnp.float32
    )
    return (features, normals)


def solution(mesh):
    placed = (
        P(("grp", "seq"), None),
        P(("grp", "seq"), None),
        P(("grp", "seq"), None),
        P(("grp", "seq")),
        P(),
        P(),
        P(),
        P(),
        P(),
        P(),
    )
    return jax.shard_map(
        shards,
        mesh=mesh,
        in_specs=placed,
        out_specs=(P(("grp", "seq"), None), P(None, ("grp", "seq"))),
        check_vma=False,
    )
```

profile of v0, /device:TPU:0, one launch (start us, length us, event | category | flops | bytes accessed | tf_op | source)
XLA Modules:
  0.0 256.1 jit_solution(8328696567048389240)
XLA Ops:
  7.2 1.3 copy.51
  8.5 0.9 fusion.239
  9.7 2.5 convolution_convert_fusion.1
  12.2 1.1 fusion.238
  13.4 0.7 all-gather.3.cloned.1.call-update
  14.1 1.2 reduce-window.6
  16.3 6.9 %gather_fusion.3 = s32[1024]{0:T(1024)S(1)} fusion(s32[512]{0:T(512)S(1)} %get-tuple-element.20, s32[1024]{0:T(1024)S(1)} %broadcast_clamp_fusion), kind=kCustom, calls=%fused_computation.3 | custom fusion | bytes 12288 | tf_op jit(solution)/shard_map/gather | solution.py:101
  23.2 0.7 select_n.61
  23.9 7.8 %all-to-all-start.1 = ((s32[32,1,32]{2,1,0:T(1,128)}), s32[32,1,32]{2,1,0:T(1,128)S(1)}, u32[]{:S(2)}, u32[]{:S(2)}) async-start(s32[32,1,32]{2,1,0:T(1,128)} %select_n.61), calls=%async_computation.1 | async-start | bytes 32768 | tf_op jit(solution)/shard_map/all_to_all | solution.py:104
  31.9 1.6 reshape.159
  33.4 30.3 %all-gather.5.cloned.1.call-done = bf16[4096,512]{1,0:T(8,128)(2,1)} async-done(((bf16[512,512]{1,0:T(8,128)(2,1)}), bf16[4096,512]{1,0:T(8,128)(2,1)}) %all-gather.5.cloned.1.call-update) | async-done | bytes 4194320 | tf_op jit(solution)/shard_map/all_gather | solution.py:68
  63.7 4.1 %gather_fusion.1 = bf16[24,64,512]{2,1,0:T(8,128)(2,1)} fusion(bf16[64,64,512]{2,1,0:T(8,128)(2,1)} %bitcast.136, s32[1024]{0:T(1024)S(1)} %pad_clamp_fusion.2), kind=kCustom, calls=%fused_computation.1 | custom fusion | bytes 3145824 | tf_op jit(solution)/shard_map/gather | solution.py:71
  67.8 1.6 pad_maximum_fusion.1
  69.4 3.6 %reshape_reshape.13 = bf16[8,256,8,64]{3,2,1,0:T(8,128)(2,1)} reshape(bf16[8,4,64,512]{3,2,1,0:T(8,128)(2,1)S(1)} %pad_maximum_fusion.1) | data formatting | bytes 4194304 | tf_op jit(solution)/shard_map/reshape;reshape | solution.py:22
  73.0 4.1 %fusion.14 = f32[8,8,64,256]{3,2,1,0:T(8,128)S(1)} fusion(bf16[8,256,8,64]{3,2,1,0:T(8,128)(2,1)} %reshape_reshape.13, bf16[8,64,8,64]{3,2,1,0:T(8,128)(2,1)} %reshape.159), kind=kOutput, calls=%fused_computation.23 | convolution fusion | flops 134217728 | bytes 6815744 | tf_op jit(solution)/shard_map/nqhd,nkhd->nhqk/dot_general | solution.py:24
  77.2 2.0 copy-done.5
  79.1 1.4 fusion.240
  80.5 31.2 %all-gather.3.cloned.1.call-done = bf16[4096,512]{1,0:T(8,128)(2,1)} async-done(((bf16[512,512]{1,0:T(8,128)(2,1)}), bf16[4096,512]{1,0:T(8,128)(2,1)}) %all-gather.3.cloned.1.call-update) | async-done | bytes 4194320 | tf_op jit(solution)/shard_map/all_gather | solution.py:69
  111.8 4.1 %gather_fusion = bf16[24,64,512]{2,1,0:T(8,128)(2,1)} fusion(bf16[64,64,512]{2,1,0:T(8,128)(2,1)} %bitcast.135, s32[1024]{0:T(1024)S(1)} %pad_clamp_fusion.2), kind=kCustom, calls=%fused_computation | custom fusion | bytes 3145824 | tf_op jit(solution)/shard_map/gather | solution.py:72
  115.9 1.6 pad_maximum_fusion
  117.5 3.7 %reshape_reshape.12 = bf16[8,256,8,64]{3,2,1,0:T(8,128)(2,1)} reshape(bf16[8,4,64,512]{3,2,1,0:T(8,128)(2,1)S(1)} %pad_maximum_fusion) | data formatting | bytes 4194304 | tf_op jit(solution)/shard_map/reshape;reshape | solution.py:23
  121.1 13.3 %fusion.75 = bf16[8,64,8,64]{1,3,2,0:T(8,128)(2,1)S(1)} fusion(f32[8,8,64]{2,1,0:T(8,128)S(1)} %fusion.240, bf16[8,256,8,64]{3,2,1,0:T(8,128)(2,1)} %reshape_reshape.12, f32[8,8,64,256]{3,2,1,0:T(8,128)} %copy-done.5), kind=kOutput, calls=%fused_computation.109 | convolution fusion | flops 139727104 | bytes 6832128 | tf_op jit(solution)/shard_map/nhqk,nkhd->nqhd/dot_general | solution.py:28
  134.5 0.9 copy.58
  136.0 1.5 convert_reduce_fusion.3
  137.8 13.8 %fusion.92 = bf16[512,512]{0,1:T(8,128)(2,1)S(1)} fusion(bf16[2,2048,512]{2,1,0:T(8,128)(2,1)} %param.18, bf16[2,512,2048]{2,1,0:T(8,128)(2,1)} %param.17, bf16[512,512]{0,1:T(8,128)(2,1)S(1)} %get-tuple-element.23, f32[512]{0:T(512)S(1)} %bitcast.144, f32[512]{0:T(512)S(1)} %add_rsqrt_fusion.2, f32[512]{0:T(512)S(1)} %broadcast_multiply_fusion.2), kind=kOutput, calls=%fused_computation.112 | convolution fusion | flops 2217738240 | bytes 5773312 | tf_op jit(solution)/shard_map/dot_general | solution.py:42
  151.8 5.1 %gather_fusion.2 = bf16[1024,512]{1,0:T(8,128)(2,1)} fusion(bf16[512,512]{1,0:T(8,128)(2,1)S(1)} %copy.61, s32[1024]{0:T(1024)S(1)} %broadcast_clamp_fusion), kind=kCustom, calls=%fused_computation.2 | custom fusion | bytes 2101248 | tf_op jit(solution)/shard_map/gather | solution.py:100
  156.9 3.3 %all-to-all-start = ((bf16[32,32,512]{2,1,0:T(8,128)(2,1)}), bf16[32,32,512]{2,1,0:T(8,128)(2,1)S(1)}, u32[]{:S(2)}, u32[]{:S(2)}) async-start(bf16[32,32,512]{2,1,0:T(8,128)(2,1)} %bitcast.19), calls=%async_computation | async-start | bytes 2097152 | tf_op jit(solution)/shard_map/all_to_all | solution.py:103
  160.9 0.7 reduce.5
  162.0 25.8 %all-to-all-done = bf16[32,32,512]{2,1,0:T(8,128)(2,1)S(1)} async-done(((bf16[32,32,512]{2,1,0:T(8,128)(2,1)}), bf16[32,32,512]{2,1,0:T(8,128)(2,1)S(1)}, u32[]{:S(2)}, u32[]{:S(2)}) %all-to-all-start) | async-done | bytes 1048608 | tf_op jit(solution)/shard_map/all_to_all | solution.py:103
  187.8 2.0 gather_fusion.4
  190.8 2.5 convolution_convert_fusion
  193.4 0.9 fusion.237
  194.3 1.9 gather_fusion.6
  196.1 1.6 pad_maximum_fusion.3
  197.7 3.7 %reshape_reshape.15 = bf16[8,256,8,64]{3,2,1,0:T(8,128)(2,1)} reshape(bf16[8,4,64,512]{3,2,1,0:T(8,128)(2,1)S(1)} %pad_maximum_fusion.3) | data formatting | bytes 4194304 | tf_op jit(solution)/shard_map/reshape;reshape | solution.py:22
  201.4 1.6 reshape.165
  203.0 3.8 %fusion.10 = f32[8,8,64,256]{3,2,1,0:T(8,128)S(1)} fusion(bf16[8,256,8,64]{3,2,1,0:T(8,128)(2,1)} %reshape_reshape.15, bf16[8,64,8,64]{3,2,1,0:T(8,128)(2,1)S(1)} %reshape.165), kind=kOutput, calls=%fused_computation.19 | convolution fusion | flops 134217728 | bytes 6815744 | tf_op jit(solution)/shard_map/nqhd,nkhd->nhqk/dot_general | solution.py:24
  206.8 1.9 copy-done.6
  208.7 1.4 fusion.241
  210.1 1.9 gather_fusion.5
  212.0 1.6 pad_maximum_fusion.2
  213.6 3.6 %reshape_reshape.14 = bf16[8,256,8,64]{3,2,1,0:T(8,128)(2,1)} reshape(bf16[8,4,64,512]{3,2,1,0:T(8,128)(2,1)S(1)} %pad_maximum_fusion.2) | data formatting | bytes 4194304 | tf_op jit(solution)/shard_map/reshape;reshape | solution.py:23
  217.2 13.3 %fusion.72 = bf16[8,64,8,64]{1,3,2,0:T(8,128)(2,1)S(1)} fusion(f32[8,8,64]{2,1,0:T(8,128)S(1)} %fusion.241, bf16[8,256,8,64]{3,2,1,0:T(8,128)(2,1)} %reshape_reshape.14, f32[8,8,64,256]{3,2,1,0:T(8,128)} %copy-done.6), kind=kOutput, calls=%fused_computation.108 | convolution fusion | flops 139727104 | bytes 6832128 | tf_op jit(solution)/shard_map/nhqk,nkhd->nqhd/dot_general | solution.py:28
  230.6 0.9 copy.69
  232.1 1.5 convert_reduce_fusion.1
  233.8 13.4 %fusion.99 = bf16[512,512]{0,1:T(8,128)(2,1)S(1)} fusion(bf16[2,2048,512]{2,1,0:T(8,128)(2,1)} %param.18, bf16[2,512,2048]{2,1,0:T(8,128)(2,1)} %param.17, bf16[512,512]{0,1:T(8,128)(2,1)S(1)} %get-tuple-element.25, f32[512]{0:T(512)S(1)} %bitcast.142, f32[512]{0:T(512)S(1)} %add_rsqrt_fusion, f32[512]{0:T(512)S(1)} %broadcast_multiply_fusion), kind=kOutput, calls=%fused_computation.113 | convolution fusion | flops 2217738240 | bytes 5773312 | tf_op jit(solution)/shard_map/dot_general | solution.py:42
  247.2 1.0 copy.71
  248.3 0.8 convolution_bitcast_fusion
  (64 shorter events, 5.6 us)
Async XLA Ops:
  7.2 241.1 %copy-start = (bf16[3,512]{1,0:T(4,128)(2,1)S(1)}, bf16[3,512]{1,0:T(4,128)(2,1)}, u32[]{:S(2)}) copy-start(bf16[3,512]{1,0:T(4,128)(2,1)} %param.19) | copy-start | bytes 9220
  7.2 56.5 %all-gather.5.cloned.1.call-start = ((), (), s32[]{:S(2)}) async-start(), calls=%async_computation.3 | async-start | bytes 4718592 | tf_op jit(solution)/shard_map/all_gather | solution.py:68
  9.7 4.4 %copy-start.7 = (s32[512]{0:T(512)S(1)}, s32[512]{0:T(512)}, u32[]{:S(2)}) copy-start(s32[512]{0:T(512)} %param.13) | copy-start | bytes 6148
  12.2 19.5 %copy-start.8 = (s32[8,3]{0,1:T(4,128)S(1)}, s32[8,3]{0,1:T(4,128)}, u32[]{:S(2)}) copy-start(s32[8,3]{0,1:T(4,128)} %param.11) | copy-start | bytes 292
  13.3 98.5 %all-gather.3.cloned.1.call-start = ((), (), s32[]{:S(2)}) async-start(), calls=%async_computation.2 | async-start | bytes 4718592 | tf_op jit(solution)/shard_map/all_gather | solution.py:69
  16.3 51.5 %copy-start.4 = (bf16[512,512]{1,0:T(8,128)(2,1)S(1)}, bf16[512,512]{1,0:T(8,128)(2,1)}, u32[]{:S(2)}) copy-start(bf16[512,512]{1,0:T(8,128)(2,1)} %get-tuple-element.14) | copy-start | bytes 1572868
  23.9 133.0 %all-to-all-start.1 = ((s32[32,1,32]{2,1,0:T(1,128)}), s32[32,1,32]{2,1,0:T(1,128)S(1)}, u32[]{:S(2)}, u32[]{:S(2)}) async-start(s32[32,1,32]{2,1,0:T(1,128)} %select_n.61), calls=%async_computation.1 | async-start | bytes 32768 | tf_op jit(solution)/shard_map/all_to_all | solution.py:104
  77.2 2.0 copy-start.5
  79.1 36.8 %copy-start.3 = (bf16[512,512]{1,0:T(8,128)(2,1)S(1)}, bf16[512,512]{1,0:T(8,128)(2,1)}, u32[]{:S(2)}) copy-start(bf16[512,512]{1,0:T(8,128)(2,1)} %get-tuple-element.13) | copy-start | bytes 1572868
  151.8 8.4 %copy-start.9 = (s32[8,3]{0,1:T(4,128)S(1)}, s32[8,3]{0,1:T(4,128)}, u32[]{:S(2)}) copy-start(s32[8,3]{0,1:T(4,128)} %param.12) | copy-start | bytes 292
  156.9 30.9 %all-to-all-start = ((bf16[32,32,512]{2,1,0:T(8,128)(2,1)}), bf16[32,32,512]{2,1,0:T(8,128)(2,1)S(1)}, u32[]{:S(2)}, u32[]{:S(2)}) async-start(bf16[32,32,512]{2,1,0:T(8,128)(2,1)} %bitcast.19), calls=%async_computation | async-start | bytes 2097152 | tf_op jit(solution)/shard_map/all_to_all | solution.py:103
  190.0 0.8 copy-start.1
  206.8 1.9 copy-start.6
  217.2 14.9 %copy-start.2 = (bf16[512,512]{0,1:T(8,128)(2,1)S(1)}, bf16[512,512]{0,1:T(8,128)(2,1)}, u32[]{:S(2)}) copy-start(bf16[512,512]{0,1:T(8,128)(2,1)} %copy-done.1) | copy-start | bytes 1572868
Sparse Core Ops, SparseCore 0:
  13.4 50.2 all-gather.4
  65.9 45.8 all-gather.2
where the time goes:
time: 260 us; the launch traced here: 256 us
  waiting for transfers between devices  88 us (34%)
  matrix products  70.6 us (27%)
  local copies, waits for them, and re-layouts  58.5 us (22%)
  between operations  14.6 us (6%)
  other arithmetic  13.1 us (5%)
  starting transfers between devices  11.2 us (4%)
    all_gather x1, waiting for transfers between devices, shards(): lax.all_gather(value_flat, 'seq', axis=0, tiled=True)  31.2 us
    all_gather x1, waiting for transfers between devices, shards(): lax.all_gather(key_flat, 'seq', axis=0, tiled=True)  30.3 us
    dot_general x2, matrix products, finish(): jnp.dot(act, w_down[section], preferred_element_type=jnp.float32)  27.2 us
    dot_general x2, matrix products, attend(): jnp.einsum('nhqk,nkhd->nqhd', probs, vh, preferred_element_type=jnp.float32)  26.7 us
    all_to_all x1, waiting for transfers between devices, shards(): lax.all_to_all(outgoing, ('grp', 'seq'), split_axis=0, concat_axis=0, til...  25.8 us
    dot_general x2, matrix products, attend(): jnp.einsum('nqhd,nkhd->nhqk', qh, kh, preferred_element_type=jnp.float32)  7.86 us
    all_to_all x1, starting transfers between devices, shards(): lax.all_to_all(out_places, ('grp', 'seq'), split_axis=0, concat_axis=0, t...  7.76 us
    another operation x2, local copies, waits for them, and re-layouts, attend(): vh = value_rows.reshape(count, -1, HEADS, head_dim)  7.29 us
  transfers between devices with their start and end apart: 4, of which 3 were waited for; matrix products, arithmetic and copies ran while one was open for 29% of the time, Pallas kernels for 0%

commit v1 on v0

v1 whole, which is shorter than its diff:
```python
import functools

import jax
import jax.numpy as jnp
from jax import lax
from jax.experimental import pallas as pl
from jax.experimental.pallas import tpu as pltpu
from jax.sharding import PartitionSpec as P

HEADS = 8
PATCH = 64
HEADS_TOGETHER = 4
VMEM_BYTES = 48 * 1024 * 1024
F32 = jnp.float32
BF16 = jnp.bfloat16


def layer_norm(rows, gains):
    values = rows.astype(F32)
    average = jnp.mean(values, axis=-1, keepdims=True)
    spread = jnp.mean((values - average) ** 2, axis=-1, keepdims=True)
    return ((values - average) * lax.rsqrt(spread + 1e-05) * gains).astype(BF16)


def head_masks(head_dim):
    lane = lax.broadcasted_iota(jnp.int32, (PATCH, HEADS_TOGETHER * head_dim), 1)
    return [
        jnp.where((lane >= h * head_dim) & (lane < (h + 1) * head_dim), 1.0, 0.0).astype(F32)
        for h in range(HEADS_TOGETHER)
    ]


def attend_patch(queries, key_rows, value_rows, masks):
    channels = queries.shape[1]
    width = HEADS_TOGETHER * (channels // HEADS)
    sides = []
    for at in range(0, channels, width):
        q = queries[:, at : at + width]
        stacked = jnp.concatenate([q * mask.astype(BF16) for mask in masks], axis=0)
        scores = lax.dot_general(
            stacked,
            key_rows[:, at : at + width],
            (((1,), (1,)), ((), ())),
            preferred_element_type=F32,
        )
        top = jnp.max(scores, axis=-1, keepdims=True)
        grown = jnp.exp(scores - top)
        total = jnp.sum(grown, axis=-1, keepdims=True)
        weights = (grown * (1.0 / total)).astype(BF16)
        mixed = jnp.dot(weights, value_rows[:, at : at + width], preferred_element_type=F32)
        side = mixed[:PATCH] * masks[0]
        for h in range(1, HEADS_TOGETHER):
            side = side + mixed[h * PATCH : (h + 1) * PATCH] * masks[h]
        sides.append(side.astype(BF16))
    return jnp.concatenate(sides, axis=1)


def weight_copies(section, sources, held, sems):
    return [
        pltpu.make_async_copy(source.at[section], kept, sems.at[at])
        for at, (source, kept) in enumerate(zip(sources, held))
    ]


def finish(rows, attended, gain, held, copies):
    w_proj, w_up, w_down = held
    copies[0].wait()
    first = (
        rows.astype(F32) + jnp.dot(attended, w_proj[...], preferred_element_type=F32)
    ).astype(BF16)
    hidden = layer_norm(first, gain)
    total = first.astype(F32)
    copies[1].wait()
    copies[2].wait()
    piece = 512
    for at in range(0, w_up.shape[1], piece):
        upper = jnp.dot(hidden, w_up[:, at : at + piece], preferred_element_type=F32)
        act = (upper * (0.5 + 0.5 * lax.erf(upper * 0.5**0.5))).astype(BF16)
        total = total + jnp.dot(act, w_down[at : at + piece, :], preferred_element_type=F32)
    return total.astype(BF16)


def first_kernel(
    pattern,
    points,
    normed,
    gathered,
    gains,
    w_qkv,
    w_proj,
    w_up,
    w_down,
    send,
    outgoing,
    keyed,
    kv,
    attended,
    qkv_held,
    proj_held,
    up_held,
    down_held,
    sems,
    weight_sems,
):
    rows, channels = points.shape
    patches, chosen = pattern.shape
    span = (1 + chosen) * PATCH
    copies = []
    for p in range(patches):
        for j in range(chosen):
            start = pl.multiple_of(pattern[p, j] * PATCH, PATCH)
            copies.append(
                pltpu.make_async_copy(
                    gathered.at[pl.ds(start, PATCH), :],
                    keyed.at[pl.ds(p * span + (1 + j) * PATCH, PATCH), :],
                    sems.at[p, j],
                )
            )
    fetches = weight_copies(
        0, (w_qkv, w_proj, w_up, w_down), (qkv_held, proj_held, up_held, down_held), weight_sems
    )
    fetches[0].start()
    for copy in copies:
        copy.start()
    for fetch in fetches[1:]:
        fetch.start()
    for p in range(patches):
        keyed[p * span : p * span + PATCH, :] = normed[p * PATCH : (p + 1) * PATCH, :]
    scale = (channels // HEADS) ** (-0.5)
    fetches[0].wait()
    queries = (
        jnp.dot(normed[...], qkv_held[:, :channels], preferred_element_type=F32).astype(BF16)
        * BF16(scale)
    ).astype(BF16)
    masks = head_masks(channels // HEADS)
    for copy in copies:
        copy.wait()
    for p in range(patches):
        kv[p * span : (p + 1) * span, :] = jnp.dot(
            keyed[p * span : (p + 1) * span, :], qkv_held[:, channels:], preferred_element_type=F32
        ).astype(BF16)
    for p in range(patches):
        attended[p * PATCH : (p + 1) * PATCH, :] = attend_patch(
            queries[p * PATCH : (p + 1) * PATCH, :],
            kv[p * span : (p + 1) * span, :channels],
            kv[p * span : (p + 1) * span, channels:],
            masks,
        )
    first = finish(
        points[...], attended[...], gains[1:2, :], (proj_held, up_held, down_held), fetches[1:]
    )
    outgoing[...] = jnp.dot(send[...], first, preferred_element_type=F32).astype(BF16)


def second_kernel(
    pattern,
    incoming,
    place,
    gains,
    w_qkv,
    w_proj,
    w_up,
    w_down,
    w_head,
    features,
    normals,
    kv,
    attended,
    qkv_held,
    proj_held,
    up_held,
    down_held,
    weight_sems,
):
    rows, channels = features.shape
    patches, chosen = pattern.shape
    fetches = weight_copies(
        1, (w_qkv, w_proj, w_up, w_down), (qkv_held, proj_held, up_held, down_held), weight_sems
    )
    for fetch in fetches:
        fetch.start()
    second = jnp.dot(place[...], incoming[...], preferred_element_type=F32).astype(BF16)
    normed = layer_norm(second, gains[2:3, :])
    scale = (channels // HEADS) ** (-0.5)
    fetches[0].wait()
    queries = (
        jnp.dot(normed, qkv_held[:, :channels], preferred_element_type=F32).astype(BF16)
        * BF16(scale)
    ).astype(BF16)
    kv[...] = jnp.dot(normed, qkv_held[:, channels:], preferred_element_type=F32).astype(BF16)
    masks = head_masks(channels // HEADS)
    for p in range(patches):
        pieces = [kv[p * PATCH : (p + 1) * PATCH, :]]
        for j in range(chosen):
            start = pl.multiple_of(pattern[p, j] * PATCH, PATCH)
            pieces.append(kv[pl.ds(start, PATCH), :])
        both = jnp.concatenate(pieces, axis=0)
        attended[p * PATCH : (p + 1) * PATCH, :] = attend_patch(
            queries[p * PATCH : (p + 1) * PATCH, :], both[:, :channels], both[:, channels:], masks
        )
    done = finish(
        second, attended[...], gains[3:4, :], (proj_held, up_held, down_held), fetches[1:]
    )
    features[...] = done
    normals[...] = lax.dot_general(
        w_head[...], done, (((1,), (1,)), ((), ())), preferred_element_type=F32
    )


def held_weights(weights):
    return [pltpu.VMEM(w.shape[1:], BF16) for w in weights]


VMEM_SPEC = pl.BlockSpec(memory_space=pltpu.VMEM)
SMEM_SPEC = pl.BlockSpec(memory_space=pltpu.SMEM)
ANY_SPEC = pl.BlockSpec(memory_space=pl.ANY)


def shards(
    points,
    pattern_first,
    pattern_second,
    destination,
    norm_gains,
    w_qkv,
    w_proj,
    w_up,
    w_down,
    w_head,
):
    rows_here, channels = points.shape
    patches, chosen = pattern_first.shape
    devices = lax.axis_size("grp") * lax.axis_size("seq")
    capacity = 2 * rows_here // devices
    slot_total = devices * capacity

    normed = layer_norm(points, norm_gains[0])
    gathered = lax.all_gather(normed, "seq", axis=0, tiled=True)

    target = destination // rows_here
    place_at = destination % rows_here
    onehot_dev = (target[:, None] == jnp.arange(devices, dtype=jnp.int32)[None, :]).astype(
        jnp.int32
    )
    earlier = jnp.cumsum(onehot_dev, axis=0) - onehot_dev
    send_rank = jnp.sum(earlier * onehot_dev, axis=1)
    slot_index = target * capacity + send_rank
    row_ids = jnp.arange(rows_here, dtype=jnp.int32)
    slot_ids = jnp.arange(slot_total, dtype=jnp.int32)
    match_send = slot_index[None, :] == slot_ids[:, None]
    send = match_send.astype(BF16)
    out_places = jnp.sum(jnp.where(match_send, place_at[None, :] + 1, 0), axis=1) - 1
    in_places = lax.all_to_all(
        out_places.reshape(devices, capacity),
        ("grp", "seq"),
        split_axis=0,
        concat_axis=0,
        tiled=True,
    ).reshape(-1)
    place = (in_places[None, :] == row_ids[:, None]).astype(BF16)

    weights = (w_qkv, w_proj, w_up, w_down)
    keyed_rows = patches * (1 + chosen) * PATCH
    outgoing = pl.pallas_call(
        first_kernel,
        out_shape=jax.ShapeDtypeStruct((slot_total, channels), BF16),
        in_specs=[SMEM_SPEC, VMEM_SPEC, VMEM_SPEC, ANY_SPEC, VMEM_SPEC]
        + [ANY_SPEC] * len(weights)
        + [VMEM_SPEC],
        out_specs=VMEM_SPEC,
        scratch_shapes=[
            pltpu.VMEM((keyed_rows, channels), BF16),
            pltpu.VMEM((keyed_rows, 2 * channels), BF16),
            pltpu.VMEM((rows_here, channels), BF16),
            *held_weights(weights),
            pltpu.SemaphoreType.DMA((patches, chosen)),
            pltpu.SemaphoreType.DMA((len(weights),)),
        ],
        compiler_params=pltpu.CompilerParams(vmem_limit_bytes=VMEM_BYTES),
        name="block_first",
    )(pattern_first, points, normed, gathered, norm_gains, *weights, send)

    incoming = lax.all_to_all(
        outgoing.reshape(devices, capacity, channels),
        ("grp", "seq"),
        split_axis=0,
        concat_axis=0,
        tiled=True,
    ).reshape(slot_total, channels)

    return pl.pallas_call(
        second_kernel,
        out_shape=(
            jax.ShapeDtypeStruct((rows_here, channels), BF16),
            jax.ShapeDtypeStruct((w_head.shape[0], rows_here), F32),
        ),
        in_specs=[SMEM_SPEC, VMEM_SPEC, VMEM_SPEC, VMEM_SPEC]
        + [ANY_SPEC] * len(weights)
        + [VMEM_SPEC],
        out_specs=(VMEM_SPEC, VMEM_SPEC),
        scratch_shapes=[
            pltpu.VMEM((rows_here, 2 * channels), BF16),
            pltpu.VMEM((rows_here, channels), BF16),
            *held_weights(weights),
            pltpu.SemaphoreType.DMA((len(weights),)),
        ],
        compiler_params=pltpu.CompilerParams(vmem_limit_bytes=VMEM_BYTES),
        name="block_second",
    )(pattern_second, incoming, place, norm_gains, *weights, w_head)


def solution(mesh):
    placed = (
        P(("grp", "seq"), None),
        P(("grp", "seq"), None),
        P(("grp", "seq"), None),
        P(("grp", "seq")),
        P(),
        P(),
        P(),
        P(),
        P(),
        P(),
    )
    return jax.shard_map(
        shards,
        mesh=mesh,
        in_specs=placed,
        out_specs=(P(("grp", "seq"), None), P(None, ("grp", "seq"))),
        check_vma=False,
    )
```

time: 260 us -> 123 us (0.47); the launches traced: 256 us -> 123 us
  matrix products: 70.6 us -> 0 us
  local copies, waits for them, and re-layouts: 58.5 us -> 2.41 us
  waiting for transfers between devices: 88 us -> 65.7 us
  Pallas kernels: 0 us -> 22 us
  other arithmetic: 13.1 us -> 7.74 us
    dot_general x11 -> x0, matrix products: 70.6 us -> none  [the longest x2 27.2 us: finish(): jnp.dot(act, w_down[section], preferred_element_type=jnp.float32)]
    gather x8 -> x0, local copies, waits for them, and re-layouts: 26.1 us -> none  [the longest x1 6.86 us: shards(): place_at[source_row]]
    pallas_call x0 -> x2, Pallas kernels: none -> 22 us  [the longest x1 12.7 us: shards(): pl.pallas_call(first_kernel, out_shape=jax.ShapeDtypeStruct((slot_total,...]
    all_gather x2 -> x1, waiting for transfers between devices: 61.5 us -> 40 us  [shards(): gathered = lax.all_gather(normed, 'seq', axis=0, tiled=True)]
    another operation x5 -> x1, local copies, waits for them, and re-layouts: 14.6 us -> 0.01 us  [the longest x2 7.29 us: attend(): vh = value_rows.reshape(count, -1, HEADS, head_dim)]
    unnamed x22 -> x18, local copies, waits for them, and re-layouts: 6.7 us -> 0.2 us
    concatenate x4 -> x0, other arithmetic: 6.36 us -> none  [the longest x1 1.59 us: shards(): jnp.concatenate([key_own[:, None], key_chosen], axis=1)]
    convert_element_type x5 -> x0, local copies, waits for them, and re-layouts: 3.28 us -> none  [the longest x4 3.06 us: attend(): return mixed.reshape(count * PATCH, channels).astype(jnp.bfloat16)]
  transfers between devices with their start and end apart: 4 -> 3, of which waited for: 3 -> 2; matrix products, arithmetic and copies ran while one was open for 29% -> 4% of each run, Pallas kernels for 0% -> 10%
where the time goes in v1:
time: 123 us
  waiting for transfers between devices  65.7 us (53%)
  Pallas kernels  22 us (18%)
  between operations  14.2 us (12%)
  starting transfers between devices  10.9 us (9%)
  other arithmetic  7.74 us (6%)
  local copies, waits for them, and re-layouts  2.41 us (2%)
    all_gather x1, waiting for transfers between devices, shards(): gathered = lax.all_gather(normed, 'seq', axis=0, tiled=True)  40 us
    all_to_all x1, waiting for transfers between devices, shards(): lax.all_to_all(outgoing.reshape(devices, capacity, channels), ('grp', 'se...  25.7 us
    pallas_call x1, Pallas kernels, shards(): pl.pallas_call(first_kernel, out_shape=jax.ShapeDtypeStruct((slot_total,...  12.7 us
    pallas_call x1, Pallas kernels, shards(): pl.pallas_call(second_kernel, out_shape=(jax.ShapeDtypeStruct((rows_here,...  9.31 us
    all_to_all x1, starting transfers between devices, shards(): lax.all_to_all(out_places.reshape(devices, capacity), ('grp', 'seq'), spl...  7.3 us
    all_to_all x1, starting transfers between devices, shards(): lax.all_to_all(outgoing.reshape(devices, capacity, channels), ('grp', 'se...  3.53 us
  transfers between devices with their start and end apart: 3, of which 2 were waited for; matrix products, arithmetic and copies ran while one was open for 4% of the time, Pallas kernels for 10%

profile of v1, /device:TPU:0, one launch (start us, length us, event | category | flops | bytes accessed | tf_op | source)
XLA Modules:
  0.0 123.0 jit_solution(16295876621175398629)
XLA Ops:
  7.2 0.0 copy-start
  7.2 0.0 copy-start.3
  7.2 0.0 copy-start.5
  7.2 0.0 copy-start.6
  7.2 0.0 copy-start.2
  7.2 0.0 all-gather.2.cloned.1.call-start
  7.3 1.3 %convert_reduce_fusion = f32[512]{0:T(512)S(1)} fusion(bf16[512,512]{1,0:T(8,128)(2,1)} %points.1), kind=kLoop, calls=%fused_computation.6 | loop fusion | flops 523776 | bytes 526336 | tf_op jit(solution)/shard_map/reduce_sum | solution.py:20
  8.6 1.3 %fusion.4 = f32[512]{0:T(512)S(1)} fusion(bf16[512,512]{1,0:T(8,128)(2,1)} %points.1, f32[512]{0:T(512)S(1)} %broadcast_multiply_fusion), kind=kLoop, calls=%fused_computation.9 | loop fusion | flops 1048064 | bytes 528384 | tf_op jit(solution)/shard_map/reduce_sum | solution.py:21
  9.9 0.7 slice.9
  10.6 2.1 %fusion.6.normed = bf16[512,512]{1,0:T(8,128)(2,1)} fusion(bf16[512,512]{1,0:T(8,128)(2,1)} %points.1, f32[512]{0:T(512)S(1)} %bitcast.25, f32[512]{0:T(512)S(1)} %add_rsqrt_fusion, f32[512]{0:T(512)S(1)} %broadcast_multiply_fusion), kind=kLoop, calls=%fused_computation.11 | loop fusion | flops 1310720 | bytes 1054720 | tf_op jit(solution)/shard_map/convert_element_type | solution.py:22
  12.7 0.0 copy-start.1
  12.7 0.0 all-gather.2.cloned.1.call-update
  12.7 0.0 copy-done.5
  12.8 1.2 reduce-window.6
  13.9 0.2 slice_reduce_fusion
  14.2 0.1 fusion.9
  14.3 0.3 select_reduce_fusion
  14.6 0.7 sub.32
  15.3 7.3 %all-to-all-start.1 = ((s32[32,1,32]{2,1,0:T(1,128)}), s32[32,1,32]{2,1,0:T(1,128)S(1)}, u32[]{:S(2)}, u32[]{:S(2)}) async-start(s32[32,1,32]{2,1,0:T(1,128)} %sub.32), calls=%async_computation.1 | async-start | bytes 32768 | tf_op jit(solution)/shard_map/all_to_all | solution.py:253
  22.6 0.4 fusion.send
  23.0 0.0 copy-done.6
  23.0 0.1 copy.15.pattern
  23.1 40.0 %all-gather.2.cloned.1.call-done.gathered = bf16[4096,512]{1,0:T(8,128)(2,1)} async-done(((bf16[512,512]{1,0:T(8,128)(2,1)}), bf16[4096,512]{1,0:T(8,128)(2,1)}) %all-gather.2.cloned.1.call-update) | async-done | bytes 4194320 | tf_op jit(solution)/shard_map/all_gather | solution.py:238
  63.1 0.0 copy-done
  63.1 0.0 copy-done.3
  63.1 0.0 copy-done.2
  63.1 0.0 copy-done.1
  63.1 12.7 %block_first.1 = bf16[1024,512]{1,0:T(8,128)(2,1)} custom-call(s32[8,3]{1,0:T(8,128)S(1)} %copy.15.pattern, bf16[512,512]{1,0:T(8,128)(2,1)S(1)} %copy-done, bf16[512,512]{1,0:T(8,128)(2,1)S(1)} %copy-done.1, bf16[4096,512]{1,0:T(8,128)(2,1)} %all-gather.2.cloned.1.call-done.gathered, f32[4,512]{1,0:T(4,128)S(1)} %copy-done.3, bf16[2,512,1536]{2,1,0:T(8,128)(2,1)} %w_qkv.3, ...), custom_call_target="tpu_custom_call" | custom-call | tf_op jit(solution)/shard_map/block_first/pallas_call | solution.py:264
  75.8 0.0 copy-start.7
  75.8 0.0 copy-start.4
  75.9 0.0 all-to-all-done.1
  75.9 3.5 %all-to-all-start = ((bf16[32,32,512]{2,1,0:T(8,128)(2,1)}), bf16[32,32,512]{2,1,0:T(8,128)(2,1)S(1)}, u32[]{:S(2)}, u32[]{:S(2)}) async-start(bf16[32,32,512]{2,1,0:T(8,128)(2,1)} %bitcast.3), calls=%async_computation | async-start | bytes 2097152 | tf_op jit(solution)/shard_map/all_to_all | solution.py:283
  79.4 0.0 copy-done.7
  79.4 0.1 copy.16.pattern
  79.5 0.5 broadcast.92
  80.0 0.7 reduce.5
  80.7 0.1 eq.63
  80.8 0.3 fusion.1.place
  81.1 25.7 %all-to-all-done = bf16[32,32,512]{2,1,0:T(8,128)(2,1)S(1)} async-done(((bf16[32,32,512]{2,1,0:T(8,128)(2,1)}), bf16[32,32,512]{2,1,0:T(8,128)(2,1)S(1)}, u32[]{:S(2)}, u32[]{:S(2)}) %all-to-all-start) | async-done | bytes 1048608 | tf_op jit(solution)/shard_map/all_to_all | solution.py:283
  106.8 0.0 copy-done.4
  106.8 9.3 %block_second.1 = (bf16[512,512]{1,0:T(8,128)(2,1)}, f32[3,512]{1,0:T(4,128)}) custom-call(s32[8,3]{1,0:T(8,128)S(1)} %copy.16.pattern, bf16[1024,512]{1,0:T(8,128)(2,1)S(1)} %bitcast.23, bf16[512,1024]{1,0:T(8,128)(2,1)S(1)} %fusion.1.place, f32[4,512]{1,0:T(4,128)S(1)} %copy-done.3, bf16[2,512,1536]{2,1,0:T(8,128)(2,1)} %w_qkv.3, ...), custom_call_target="tpu_custom_call" | custom-call | tf_op jit(solution)/shard_map/block_second/pallas_call | solution.py:291
  (8 shorter events, 0.1 us)
Async XLA Ops:
  7.2 56.0 %copy-start = (bf16[512,512]{1,0:T(8,128)(2,1)S(1)}, bf16[512,512]{1,0:T(8,128)(2,1)}, u32[]{:S(2)}) copy-start(bf16[512,512]{1,0:T(8,128)(2,1)} %points.1) | copy-start | bytes 1572868
  7.2 55.9 %copy-start.3 = (f32[4,512]{1,0:T(4,128)S(1)}, f32[4,512]{1,0:T(4,128)}, u32[]{:S(2)}) copy-start(f32[4,512]{1,0:T(4,128)} %gains.3) | copy-start | bytes 24580
  7.2 5.5 %copy-start.5 = (s32[512]{0:T(512)S(1)}, s32[512]{0:T(512)}, u32[]{:S(2)}) copy-start(s32[512]{0:T(512)} %param.13) | copy-start | bytes 6148
  7.2 15.8 %copy-start.6 = (s32[8,3]{0,1:T(4,128)S(1)}, s32[8,3]{0,1:T(4,128)}, u32[]{:S(2)}) copy-start(s32[8,3]{0,1:T(4,128)} %param.11) | copy-start | bytes 292
  7.2 55.9 %copy-start.2 = (bf16[2,512,512]{2,1,0:T(8,128)(2,1)S(1)}, bf16[2,512,512]{2,1,0:T(8,128)(2,1)}, u32[]{:S(2)}) copy-start(bf16[2,512,512]{2,1,0:T(8,128)(2,1)} %w_proj.3) | copy-start | bytes 3145732
  7.2 55.9 %all-gather.2.cloned.1.call-start = ((), (), s32[]{:S(2)}) async-start(), calls=%async_computation.2 | async-start | bytes 4718592 | tf_op jit(solution)/shard_map/all_gather | solution.py:238
  12.7 50.4 %copy-start.1 = (bf16[512,512]{1,0:T(8,128)(2,1)S(1)}, bf16[512,512]{1,0:T(8,128)(2,1)}, u32[]{:S(2)}) copy-start(bf16[512,512]{1,0:T(8,128)(2,1)} %fusion.6.normed) | copy-start | bytes 1572868
  15.3 60.6 %all-to-all-start.1 = ((s32[32,1,32]{2,1,0:T(1,128)}), s32[32,1,32]{2,1,0:T(1,128)S(1)}, u32[]{:S(2)}, u32[]{:S(2)}) async-start(s32[32,1,32]{2,1,0:T(1,128)} %sub.32), calls=%async_computation.1 | async-start | bytes 32768 | tf_op jit(solution)/shard_map/all_to_all | solution.py:253
  75.8 3.6 %copy-start.7 = (s32[8,3]{0,1:T(4,128)S(1)}, s32[8,3]{0,1:T(4,128)}, u32[]{:S(2)}) copy-start(s32[8,3]{0,1:T(4,128)} %param.12) | copy-start | bytes 292
  75.8 31.0 %copy-start.4 = (bf16[3,512]{1,0:T(4,128)(2,1)S(1)}, bf16[3,512]{1,0:T(4,128)(2,1)}, u32[]{:S(2)}) copy-start(bf16[3,512]{1,0:T(4,128)(2,1)} %w_head.1) | copy-start | bytes 9220
  75.9 30.9 %all-to-all-start = ((bf16[32,32,512]{2,1,0:T(8,128)(2,1)}), bf16[32,32,512]{2,1,0:T(8,128)(2,1)S(1)}, u32[]{:S(2)}, u32[]{:S(2)}) async-start(bf16[32,32,512]{2,1,0:T(8,128)(2,1)} %bitcast.3), calls=%async_computation | async-start | bytes 2097152 | tf_op jit(solution)/shard_map/all_to_all | solution.py:283
Sparse Core Ops, SparseCore 0:
  12.8 50.2 all-gather.1

commit v2 on v1

--- a/solution.py
+++ b/solution.py
@@ -10,7 +10,18 @@
 HEADS = 8
 PATCH = 64
 HEADS_TOGETHER = 4
+RING_PARTS = 2
 VMEM_BYTES = 48 * 1024 * 1024
+ERF_TOP = 30.0
+ERF_TERMS = (
+    1.81392502e-09,
+    -1.33783099e-07,
+    3.97406914e-06,
+    -5.52733748e-05,
+    -3.30267412e-05,
+    3.63341492e-02,
+    7.97884268e-01,
+)
 F32 = jnp.float32
 BF16 = jnp.bfloat16
 
@@ -20,6 +31,15 @@
     average = jnp.mean(values, axis=-1, keepdims=True)
     spread = jnp.mean((values - average) ** 2, axis=-1, keepdims=True)
     return ((values - average) * lax.rsqrt(spread + 1e-05) * gains).astype(BF16)
+
+
+def gelu(x):
+    square = jnp.minimum(x * x, ERF_TOP)
+    inner = jnp.full_like(square, ERF_TERMS[0])
+    for term in ERF_TERMS[1:]:
+        inner = inner * square + term
+    half = 0.5 * x
+    return half + half * jnp.tanh(x * inner)
 
 
 def head_masks(head_dim):
@@ -75,27 +95,71 @@
     piece = 512
     for at in range(0, w_up.shape[1], piece):
         upper = jnp.dot(hidden, w_up[:, at : at + piece], preferred_element_type=F32)
-        act = (upper * (0.5 + 0.5 * lax.erf(upper * 0.5**0.5))).astype(BF16)
+        act = gelu(upper).astype(BF16)
         total = total + jnp.dot(act, w_down[at : at + piece, :], preferred_element_type=F32)
     return total.astype(BF16)
+
+
+def project_kernel(slot, *refs):
+    *parts, gains, w_qkv, _, whole, kv, sems = refs
+    channels = w_qkv.shape[1]
+    rows = parts[0].shape[0]
+    copies = []
+    for i, part in enumerate(parts):
+        here = pl.ds(i * rows, rows)
+        normed = layer_norm(part[...], gains[0:1, :])
+        kv[here, :] = jnp.dot(
+            normed, w_qkv[0, :, channels:], preferred_element_type=F32
+        ).astype(BF16)
+        copies.append(
+            pltpu.make_async_copy(
+                kv.at[here, :],
+                whole.at[pl.ds(slot * len(parts) * rows + i * rows, rows), :],
+                sems.at[i],
+            )
+        )
+        copies[-1].start()
+    for copy in copies:
+        copy.wait()
+
+
+def own_kernel(*refs):
+    *parts, gains, w_qkv, whole, queries, kv, sems = refs
+    channels = w_qkv.shape[1]
+    rows = parts[0].shape[0]
+    scale = (channels // HEADS) ** (-0.5)
+    copies = []
+    for i, part in enumerate(parts):
+        here = pl.ds(i * rows, rows)
+        normed = layer_norm(part[...], gains[0:1, :])
+        kv[here, :] = jnp.dot(
+            normed, w_qkv[0, :, channels:], preferred_element_type=F32
+        ).astype(BF16)
+        copies.append(
+            pltpu.make_async_copy(
+                kv.at[here, :], whole.at[pl.ds(i * rows, rows), :], sems.at[i]
+            )
+        )
+        copies[-1].start()
+        own = jnp.dot(normed, w_qkv[0, :, :channels], preferred_element_type=F32).astype(BF16)
+        queries[here, :] = (own * BF16(scale)).astype(BF16)
+    for copy in copies:
+        copy.wait()
 
 
 def first_kernel(
     pattern,
     points,
-    normed,
-    gathered,
+    queries,
+    keyed,
     gains,
-    w_qkv,
     w_proj,
     w_up,
     w_down,
     send,
     outgoing,
-    keyed,
     kv,
     attended,
-    qkv_held,
     proj_held,
     up_held,
     down_held,
@@ -107,39 +171,26 @@
     span = (1 + chosen) * PATCH
     copies = []
     for p in range(patches):
-        for j in range(chosen):
-            start = pl.multiple_of(pattern[p, j] * PATCH, PATCH)
+        for j in range(1 + chosen):
+            start = p * PATCH if j == 0 else pl.multiple_of(pattern[p, j - 1] * PATCH, PATCH)
             copies.append(
                 pltpu.make_async_copy(
-                    gathered.at[pl.ds(start, PATCH), :],
-                    keyed.at[pl.ds(p * span + (1 + j) * PATCH, PATCH), :],
+                    keyed.at[pl.ds(start, PATCH), :],
+                    kv.at[pl.ds(p * span + j * PATCH, PATCH), :],
                     sems.at[p, j],
                 )
             )
-    fetches = weight_copies(
-        0, (w_qkv, w_proj, w_up, w_down), (qkv_held, proj_held, up_held, down_held), weight_sems
-    )
-    fetches[0].start()
     for copy in copies:
         copy.start()
-    for fetch in fetches[1:]:
+    fetches = weight_copies(
+        0, (w_proj, w_up, w_down), (proj_held, up_held, down_held), weight_sems
+    )
+    for fetch in fetches:
         fetch.start()
+    masks = head_masks(channels // HEADS)
     for p in range(patches):
-        keyed[p * span : p * span + PATCH, :] = normed[p * PATCH : (p + 1) * PATCH, :]
-    scale = (channels // HEADS) ** (-0.5)
-    fetches[0].wait()
-    queries = (
-        jnp.dot(normed[...], qkv_held[:, :channels], preferred_element_type=F32).astype(BF16)
-        * BF16(scale)
-    ).astype(BF16)
-    masks = head_masks(channels // HEADS)
-    for copy in copies:
-        copy.wait()
-    for p in range(patches):
-        kv[p * span : (p + 1) * span, :] = jnp.dot(
-            keyed[p * span : (p + 1) * span, :], qkv_held[:, channels:], preferred_element_type=F32
-        ).astype(BF16)
-    for p in range(patches):
+        for j in range(1 + chosen):
+            copies[p * (1 + chosen) + j].wait()
         attended[p * PATCH : (p + 1) * PATCH, :] = attend_patch(
             queries[p * PATCH : (p + 1) * PATCH, :],
             kv[p * span : (p + 1) * span, :channels],
@@ -147,7 +198,7 @@
             masks,
         )
     first = finish(
-        points[...], attended[...], gains[1:2, :], (proj_held, up_held, down_held), fetches[1:]
+        points[...], attended[...], gains[1:2, :], (proj_held, up_held, down_held), fetches
     )
     outgoing[...] = jnp.dot(send[...], first, preferred_element_type=F32).astype(BF16)
 
@@ -234,8 +285,54 @@
     capacity = 2 * rows_here // devices
     slot_total = devices * capacity
 
-    normed = layer_norm(points, norm_gains[0])
-    gathered = lax.all_gather(normed, "seq", axis=0, tiled=True)
+    shards_in_group = lax.axis_size("seq")
+    chips = shards_in_group // 2
+    onward = [(i, (i + 2) % shards_in_group) for i in range(shards_in_group)]
+    swap = [(i, i ^ 1) for i in range(shards_in_group)]
+    part = rows_here // RING_PARTS
+    column = [points[i * part : (i + 1) * part] for i in range(RING_PARTS)]
+    blocks = [column, [lax.ppermute(rows, "seq", swap) for rows in column]]
+    for _ in range(1, chips):
+        column = [lax.ppermute(rows, "seq", onward) for rows in column]
+        blocks += [column, [lax.ppermute(rows, "seq", swap) for rows in column]]
+
+    block_bytes = rows_here * channels * 2
+    kv_shape = jax.ShapeDtypeStruct((shards_in_group * rows_here, 2 * channels), BF16)
+    kv_scratch = [
+        pltpu.VMEM((rows_here, 2 * channels), BF16),
+        pltpu.SemaphoreType.DMA((RING_PARTS,)),
+    ]
+    keyed, queries = pl.pallas_call(
+        own_kernel,
+        out_shape=(kv_shape, jax.ShapeDtypeStruct((rows_here, channels), BF16)),
+        in_specs=[VMEM_SPEC] * (RING_PARTS + 2),
+        out_specs=(ANY_SPEC, VMEM_SPEC),
+        scratch_shapes=kv_scratch,
+        cost_estimate=pl.CostEstimate(
+            flops=6 * rows_here * channels**2, bytes_accessed=6 * block_bytes, transcendentals=0
+        ),
+        compiler_params=pltpu.CompilerParams(vmem_limit_bytes=VMEM_BYTES),
+        name="project_own",
+    )(*blocks[0], norm_gains, w_qkv)
+    for slot in range(1, 2 * chips):
+        keyed = pl.pallas_call(
+            functools.partial(project_kernel, slot),
+            out_shape=kv_shape,
+            in_specs=[VMEM_SPEC] * (RING_PARTS + 2) + [ANY_SPEC],
+            out_specs=ANY_SPEC,
+            scratch_shapes=kv_scratch,
+            input_output_aliases={RING_PARTS + 2: 0},
+            cost_estimate=pl.CostEstimate(
+                flops=4 * rows_here * channels**2, bytes_accessed=5 * block_bytes, transcendentals=0
+            ),
+            compiler_params=pltpu.CompilerParams(vmem_limit_bytes=VMEM_BYTES),
+            name="project",
+        )(*blocks[slot], norm_gains, w_qkv, keyed)
+
+    me = lax.axis_index("seq")
+    owner = pattern_first // patches
+    slot_of = 2 * ((me // 2 - owner // 2) % chips) + (me % 2 != owner % 2).astype(jnp.int32)
+    pattern_slots = slot_of * patches + pattern_first % patches
 
     target = destination // rows_here
     place_at = destination % rows_here
@@ -265,20 +362,19 @@
         first_kernel,
         out_shape=jax.ShapeDtypeStruct((slot_total, channels), BF16),
         in_specs=[SMEM_SPEC, VMEM_SPEC, VMEM_SPEC, ANY_SPEC, VMEM_SPEC]
-        + [ANY_SPEC] * len(weights)
+        + [ANY_SPEC] * 3
         + [VMEM_SPEC],
         out_specs=VMEM_SPEC,
         scratch_shapes=[
-            pltpu.VMEM((keyed_rows, channels), BF16),
             pltpu.VMEM((keyed_rows, 2 * channels), BF16),
             pltpu.VMEM((rows_here, channels), BF16),
-            *held_weights(weights),
-            pltpu.SemaphoreType.DMA((patches, chosen)),
-            pltpu.SemaphoreType.DMA((len(weights),)),
+            *held_weights(weights[1:]),
+            pltpu.SemaphoreType.DMA((patches, 1 + chosen)),
+            pltpu.SemaphoreType.DMA((3,)),
         ],
         compiler_params=pltpu.CompilerParams(vmem_limit_bytes=VMEM_BYTES),
         name="block_first",
-    )(pattern_first, points, normed, gathered, norm_gains, *weights, send)
+    )(pattern_slots, points, queries, keyed, norm_gains, *weights[1:], send)
 
     incoming = lax.all_to_all(
         outgoing.reshape(devices, capacity, channels),

time: 123 us -> 121 us (0.984)
  waiting for transfers between devices: 65.7 us -> 41.8 us
  Pallas kernels: 22 us -> 41.9 us
  between operations: 14.2 us -> 1.16 us
  starting transfers between devices: 10.9 us -> 19.7 us
  local copies, waits for them, and re-layouts: 2.41 us -> 11 us
  other arithmetic: 7.74 us -> 4.79 us
    all_gather x1 -> x0, waiting for transfers between devices: 40 us -> none  [shards(): gathered = lax.all_gather(normed, 'seq', axis=0, tiled=True)]
    ppermute x0 -> x14, waiting for transfers between devices: none -> 16.1 us  [the longest x6 16.1 us: shards(): column = [lax.ppermute(rows, 'seq', onward) for rows in column]]
    pallas_call x0 -> x8, Pallas kernels: none -> 16.1 us  [the longest x7 14.2 us: shards(): pl.pallas_call(functools.partial(project_kernel, slot), out_shape=kv_shap...]
    ppermute x0 -> x14, starting transfers between devices: none -> 9.22 us  [the longest x6 7.46 us: shards(): column = [lax.ppermute(rows, 'seq', onward) for rows in column]]
    unnamed x18 -> x42, local copies, waits for them, and re-layouts: 0.2 us -> 8.43 us
    reduce_sum x2 -> x0, other arithmetic: 2.61 us -> none  [the longest x1 1.32 us: layer_norm(): spread = jnp.mean((values - average) ** 2, axis=-1, keepdims=True)]
    convert_element_type x1 -> x0, other arithmetic: 2.07 us -> none  [layer_norm(): return ((values - average) * lax.rsqrt(spread + 1e-05) * gains).astype(BF16)]
    pallas_call x1, Pallas kernels: 9.31 us -> 11.2 us  [shards(): pl.pallas_call(second_kernel, out_shape=(jax.ShapeDtypeStruct((rows_here,...]
  transfers between devices with their start and end apart: 3 -> 16, of which waited for: 2 -> 5; matrix products, arithmetic and copies ran while one was open for 4% -> 6% of each run, Pallas kernels for 10% -> 25%
where the time goes in v2:
time: 121 us; the launch traced here: 120 us
  Pallas kernels  41.9 us (35%)
  waiting for transfers between devices  41.8 us (35%)
  starting transfers between devices  19.7 us (16%)
  local copies, waits for them, and re-layouts  11 us (9%)
  other arithmetic  4.79 us (4%)
    all_to_all x1, waiting for transfers between devices, shards(): lax.all_to_all(outgoing.reshape(devices, capacity, channels), ('grp', 'se...  25.7 us
    ppermute x6, waiting for transfers between devices, shards(): column = [lax.ppermute(rows, 'seq', onward) for rows in column]  16.1 us
    pallas_call x1, Pallas kernels, shards(): pl.pallas_call(first_kernel, out_shape=jax.ShapeDtypeStruct((slot_total,...  14.5 us
    pallas_call x7, Pallas kernels, shards(): pl.pallas_call(functools.partial(project_kernel, slot), out_shape=kv_shap...  14.2 us
    pallas_call x1, Pallas kernels, shards(): pl.pallas_call(second_kernel, out_shape=(jax.ShapeDtypeStruct((rows_here,...  11.2 us
    unnamed x42, local copies, waits for them, and re-layouts  8.43 us
    ppermute x6, starting transfers between devices, shards(): column = [lax.ppermute(rows, 'seq', onward) for rows in column]  7.46 us
    all_to_all x1, starting transfers between devices, shards(): lax.all_to_all(out_places.reshape(devices, capacity), ('grp', 'seq'), spl...  6.2 us
  transfers between devices with their start and end apart: 16, of which 5 were waited for; matrix products, arithmetic and copies ran while one was open for 6% of the time, Pallas kernels for 25%

profile of v2, /device:TPU:0, one launch (start us, length us, event | category | flops | bytes accessed | tf_op | source)
XLA Modules:
  0.0 120.3 jit_solution(1844908069358983690)
XLA Ops:
  0.6 1.1 fusion.17
  1.7 0.5 collective-permute-start.12
  2.2 2.6 %collective-permute-start = (bf16[256,512]{1,0:T(8,128)(2,1)S(1)}, bf16[256,512]{1,0:T(8,128)(2,1)S(1)}, u32[]{:S(2)}, u32[]{:S(2)}) collective-permute-start(bf16[256,512]{1,0:T(8,128)(2,1)S(1)} %get-tuple-element.7.refs_0_), channel_id=1, source_target_pairs={{0,2},{1,3},{2,4},{3,5},{4,6},{5,7},{6,0},{7,1},{8,10},{9,11},{10,... | collective-permute-start | bytes 786440 | tf_op jit(solution)/shard_map/ppermute | solution.py:296
  4.9 0.2 collective-permute-start.13
  5.0 1.6 %collective-permute-start.4 = (bf16[256,512]{1,0:T(8,128)(2,1)S(1)}, bf16[256,512]{1,0:T(8,128)(2,1)}, u32[]{:S(2)}, u32[]{:S(2)}) collective-permute-start(bf16[256,512]{1,0:T(8,128)(2,1)S(1)} %get-tuple-element.6.refs_1_), channel_id=1, source_target_pairs={{0,2},{1,3},{2,4},{3,5},{4,6},{5,7},{6,0},{7,1},{8,10},{9,11},{10,... | collective-permute-start | bytes 786440 | tf_op jit(solution)/shard_map/ppermute | solution.py:296
  6.6 0.7 fusion.15
  7.3 1.2 reduce-window.6
  8.5 0.2 slice_reduce_fusion
  8.7 0.1 fusion.4
  8.9 0.3 select_reduce_fusion
  9.2 4.9 %collective-permute-done.refs_0_ = bf16[256,512]{1,0:T(8,128)(2,1)S(1)} collective-permute-done((bf16[256,512]{1,0:T(8,128)(2,1)S(1)}, bf16[256,512]{1,0:T(8,128)(2,1)S(1)}, u32[]{:S(2)}, u32[]{:S(2)}) %collective-permute-start) | collective-permute-done | bytes 262176 | tf_op jit(solution)/shard_map/ppermute | solution.py:296
  14.1 5.7 %collective-permute-done.4.refs_1_ = bf16[256,512]{1,0:T(8,128)(2,1)} collective-permute-done((bf16[256,512]{1,0:T(8,128)(2,1)S(1)}, bf16[256,512]{1,0:T(8,128)(2,1)}, u32[]{:S(2)}, u32[]{:S(2)}) %collective-permute-start.4) | collective-permute-done | bytes 262176 | tf_op jit(solution)/shard_map/ppermute | solution.py:296
  19.8 0.7 sub.40
  20.5 6.2 %all-to-all-start.1 = ((s32[32,1,32]{2,1,0:T(1,128)}), s32[32,1,32]{2,1,0:T(1,128)S(1)}, u32[]{:S(2)}, u32[]{:S(2)}) async-start(s32[32,1,32]{2,1,0:T(1,128)} %sub.40), calls=%async_computation.1 | async-start | bytes 32768 | tf_op jit(solution)/shard_map/all_to_all | solution.py:350
  26.7 0.3 collective-permute-start.10
  27.0 1.5 %fusion.send = bf16[1024,512]{1,0:T(8,128)(2,1)} fusion(s32[512]{0:T(512)S(1)} %multiply_add_fusion), kind=kLoop, calls=%fused_computation.3 | loop fusion | flops 1048576 | bytes 1050624 | tf_op jit(solution)/shard_map/convert_element_type | solution.py:348
  28.5 0.8 copy.24
  29.2 0.7 copy-done.10
  29.9 0.3 collective-permute-start.11
  30.2 1.8 %collective-permute-start.2 = (bf16[256,512]{1,0:T(8,128)(2,1)}, bf16[256,512]{1,0:T(8,128)(2,1)S(1)}, u32[]{:S(2)}, u32[]{:S(2)}) collective-permute-start(bf16[256,512]{1,0:T(8,128)(2,1)} %collective-permute-done.1.refs_0_), channel_id=1, source_target_pairs={{0,2},{1,3},{2,4},{3,5},{4,6},{5,7},{6,0},{7,1},{8,10},{9,11},{10,... | collective-permute-start | bytes 786440 | tf_op jit(solution)/shard_map/ppermute | solution.py:296
  32.0 1.5 %collective-permute-start.6 = (bf16[256,512]{1,0:T(8,128)(2,1)}, bf16[256,512]{1,0:T(8,128)(2,1)S(1)}, u32[]{:S(2)}, u32[]{:S(2)}) collective-permute-start(bf16[256,512]{1,0:T(8,128)(2,1)} %collective-permute-done.5.refs_1_), channel_id=1, source_target_pairs={{0,2},{1,3},{2,4},{3,5},{4,6},{5,7},{6,0},{7,1},{8,10},{9,11},{10,... | collective-permute-start | bytes 786440 | tf_op jit(solution)/shard_map/ppermute | solution.py:296
  33.5 0.7 copy-done.14
  34.2 0.7 copy-done.16
  34.9 0.5 collective-permute-start.9
  35.4 1.9 %copy-done = bf16[2,512,1536]{2,1,0:T(8,128)(2,1)S(1)} copy-done((bf16[2,512,1536]{2,1,0:T(8,128)(2,1)S(1)}, bf16[2,512,1536]{2,1,0:T(8,128)(2,1)}, u32[]{:S(2)}) %copy-start) | copy-done | bytes 3145752
  37.3 0.9 copy-done.7
  38.3 0.7 copy-done.8
  38.9 1.8 %project_own.1 = (bf16[4096,1024]{1,0:T(8,128)(2,1)}, bf16[512,512]{1,0:T(8,128)(2,1)S(1)}) custom-call(bf16[256,512]{1,0:T(8,128)(2,1)S(1)} %copy-done.7, bf16[256,512]{1,0:T(8,128)(2,1)S(1)} %get-tuple-element.6.refs_1_, f32[4,512]{1,0:T(4,128)S(1)} %copy-done.8, bf16[2,512,1536]{2,1,0:T(8,128)(2,1)S(1)} %copy-done), custom_call_target="tpu_custom_call" | custom-call | flops 805306368 | bytes 3145728 | tf_op jit(solution)/shard_map/project_own/pallas_call | solution.py:305
  40.8 0.5 collective-permute-done.2.refs_0_
  41.3 4.9 %collective-permute-done.6.refs_1_ = bf16[256,512]{1,0:T(8,128)(2,1)S(1)} collective-permute-done((bf16[256,512]{1,0:T(8,128)(2,1)}, bf16[256,512]{1,0:T(8,128)(2,1)S(1)}, u32[]{:S(2)}, u32[]{:S(2)}) %collective-permute-start.6) | collective-permute-done | bytes 262176 | tf_op jit(solution)/shard_map/ppermute | solution.py:296
  46.3 0.9 copy-done.11
  47.2 0.9 copy-done.15
  48.2 1.7 %project.7.refs_4_ = bf16[4096,1024]{1,0:T(8,128)(2,1)} custom-call(bf16[256,512]{1,0:T(8,128)(2,1)S(1)} %copy-done.11, bf16[256,512]{1,0:T(8,128)(2,1)S(1)} %copy-done.15, f32[4,512]{1,0:T(4,128)S(1)} %copy-done.8, bf16[2,512,1536]{2,1,0:T(8,128)(2,1)S(1)} %copy-done.1, bf16[4096,1024]{1,0:T(8,128)(2,1)} %get-tuple-element.5.refs_4_), custom_call_target="tpu_custom_call", output_to_operand_aliasing={{}: (4, {})} | custom-call | flops 536870912 | bytes 2621440 | tf_op jit(solution)/shard_map/project/pallas_call | solution.py:318
  50.0 2.7 %project.8.refs_4_ = bf16[4096,1024]{1,0:T(8,128)(2,1)} custom-call(bf16[256,512]{1,0:T(8,128)(2,1)S(1)} %copy-done.13, bf16[256,512]{1,0:T(8,128)(2,1)} %collective-permute-done.4.refs_1_, f32[4,512]{1,0:T(4,128)S(1)} %copy-done.8, bf16[2,512,1536]{2,1,0:T(8,128)(2,1)S(1)} %copy-done.1, ...), custom_call_target="tpu_custom_call", output_to_operand_aliasing={{}: (4, {})} | custom-call | flops 536870912 | bytes 2621440 | tf_op jit(solution)/shard_map/project/pallas_call | solution.py:318
  52.7 1.7 %project.9.refs_4_ = bf16[4096,1024]{1,0:T(8,128)(2,1)} custom-call(bf16[256,512]{1,0:T(8,128)(2,1)S(1)} %copy-done.17, bf16[256,512]{1,0:T(8,128)(2,1)S(1)} %collective-permute-done.11.refs_1_, f32[4,512]{1,0:T(4,128)S(1)} %copy-done.8, bf16[2,512,1536]{2,1,0:T(8,128)(2,1)S(1)} %copy-done.1, ...), custom_call_target="tpu_custom_call", output_to_operand_aliasing={{}: (4, {})} | custom-call | flops 536870912 | bytes 2621440 | tf_op jit(solution)/shard_map/project/pallas_call | solution.py:318
  54.5 2.8 %project.10.refs_4_ = bf16[4096,1024]{1,0:T(8,128)(2,1)} custom-call(bf16[256,512]{1,0:T(8,128)(2,1)} %collective-permute-done.1.refs_0_, bf16[256,512]{1,0:T(8,128)(2,1)} %collective-permute-done.5.refs_1_, f32[4,512]{1,0:T(4,128)S(1)} %copy-done.8, bf16[2,512,1536]{2,1,0:T(8,128)(2,1)S(1)} %copy-done.1, ...), custom_call_target="tpu_custom_call", output_to_operand_aliasing={{}: (4, {})} | custom-call | flops 536870912 | bytes 2621440 | tf_op jit(solution)/shard_map/project/pallas_call | solution.py:318
  57.3 1.8 %project.11.refs_4_ = bf16[4096,1024]{1,0:T(8,128)(2,1)} custom-call(bf16[256,512]{1,0:T(8,128)(2,1)S(1)} %collective-permute-done.8.refs_0_, bf16[256,512]{1,0:T(8,128)(2,1)S(1)} %collective-permute-done.9.refs_1_, f32[4,512]{1,0:T(4,128)S(1)} %copy-done.8, bf16[2,512,1536]{2,1,0:T(8,128)(2,1)S(1)} %copy-done.1, ...), custom_call_target="tpu_custom_call", output_to_operand_aliasing={{}: (4, {})} | custom-call | flops 536870912 | bytes 2621440 | tf_op jit(solution)/shard_map/project/pallas_call | solution.py:318
  59.0 1.7 %project.12.refs_4_ = bf16[4096,1024]{1,0:T(8,128)(2,1)} custom-call(bf16[256,512]{1,0:T(8,128)(2,1)S(1)} %collective-permute-done.2.refs_0_, bf16[256,512]{1,0:T(8,128)(2,1)S(1)} %collective-permute-done.6.refs_1_, f32[4,512]{1,0:T(4,128)S(1)} %copy-done.8, bf16[2,512,1536]{2,1,0:T(8,128)(2,1)S(1)} %copy-done.1, ...), custom_call_target="tpu_custom_call", output_to_operand_aliasing={{}: (4, {})} | custom-call | flops 536870912 | bytes 2621440 | tf_op jit(solution)/shard_map/project/pallas_call | solution.py:318
  60.8 1.8 %project.13.keyed = bf16[4096,1024]{1,0:T(8,128)(2,1)} custom-call(bf16[256,512]{1,0:T(8,128)(2,1)S(1)} %collective-permute-done.3.refs_0_, bf16[256,512]{1,0:T(8,128)(2,1)S(1)} %collective-permute-done.7.refs_1_, f32[4,512]{1,0:T(4,128)S(1)} %copy-done.8, bf16[2,512,1536]{2,1,0:T(8,128)(2,1)S(1)} %copy-done.1, ...), custom_call_target="tpu_custom_call", output_to_operand_aliasing={{}: (4, {})} | custom-call | flops 536870912 | bytes 2621440 | tf_op jit(solution)/shard_map/project/pallas_call | solution.py:318
  62.7 14.5 %block_first.1 = bf16[1024,512]{1,0:T(8,128)(2,1)} custom-call(s32[8,3]{1,0:T(8,128)S(1)} %fusion.11.pattern, bf16[512,512]{1,0:T(8,128)(2,1)S(1)} %copy-done.5, bf16[512,512]{1,0:T(8,128)(2,1)S(1)} %get-tuple-element.4.queries, bf16[4096,1024]{1,0:T(8,128)(2,1)} %project.13.keyed, f32[4,512]{1,0:T(4,128)S(1)} %copy-done.9, ...), custom_call_target="tpu_custom_call" | custom-call | tf_op jit(solution)/shard_map/block_first/pallas_call | solution.py:361
  77.3 4.3 %all-to-all-start = ((bf16[32,32,512]{2,1,0:T(8,128)(2,1)}), bf16[32,32,512]{2,1,0:T(8,128)(2,1)S(1)}, u32[]{:S(2)}, u32[]{:S(2)}) async-start(bf16[32,32,512]{2,1,0:T(8,128)(2,1)} %bitcast.2), calls=%async_computation | async-start | bytes 2097152 | tf_op jit(solution)/shard_map/all_to_all | solution.py:379
  81.6 0.1 copy.29.pattern
  81.6 0.5 broadcast.107
  82.1 0.7 reduce.5
  82.8 0.1 eq.69
  82.9 0.3 fusion.1.place
  83.2 25.7 %all-to-all-done = bf16[32,32,512]{2,1,0:T(8,128)(2,1)S(1)} async-done(((bf16[32,32,512]{2,1,0:T(8,128)(2,1)}), bf16[32,32,512]{2,1,0:T(8,128)(2,1)S(1)}, u32[]{:S(2)}, u32[]{:S(2)}) %all-to-all-start) | async-done | bytes 1048608 | tf_op jit(solution)/shard_map/all_to_all | solution.py:379
  108.9 11.2 %block_second.1 = (bf16[512,512]{1,0:T(8,128)(2,1)}, f32[3,512]{1,0:T(4,128)}) custom-call(s32[8,3]{1,0:T(8,128)S(1)} %copy.29.pattern, bf16[1024,512]{1,0:T(8,128)(2,1)S(1)} %bitcast.22, bf16[512,1024]{1,0:T(8,128)(2,1)S(1)} %fusion.1.place, f32[4,512]{1,0:T(4,128)S(1)} %copy-done.9, bf16[2,512,1536]{2,1,0:T(8,128)(2,1)} %w_qkv.1, ...), custom_call_target="tpu_custom_call" | custom-call | tf_op jit(solution)/shard_map/block_second/pallas_call | solution.py:387
  (54 shorter events, 0.2 us)
Async XLA Ops:
  1.7 32.5 %copy-start.6 = (bf16[256,512]{1,0:T(8,128)(2,1)}, bf16[256,512]{1,0:T(8,128)(2,1)S(1)}, u32[]{:S(2)}) copy-start(bf16[256,512]{1,0:T(8,128)(2,1)S(1)} %get-tuple-element.7.refs_0_) | copy-start | bytes 786436
  1.7 27.5 %collective-permute-start.12 = (bf16[256,512]{1,0:T(8,128)(2,1)S(1)}, bf16[256,512]{1,0:T(8,128)(2,1)S(1)}, u32[]{:S(2)}, u32[]{:S(2)}) collective-permute-start(bf16[256,512]{1,0:T(8,128)(2,1)S(1)} %get-tuple-element.7.refs_0_), channel_id=1, source_target_pairs={{0,1},{1,0},{2,3},{3,2},{4,5},{5,4},{6,7},{7,6},{8,9},{9,8},{10,11... | collective-permute-start | bytes 786440 | tf_op jit(solution)/shard_map/ppermute | solution.py:294
  2.2 11.8 %collective-permute-start = (bf16[256,512]{1,0:T(8,128)(2,1)S(1)}, bf16[256,512]{1,0:T(8,128)(2,1)S(1)}, u32[]{:S(2)}, u32[]{:S(2)}) collective-permute-start(bf16[256,512]{1,0:T(8,128)(2,1)S(1)} %get-tuple-element.7.refs_0_), channel_id=1, source_target_pairs={{0,2},{1,3},{2,4},{3,5},{4,6},{5,7},{6,0},{7,1},{8,10},{9,11},{10,... | collective-permute-start | bytes 786440 | tf_op jit(solution)/shard_map/ppermute | solution.py:296
  4.9 28.6 %collective-permute-start.13 = (bf16[256,512]{1,0:T(8,128)(2,1)S(1)}, bf16[256,512]{1,0:T(8,128)(2,1)S(1)}, u32[]{:S(2)}, u32[]{:S(2)}) collective-permute-start(bf16[256,512]{1,0:T(8,128)(2,1)S(1)} %get-tuple-element.6.refs_1_), channel_id=1, source_target_pairs={{0,1},{1,0},{2,3},{3,2},{4,5},{5,4},{6,7},{7,6},{8,9},{9,8},{10,11... | collective-permute-start | bytes 786440 | tf_op jit(solution)/shard_map/ppermute | solution.py:294
  5.0 14.7 %collective-permute-start.4 = (bf16[256,512]{1,0:T(8,128)(2,1)S(1)}, bf16[256,512]{1,0:T(8,128)(2,1)}, u32[]{:S(2)}, u32[]{:S(2)}) collective-permute-start(bf16[256,512]{1,0:T(8,128)(2,1)S(1)} %get-tuple-element.6.refs_1_), channel_id=1, source_target_pairs={{0,2},{1,3},{2,4},{3,5},{4,6},{5,7},{6,0},{7,1},{8,10},{9,11},{10,... | collective-permute-start | bytes 786440 | tf_op jit(solution)/shard_map/ppermute | solution.py:296
  14.1 20.1 %copy-start.12 = (bf16[256,512]{1,0:T(8,128)(2,1)}, bf16[256,512]{1,0:T(8,128)(2,1)S(1)}, u32[]{:S(2)}) copy-start(bf16[256,512]{1,0:T(8,128)(2,1)S(1)} %collective-permute-done.refs_0_) | copy-start | bytes 786436
  14.1 16.1 %collective-permute-start.1 = (bf16[256,512]{1,0:T(8,128)(2,1)S(1)}, bf16[256,512]{1,0:T(8,128)(2,1)}, u32[]{:S(2)}, u32[]{:S(2)}) collective-permute-start(bf16[256,512]{1,0:T(8,128)(2,1)S(1)} %collective-permute-done.refs_0_), channel_id=1, source_target_pairs={{0,2},{1,3},{2,4},{3,5},{4,6},{5,7},{6,0},{7,1},{8,10},{9,11},{10,... | collective-permute-start | bytes 786440 | tf_op jit(solution)/shard_map/ppermute | solution.py:296
  19.8 12.2 %collective-permute-start.5 = (bf16[256,512]{1,0:T(8,128)(2,1)}, bf16[256,512]{1,0:T(8,128)(2,1)}, u32[]{:S(2)}, u32[]{:S(2)}) collective-permute-start(bf16[256,512]{1,0:T(8,128)(2,1)} %collective-permute-done.4.refs_1_), channel_id=1, source_target_pairs={{0,2},{1,3},{2,4},{3,5},{4,6},{5,7},{6,0},{7,1},{8,10},{9,11},{10,... | collective-permute-start | bytes 786440 | tf_op jit(solution)/shard_map/ppermute | solution.py:296
  20.5 56.8 %all-to-all-start.1 = ((s32[32,1,32]{2,1,0:T(1,128)}), s32[32,1,32]{2,1,0:T(1,128)S(1)}, u32[]{:S(2)}, u32[]{:S(2)}) async-start(s32[32,1,32]{2,1,0:T(1,128)} %sub.40), calls=%async_computation.1 | async-start | bytes 32768 | tf_op jit(solution)/shard_map/all_to_all | solution.py:350
  26.7 7.5 %collective-permute-start.10 = (bf16[256,512]{1,0:T(8,128)(2,1)S(1)}, bf16[256,512]{1,0:T(8,128)(2,1)S(1)}, u32[]{:S(2)}, u32[]{:S(2)}) collective-permute-start(bf16[256,512]{1,0:T(8,128)(2,1)S(1)} %collective-permute-done.refs_0_), channel_id=1, source_target_pairs={{0,1},{1,0},{2,3},{3,2},{4,5},{5,4},{6,7},{7,6},{8,9},{9,8},{10,11... | collective-permute-start | bytes 786440 | tf_op jit(solution)/shard_map/ppermute | solution.py:297
  29.2 0.7 copy-start.10
  29.9 22.8 %collective-permute-start.11 = (bf16[256,512]{1,0:T(8,128)(2,1)}, bf16[256,512]{1,0:T(8,128)(2,1)S(1)}, u32[]{:S(2)}, u32[]{:S(2)}) collective-permute-start(bf16[256,512]{1,0:T(8,128)(2,1)} %collective-permute-done.4.refs_1_), channel_id=1, source_target_pairs={{0,1},{1,0},{2,3},{3,2},{4,5},{5,4},{6,7},{7,6},{8,9},{9,8},{10,11... | collective-permute-start | bytes 786440 | tf_op jit(solution)/shard_map/ppermute | solution.py:297
  30.2 11.1 %collective-permute-start.2 = (bf16[256,512]{1,0:T(8,128)(2,1)}, bf16[256,512]{1,0:T(8,128)(2,1)S(1)}, u32[]{:S(2)}, u32[]{:S(2)}) collective-permute-start(bf16[256,512]{1,0:T(8,128)(2,1)} %collective-permute-done.1.refs_0_), channel_id=1, source_target_pairs={{0,2},{1,3},{2,4},{3,5},{4,6},{5,7},{6,0},{7,1},{8,10},{9,11},{10,... | collective-permute-start | bytes 786440 | tf_op jit(solution)/shard_map/ppermute | solution.py:296
  32.0 14.3 %collective-permute-start.6 = (bf16[256,512]{1,0:T(8,128)(2,1)}, bf16[256,512]{1,0:T(8,128)(2,1)S(1)}, u32[]{:S(2)}, u32[]{:S(2)}) collective-permute-start(bf16[256,512]{1,0:T(8,128)(2,1)} %collective-permute-done.5.refs_1_), channel_id=1, source_target_pairs={{0,2},{1,3},{2,4},{3,5},{4,6},{5,7},{6,0},{7,1},{8,10},{9,11},{10,... | collective-permute-start | bytes 786440 | tf_op jit(solution)/shard_map/ppermute | solution.py:296
  33.5 0.7 copy-start.14
  34.2 23.1 %collective-permute-start.8 = (bf16[256,512]{1,0:T(8,128)(2,1)}, bf16[256,512]{1,0:T(8,128)(2,1)S(1)}, u32[]{:S(2)}, u32[]{:S(2)}) collective-permute-start(bf16[256,512]{1,0:T(8,128)(2,1)} %collective-permute-done.1.refs_0_), channel_id=1, source_target_pairs={{0,1},{1,0},{2,3},{3,2},{4,5},{5,4},{6,7},{7,6},{8,9},{9,8},{10,11... | collective-permute-start | bytes 786440 | tf_op jit(solution)/shard_map/ppermute | solution.py:297
  34.2 0.7 copy-start.16
  34.9 22.3 %collective-permute-start.9 = (bf16[256,512]{1,0:T(8,128)(2,1)}, bf16[256,512]{1,0:T(8,128)(2,1)S(1)}, u32[]{:S(2)}, u32[]{:S(2)}) collective-permute-start(bf16[256,512]{1,0:T(8,128)(2,1)} %collective-permute-done.5.refs_1_), channel_id=1, source_target_pairs={{0,1},{1,0},{2,3},{3,2},{4,5},{5,4},{6,7},{7,6},{8,9},{9,8},{10,11... | collective-permute-start | bytes 786440 | tf_op jit(solution)/shard_map/ppermute | solution.py:297
  35.4 1.9 %copy-start = (bf16[2,512,1536]{2,1,0:T(8,128)(2,1)S(1)}, bf16[2,512,1536]{2,1,0:T(8,128)(2,1)}, u32[]{:S(2)}) copy-start(bf16[2,512,1536]{2,1,0:T(8,128)(2,1)} %w_qkv.1) | copy-start | bytes 9437188
  37.3 0.9 copy-start.7
  38.2 0.7 copy-start.8
  38.9 7.3 %copy-start.1 = (bf16[2,512,1536]{2,1,0:T(8,128)(2,1)S(1)}, bf16[2,512,1536]{2,1,0:T(8,128)(2,1)}, u32[]{:S(2)}) copy-start(bf16[2,512,1536]{2,1,0:T(8,128)(2,1)} %w_qkv.1) | copy-start | bytes 9437188
  41.3 19.5 %collective-permute-start.3 = (bf16[256,512]{1,0:T(8,128)(2,1)S(1)}, bf16[256,512]{1,0:T(8,128)(2,1)S(1)}, u32[]{:S(2)}, u32[]{:S(2)}) collective-permute-start(bf16[256,512]{1,0:T(8,128)(2,1)S(1)} %collective-permute-done.2.refs_0_), channel_id=1, source_target_pairs={{0,1},{1,0},{2,3},{3,2},{4,5},{5,4},{6,7},{7,6},{8,9},{9,8},{10,11... | collective-permute-start | bytes 786440 | tf_op jit(solution)/shard_map/ppermute | solution.py:297
  46.3 14.5 %collective-permute-start.7 = (bf16[256,512]{1,0:T(8,128)(2,1)S(1)}, bf16[256,512]{1,0:T(8,128)(2,1)S(1)}, u32[]{:S(2)}, u32[]{:S(2)}) collective-permute-start(bf16[256,512]{1,0:T(8,128)(2,1)S(1)} %collective-permute-done.6.refs_1_), channel_id=1, source_target_pairs={{0,1},{1,0},{2,3},{3,2},{4,5},{5,4},{6,7},{7,6},{8,9},{9,8},{10,11... | collective-permute-start | bytes 786440 | tf_op jit(solution)/shard_map/ppermute | solution.py:297
  46.3 1.0 copy-start.11
  47.2 0.9 copy-start.15
  48.2 1.8 %copy-start.13 = (bf16[256,512]{1,0:T(8,128)(2,1)S(1)}, bf16[256,512]{1,0:T(8,128)(2,1)}, u32[]{:S(2)}) copy-start(bf16[256,512]{1,0:T(8,128)(2,1)} %copy-done.12) | copy-start | bytes 786436
  50.0 2.8 %copy-start.17 = (bf16[256,512]{1,0:T(8,128)(2,1)S(1)}, bf16[256,512]{1,0:T(8,128)(2,1)}, u32[]{:S(2)}) copy-start(bf16[256,512]{1,0:T(8,128)(2,1)} %copy-done.16) | copy-start | bytes 786436
  60.8 1.9 %copy-start.2 = (bf16[2,512,512]{2,1,0:T(8,128)(2,1)S(1)}, bf16[2,512,512]{2,1,0:T(8,128)(2,1)}, u32[]{:S(2)}) copy-start(bf16[2,512,512]{2,1,0:T(8,128)(2,1)} %w_proj.3) | copy-start | bytes 3145732
  60.8 1.9 %copy-start.4 = (bf16[1024,512]{1,0:T(8,128)(2,1)S(1)}, bf16[1024,512]{1,0:T(8,128)(2,1)}, u32[]{:S(2)}) copy-start(bf16[1024,512]{1,0:T(8,128)(2,1)} %fusion.send) | copy-start | bytes 3145732
  60.8 1.9 %copy-start.5 = (bf16[512,512]{1,0:T(8,128)(2,1)S(1)}, bf16[512,512]{1,0:T(8,128)(2,1)}, u32[]{:S(2)}) copy-start(bf16[512,512]{1,0:T(8,128)(2,1)} %points.1) | copy-start | bytes 1572868
  60.8 1.9 %copy-start.9 = (f32[4,512]{1,0:T(4,128)S(1)}, f32[4,512]{1,0:T(4,128)}, u32[]{:S(2)}) copy-start(f32[4,512]{1,0:T(4,128)} %gains.3) | copy-start | bytes 24580
  62.7 18.9 %copy-start.19 = (s32[8,3]{0,1:T(4,128)S(1)}, s32[8,3]{0,1:T(4,128)}, u32[]{:S(2)}) copy-start(s32[8,3]{0,1:T(4,128)} %param.12) | copy-start | bytes 292
  62.7 46.2 %copy-start.3 = (bf16[2,512,512]{2,1,0:T(8,128)(2,1)S(1)}, bf16[2,512,512]{2,1,0:T(8,128)(2,1)}, u32[]{:S(2)}) copy-start(bf16[2,512,512]{2,1,0:T(8,128)(2,1)} %w_proj.3) | copy-start | bytes 3145732
  62.7 46.2 %copy-start.18 = (bf16[3,512]{1,0:T(4,128)(2,1)S(1)}, bf16[3,512]{1,0:T(4,128)(2,1)}, u32[]{:S(2)}) copy-start(bf16[3,512]{1,0:T(4,128)(2,1)} %w_head.1) | copy-start | bytes 9220
  77.3 31.7 %all-to-all-start = ((bf16[32,32,512]{2,1,0:T(8,128)(2,1)}), bf16[32,32,512]{2,1,0:T(8,128)(2,1)S(1)}, u32[]{:S(2)}, u32[]{:S(2)}) async-start(bf16[32,32,512]{2,1,0:T(8,128)(2,1)} %bitcast.2), calls=%async_computation | async-start | bytes 2097152 | tf_op jit(solution)/shard_map/all_to_all | solution.py:379

commit v3 on v1

v3 whole, which is shorter than its diff:
```python
import functools

import jax
import jax.numpy as jnp
from jax import lax
from jax.experimental import pallas as pl
from jax.experimental.pallas import tpu as pltpu
from jax.sharding import PartitionSpec as P

HEADS = 8
PATCH = 64
HEADS_TOGETHER = 4
RING_PARTS = 2
VMEM_BYTES = 32 * 1024 * 1024
RING_BYTES = 16 * 1024 * 1024
F32 = jnp.float32
BF16 = jnp.bfloat16


def layer_norm(rows, gains):
    values = rows.astype(F32)
    average = jnp.mean(values, axis=-1, keepdims=True)
    spread = jnp.mean((values - average) ** 2, axis=-1, keepdims=True)
    return ((values - average) * lax.rsqrt(spread + 1e-05) * gains).astype(BF16)


def gelu(x):
    half = 0.5 * x
    return half + half * lax.erf(x * 0.5**0.5)


def head_masks(head_dim):
    lane = lax.broadcasted_iota(jnp.int32, (PATCH, HEADS_TOGETHER * head_dim), 1)
    return [
        jnp.where((lane >= h * head_dim) & (lane < (h + 1) * head_dim), 1.0, 0.0).astype(F32)
        for h in range(HEADS_TOGETHER)
    ]


def attend_patch(queries, key_rows, value_rows, masks):
    channels = queries.shape[1]
    width = HEADS_TOGETHER * (channels // HEADS)
    sides = []
    for at in range(0, channels, width):
        q = queries[:, at : at + width]
        stacked = jnp.concatenate([q * mask.astype(BF16) for mask in masks], axis=0)
        scores = lax.dot_general(
            stacked,
            key_rows[:, at : at + width],
            (((1,), (1,)), ((), ())),
            preferred_element_type=F32,
        )
        top = jnp.max(scores, axis=-1, keepdims=True)
        grown = jnp.exp(scores - top)
        total = jnp.sum(grown, axis=-1, keepdims=True)
        weights = (grown * (1.0 / total)).astype(BF16)
        mixed = jnp.dot(weights, value_rows[:, at : at + width], preferred_element_type=F32)
        side = mixed[:PATCH] * masks[0]
        for h in range(1, HEADS_TOGETHER):
            side = side + mixed[h * PATCH : (h + 1) * PATCH] * masks[h]
        sides.append(side.astype(BF16))
    return jnp.concatenate(sides, axis=1)


def finish(rows, attended, gain, w_proj, w_up, w_down):
    first = (
        rows.astype(F32) + jnp.dot(attended, w_proj[...], preferred_element_type=F32)
    ).astype(BF16)
    hidden = layer_norm(first, gain)
    total = first.astype(F32)
    piece = 512
    for at in range(0, w_up.shape[1], piece):
        upper = jnp.dot(hidden, w_up[:, at : at + piece], preferred_element_type=F32)
        act = gelu(upper).astype(BF16)
        total = total + jnp.dot(act, w_down[at : at + piece, :], preferred_element_type=F32)
    return total.astype(BF16)


def project_rows(parts, first_row, gains, w_qkv, whole):
    channels = w_qkv.shape[1]
    rows = parts[0].shape[0]
    all_normed = []
    for i, part in enumerate(parts):
        normed = layer_norm(part[...], gains[0:1, :])
        whole[first_row + i * rows : first_row + (i + 1) * rows, :] = jnp.dot(
            normed, w_qkv[0, :, channels:], preferred_element_type=F32
        ).astype(BF16)
        all_normed.append(normed)
    return all_normed


def project_kernel(first_row, *refs):
    *parts, gains, w_qkv, _, whole = refs
    project_rows(parts, first_row, gains, w_qkv, whole)


def own_kernel(*refs):
    *parts, gains, w_qkv, whole, queries = refs
    channels = w_qkv.shape[1]
    rows = parts[0].shape[0]
    scale = (channels // HEADS) ** (-0.5)
    for i, normed in enumerate(project_rows(parts, 0, gains, w_qkv, whole)):
        own = jnp.dot(normed, w_qkv[0, :, :channels], preferred_element_type=F32).astype(BF16)
        queries[i * rows : (i + 1) * rows, :] = (own * BF16(scale)).astype(BF16)


def first_kernel(
    pattern,
    points,
    queries,
    keyed,
    gains,
    w_proj,
    w_up,
    w_down,
    send,
    outgoing,
    attended,
):
    channels = points.shape[1]
    patches, chosen = pattern.shape
    masks = head_masks(channels // HEADS)
    for p in range(patches):
        pieces = [keyed[p * PATCH : (p + 1) * PATCH, :]]
        for j in range(chosen):
            start = pl.multiple_of(pattern[p, j] * PATCH, PATCH)
            pieces.append(keyed[pl.ds(start, PATCH), :])
        both = jnp.concatenate(pieces, axis=0)
        attended[p * PATCH : (p + 1) * PATCH, :] = attend_patch(
            queries[p * PATCH : (p + 1) * PATCH, :], both[:, :channels], both[:, channels:], masks
        )
    first = finish(
        points[...], attended[...], gains[1:2, :], w_proj.at[0], w_up.at[0], w_down.at[0]
    )
    outgoing[...] = jnp.dot(send[...], first, preferred_element_type=F32).astype(BF16)


def second_kernel(
    pattern,
    incoming,
    place,
    gains,
    w_qkv,
    w_proj,
    w_up,
    w_down,
    w_head,
    features,
    normals,
    kv,
    attended,
):
    channels = features.shape[1]
    patches, chosen = pattern.shape
    second = jnp.dot(place[...], incoming[...], preferred_element_type=F32).astype(BF16)
    normed = layer_norm(second, gains[2:3, :])
    scale = (channels // HEADS) ** (-0.5)
    queries = (
        jnp.dot(normed, w_qkv[1, :, :channels], preferred_element_type=F32).astype(BF16)
        * BF16(scale)
    ).astype(BF16)
    kv[...] = jnp.dot(normed, w_qkv[1, :, channels:], preferred_element_type=F32).astype(BF16)
    masks = head_masks(channels // HEADS)
    for p in range(patches):
        pieces = [kv[p * PATCH : (p + 1) * PATCH, :]]
        for j in range(chosen):
            start = pl.multiple_of(pattern[p, j] * PATCH, PATCH)
            pieces.append(kv[pl.ds(start, PATCH), :])
        both = jnp.concatenate(pieces, axis=0)
        attended[p * PATCH : (p + 1) * PATCH, :] = attend_patch(
            queries[p * PATCH : (p + 1) * PATCH, :], both[:, :channels], both[:, channels:], masks
        )
    done = finish(
        second, attended[...], gains[3:4, :], w_proj.at[1], w_up.at[1], w_down.at[1]
    )
    features[...] = done
    normals[...] = lax.dot_general(
        w_head[...], done, (((1,), (1,)), ((), ())), preferred_element_type=F32
    )


VMEM_SPEC = pl.BlockSpec(memory_space=pltpu.VMEM)
SMEM_SPEC = pl.BlockSpec(memory_space=pltpu.SMEM)


def shards(
    points,
    pattern_first,
    pattern_second,
    destination,
    norm_gains,
    w_qkv,
    w_proj,
    w_up,
    w_down,
    w_head,
):
    rows_here, channels = points.shape
    patches, chosen = pattern_first.shape
    devices = lax.axis_size("grp") * lax.axis_size("seq")
    capacity = 2 * rows_here // devices
    slot_total = devices * capacity

    shards_in_group = lax.axis_size("seq")
    chips = shards_in_group // 2
    onward = [(i, (i + 2) % shards_in_group) for i in range(shards_in_group)]
    swap = [(i, i ^ 1) for i in range(shards_in_group)]
    ring = shards_in_group * rows_here * 2 * channels * 2 <= RING_BYTES
    kept_rows = shards_in_group * rows_here if ring else patches * (1 + chosen) * PATCH
    part = rows_here // RING_PARTS
    column = [points[i * part : (i + 1) * part] for i in range(RING_PARTS)]

    block_bytes = rows_here * channels * 2
    kv_shape = jax.ShapeDtypeStruct((kept_rows, 2 * channels), BF16)

    def project(keyed, slot, parts):
        return pl.pallas_call(
            functools.partial(project_kernel, slot * rows_here),
            out_shape=kv_shape,
            in_specs=[VMEM_SPEC] * (len(parts) + 3),
            out_specs=VMEM_SPEC,
            input_output_aliases={len(parts) + 2: 0},
            cost_estimate=pl.CostEstimate(
                flops=4 * rows_here * channels**2 * len(parts) // RING_PARTS,
                bytes_accessed=5 * block_bytes * len(parts) // RING_PARTS,
                transcendentals=0,
            ),
            compiler_params=pltpu.CompilerParams(vmem_limit_bytes=VMEM_BYTES),
            name="project",
        )(*parts, norm_gains, w_qkv, keyed)

    keyed, queries = pl.pallas_call(
        own_kernel,
        out_shape=(kv_shape, jax.ShapeDtypeStruct((rows_here, channels), BF16)),
        in_specs=[VMEM_SPEC] * (RING_PARTS + 2),
        out_specs=(VMEM_SPEC, VMEM_SPEC),
        cost_estimate=pl.CostEstimate(
            flops=6 * rows_here * channels**2, bytes_accessed=6 * block_bytes, transcendentals=0
        ),
        compiler_params=pltpu.CompilerParams(vmem_limit_bytes=VMEM_BYTES),
        name="project_own",
    )(*column, norm_gains, w_qkv)
    me = lax.axis_index("seq")
    if ring:
        beside = [lax.ppermute(rows, "seq", swap) for rows in column]
        waiting = [(1, beside)]
        for step in range(1, chips):
            column = [lax.ppermute(rows, "seq", onward) for rows in column]
            for slot, parts in waiting:
                keyed = project(keyed, slot, parts)
            column, keyed = lax.optimization_barrier((column, keyed))
            beside = [lax.ppermute(rows, "seq", swap) for rows in column]
            waiting = [(2 * step, column), (2 * step + 1, beside)]
        for slot, parts in waiting:
            keyed = project(keyed, slot, parts)
        owner = pattern_first // patches
        slot_of = 2 * ((me // 2 - owner // 2) % chips) + (me % 2 != owner % 2).astype(jnp.int32)
        pattern_slots = slot_of * patches + pattern_first % patches
    else:
        group = lax.all_gather(points, "seq", axis=0, tiled=True)
        picked = group.reshape(-1, PATCH, channels)[pattern_first].reshape(-1, channels)
        keyed = project(keyed, 1, [picked])
        pattern_slots = patches + jnp.arange(patches * chosen, dtype=jnp.int32).reshape(
            patches, chosen
        )

    target = destination // rows_here
    place_at = destination % rows_here
    onehot_dev = (target[:, None] == jnp.arange(devices, dtype=jnp.int32)[None, :]).astype(
        jnp.int32
    )
    earlier = jnp.cumsum(onehot_dev, axis=0) - onehot_dev
    send_rank = jnp.sum(earlier * onehot_dev, axis=1)
    slot_index = target * capacity + send_rank
    row_ids = jnp.arange(rows_here, dtype=jnp.int32)
    slot_ids = jnp.arange(slot_total, dtype=jnp.int32)
    match_send = slot_index[None, :] == slot_ids[:, None]
    send = match_send.astype(BF16)
    out_places = jnp.sum(jnp.where(match_send, place_at[None, :] + 1, 0), axis=1) - 1
    in_places = lax.all_to_all(
        out_places.reshape(devices, capacity),
        ("grp", "seq"),
        split_axis=0,
        concat_axis=0,
        tiled=True,
    ).reshape(-1)
    place = (in_places[None, :] == row_ids[:, None]).astype(BF16)

    weights = (w_proj, w_up, w_down)
    outgoing = pl.pallas_call(
        first_kernel,
        out_shape=jax.ShapeDtypeStruct((slot_total, channels), BF16),
        in_specs=[SMEM_SPEC] + [VMEM_SPEC] * 8,
        out_specs=VMEM_SPEC,
        scratch_shapes=[pltpu.VMEM((rows_here, channels), BF16)],
        compiler_params=pltpu.CompilerParams(vmem_limit_bytes=VMEM_BYTES),
        name="block_first",
    )(pattern_slots, points, queries, keyed, norm_gains, *weights, send)

    incoming = lax.all_to_all(
        outgoing.reshape(devices, capacity, channels),
        ("grp", "seq"),
        split_axis=0,
        concat_axis=0,
        tiled=True,
    ).reshape(slot_total, channels)

    return pl.pallas_call(
        second_kernel,
        out_shape=(
            jax.ShapeDtypeStruct((rows_here, channels), BF16),
            jax.ShapeDtypeStruct((w_head.shape[0], rows_here), F32),
        ),
        in_specs=[SMEM_SPEC] + [VMEM_SPEC] * 8,
        out_specs=(VMEM_SPEC, VMEM_SPEC),
        scratch_shapes=[
            pltpu.VMEM((rows_here, 2 * channels), BF16),
            pltpu.VMEM((rows_here, channels), BF16),
        ],
        compiler_params=pltpu.CompilerParams(vmem_limit_bytes=VMEM_BYTES),
        name="block_second",
    )(pattern_second, incoming, place, norm_gains, w_qkv, *weights, w_head)


def solution(mesh):
    placed = (
        P(("grp", "seq"), None),
        P(("grp", "seq"), None),
        P(("grp", "seq"), None),
        P(("grp", "seq")),
        P(),
        P(),
        P(),
        P(),
        P(),
        P(),
    )
    return jax.shard_map(
        shards,
        mesh=mesh,
        in_specs=placed,
        out_specs=(P(("grp", "seq"), None), P(None, ("grp", "seq"))),
        check_vma=False,
    )
```

time: 123 us -> 123 us (level)
  local copies, waits for them, and re-layouts: 2.41 us -> 33.6 us
  waiting for transfers between devices: 65.7 us -> 35.7 us
  between operations: 14.2 us -> 0.95 us
  starting transfers between devices: 10.9 us -> 20 us
  Pallas kernels: 22 us -> 27.4 us
  other arithmetic: 7.74 us -> 4.73 us
    all_gather x1 -> x0, waiting for transfers between devices: 40 us -> none  [shards(): gathered = lax.all_gather(normed, 'seq', axis=0, tiled=True)]
    unnamed x18 -> x54, local copies, waits for them, and re-layouts: 0.2 us -> 30.3 us
    pallas_call x0 -> x8, Pallas kernels: none -> 11.6 us  [the longest x7 9.43 us: project(): pl.pallas_call(functools.partial(project_kernel, slot * rows_here), out_s...]
    ppermute x0 -> x14, waiting for transfers between devices: none -> 11 us  [the longest x6 10.6 us: shards(): column = [lax.ppermute(rows, 'seq', onward) for rows in column]]
    ppermute x0 -> x14, starting transfers between devices: none -> 10.4 us  [the longest x6 8.92 us: shards(): column = [lax.ppermute(rows, 'seq', onward) for rows in column]]
    pallas_call x1, Pallas kernels: 12.7 us -> 6.7 us  [shards(): pl.pallas_call(first_kernel, out_shape=jax.ShapeDtypeStruct((slot_total,...]
    reduce_sum x2 -> x0, other arithmetic: 2.61 us -> none  [the longest x1 1.32 us: layer_norm(): spread = jnp.mean((values - average) ** 2, axis=-1, keepdims=True)]
    convert_element_type x1 -> x0, other arithmetic: 2.07 us -> none  [layer_norm(): return ((values - average) * lax.rsqrt(spread + 1e-05) * gains).astype(BF16)]
  transfers between devices with their start and end apart: 3 -> 16, of which waited for: 2 -> 5; matrix products, arithmetic and copies ran while one was open for 4% -> 5% of each run, Pallas kernels for 10% -> 15%
where the time goes in v3:
time: 123 us; the launch traced here: 122 us
  waiting for transfers between devices  35.7 us (29%)
  local copies, waits for them, and re-layouts  33.6 us (27%)
  Pallas kernels  27.4 us (22%)
  starting transfers between devices  20 us (16%)
  other arithmetic  4.73 us (4%)
    unnamed x54, local copies, waits for them, and re-layouts  30.3 us
    all_to_all x1, waiting for transfers between devices, shards(): lax.all_to_all(outgoing.reshape(devices, capacity, channels), ('grp', 'se...  24.7 us
    ppermute x6, waiting for transfers between devices, shards(): column = [lax.ppermute(rows, 'seq', onward) for rows in column]  10.6 us
    pallas_call x7, Pallas kernels, project(): pl.pallas_call(functools.partial(project_kernel, slot * rows_here), out_s...  9.43 us
    pallas_call x1, Pallas kernels, shards(): pl.pallas_call(second_kernel, out_shape=(jax.ShapeDtypeStruct((rows_here,...  9.12 us
    ppermute x6, starting transfers between devices, shards(): column = [lax.ppermute(rows, 'seq', onward) for rows in column]  8.92 us
    pallas_call x1, Pallas kernels, shards(): pl.pallas_call(first_kernel, out_shape=jax.ShapeDtypeStruct((slot_total,...  6.7 us
    all_to_all x1, starting transfers between devices, shards(): lax.all_to_all(out_places.reshape(devices, capacity), ('grp', 'seq'), spl...  5.79 us
  transfers between devices with their start and end apart: 16, of which 5 were waited for; matrix products, arithmetic and copies ran while one was open for 5% of the time, Pallas kernels for 15%

profile of v3, /device:TPU:0, one launch (start us, length us, event | category | flops | bytes accessed | tf_op | source)
XLA Modules:
  0.0 122.3 jit_solution(12323045677933251247)
XLA Ops:
  0.6 1.8 %fusion.17 = (bf16[256,512]{1,0:T(8,128)(2,1)S(1)}, bf16[256,512]{1,0:T(8,128)(2,1)}) fusion(bf16[512,512]{1,0:T(8,128)(2,1)} %points.1), kind=kLoop, calls=%fused_computation.49 | loop fusion | bytes 1048576 | tf_op jit(solution)/shard_map/slice | solution.py:211
  2.4 0.5 collective-permute-start.2
  2.9 2.6 %collective-permute-start = (bf16[256,512]{1,0:T(8,128)(2,1)}, bf16[256,512]{1,0:T(8,128)(2,1)}, u32[]{:S(2)}, u32[]{:S(2)}) collective-permute-start(bf16[256,512]{1,0:T(8,128)(2,1)} %get-tuple-element.25.refs_0_), channel_id=1, source_target_pairs={{0,2},{1,3},{2,4},{3,5},{4,6},{5,7},{6,0},{7,1},{8,10},{9,11},{10,... | collective-permute-start | bytes 786440 | tf_op jit(solution)/shard_map/ppermute | solution.py:248
  5.7 1.6 %collective-permute-start.1 = (bf16[256,512]{1,0:T(8,128)(2,1)S(1)}, bf16[256,512]{1,0:T(8,128)(2,1)}, u32[]{:S(2)}, u32[]{:S(2)}) collective-permute-start(bf16[256,512]{1,0:T(8,128)(2,1)S(1)} %get-tuple-element.24.refs_1_), channel_id=1, source_target_pairs={{0,2},{1,3},{2,4},{3,5},{4,6},{5,7},{6,0},{7,1},{8,10},{9,11},{10,... | collective-permute-start | bytes 786440 | tf_op jit(solution)/shard_map/ppermute | solution.py:248
  7.3 0.7 fusion.15
  8.0 1.2 reduce-window.6
  9.5 1.9 %copy-done.4 = bf16[2,512,1536]{2,1,0:T(8,128)(2,1)S(1)} copy-done((bf16[2,512,1536]{2,1,0:T(8,128)(2,1)S(1)}, bf16[2,512,1536]{2,1,0:T(8,128)(2,1)}, u32[]{:S(2)}) %copy-start.4) | copy-done | bytes 3145752
  11.4 0.7 copy-done.15
  12.1 2.1 %project_own.1 = (bf16[4096,1024]{1,0:T(8,128)(2,1)S(1)}, bf16[512,512]{1,0:T(8,128)(2,1)S(1)}) custom-call(bf16[256,512]{1,0:T(8,128)(2,1)} %get-tuple-element.25.refs_0_, bf16[256,512]{1,0:T(8,128)(2,1)S(1)} %get-tuple-element.24.refs_1_, f32[4,512]{1,0:T(4,128)S(1)} %copy-done.15, bf16[2,512,1536]{2,1,0:T(8,128)(2,1)S(1)} %copy-done.4), custom_call_target="tpu_custom_call" | custom-call | flops 805306368 | bytes 3145728 | tf_op jit(solution)/shard_map/project_own/pallas_call | solution.py:232
  14.3 0.8 copy-done.17
  15.4 0.7 copy-done.19
  16.1 0.7 copy-done.21
  16.8 0.9 copy-done.20
  17.7 0.9 copy-done.22
  18.7 0.9 project.7.refs_4_
  19.6 3.3 %copy-done = bf16[4096,1024]{1,0:T(8,128)(2,1)} copy-done((bf16[4096,1024]{1,0:T(8,128)(2,1)}, bf16[4096,1024]{1,0:T(8,128)(2,1)S(1)}, u32[]{:S(2)}) %copy-start) | copy-done | bytes 8388632
  22.9 1.6 %collective-permute-start.4 = (bf16[256,512]{1,0:T(8,128)(2,1)}, bf16[256,512]{1,0:T(8,128)(2,1)S(1)}, u32[]{:S(2)}, u32[]{:S(2)}) collective-permute-start(bf16[256,512]{1,0:T(8,128)(2,1)} %collective-permute-done.refs_0_), channel_id=1, source_target_pairs={{0,2},{1,3},{2,4},{3,5},{4,6},{5,7},{6,0},{7,1},{8,10},{9,11},{10,... | collective-permute-start | bytes 786440 | tf_op jit(solution)/shard_map/ppermute | solution.py:248
  25.0 0.7 sub.40
  25.7 5.8 %all-to-all-start.1 = ((s32[32,1,32]{2,1,0:T(1,128)}), s32[32,1,32]{2,1,0:T(1,128)S(1)}, u32[]{:S(2)}, u32[]{:S(2)}) async-start(s32[32,1,32]{2,1,0:T(1,128)} %sub.40), calls=%async_computation.1 | async-start | bytes 32768 | tf_op jit(solution)/shard_map/all_to_all | solution.py:280
  31.6 3.4 %copy-done.1 = bf16[4096,1024]{1,0:T(8,128)(2,1)S(1)} copy-done((bf16[4096,1024]{1,0:T(8,128)(2,1)S(1)}, bf16[4096,1024]{1,0:T(8,128)(2,1)}, u32[]{:S(2)}) %copy-start.1) | copy-done | bytes 8388632
  34.9 2.0 %project.8.refs_4_ = bf16[4096,1024]{1,0:T(8,128)(2,1)S(1)} custom-call(bf16[256,512]{1,0:T(8,128)(2,1)} %collective-permute-done.refs_0_, bf16[256,512]{1,0:T(8,128)(2,1)} %collective-permute-done.1.refs_1_, f32[4,512]{1,0:T(4,128)S(1)} %copy-done.16, bf16[2,512,1536]{2,1,0:T(8,128)(2,1)S(1)} %copy-done.5, ...), custom_call_target="tpu_custom_call", output_to_operand_aliasing={{}: (4, {})} | custom-call | flops 536870912 | bytes 2621440 | tf_op jit(solution)/shard_map/project/pallas_call | solution.py:217
  36.9 2.0 %project.9.refs_4_ = bf16[4096,1024]{1,0:T(8,128)(2,1)S(1)} custom-call(bf16[256,512]{1,0:T(8,128)(2,1)} %collective-permute-done.6.refs_0_, bf16[256,512]{1,0:T(8,128)(2,1)} %collective-permute-done.7.refs_1_, f32[4,512]{1,0:T(4,128)S(1)} %copy-done.16, bf16[2,512,1536]{2,1,0:T(8,128)(2,1)S(1)} %copy-done.5, ...), custom_call_target="tpu_custom_call", output_to_operand_aliasing={{}: (4, {})} | custom-call | flops 536870912 | bytes 2621440 | tf_op jit(solution)/shard_map/project/pallas_call | solution.py:217
  38.9 0.6 collective-permute-done.5.refs_1_
  39.5 1.4 %collective-permute-start.8 = (bf16[256,512]{1,0:T(8,128)(2,1)S(1)}, bf16[256,512]{1,0:T(8,128)(2,1)S(1)}, u32[]{:S(2)}, u32[]{:S(2)}) collective-permute-start(bf16[256,512]{1,0:T(8,128)(2,1)S(1)} %collective-permute-done.4.refs_0_), channel_id=1, source_target_pairs={{0,2},{1,3},{2,4},{3,5},{4,6},{5,7},{6,0},{7,1},{8,10},{9,11},{10,... | collective-permute-start | bytes 786440 | tf_op jit(solution)/shard_map/ppermute | solution.py:248
  41.0 1.5 %collective-permute-start.9 = (bf16[256,512]{1,0:T(8,128)(2,1)}, bf16[256,512]{1,0:T(8,128)(2,1)S(1)}, u32[]{:S(2)}, u32[]{:S(2)}) collective-permute-start(bf16[256,512]{1,0:T(8,128)(2,1)} %collective-permute-done.5.refs_1_), channel_id=1, source_target_pairs={{0,2},{1,3},{2,4},{3,5},{4,6},{5,7},{6,0},{7,1},{8,10},{9,11},{10,... | collective-permute-start | bytes 786440 | tf_op jit(solution)/shard_map/ppermute | solution.py:248
  42.9 1.9 %project.10.refs_4_ = bf16[4096,1024]{1,0:T(8,128)(2,1)S(1)} custom-call(bf16[256,512]{1,0:T(8,128)(2,1)S(1)} %collective-permute-done.4.refs_0_, bf16[256,512]{1,0:T(8,128)(2,1)} %collective-permute-done.5.refs_1_, f32[4,512]{1,0:T(4,128)S(1)} %copy-done.16, bf16[2,512,1536]{2,1,0:T(8,128)(2,1)S(1)} %copy-done.5, ...), custom_call_target="tpu_custom_call", output_to_operand_aliasing={{}: (4, {})} | custom-call | flops 536870912 | bytes 2621440 | tf_op jit(solution)/shard_map/project/pallas_call | solution.py:217
  44.8 0.9 project.11.refs_4_
  45.7 4.7 %collective-permute-done.8.refs_0_ = bf16[256,512]{1,0:T(8,128)(2,1)S(1)} collective-permute-done((bf16[256,512]{1,0:T(8,128)(2,1)S(1)}, bf16[256,512]{1,0:T(8,128)(2,1)S(1)}, u32[]{:S(2)}, u32[]{:S(2)}) %collective-permute-start.8) | collective-permute-done | bytes 262176 | tf_op jit(solution)/shard_map/ppermute | solution.py:248
  50.4 5.2 %collective-permute-done.9.refs_1_ = bf16[256,512]{1,0:T(8,128)(2,1)S(1)} collective-permute-done((bf16[256,512]{1,0:T(8,128)(2,1)}, bf16[256,512]{1,0:T(8,128)(2,1)S(1)}, u32[]{:S(2)}, u32[]{:S(2)}) %collective-permute-start.9) | collective-permute-done | bytes 262176 | tf_op jit(solution)/shard_map/ppermute | solution.py:248
  55.7 0.5 collective-permute-start.13
  56.2 0.9 project.12.refs_4_
  57.6 0.9 project.13.keyed
  58.5 4.2 %copy-done.2 = bf16[4096,1024]{1,0:T(8,128)(2,1)} copy-done((bf16[4096,1024]{1,0:T(8,128)(2,1)}, bf16[4096,1024]{1,0:T(8,128)(2,1)S(1)}, u32[]{:S(2)}) %copy-start.2) | copy-done | bytes 8388632
  62.7 0.5 copy-done.8
  63.3 0.6 copy-done.11
  64.1 3.4 %copy-done.3 = bf16[4096,1024]{1,0:T(8,128)(2,1)S(1)} copy-done((bf16[4096,1024]{1,0:T(8,128)(2,1)S(1)}, bf16[4096,1024]{1,0:T(8,128)(2,1)}, u32[]{:S(2)}) %copy-start.3) | copy-done | bytes 8388632
  67.5 6.7 %block_first.1 = bf16[1024,512]{1,0:T(8,128)(2,1)S(1)} custom-call(s32[8,3]{1,0:T(8,128)S(1)} %fusion.11.pattern, bf16[512,512]{1,0:T(8,128)(2,1)S(1)} %copy-done.14, bf16[512,512]{1,0:T(8,128)(2,1)S(1)} %copy-done.18, bf16[4096,1024]{1,0:T(8,128)(2,1)S(1)} %copy-done.3, f32[4,512]{1,0:T(4,128)S(1)} %copy-done.16, bf16[2,512,512]{2,1,0:T(8,128)(2,1)S(1)} %copy-done.11, ...), custom_call_target="tpu_custom_call" | custom-call | tf_op jit(solution)/shard_map/block_first/pallas_call | solution.py:290
  74.2 0.9 copy-done.13
  75.1 3.9 %all-to-all-start = ((bf16[32,32,512]{2,1,0:T(8,128)(2,1)}), bf16[32,32,512]{2,1,0:T(8,128)(2,1)}, u32[]{:S(2)}, u32[]{:S(2)}) async-start(bf16[32,32,512]{2,1,0:T(8,128)(2,1)} %bitcast.22), calls=%async_computation | async-start | bytes 2097152 | tf_op jit(solution)/shard_map/all_to_all | solution.py:300
  79.1 0.5 broadcast.107
  79.6 0.7 reduce.5
  80.4 1.3 %fusion.1.place = bf16[512,1024]{1,0:T(8,128)(2,1)} fusion(s32[1024]{0:T(1024)S(1)} %eq.69), kind=kLoop, calls=%fused_computation.4 | loop fusion | flops 1048576 | bytes 1052672 | tf_op jit(solution)/shard_map/convert_element_type | solution.py:287
  81.6 24.7 %all-to-all-done = bf16[32,32,512]{2,1,0:T(8,128)(2,1)} async-done(((bf16[32,32,512]{2,1,0:T(8,128)(2,1)}), bf16[32,32,512]{2,1,0:T(8,128)(2,1)}, u32[]{:S(2)}, u32[]{:S(2)}) %all-to-all-start) | async-done | bytes 1048608 | tf_op jit(solution)/shard_map/all_to_all | solution.py:300
  106.3 2.2 %copy-done.7 = bf16[2,512,2048]{2,1,0:T(8,128)(2,1)S(1)} copy-done((bf16[2,512,2048]{2,1,0:T(8,128)(2,1)S(1)}, bf16[2,512,2048]{2,1,0:T(8,128)(2,1)}, u32[]{:S(2)}) %copy-start.7) | copy-done | bytes 4194328
  108.5 2.2 %copy-done.9 = bf16[2,2048,512]{2,1,0:T(8,128)(2,1)S(1)} copy-done((bf16[2,2048,512]{2,1,0:T(8,128)(2,1)S(1)}, bf16[2,2048,512]{2,1,0:T(8,128)(2,1)}, u32[]{:S(2)}) %copy-start.9) | copy-done | bytes 4194328
  110.7 1.2 copy-done.10
  111.9 1.2 copy-done.12
  113.2 9.1 %block_second.1 = (bf16[512,512]{1,0:T(8,128)(2,1)}, f32[3,512]{1,0:T(4,128)}) custom-call(s32[8,3]{1,0:T(8,128)S(1)} %copy.29.pattern, bf16[1024,512]{1,0:T(8,128)(2,1)} %bitcast.3.incoming, bf16[512,1024]{1,0:T(8,128)(2,1)S(1)} %copy-done.10, f32[4,512]{1,0:T(4,128)S(1)} %copy-done.16, bf16[2,512,1536]{2,1,0:T(8,128)(2,1)S(1)} %copy-done.5, ...), custom_call_target="tpu_custom_call" | custom-call | tf_op jit(solution)/shard_map/block_second/pallas_call | solution.py:308
  (66 shorter events, 2.9 us)
Async XLA Ops:
  0.6 16.1 %copy-start.16 = (f32[4,512]{1,0:T(4,128)S(1)}, f32[4,512]{1,0:T(4,128)}, u32[]{:S(2)}) copy-start(f32[4,512]{1,0:T(4,128)} %gains.3) | copy-start | bytes 24580
  2.4 12.9 %collective-permute-start.2 = (bf16[256,512]{1,0:T(8,128)(2,1)}, bf16[256,512]{1,0:T(8,128)(2,1)S(1)}, u32[]{:S(2)}, u32[]{:S(2)}) collective-permute-start(bf16[256,512]{1,0:T(8,128)(2,1)} %get-tuple-element.25.refs_0_), channel_id=1, source_target_pairs={{0,1},{1,0},{2,3},{3,2},{4,5},{5,4},{6,7},{7,6},{8,9},{9,8},{10,11... | collective-permute-start | bytes 786440 | tf_op jit(solution)/shard_map/ppermute | solution.py:245
  2.9 20.0 %collective-permute-start = (bf16[256,512]{1,0:T(8,128)(2,1)}, bf16[256,512]{1,0:T(8,128)(2,1)}, u32[]{:S(2)}, u32[]{:S(2)}) collective-permute-start(bf16[256,512]{1,0:T(8,128)(2,1)} %get-tuple-element.25.refs_0_), channel_id=1, source_target_pairs={{0,2},{1,3},{2,4},{3,5},{4,6},{5,7},{6,0},{7,1},{8,10},{9,11},{10,... | collective-permute-start | bytes 786440 | tf_op jit(solution)/shard_map/ppermute | solution.py:248
  5.5 10.6 %collective-permute-start.3 = (bf16[256,512]{1,0:T(8,128)(2,1)S(1)}, bf16[256,512]{1,0:T(8,128)(2,1)S(1)}, u32[]{:S(2)}, u32[]{:S(2)}) collective-permute-start(bf16[256,512]{1,0:T(8,128)(2,1)S(1)} %get-tuple-element.24.refs_1_), channel_id=1, source_target_pairs={{0,1},{1,0},{2,3},{3,2},{4,5},{5,4},{6,7},{7,6},{8,9},{9,8},{10,11... | collective-permute-start | bytes 786440 | tf_op jit(solution)/shard_map/ppermute | solution.py:245
  5.7 17.2 %collective-permute-start.1 = (bf16[256,512]{1,0:T(8,128)(2,1)S(1)}, bf16[256,512]{1,0:T(8,128)(2,1)}, u32[]{:S(2)}, u32[]{:S(2)}) collective-permute-start(bf16[256,512]{1,0:T(8,128)(2,1)S(1)} %get-tuple-element.24.refs_1_), channel_id=1, source_target_pairs={{0,2},{1,3},{2,4},{3,5},{4,6},{5,7},{6,0},{7,1},{8,10},{9,11},{10,... | collective-permute-start | bytes 786440 | tf_op jit(solution)/shard_map/ppermute | solution.py:248
  9.5 1.9 %copy-start.4 = (bf16[2,512,1536]{2,1,0:T(8,128)(2,1)S(1)}, bf16[2,512,1536]{2,1,0:T(8,128)(2,1)}, u32[]{:S(2)}) copy-start(bf16[2,512,1536]{2,1,0:T(8,128)(2,1)} %w_qkv.1) | copy-start | bytes 9437188
  11.4 0.7 copy-start.15
  14.3 0.8 copy-start.17
  15.3 0.7 copy-start.19
  16.1 0.7 copy-start.21
  16.8 1.0 copy-start.20
  17.7 0.9 copy-start.22
  18.7 12.8 %copy-start.24 = (s32[8,3]{0,1:T(4,128)S(1)}, s32[8,3]{0,1:T(4,128)}, u32[]{:S(2)}) copy-start(s32[8,3]{0,1:T(4,128)} %param.11) | copy-start | bytes 292
  18.7 12.9 %copy-start.5 = (bf16[2,512,1536]{2,1,0:T(8,128)(2,1)S(1)}, bf16[2,512,1536]{2,1,0:T(8,128)(2,1)}, u32[]{:S(2)}) copy-start(bf16[2,512,1536]{2,1,0:T(8,128)(2,1)} %w_qkv.1) | copy-start | bytes 9437188
  19.6 3.3 %copy-start = (bf16[4096,1024]{1,0:T(8,128)(2,1)}, bf16[4096,1024]{1,0:T(8,128)(2,1)S(1)}, u32[]{:S(2)}) copy-start(bf16[4096,1024]{1,0:T(8,128)(2,1)S(1)} %project.7.refs_4_) | copy-start | bytes 25165828
  22.9 14.0 %collective-permute-start.6 = (bf16[256,512]{1,0:T(8,128)(2,1)}, bf16[256,512]{1,0:T(8,128)(2,1)}, u32[]{:S(2)}, u32[]{:S(2)}) collective-permute-start(bf16[256,512]{1,0:T(8,128)(2,1)} %collective-permute-done.refs_0_), channel_id=1, source_target_pairs={{0,1},{1,0},{2,3},{3,2},{4,5},{5,4},{6,7},{7,6},{8,9},{9,8},{10,11... | collective-permute-start | bytes 786440 | tf_op jit(solution)/shard_map/ppermute | solution.py:252
  22.9 16.0 %collective-permute-start.4 = (bf16[256,512]{1,0:T(8,128)(2,1)}, bf16[256,512]{1,0:T(8,128)(2,1)S(1)}, u32[]{:S(2)}, u32[]{:S(2)}) collective-permute-start(bf16[256,512]{1,0:T(8,128)(2,1)} %collective-permute-done.refs_0_), channel_id=1, source_target_pairs={{0,2},{1,3},{2,4},{3,5},{4,6},{5,7},{6,0},{7,1},{8,10},{9,11},{10,... | collective-permute-start | bytes 786440 | tf_op jit(solution)/shard_map/ppermute | solution.py:248
  24.5 12.4 %collective-permute-start.7 = (bf16[256,512]{1,0:T(8,128)(2,1)}, bf16[256,512]{1,0:T(8,128)(2,1)}, u32[]{:S(2)}, u32[]{:S(2)}) collective-permute-start(bf16[256,512]{1,0:T(8,128)(2,1)} %collective-permute-done.1.refs_1_), channel_id=1, source_target_pairs={{0,1},{1,0},{2,3},{3,2},{4,5},{5,4},{6,7},{7,6},{8,9},{9,8},{10,11... | collective-permute-start | bytes 786440 | tf_op jit(solution)/shard_map/ppermute | solution.py:252
  24.7 14.8 %collective-permute-start.5 = (bf16[256,512]{1,0:T(8,128)(2,1)}, bf16[256,512]{1,0:T(8,128)(2,1)}, u32[]{:S(2)}, u32[]{:S(2)}) collective-permute-start(bf16[256,512]{1,0:T(8,128)(2,1)} %collective-permute-done.1.refs_1_), channel_id=1, source_target_pairs={{0,2},{1,3},{2,4},{3,5},{4,6},{5,7},{6,0},{7,1},{8,10},{9,11},{10,... | collective-permute-start | bytes 786440 | tf_op jit(solution)/shard_map/ppermute | solution.py:248
  25.7 49.5 %all-to-all-start.1 = ((s32[32,1,32]{2,1,0:T(1,128)}), s32[32,1,32]{2,1,0:T(1,128)S(1)}, u32[]{:S(2)}, u32[]{:S(2)}) async-start(s32[32,1,32]{2,1,0:T(1,128)} %sub.40), calls=%async_computation.1 | async-start | bytes 32768 | tf_op jit(solution)/shard_map/all_to_all | solution.py:280
  31.6 3.4 %copy-start.1 = (bf16[4096,1024]{1,0:T(8,128)(2,1)S(1)}, bf16[4096,1024]{1,0:T(8,128)(2,1)}, u32[]{:S(2)}) copy-start(bf16[4096,1024]{1,0:T(8,128)(2,1)} %copy-done) | copy-start | bytes 25165828
  39.5 5.2 %collective-permute-start.10 = (bf16[256,512]{1,0:T(8,128)(2,1)S(1)}, bf16[256,512]{1,0:T(8,128)(2,1)S(1)}, u32[]{:S(2)}, u32[]{:S(2)}) collective-permute-start(bf16[256,512]{1,0:T(8,128)(2,1)S(1)} %collective-permute-done.4.refs_0_), channel_id=1, source_target_pairs={{0,1},{1,0},{2,3},{3,2},{4,5},{5,4},{6,7},{7,6},{8,9},{9,8},{10,11... | collective-permute-start | bytes 786440 | tf_op jit(solution)/shard_map/ppermute | solution.py:252
  39.5 10.9 %collective-permute-start.8 = (bf16[256,512]{1,0:T(8,128)(2,1)S(1)}, bf16[256,512]{1,0:T(8,128)(2,1)S(1)}, u32[]{:S(2)}, u32[]{:S(2)}) collective-permute-start(bf16[256,512]{1,0:T(8,128)(2,1)S(1)} %collective-permute-done.4.refs_0_), channel_id=1, source_target_pairs={{0,2},{1,3},{2,4},{3,5},{4,6},{5,7},{6,0},{7,1},{8,10},{9,11},{10,... | collective-permute-start | bytes 786440 | tf_op jit(solution)/shard_map/ppermute | solution.py:248
  40.9 3.9 %collective-permute-start.11 = (bf16[256,512]{1,0:T(8,128)(2,1)}, bf16[256,512]{1,0:T(8,128)(2,1)S(1)}, u32[]{:S(2)}, u32[]{:S(2)}) collective-permute-start(bf16[256,512]{1,0:T(8,128)(2,1)} %collective-permute-done.5.refs_1_), channel_id=1, source_target_pairs={{0,1},{1,0},{2,3},{3,2},{4,5},{5,4},{6,7},{7,6},{8,9},{9,8},{10,11... | collective-permute-start | bytes 786440 | tf_op jit(solution)/shard_map/ppermute | solution.py:252
  41.0 14.7 %collective-permute-start.9 = (bf16[256,512]{1,0:T(8,128)(2,1)}, bf16[256,512]{1,0:T(8,128)(2,1)S(1)}, u32[]{:S(2)}, u32[]{:S(2)}) collective-permute-start(bf16[256,512]{1,0:T(8,128)(2,1)} %collective-permute-done.5.refs_1_), channel_id=1, source_target_pairs={{0,2},{1,3},{2,4},{3,5},{4,6},{5,7},{6,0},{7,1},{8,10},{9,11},{10,... | collective-permute-start | bytes 786440 | tf_op jit(solution)/shard_map/ppermute | solution.py:248
  55.6 1.5 %collective-permute-start.12 = (bf16[256,512]{1,0:T(8,128)(2,1)S(1)}, bf16[256,512]{1,0:T(8,128)(2,1)S(1)}, u32[]{:S(2)}, u32[]{:S(2)}) collective-permute-start(bf16[256,512]{1,0:T(8,128)(2,1)S(1)} %collective-permute-done.8.refs_0_), channel_id=1, source_target_pairs={{0,1},{1,0},{2,3},{3,2},{4,5},{5,4},{6,7},{7,6},{8,9},{9,8},{10,11... | collective-permute-start | bytes 786440 | tf_op jit(solution)/shard_map/ppermute | solution.py:252
  55.7 1.9 %collective-permute-start.13 = (bf16[256,512]{1,0:T(8,128)(2,1)S(1)}, bf16[256,512]{1,0:T(8,128)(2,1)S(1)}, u32[]{:S(2)}, u32[]{:S(2)}) collective-permute-start(bf16[256,512]{1,0:T(8,128)(2,1)S(1)} %collective-permute-done.9.refs_1_), channel_id=1, source_target_pairs={{0,1},{1,0},{2,3},{3,2},{4,5},{5,4},{6,7},{7,6},{8,9},{9,8},{10,11... | collective-permute-start | bytes 786440 | tf_op jit(solution)/shard_map/ppermute | solution.py:252
  57.1 5.6 %copy-start.6 = (bf16[2,512,2048]{2,1,0:T(8,128)(2,1)S(1)}, bf16[2,512,2048]{2,1,0:T(8,128)(2,1)}, u32[]{:S(2)}) copy-start(bf16[2,512,2048]{2,1,0:T(8,128)(2,1)} %w_up.3) | copy-start | bytes 12582916
  57.1 6.1 %copy-start.8 = (bf16[2,2048,512]{2,1,0:T(8,128)(2,1)S(1)}, bf16[2,2048,512]{2,1,0:T(8,128)(2,1)}, u32[]{:S(2)}) copy-start(bf16[2,2048,512]{2,1,0:T(8,128)(2,1)} %w_down.3) | copy-start | bytes 12582916
  57.1 6.7 %copy-start.11 = (bf16[2,512,512]{2,1,0:T(8,128)(2,1)S(1)}, bf16[2,512,512]{2,1,0:T(8,128)(2,1)}, u32[]{:S(2)}) copy-start(bf16[2,512,512]{2,1,0:T(8,128)(2,1)} %w_proj.3) | copy-start | bytes 3145732
  57.1 6.8 %copy-start.14 = (bf16[512,512]{1,0:T(8,128)(2,1)S(1)}, bf16[512,512]{1,0:T(8,128)(2,1)}, u32[]{:S(2)}) copy-start(bf16[512,512]{1,0:T(8,128)(2,1)} %points.1) | copy-start | bytes 1572868
  57.2 6.9 %copy-start.18 = (bf16[512,512]{1,0:T(8,128)(2,1)S(1)}, bf16[512,512]{1,0:T(8,128)(2,1)}, u32[]{:S(2)}) copy-start(bf16[512,512]{1,0:T(8,128)(2,1)} %copy-done.17) | copy-start | bytes 1572868
  58.5 4.3 %copy-start.2 = (bf16[4096,1024]{1,0:T(8,128)(2,1)}, bf16[4096,1024]{1,0:T(8,128)(2,1)S(1)}, u32[]{:S(2)}) copy-start(bf16[4096,1024]{1,0:T(8,128)(2,1)S(1)} %project.13.keyed) | copy-start | bytes 25165828
  64.1 3.4 %copy-start.3 = (bf16[4096,1024]{1,0:T(8,128)(2,1)S(1)}, bf16[4096,1024]{1,0:T(8,128)(2,1)}, u32[]{:S(2)}) copy-start(bf16[4096,1024]{1,0:T(8,128)(2,1)} %copy-done.2) | copy-start | bytes 25165828
  67.5 11.5 %copy-start.25 = (s32[8,3]{0,1:T(4,128)S(1)}, s32[8,3]{0,1:T(4,128)}, u32[]{:S(2)}) copy-start(s32[8,3]{0,1:T(4,128)} %param.12) | copy-start | bytes 292
  67.5 38.9 %copy-start.23 = (bf16[3,512]{1,0:T(4,128)(2,1)S(1)}, bf16[3,512]{1,0:T(4,128)(2,1)}, u32[]{:S(2)}) copy-start(bf16[3,512]{1,0:T(4,128)(2,1)} %w_head.1) | copy-start | bytes 9220
  74.2 1.0 copy-start.13
  75.1 31.2 %all-to-all-start = ((bf16[32,32,512]{2,1,0:T(8,128)(2,1)}), bf16[32,32,512]{2,1,0:T(8,128)(2,1)}, u32[]{:S(2)}, u32[]{:S(2)}) async-start(bf16[32,32,512]{2,1,0:T(8,128)(2,1)} %bitcast.22), calls=%async_computation | async-start | bytes 2097152 | tf_op jit(solution)/shard_map/all_to_all | solution.py:300
  106.3 2.2 %copy-start.7 = (bf16[2,512,2048]{2,1,0:T(8,128)(2,1)S(1)}, bf16[2,512,2048]{2,1,0:T(8,128)(2,1)}, u32[]{:S(2)}) copy-start(bf16[2,512,2048]{2,1,0:T(8,128)(2,1)} %w_up.3) | copy-start | bytes 12582916
  108.5 2.2 %copy-start.9 = (bf16[2,2048,512]{2,1,0:T(8,128)(2,1)S(1)}, bf16[2,2048,512]{2,1,0:T(8,128)(2,1)}, u32[]{:S(2)}) copy-start(bf16[2,2048,512]{2,1,0:T(8,128)(2,1)} %w_down.3) | copy-start | bytes 12582916
  110.7 1.2 %copy-start.10 = (bf16[512,1024]{1,0:T(8,128)(2,1)S(1)}, bf16[512,1024]{1,0:T(8,128)(2,1)}, u32[]{:S(2)}) copy-start(bf16[512,1024]{1,0:T(8,128)(2,1)} %fusion.1.place) | copy-start | bytes 3145732
  111.9 1.2 %copy-start.12 = (bf16[2,512,512]{2,1,0:T(8,128)(2,1)S(1)}, bf16[2,512,512]{2,1,0:T(8,128)(2,1)}, u32[]{:S(2)}) copy-start(bf16[2,512,512]{2,1,0:T(8,128)(2,1)} %w_proj.3) | copy-start | bytes 3145732

commit v4 on v3

v4 whole, which is shorter than its diff:
```python
import functools

import jax
import jax.numpy as jnp
from jax import lax
from jax.experimental import pallas as pl
from jax.experimental.pallas import tpu as pltpu
from jax.sharding import PartitionSpec as P

HEADS = 8
PATCH = 64
HEADS_TOGETHER = 4
RING_PARTS = 2
SEND_PARTS = 4
FIRST_BYTES = 28 * 1024 * 1024
SECOND_BYTES = 50 * 1024 * 1024
PROJECT_BYTES = 16 * 1024 * 1024
OWN_BYTES = 16 * 1024 * 1024
NORMALIZE_BYTES = 60 * 1024 * 1024
RING_BYTES = 16 * 1024 * 1024
F32 = jnp.float32
BF16 = jnp.bfloat16


def layer_norm(rows, gains):
    values = rows.astype(F32)
    average = jnp.mean(values, axis=-1, keepdims=True)
    spread = jnp.mean((values - average) ** 2, axis=-1, keepdims=True)
    return ((values - average) * lax.rsqrt(spread + 1e-05) * gains).astype(BF16)


def gelu(x):
    half = 0.5 * x
    return half + half * lax.erf(x * 0.5**0.5)


def head_masks(head_dim):
    lane = lax.broadcasted_iota(jnp.int32, (PATCH, HEADS_TOGETHER * head_dim), 1)
    return [
        jnp.where((lane >= h * head_dim) & (lane < (h + 1) * head_dim), 1.0, 0.0).astype(F32)
        for h in range(HEADS_TOGETHER)
    ]


def attend_patch(queries, key_rows, value_rows, masks):
    channels = queries.shape[1]
    width = HEADS_TOGETHER * (channels // HEADS)
    sides = []
    for at in range(0, channels, width):
        q = queries[:, at : at + width]
        stacked = jnp.concatenate([q * mask.astype(BF16) for mask in masks], axis=0)
        scores = lax.dot_general(
            stacked,
            key_rows[:, at : at + width],
            (((1,), (1,)), ((), ())),
            preferred_element_type=F32,
        )
        top = jnp.max(scores, axis=-1, keepdims=True)
        grown = jnp.exp(scores - top)
        total = jnp.sum(grown, axis=-1, keepdims=True)
        weights = (grown * (1.0 / total)).astype(BF16)
        mixed = jnp.dot(weights, value_rows[:, at : at + width], preferred_element_type=F32)
        side = mixed[:PATCH] * masks[0]
        for h in range(1, HEADS_TOGETHER):
            side = side + mixed[h * PATCH : (h + 1) * PATCH] * masks[h]
        sides.append(side.astype(BF16))
    return jnp.concatenate(sides, axis=1)


def one_hot_rows(places, rows):
    row = lax.broadcasted_iota(jnp.int32, (rows, places.shape[1]), 0)
    return jnp.where(row == places, 1.0, 0.0).astype(BF16)


def started(pairs, sems):
    copies = [
        pltpu.make_async_copy(source, place, sems.at[at])
        for at, (source, place) in enumerate(pairs)
    ]
    for copy in copies:
        copy.start()
    return copies


def finish(rows, attended, gain, held, copies=()):
    w_proj, w_up, w_down = held
    for copy in copies[:1]:
        copy.wait()
    first = (
        rows.astype(F32) + jnp.dot(attended, w_proj[...], preferred_element_type=F32)
    ).astype(BF16)
    hidden = layer_norm(first, gain)
    total = first.astype(F32)
    for copy in copies[1:]:
        copy.wait()
    piece = 512
    for at in range(0, w_up.shape[1], piece):
        upper = jnp.dot(hidden, w_up[:, at : at + piece], preferred_element_type=F32)
        act = gelu(upper).astype(BF16)
        total = total + jnp.dot(act, w_down[at : at + piece, :], preferred_element_type=F32)
    return total.astype(BF16)


def normalize_kernel(points, gains, *refs):
    *parts, held, gains_held, sems = refs
    rows = parts[0].shape[0]
    fetch, *copies = started(
        [(gains, gains_held)]
        + [(points.at[pl.ds(i * rows, rows), :], held.at[i]) for i in range(len(parts))],
        sems,
    )
    fetch.wait()
    for i, part in enumerate(parts):
        copies[i].wait()
        part[...] = layer_norm(held[i], gains_held[0:1, :])


def project_kernel(first_rows, *refs):
    count = len(first_rows)
    parts, w_qkv, whole = refs[:count], refs[count], refs[count + 2]
    held, held_w, sems = refs[count + 3 :]
    channels = w_qkv.shape[1]
    rows = held.shape[1]
    fetch, *copies = started(
        [(w_qkv.at[0, :, pl.ds(channels, 2 * channels)], held_w)]
        + [(part, held.at[i]) for i, part in enumerate(parts)],
        sems,
    )
    fetch.wait()
    for i, first in enumerate(first_rows):
        copies[i].wait()
        whole[first : first + rows, :] = jnp.dot(
            held[i], held_w[...], preferred_element_type=F32
        ).astype(BF16)


def own_kernel(first_rows, *refs):
    count = len(first_rows)
    parts, w_qkv, others = refs[:count], refs[count], refs[count + 1 : count + 4]
    whole, queries, *kept = refs[count + 4 : count + 9]
    held, held_w, sems, kept_sems = refs[count + 9 :]
    channels = w_qkv.shape[1]
    rows = held.shape[1]
    scale = (channels // HEADS) ** (-0.5)
    fetch, *copies = started(
        [(w_qkv.at[0], held_w)] + [(part, held.at[i]) for i, part in enumerate(parts)], sems
    )
    keeping = started([(w.at[0], place) for w, place in zip(others, kept)], kept_sems)
    fetch.wait()
    for i, first in enumerate(first_rows):
        copies[i].wait()
        whole[first : first + rows, :] = jnp.dot(
            held[i], held_w[:, channels:], preferred_element_type=F32
        ).astype(BF16)
        if i * rows < queries.shape[0]:
            own = jnp.dot(held[i], held_w[:, :channels], preferred_element_type=F32).astype(BF16)
            queries[i * rows : (i + 1) * rows, :] = (own * BF16(scale)).astype(BF16)
    for copy in keeping:
        copy.wait()


def first_kernel(
    pattern,
    slot_of_row,
    gains,
    keyed,
    queries,
    points,
    w_proj,
    w_up,
    w_down,
    outgoing,
    attended,
    points_held,
    gains_held,
    slots_held,
    outgoing_held,
    sems,
):
    rows, channels = points.shape
    patches = rows // PATCH
    chosen = pattern.shape[0] // patches
    copies = started(
        [
            (points, points_held),
            (gains, gains_held),
            (slot_of_row, slots_held),
        ],
        sems,
    )
    masks = head_masks(channels // HEADS)
    for p in range(patches):
        pieces = [keyed[p * PATCH : (p + 1) * PATCH, :]]
        for j in range(chosen):
            start = pl.multiple_of(pattern[p * chosen + j] * PATCH, PATCH)
            pieces.append(keyed[pl.ds(start, PATCH), :])
        both = jnp.concatenate(pieces, axis=0)
        attended[p * PATCH : (p + 1) * PATCH, :] = attend_patch(
            queries[p * PATCH : (p + 1) * PATCH, :],
            both[:, :channels],
            both[:, channels:],
            masks,
        )
    for copy in copies:
        copy.wait()
    first = finish(
        points_held[...], attended[...], gains_held[1:2, :], (w_proj, w_up, w_down)
    )
    slots = slots_held[...]
    piece = outgoing.shape[0] // SEND_PARTS
    leaving = []
    for i in range(SEND_PARTS):
        here = pl.ds(i * piece, piece)
        send = one_hot_rows(slots - i * piece, piece)
        outgoing_held[here, :] = jnp.dot(send, first, preferred_element_type=F32).astype(BF16)
        leaving.append(
            pltpu.make_async_copy(
                outgoing_held.at[here, :], outgoing.at[here, :], sems.at[len(copies) + i]
            )
        )
        leaving[-1].start()
    for copy in leaving:
        copy.wait()


def second_kernel(
    pattern,
    slot_places,
    gains,
    incoming,
    w_qkv,
    w_proj,
    w_up,
    w_down,
    w_head,
    features,
    normals,
    kv,
    attended,
    incoming_held,
    qkv_held,
    proj_held,
    up_held,
    down_held,
    gains_held,
    places_held,
    head_held,
    sems,
):
    rows, channels = features.shape
    patches = rows // PATCH
    chosen = pattern.shape[0] // patches
    small = started(
        [(slot_places, places_held), (gains, gains_held), (w_head, head_held)], sems.at[1]
    )
    copies = started(
        [
            (incoming, incoming_held),
            (w_qkv.at[1], qkv_held),
            (w_proj.at[1], proj_held),
            (w_up.at[1], up_held),
            (w_down.at[1], down_held),
        ],
        sems.at[0],
    )
    for copy in small:
        copy.wait()
    place = one_hot_rows(places_held[...], rows)
    copies[0].wait()
    second = jnp.dot(place, incoming_held[...], preferred_element_type=F32).astype(BF16)
    normed = layer_norm(second, gains_held[2:3, :])
    scale = (channels // HEADS) ** (-0.5)
    copies[1].wait()
    queries = (
        jnp.dot(normed, qkv_held[:, :channels], preferred_element_type=F32).astype(BF16)
        * BF16(scale)
    ).astype(BF16)
    kv[...] = jnp.dot(normed, qkv_held[:, channels:], preferred_element_type=F32).astype(BF16)
    masks = head_masks(channels // HEADS)
    for p in range(patches):
        pieces = [kv[p * PATCH : (p + 1) * PATCH, :]]
        for j in range(chosen):
            start = pl.multiple_of(pattern[p * chosen + j] * PATCH, PATCH)
            pieces.append(kv[pl.ds(start, PATCH), :])
        both = jnp.concatenate(pieces, axis=0)
        attended[p * PATCH : (p + 1) * PATCH, :] = attend_patch(
            queries[p * PATCH : (p + 1) * PATCH, :], both[:, :channels], both[:, channels:], masks
        )
    done = finish(
        second, attended[...], gains_held[3:4, :], (proj_held, up_held, down_held), copies[2:]
    )
    features[...] = done
    normals[...] = lax.dot_general(
        head_held[...], done, (((1,), (1,)), ((), ())), preferred_element_type=F32
    )


VMEM_SPEC = pl.BlockSpec(memory_space=pltpu.VMEM)
SMEM_SPEC = pl.BlockSpec(memory_space=pltpu.SMEM)
ANY_SPEC = pl.BlockSpec(memory_space=pl.ANY)


def shards(
    points,
    pattern_first,
    pattern_second,
    destination,
    norm_gains,
    w_qkv,
    w_proj,
    w_up,
    w_down,
    w_head,
):
    rows_here, channels = points.shape
    patches, chosen = pattern_first.shape
    devices = lax.axis_size("grp") * lax.axis_size("seq")
    capacity = 2 * rows_here // devices
    slot_total = devices * capacity

    shards_in_group = lax.axis_size("seq")
    chips = shards_in_group // 2
    onward = [(i, (i + 2) % shards_in_group) for i in range(shards_in_group)]
    swap = [(i, i ^ 1) for i in range(shards_in_group)]
    ring = shards_in_group * rows_here * 2 * channels * 2 <= RING_BYTES
    kept_rows = shards_in_group * rows_here if ring else patches * (1 + chosen) * PATCH
    part = rows_here // RING_PARTS
    part_bytes = part * channels * 2

    column = pl.pallas_call(
        normalize_kernel,
        out_shape=[jax.ShapeDtypeStruct((part, channels), BF16)] * RING_PARTS,
        in_specs=[ANY_SPEC, ANY_SPEC],
        out_specs=[VMEM_SPEC] * RING_PARTS,
        scratch_shapes=[
            pltpu.VMEM((RING_PARTS, part, channels), BF16),
            pltpu.VMEM(norm_gains.shape, F32),
            pltpu.SemaphoreType.DMA((1 + RING_PARTS,)),
        ],
        compiler_params=pltpu.CompilerParams(vmem_limit_bytes=NORMALIZE_BYTES),
        name="normalize",
    )(points, norm_gains)

    weights = (w_proj, w_up, w_down)
    kv_shape = jax.ShapeDtypeStruct((kept_rows, 2 * channels), BF16)

    def project(keyed, blocks):
        parts = [rows for _, block in blocks for rows in block]
        count = len(parts)
        rows = parts[0].shape[0]
        first_rows = [
            slot * rows_here + i * rows for slot, block in blocks for i in range(len(block))
        ]
        own = keyed is None
        own_shapes = [jax.ShapeDtypeStruct((rows_here, channels), BF16)]
        own_shapes += [jax.ShapeDtypeStruct(w.shape[1:], BF16) for w in weights]
        return pl.pallas_call(
            functools.partial(own_kernel if own else project_kernel, first_rows),
            out_shape=[kv_shape] + own_shapes if own else kv_shape,
            in_specs=[ANY_SPEC] * (count + 1) + ([ANY_SPEC] * 3 if own else [VMEM_SPEC]),
            out_specs=[VMEM_SPEC] * 5 if own else VMEM_SPEC,
            scratch_shapes=[
                pltpu.VMEM((count, rows, channels), BF16),
                pltpu.VMEM((channels, (3 if own else 2) * channels), BF16),
                pltpu.SemaphoreType.DMA((count + 1,)),
            ]
            + ([pltpu.SemaphoreType.DMA((3,))] if own else []),
            input_output_aliases={} if own else {count + 1: 0},
            cost_estimate=pl.CostEstimate(
                flops=4 * count * rows * channels**2,
                bytes_accessed=3 * count * rows * channels * 2 + 3 * channels**2 * 2,
                transcendentals=0,
            ),
            compiler_params=pltpu.CompilerParams(
                vmem_limit_bytes=OWN_BYTES if own else PROJECT_BYTES
            ),
            name="project_own" if own else "project",
        )(*parts, w_qkv, *(weights if own else [keyed]))

    target = destination // rows_here
    place_at = destination % rows_here
    onehot_dev = (target[:, None] == jnp.arange(devices, dtype=jnp.int32)[None, :]).astype(
        jnp.int32
    )
    earlier = jnp.cumsum(onehot_dev, axis=0) - onehot_dev
    send_rank = jnp.sum(earlier * onehot_dev, axis=1)
    slot_index = target * capacity + send_rank
    slot_ids = jnp.arange(slot_total, dtype=jnp.int32)
    match_send = slot_index[None, :] == slot_ids[:, None]
    out_places = jnp.sum(jnp.where(match_send, place_at[None, :] + 1, 0), axis=1) - 1
    in_places = lax.all_to_all(
        out_places.reshape(devices, capacity),
        ("grp", "seq"),
        split_axis=0,
        concat_axis=0,
        tiled=True,
    ).reshape(1, slot_total)
    slot_index = slot_index.reshape(1, rows_here)

    pattern_second = pattern_second.reshape(-1)
    me = lax.axis_index("seq")
    if ring:
        owner = pattern_first // patches
        slot_of = 2 * ((me // 2 - owner // 2) % chips) + (me % 2 != owner % 2).astype(jnp.int32)
        pattern_slots = (slot_of * patches + pattern_first % patches).reshape(-1)
    else:
        pattern_slots = patches + jnp.arange(patches * chosen, dtype=jnp.int32)

    if ring:
        beside = [lax.ppermute(rows, "seq", swap) for rows in column]
        waiting = [(0, column), (1, beside)]
        keyed = None
        for step in range(1, chips):
            column = [lax.ppermute(rows, "seq", onward) for rows in column]
            if step == 1:
                tied = (column, waiting[0][1], beside, pattern_slots, pattern_second, slot_index)
                tied, in_places = lax.optimization_barrier((tied, in_places))
                column, own, beside, pattern_slots, pattern_second, slot_index = tied
                waiting = [(0, own), (1, beside)]
            elif step == 2:
                keyed, queries, *kept = project(None, waiting)
                waiting = []
            else:
                keyed = project(keyed, waiting)
                waiting = []
            if step > 1:
                column, keyed = lax.optimization_barrier((column, keyed))
            beside = [lax.ppermute(rows, "seq", swap) for rows in column]
            waiting = waiting + [(2 * step, column), (2 * step + 1, beside)]
        for block in waiting:
            keyed = project(keyed, [block])
    else:
        group = lax.all_gather(jnp.concatenate(column), "seq", axis=0, tiled=True)
        picked = group.reshape(-1, PATCH, channels)[pattern_first].reshape(-1, channels)
        keyed, queries, *kept = project(None, [(0, column)])
        keyed = project(keyed, [(1, [picked])])

    held_weights = [pltpu.VMEM(w.shape[1:], BF16) for w in weights]
    held_rows = pltpu.VMEM((rows_here, channels), BF16)
    outgoing = pl.pallas_call(
        first_kernel,
        out_shape=jax.ShapeDtypeStruct((slot_total, channels), BF16),
        in_specs=[SMEM_SPEC, ANY_SPEC, ANY_SPEC, VMEM_SPEC, VMEM_SPEC, ANY_SPEC]
        + [VMEM_SPEC] * 3,
        out_specs=ANY_SPEC,
        scratch_shapes=[
            held_rows,
            held_rows,
            pltpu.VMEM(norm_gains.shape, F32),
            pltpu.VMEM(slot_index.shape, jnp.int32),
            pltpu.VMEM((slot_total, channels), BF16),
            pltpu.SemaphoreType.DMA((3 + SEND_PARTS,)),
        ],
        compiler_params=pltpu.CompilerParams(vmem_limit_bytes=FIRST_BYTES),
        name="block_first",
    )(pattern_slots, slot_index, norm_gains, keyed, queries, points, *kept)

    incoming = lax.all_to_all(
        outgoing.reshape(devices, capacity, channels),
        ("grp", "seq"),
        split_axis=0,
        concat_axis=0,
        tiled=True,
    ).reshape(slot_total, channels)

    return pl.pallas_call(
        second_kernel,
        out_shape=(
            jax.ShapeDtypeStruct((rows_here, channels), BF16),
            jax.ShapeDtypeStruct((w_head.shape[0], rows_here), F32),
        ),
        in_specs=[SMEM_SPEC] + [ANY_SPEC] * 8,
        out_specs=(VMEM_SPEC, VMEM_SPEC),
        scratch_shapes=[
            pltpu.VMEM((rows_here, 2 * channels), BF16),
            held_rows,
            pltpu.VMEM((slot_total, channels), BF16),
            pltpu.VMEM(w_qkv.shape[1:], BF16),
            *held_weights,
            pltpu.VMEM(norm_gains.shape, F32),
            pltpu.VMEM(in_places.shape, jnp.int32),
            pltpu.VMEM(w_head.shape, BF16),
            pltpu.SemaphoreType.DMA((2, 5)),
        ],
        compiler_params=pltpu.CompilerParams(vmem_limit_bytes=SECOND_BYTES),
        name="block_second",
    )(pattern_second, in_places, norm_gains, incoming, w_qkv, *weights, w_head)


def solution(mesh):
    placed = (
        P(("grp", "seq"), None),
        P(("grp", "seq"), None),
        P(("grp", "seq"), None),
        P(("grp", "seq")),
        P(),
        P(),
        P(),
        P(),
        P(),
        P(),
    )
    return jax.shard_map(
        shards,
        mesh=mesh,
        in_specs=placed,
        out_specs=(P(("grp", "seq"), None), P(None, ("grp", "seq"))),
        check_vma=False,
    )
```

time: 123 us -> 107 us (0.87)
  blocking collectives: 0 us -> 29.3 us
  local copies, waits for them, and re-layouts: 33.6 us -> 11.9 us
  waiting for transfers between devices: 35.7 us -> 16.8 us
  starting transfers between devices: 20 us -> 15.3 us
    all_to_all x0 -> x1, blocking collectives: none -> 29.3 us  [shards(): lax.all_to_all(outgoing.reshape(devices, capacity, channels), ('grp', 'se...]
    all_to_all x1 -> x0, waiting for transfers between devices: 24.7 us -> none  [shards(): lax.all_to_all(outgoing.reshape(devices, capacity, channels), ('grp', 'se...]
    unnamed x54 -> x21, local copies, waits for them, and re-layouts: 30.3 us -> 10.2 us
    all_to_all x1, waiting for transfers between devices: 0.01 us -> 5.4 us  [shards(): lax.all_to_all(out_places.reshape(devices, capacity), ('grp', 'seq'), spl...]
    all_to_all x1 -> x0, starting transfers between devices: 3.85 us -> none  [shards(): lax.all_to_all(outgoing.reshape(devices, capacity, channels), ('grp', 'se...]
    slice x2 -> x1, local copies, waits for them, and re-layouts: 2.01 us -> 0.22 us  [the longest x1 1.79 us: shards(): column = [points[i * part:(i + 1) * part] for i in range(RING_PARTS)]]
    convert_element_type x2 -> x0, other arithmetic: 1.7 us -> none  [the longest x1 1.28 us: shards(): place = (in_places[None, :] == row_ids[:, None]).astype(BF16)]
    all_to_all x1, starting transfers between devices: 5.79 us -> 4.5 us  [shards(): lax.all_to_all(out_places.reshape(devices, capacity), ('grp', 'seq'), spl...]
  transfers between devices with their start and end apart: 16 -> 15, of which waited for: 5 -> 6; matrix products, arithmetic and copies ran while one was open for 5% -> 6% of each run, Pallas kernels for 15% -> 7%
where the time goes in v4:
time: 107 us; the launch traced here: 106 us
  blocking collectives  29.3 us (27%)
  Pallas kernels  28.2 us (26%)
  waiting for transfers between devices  16.8 us (16%)
  starting transfers between devices  15.3 us (14%)
  local copies, waits for them, and re-layouts  11.9 us (11%)
  other arithmetic  3.72 us (3%)
    all_to_all x1, blocking collectives, shards(): lax.all_to_all(outgoing.reshape(devices, capacity, channels), ('grp', 'se...  29.3 us
    ppermute x6, waiting for transfers between devices, shards(): column = [lax.ppermute(rows, 'seq', onward) for rows in column]  10.8 us
    unnamed x21, local copies, waits for them, and re-layouts  10.2 us
    pallas_call x1, Pallas kernels, shards(): pl.pallas_call(second_kernel, out_shape=(jax.ShapeDtypeStruct((rows_here,...  9.48 us
    ppermute x6, starting transfers between devices, shards(): column = [lax.ppermute(rows, 'seq', onward) for rows in column]  8.94 us
    pallas_call x4, Pallas kernels, project(): pl.pallas_call(functools.partial(own_kernel if own else project_kernel, f...  8.73 us
    pallas_call x1, Pallas kernels, shards(): pl.pallas_call(first_kernel, out_shape=jax.ShapeDtypeStruct((slot_total,...  7.77 us
    all_to_all x1, waiting for transfers between devices, shards(): lax.all_to_all(out_places.reshape(devices, capacity), ('grp', 'seq'), spl...  5.4 us
  transfers between devices with their start and end apart: 15, of which 6 were waited for; matrix products, arithmetic and copies ran while one was open for 6% of the time, Pallas kernels for 7%

profile of v4, /device:TPU:0, one launch (start us, length us, event | category | flops | bytes accessed | tf_op | source)
XLA Modules:
  0.0 106.2 jit_solution(7101588298114654761)
XLA Ops:
  0.6 2.2 %normalize.1 = (bf16[256,512]{1,0:T(8,128)(2,1)}, bf16[256,512]{1,0:T(8,128)(2,1)}) custom-call(bf16[512,512]{1,0:T(8,128)(2,1)} %points.3, f32[4,512]{1,0:T(4,128)} %gains.5), custom_call_target="tpu_custom_call" | custom-call | tf_op jit(solution)/shard_map/normalize/pallas_call | solution.py:330
  2.8 3.1 %collective-permute-start = (bf16[256,512]{1,0:T(8,128)(2,1)}, bf16[256,512]{1,0:T(8,128)(2,1)S(1)}, u32[]{:S(2)}, u32[]{:S(2)}) collective-permute-start(bf16[256,512]{1,0:T(8,128)(2,1)} %get-tuple-element.33.refs_0_), channel_id=1, source_target_pairs={{0,2},{1,3},{2,4},{3,5},{4,6},{5,7},{6,0},{7,1},{8,10},{9,11},{10,... | collective-permute-start | bytes 786440 | tf_op jit(solution)/shard_map/ppermute | solution.py:414
  5.9 1.6 %collective-permute-start.1 = (bf16[256,512]{1,0:T(8,128)(2,1)}, bf16[256,512]{1,0:T(8,128)(2,1)S(1)}, u32[]{:S(2)}, u32[]{:S(2)}) collective-permute-start(bf16[256,512]{1,0:T(8,128)(2,1)} %get-tuple-element.34.refs_1_), channel_id=1, source_target_pairs={{0,2},{1,3},{2,4},{3,5},{4,6},{5,7},{6,0},{7,1},{8,10},{9,11},{10,... | collective-permute-start | bytes 786440 | tf_op jit(solution)/shard_map/ppermute | solution.py:414
  7.5 0.2 collective-permute-start.3
  7.7 0.7 fusion.11
  8.4 1.2 %reduce-window.6 = s32[32,4,128]{2,0,1:T(8,128)S(1)} reduce-window(s32[32,4,128]{2,0,1:T(8,128)S(1)} %fusion.3, s32[]{:T(128)} %constant.101.clone.1), window={size=1x1x128 pad=0_0x0_0x127_0}, to_apply=%region_0.1 | reduce-window | flops 2080768 | bytes 131076 | tf_op jit(solution)/shard_map/reduce-window
  9.6 0.2 slice_reduce_fusion
  9.8 0.1 fusion.2
  10.0 0.3 select_reduce_fusion
  10.3 0.7 sub.40
  11.0 4.5 %all-to-all-start = ((s32[32,1,32]{2,1,0:T(1,128)}), s32[32,1,32]{2,1,0:T(1,128)S(1)}, u32[]{:S(2)}, u32[]{:S(2)}) async-start(s32[32,1,32]{2,1,0:T(1,128)} %sub.40), calls=%async_computation | async-start | bytes 32768 | tf_op jit(solution)/shard_map/all_to_all | solution.py:391
  15.5 0.7 fusion.9
  16.2 0.1 copy.23
  16.3 0.1 reshape.58.pattern
  16.4 0.8 copy.24
  17.1 0.1 reshape.59.pattern
  17.2 5.4 %all-to-all-done = s32[32,1,32]{2,1,0:T(1,128)S(1)} async-done(((s32[32,1,32]{2,1,0:T(1,128)}), s32[32,1,32]{2,1,0:T(1,128)S(1)}, u32[]{:S(2)}, u32[]{:S(2)}) %all-to-all-start) | async-done | bytes 4128 | tf_op jit(solution)/shard_map/all_to_all | solution.py:391
  22.6 0.5 broadcast.107
  23.1 0.7 reduce.5
  23.8 0.1 reshape.62.slot_places
  23.9 0.1 collective-permute-start.6
  24.0 0.5 collective-permute-start.7
  24.5 0.5 collective-permute-start.4
  25.0 0.5 collective-permute-start.5
  25.6 0.3 collective-permute-done.7.refs_7_
  25.9 1.9 %copy-done = bf16[2,512,1536]{2,1,0:T(8,128)(2,1)S(1)} copy-done((bf16[2,512,1536]{2,1,0:T(8,128)(2,1)S(1)}, bf16[2,512,1536]{2,1,0:T(8,128)(2,1)}, u32[]{:S(2)}) %copy-start) | copy-done | bytes 3145752
  27.8 2.2 %copy-done.1 = bf16[2,512,2048]{2,1,0:T(8,128)(2,1)S(1)} copy-done((bf16[2,512,2048]{2,1,0:T(8,128)(2,1)S(1)}, bf16[2,512,2048]{2,1,0:T(8,128)(2,1)}, u32[]{:S(2)}) %copy-start.1) | copy-done | bytes 4194328
  30.0 2.2 %copy-done.2 = bf16[2,2048,512]{2,1,0:T(8,128)(2,1)S(1)} copy-done((bf16[2,2048,512]{2,1,0:T(8,128)(2,1)S(1)}, bf16[2,2048,512]{2,1,0:T(8,128)(2,1)}, u32[]{:S(2)}) %copy-start.2) | copy-done | bytes 4194328
  32.2 1.2 %copy-done.3 = bf16[2,512,512]{2,1,0:T(8,128)(2,1)S(1)} copy-done((bf16[2,512,512]{2,1,0:T(8,128)(2,1)S(1)}, bf16[2,512,512]{2,1,0:T(8,128)(2,1)}, u32[]{:S(2)}) %copy-start.3) | copy-done | bytes 1048600
  33.4 0.9 copy-done.6
  34.3 0.9 copy-done.7
  35.3 4.5 %project_own.1 = (bf16[4096,1024]{1,0:T(8,128)(2,1)S(1)}, bf16[512,512]{1,0:T(8,128)(2,1)S(1)}, bf16[512,512]{1,0:T(8,128)(2,1)S(1)}, bf16[512,2048]{1,0:T(8,128)(2,1)S(1)}, bf16[2048,512]{1,0:T(8,128)(2,1)S(1)}) custom-call(bf16[256,512]{1,0:T(8,128)(2,1)S(1)} %copy-done.6, bf16[256,512]{1,0:T(8,128)(2,1)S(1)} %copy-done.7, ...), custom_call_target="tpu_custom_call" | custom-call | flops 2147483648 | bytes 7864320 | tf_op jit(solution)/shard_map/project_own/pallas_call | solution.py:357
  39.8 0.4 collective-permute-done.5.refs_1_
  40.2 0.5 collective-permute-start.11
  40.7 0.7 collective-permute-start.8
  41.4 2.6 %collective-permute-start.9 = (bf16[256,512]{1,0:T(8,128)(2,1)S(1)}, bf16[256,512]{1,0:T(8,128)(2,1)S(1)}, u32[]{:S(2)}, u32[]{:S(2)}) collective-permute-start(bf16[256,512]{1,0:T(8,128)(2,1)S(1)} %collective-permute-done.5.refs_1_), channel_id=1, source_target_pairs={{0,2},{1,3},{2,4},{3,5},{4,6},{5,7},{6,0},{7,1},{8,10},{9,11},{10,... | collective-permute-start | bytes 786440 | tf_op jit(solution)/shard_map/ppermute | solution.py:414
  43.9 2.0 %project.3.refs_3_ = bf16[4096,1024]{1,0:T(8,128)(2,1)S(1)} custom-call(bf16[256,512]{1,0:T(8,128)(2,1)S(1)} %collective-permute-done.4.refs_0_, bf16[256,512]{1,0:T(8,128)(2,1)S(1)} %collective-permute-done.5.refs_1_, bf16[256,512]{1,0:T(8,128)(2,1)S(1)} %collective-permute-done.10.refs_2_, ...), custom_call_target="tpu_custom_call", output_to_operand_aliasing={{}: (5, {})} | custom-call | flops 1073741824 | bytes 4718592 | tf_op jit(solution)/shard_map/project/pallas_call | solution.py:357
  46.0 5.7 %collective-permute-done.8.refs_0_ = bf16[256,512]{1,0:T(8,128)(2,1)S(1)} collective-permute-done((bf16[256,512]{1,0:T(8,128)(2,1)S(1)}, bf16[256,512]{1,0:T(8,128)(2,1)S(1)}, u32[]{:S(2)}, u32[]{:S(2)}) %collective-permute-start.8) | collective-permute-done | bytes 262176 | tf_op jit(solution)/shard_map/ppermute | solution.py:414
  51.7 4.7 %collective-permute-done.9.refs_1_ = bf16[256,512]{1,0:T(8,128)(2,1)S(1)} collective-permute-done((bf16[256,512]{1,0:T(8,128)(2,1)S(1)}, bf16[256,512]{1,0:T(8,128)(2,1)S(1)}, u32[]{:S(2)}, u32[]{:S(2)}) %collective-permute-start.9) | collective-permute-done | bytes 262176 | tf_op jit(solution)/shard_map/ppermute | solution.py:414
  56.3 0.5 collective-permute-start.13
  56.9 1.1 %project.4.refs_3_ = bf16[4096,1024]{1,0:T(8,128)(2,1)S(1)} custom-call(bf16[256,512]{1,0:T(8,128)(2,1)S(1)} %collective-permute-done.8.refs_0_, bf16[256,512]{1,0:T(8,128)(2,1)S(1)} %collective-permute-done.9.refs_1_, bf16[2,512,1536]{2,1,0:T(8,128)(2,1)S(1)} %copy-done, bf16[4096,1024]{1,0:T(8,128)(2,1)S(1)} %project.3.refs_3_), custom_call_target="tpu_custom_call", output_to_operand_aliasing={{}: (3, {})} | custom-call | flops 536870912 | bytes 3145728 | tf_op jit(solution)/shard_map/project/pallas_call | solution.py:357
  58.0 0.0 copy-start.5
  58.0 0.0 copy-start.8
  58.0 0.3 collective-permute-done.13.refs_1_
  58.3 1.1 %project.5.keyed = bf16[4096,1024]{1,0:T(8,128)(2,1)S(1)} custom-call(bf16[256,512]{1,0:T(8,128)(2,1)S(1)} %collective-permute-done.12.refs_0_, bf16[256,512]{1,0:T(8,128)(2,1)S(1)} %collective-permute-done.13.refs_1_, bf16[2,512,1536]{2,1,0:T(8,128)(2,1)S(1)} %copy-done, bf16[4096,1024]{1,0:T(8,128)(2,1)S(1)} %project.4.refs_3_), custom_call_target="tpu_custom_call", output_to_operand_aliasing={{}: (3, {})} | custom-call | flops 536870912 | bytes 3145728 | tf_op jit(solution)/shard_map/project/pallas_call | solution.py:357
  59.4 7.8 %block_first.1 = bf16[1024,512]{1,0:T(8,128)(2,1)S(1)} custom-call(s32[24]{0:T(128)S(1)} %reshape.58.pattern, s32[1,512]{1,0:T(1,128)S(1)} %bitcast.25, f32[4,512]{1,0:T(4,128)S(1)} %copy-done.8, bf16[4096,1024]{1,0:T(8,128)(2,1)S(1)} %project.5.keyed, bf16[512,512]{1,0:T(8,128)(2,1)S(1)} %get-tuple-element.44.queries, bf16[512,512]{1,0:T(8,128)(2,1)S(1)} %copy-done.5, ...), custom_call_target="tpu_custom_call" | custom-call | tf_op jit(solution)/shard_map/block_first/pallas_call | solution.py:440
  67.2 29.3 %all_to_all.11 = bf16[32,32,512]{2,1,0:T(8,128)(2,1)S(1)} all-to-all(bf16[32,32,512]{2,1,0:T(8,128)(2,1)S(1)} %bitcast.23), channel_id=1, replica_groups=mesh['grp'=4,'seq'=8] {'grp','seq'}, dimensions={0} | all-to-all | bytes 2097152 | tf_op jit(solution)/shard_map/all_to_all | solution.py:458
  96.5 9.5 %block_second.1 = (bf16[512,512]{1,0:T(8,128)(2,1)}, f32[3,512]{1,0:T(4,128)}) custom-call(s32[24]{0:T(128)S(1)} %reshape.59.pattern, s32[1,1024]{1,0:T(1,128)S(1)} %reshape.62.slot_places, f32[4,512]{1,0:T(4,128)S(1)} %copy-done.8, bf16[1024,512]{1,0:T(8,128)(2,1)S(1)} %bitcast.24, bf16[2,512,1536]{2,1,0:T(8,128)(2,1)} %w_qkv.1, ...), custom_call_target="tpu_custom_call" | custom-call | tf_op jit(solution)/shard_map/block_second/pallas_call | solution.py:466
  (29 shorter events, 0.1 us)
Async XLA Ops:
  2.8 21.1 %collective-permute-start = (bf16[256,512]{1,0:T(8,128)(2,1)}, bf16[256,512]{1,0:T(8,128)(2,1)S(1)}, u32[]{:S(2)}, u32[]{:S(2)}) collective-permute-start(bf16[256,512]{1,0:T(8,128)(2,1)} %get-tuple-element.33.refs_0_), channel_id=1, source_target_pairs={{0,2},{1,3},{2,4},{3,5},{4,6},{5,7},{6,0},{7,1},{8,10},{9,11},{10,... | collective-permute-start | bytes 786440 | tf_op jit(solution)/shard_map/ppermute | solution.py:414
  5.9 18.0 %collective-permute-start.2 = (bf16[256,512]{1,0:T(8,128)(2,1)}, bf16[256,512]{1,0:T(8,128)(2,1)S(1)}, u32[]{:S(2)}, u32[]{:S(2)}) collective-permute-start(bf16[256,512]{1,0:T(8,128)(2,1)} %get-tuple-element.33.refs_0_), channel_id=1, source_target_pairs={{0,1},{1,0},{2,3},{3,2},{4,5},{5,4},{6,7},{7,6},{8,9},{9,8},{10,11... | collective-permute-start | bytes 786440 | tf_op jit(solution)/shard_map/ppermute | solution.py:410
  5.9 18.0 %collective-permute-start.1 = (bf16[256,512]{1,0:T(8,128)(2,1)}, bf16[256,512]{1,0:T(8,128)(2,1)S(1)}, u32[]{:S(2)}, u32[]{:S(2)}) collective-permute-start(bf16[256,512]{1,0:T(8,128)(2,1)} %get-tuple-element.34.refs_1_), channel_id=1, source_target_pairs={{0,2},{1,3},{2,4},{3,5},{4,6},{5,7},{6,0},{7,1},{8,10},{9,11},{10,... | collective-permute-start | bytes 786440 | tf_op jit(solution)/shard_map/ppermute | solution.py:414
  7.5 16.4 %collective-permute-start.3 = (bf16[256,512]{1,0:T(8,128)(2,1)}, bf16[256,512]{1,0:T(8,128)(2,1)S(1)}, u32[]{:S(2)}, u32[]{:S(2)}) collective-permute-start(bf16[256,512]{1,0:T(8,128)(2,1)} %get-tuple-element.34.refs_1_), channel_id=1, source_target_pairs={{0,1},{1,0},{2,3},{3,2},{4,5},{5,4},{6,7},{7,6},{8,9},{9,8},{10,11... | collective-permute-start | bytes 786440 | tf_op jit(solution)/shard_map/ppermute | solution.py:410
  11.0 11.6 %all-to-all-start = ((s32[32,1,32]{2,1,0:T(1,128)}), s32[32,1,32]{2,1,0:T(1,128)S(1)}, u32[]{:S(2)}, u32[]{:S(2)}) async-start(s32[32,1,32]{2,1,0:T(1,128)} %sub.40), calls=%async_computation | async-start | bytes 32768 | tf_op jit(solution)/shard_map/all_to_all | solution.py:391
  23.9 1.7 %collective-permute-start.6 = (bf16[256,512]{1,0:T(8,128)(2,1)S(1)}, bf16[256,512]{1,0:T(8,128)(2,1)S(1)}, u32[]{:S(2)}, u32[]{:S(2)}) collective-permute-start(bf16[256,512]{1,0:T(8,128)(2,1)S(1)} %collective-permute-done.refs_4_), channel_id=1, source_target_pairs={{0,1},{1,0},{2,3},{3,2},{4,5},{5,4},{6,7},{7,6},{8,9},{9,8},{10,11... | collective-permute-start | bytes 786440 | tf_op jit(solution)/shard_map/ppermute | solution.py:428
  24.0 1.9 %collective-permute-start.7 = (bf16[256,512]{1,0:T(8,128)(2,1)S(1)}, bf16[256,512]{1,0:T(8,128)(2,1)S(1)}, u32[]{:S(2)}, u32[]{:S(2)}) collective-permute-start(bf16[256,512]{1,0:T(8,128)(2,1)S(1)} %collective-permute-done.1.refs_5_), channel_id=1, source_target_pairs={{0,1},{1,0},{2,3},{3,2},{4,5},{5,4},{6,7},{7,6},{8,9},{9,8},{10,11... | collective-permute-start | bytes 786440 | tf_op jit(solution)/shard_map/ppermute | solution.py:428
  24.5 15.3 %collective-permute-start.4 = (bf16[256,512]{1,0:T(8,128)(2,1)S(1)}, bf16[256,512]{1,0:T(8,128)(2,1)S(1)}, u32[]{:S(2)}, u32[]{:S(2)}) collective-permute-start(bf16[256,512]{1,0:T(8,128)(2,1)S(1)} %collective-permute-done.refs_4_), channel_id=1, source_target_pairs={{0,2},{1,3},{2,4},{3,5},{4,6},{5,7},{6,0},{7,1},{8,10},{9,11},{10,... | collective-permute-start | bytes 786440 | tf_op jit(solution)/shard_map/ppermute | solution.py:414
  25.0 15.2 %collective-permute-start.5 = (bf16[256,512]{1,0:T(8,128)(2,1)S(1)}, bf16[256,512]{1,0:T(8,128)(2,1)S(1)}, u32[]{:S(2)}, u32[]{:S(2)}) collective-permute-start(bf16[256,512]{1,0:T(8,128)(2,1)S(1)} %collective-permute-done.1.refs_5_), channel_id=1, source_target_pairs={{0,2},{1,3},{2,4},{3,5},{4,6},{5,7},{6,0},{7,1},{8,10},{9,11},{10,... | collective-permute-start | bytes 786440 | tf_op jit(solution)/shard_map/ppermute | solution.py:414
  25.9 1.9 %copy-start = (bf16[2,512,1536]{2,1,0:T(8,128)(2,1)S(1)}, bf16[2,512,1536]{2,1,0:T(8,128)(2,1)}, u32[]{:S(2)}) copy-start(bf16[2,512,1536]{2,1,0:T(8,128)(2,1)} %w_qkv.1) | copy-start | bytes 9437188
  27.8 2.2 %copy-start.1 = (bf16[2,512,2048]{2,1,0:T(8,128)(2,1)S(1)}, bf16[2,512,2048]{2,1,0:T(8,128)(2,1)}, u32[]{:S(2)}) copy-start(bf16[2,512,2048]{2,1,0:T(8,128)(2,1)} %w_up.1) | copy-start | bytes 12582916
  30.0 2.2 %copy-start.2 = (bf16[2,2048,512]{2,1,0:T(8,128)(2,1)S(1)}, bf16[2,2048,512]{2,1,0:T(8,128)(2,1)}, u32[]{:S(2)}) copy-start(bf16[2,2048,512]{2,1,0:T(8,128)(2,1)} %w_down.1) | copy-start | bytes 12582916
  32.2 1.2 %copy-start.3 = (bf16[2,512,512]{2,1,0:T(8,128)(2,1)S(1)}, bf16[2,512,512]{2,1,0:T(8,128)(2,1)}, u32[]{:S(2)}) copy-start(bf16[2,512,512]{2,1,0:T(8,128)(2,1)} %w_proj.1) | copy-start | bytes 3145732
  33.4 0.9 copy-start.6
  34.3 0.9 copy-start.7
  40.2 3.7 %collective-permute-start.10 = (bf16[256,512]{1,0:T(8,128)(2,1)S(1)}, bf16[256,512]{1,0:T(8,128)(2,1)S(1)}, u32[]{:S(2)}, u32[]{:S(2)}) collective-permute-start(bf16[256,512]{1,0:T(8,128)(2,1)S(1)} %collective-permute-done.4.refs_0_), channel_id=1, source_target_pairs={{0,1},{1,0},{2,3},{3,2},{4,5},{5,4},{6,7},{7,6},{8,9},{9,8},{10,11... | collective-permute-start | bytes 786440 | tf_op jit(solution)/shard_map/ppermute | solution.py:428
  40.2 3.7 %collective-permute-start.11 = (bf16[256,512]{1,0:T(8,128)(2,1)S(1)}, bf16[256,512]{1,0:T(8,128)(2,1)S(1)}, u32[]{:S(2)}, u32[]{:S(2)}) collective-permute-start(bf16[256,512]{1,0:T(8,128)(2,1)S(1)} %collective-permute-done.5.refs_1_), channel_id=1, source_target_pairs={{0,1},{1,0},{2,3},{3,2},{4,5},{5,4},{6,7},{7,6},{8,9},{9,8},{10,11... | collective-permute-start | bytes 786440 | tf_op jit(solution)/shard_map/ppermute | solution.py:428
  40.7 11.0 %collective-permute-start.8 = (bf16[256,512]{1,0:T(8,128)(2,1)S(1)}, bf16[256,512]{1,0:T(8,128)(2,1)S(1)}, u32[]{:S(2)}, u32[]{:S(2)}) collective-permute-start(bf16[256,512]{1,0:T(8,128)(2,1)S(1)} %collective-permute-done.4.refs_0_), channel_id=1, source_target_pairs={{0,2},{1,3},{2,4},{3,5},{4,6},{5,7},{6,0},{7,1},{8,10},{9,11},{10,... | collective-permute-start | bytes 786440 | tf_op jit(solution)/shard_map/ppermute | solution.py:414
  41.4 15.0 %collective-permute-start.9 = (bf16[256,512]{1,0:T(8,128)(2,1)S(1)}, bf16[256,512]{1,0:T(8,128)(2,1)S(1)}, u32[]{:S(2)}, u32[]{:S(2)}) collective-permute-start(bf16[256,512]{1,0:T(8,128)(2,1)S(1)} %collective-permute-done.5.refs_1_), channel_id=1, source_target_pairs={{0,2},{1,3},{2,4},{3,5},{4,6},{5,7},{6,0},{7,1},{8,10},{9,11},{10,... | collective-permute-start | bytes 786440 | tf_op jit(solution)/shard_map/ppermute | solution.py:414
  56.3 1.7 %collective-permute-start.12 = (bf16[256,512]{1,0:T(8,128)(2,1)S(1)}, bf16[256,512]{1,0:T(8,128)(2,1)S(1)}, u32[]{:S(2)}, u32[]{:S(2)}) collective-permute-start(bf16[256,512]{1,0:T(8,128)(2,1)S(1)} %collective-permute-done.8.refs_0_), channel_id=1, source_target_pairs={{0,1},{1,0},{2,3},{3,2},{4,5},{5,4},{6,7},{7,6},{8,9},{9,8},{10,11... | collective-permute-start | bytes 786440 | tf_op jit(solution)/shard_map/ppermute | solution.py:428
  56.3 1.9 %collective-permute-start.13 = (bf16[256,512]{1,0:T(8,128)(2,1)S(1)}, bf16[256,512]{1,0:T(8,128)(2,1)S(1)}, u32[]{:S(2)}, u32[]{:S(2)}) collective-permute-start(bf16[256,512]{1,0:T(8,128)(2,1)S(1)} %collective-permute-done.9.refs_1_), channel_id=1, source_target_pairs={{0,1},{1,0},{2,3},{3,2},{4,5},{5,4},{6,7},{7,6},{8,9},{9,8},{10,11... | collective-permute-start | bytes 786440 | tf_op jit(solution)/shard_map/ppermute | solution.py:428
  58.0 1.4 %copy-start.5 = (bf16[512,512]{1,0:T(8,128)(2,1)S(1)}, bf16[512,512]{1,0:T(8,128)(2,1)}, u32[]{:S(2)}) copy-start(bf16[512,512]{1,0:T(8,128)(2,1)} %points.3) | copy-start | bytes 1572868
  58.0 1.4 %copy-start.8 = (f32[4,512]{1,0:T(4,128)S(1)}, f32[4,512]{1,0:T(4,128)}, u32[]{:S(2)}) copy-start(f32[4,512]{1,0:T(4,128)} %gains.5) | copy-start | bytes 24580
  59.4 37.1 %copy-start.4 = (bf16[2,512,512]{2,1,0:T(8,128)(2,1)S(1)}, bf16[2,512,512]{2,1,0:T(8,128)(2,1)}, u32[]{:S(2)}) copy-start(bf16[2,512,512]{2,1,0:T(8,128)(2,1)} %w_proj.1) | copy-start | bytes 3145732
  59.4 37.1 %copy-start.9 = (bf16[3,512]{1,0:T(4,128)(2,1)S(1)}, bf16[3,512]{1,0:T(4,128)(2,1)}, u32[]{:S(2)}) copy-start(bf16[3,512]{1,0:T(4,128)(2,1)} %w_head.1) | copy-start | bytes 9220

commit v5 on v4

--- a/solution.py
+++ b/solution.py
@@ -12,10 +12,12 @@
 HEADS_TOGETHER = 4
 RING_PARTS = 2
 SEND_PARTS = 4
+LANES = 128
+TAIL = 8
+DIGIT = 256
 FIRST_BYTES = 28 * 1024 * 1024
 SECOND_BYTES = 50 * 1024 * 1024
 PROJECT_BYTES = 16 * 1024 * 1024
-OWN_BYTES = 16 * 1024 * 1024
 NORMALIZE_BYTES = 60 * 1024 * 1024
 RING_BYTES = 16 * 1024 * 1024
 F32 = jnp.float32
@@ -115,48 +117,55 @@
         part[...] = layer_norm(held[i], gains_held[0:1, :])
 
 
-def project_kernel(first_rows, *refs):
+def project_kernel(first_rows, own, keep, *refs):
+    refs = list(refs)
+
+    def take(count):
+        taken = refs[:count]
+        del refs[:count]
+        return taken
+
     count = len(first_rows)
-    parts, w_qkv, whole = refs[:count], refs[count], refs[count + 2]
-    held, held_w, sems = refs[count + 3 :]
+    parts = take(count)
+    (w_qkv,) = take(1)
+    others = take(3 * keep)
+    take(not own)
+    (whole,) = take(1)
+    queries = take(own)
+    kept = take(3 * keep)
+    held, held_w, sems, kept_sems = refs
     channels = w_qkv.shape[1]
     rows = held.shape[1]
+    first_column = 0 if own else channels
     fetch, *copies = started(
-        [(w_qkv.at[0, :, pl.ds(channels, 2 * channels)], held_w)]
+        [(w_qkv.at[0, :, pl.ds(first_column, held_w.shape[1])], held_w)]
         + [(part, held.at[i]) for i, part in enumerate(parts)],
         sems,
-    )
-    fetch.wait()
-    for i, first in enumerate(first_rows):
-        copies[i].wait()
-        whole[first : first + rows, :] = jnp.dot(
-            held[i], held_w[...], preferred_element_type=F32
-        ).astype(BF16)
-
-
-def own_kernel(first_rows, *refs):
-    count = len(first_rows)
-    parts, w_qkv, others = refs[:count], refs[count], refs[count + 1 : count + 4]
-    whole, queries, *kept = refs[count + 4 : count + 9]
-    held, held_w, sems, kept_sems = refs[count + 9 :]
-    channels = w_qkv.shape[1]
-    rows = held.shape[1]
-    scale = (channels // HEADS) ** (-0.5)
-    fetch, *copies = started(
-        [(w_qkv.at[0], held_w)] + [(part, held.at[i]) for i, part in enumerate(parts)], sems
     )
     keeping = started([(w.at[0], place) for w, place in zip(others, kept)], kept_sems)
     fetch.wait()
     for i, first in enumerate(first_rows):
         copies[i].wait()
         whole[first : first + rows, :] = jnp.dot(
-            held[i], held_w[:, channels:], preferred_element_type=F32
+            held[i], held_w[:, channels - first_column :], preferred_element_type=F32
         ).astype(BF16)
-        if i * rows < queries.shape[0]:
-            own = jnp.dot(held[i], held_w[:, :channels], preferred_element_type=F32).astype(BF16)
-            queries[i * rows : (i + 1) * rows, :] = (own * BF16(scale)).astype(BF16)
+        if own and i * rows < queries[0].shape[0]:
+            scale = BF16((channels // HEADS) ** (-0.5))
+            query = jnp.dot(held[i], held_w[:, :channels], preferred_element_type=F32).astype(BF16)
+            queries[0][i * rows : (i + 1) * rows, :] = (query * scale).astype(BF16)
     for copy in keeping:
         copy.wait()
+
+
+def lane_tiles(packed, rows):
+    capacity, channels = rows.shape[1:]
+    return [
+        (
+            packed.at[:, pl.ds(j * capacity, capacity), :],
+            rows.at[:, :, pl.ds(j * LANES, LANES)],
+        )
+        for j in range(channels // LANES)
+    ]
 
 
 def first_kernel(
@@ -169,6 +178,7 @@
     w_proj,
     w_up,
     w_down,
+    tail,
     outgoing,
     attended,
     points_held,
@@ -178,6 +188,9 @@
     sems,
 ):
     rows, channels = points.shape
+    devices, capacity, _ = outgoing_held.shape
+    packed = outgoing.shape[2] == LANES
+    row_tiles = channels // LANES * capacity
     patches = rows // PATCH
     chosen = pattern.shape[0] // patches
     copies = started(
@@ -185,8 +198,9 @@
             (points, points_held),
             (gains, gains_held),
             (slot_of_row, slots_held),
-        ],
-        sems,
+        ]
+        + ([(tail, outgoing.at[:, pl.ds(row_tiles, TAIL), :])] if packed else []),
+        sems.at[0],
     )
     masks = head_masks(channels // HEADS)
     for p in range(patches):
@@ -207,26 +221,27 @@
         points_held[...], attended[...], gains_held[1:2, :], (w_proj, w_up, w_down)
     )
     slots = slots_held[...]
-    piece = outgoing.shape[0] // SEND_PARTS
+    targets = devices // SEND_PARTS
+    piece = targets * capacity
     leaving = []
     for i in range(SEND_PARTS):
-        here = pl.ds(i * piece, piece)
+        here = pl.ds(i * targets, targets)
         send = one_hot_rows(slots - i * piece, piece)
-        outgoing_held[here, :] = jnp.dot(send, first, preferred_element_type=F32).astype(BF16)
-        leaving.append(
-            pltpu.make_async_copy(
-                outgoing_held.at[here, :], outgoing.at[here, :], sems.at[len(copies) + i]
-            )
-        )
-        leaving[-1].start()
+        moved = jnp.dot(send, first, preferred_element_type=F32).astype(BF16)
+        outgoing_held[here] = moved.reshape(targets, capacity, channels)
+        there = outgoing.at[here]
+        pairs = [(there, outgoing_held.at[here])]
+        if packed:
+            pairs = lane_tiles(there, outgoing_held.at[here])
+        leaving += started([(source, place) for place, source in pairs], sems.at[1 + i])
     for copy in leaving:
         copy.wait()
 
 
 def second_kernel(
     pattern,
-    slot_places,
     gains,
+    tail,
     incoming,
     w_qkv,
     w_proj,
@@ -243,34 +258,52 @@
     up_held,
     down_held,
     gains_held,
-    places_held,
+    tail_held,
     head_held,
     sems,
 ):
     rows, channels = features.shape
+    devices, capacity, _ = incoming_held.shape
+    packed = incoming.shape[2] == LANES
+    arriving = [(incoming, incoming_held)]
+    if packed:
+        arriving = lane_tiles(incoming, incoming_held)
+        tail = incoming.at[:, pl.ds(channels // LANES * capacity, TAIL), :]
     patches = rows // PATCH
     chosen = pattern.shape[0] // patches
     small = started(
-        [(slot_places, places_held), (gains, gains_held), (w_head, head_held)], sems.at[1]
-    )
+        [(tail, tail_held), (gains, gains_held), (w_head, head_held)], sems.at[0]
+    )
+    landing = started(arriving, sems.at[1])
     copies = started(
         [
-            (incoming, incoming_held),
             (w_qkv.at[1], qkv_held),
             (w_proj.at[1], proj_held),
             (w_up.at[1], up_held),
             (w_down.at[1], down_held),
         ],
-        sems.at[0],
+        sems.at[2],
     )
     for copy in small:
         copy.wait()
-    place = one_hot_rows(places_held[...], rows)
-    copies[0].wait()
-    second = jnp.dot(place, incoming_held[...], preferred_element_type=F32).astype(BF16)
+    per_row = LANES // capacity
+    digits = tail_held[...].astype(F32)
+    codes = digits[:, 0:1, :] + DIGIT * digits[:, 1:2, :]
+    pieces = []
+    for at in range(0, devices, per_row):
+        code = codes[at]
+        for i in range(1, per_row):
+            code = code + codes[at + i]
+        pieces.append(code)
+    places = jnp.concatenate(pieces, axis=1).astype(jnp.int32) - 1
+    place = one_hot_rows(places, rows)
+    for copy in landing:
+        copy.wait()
+    moved = incoming_held[...].reshape(devices * capacity, channels)
+    second = jnp.dot(place, moved, preferred_element_type=F32).astype(BF16)
     normed = layer_norm(second, gains_held[2:3, :])
     scale = (channels // HEADS) ** (-0.5)
-    copies[1].wait()
+    copies[0].wait()
     queries = (
         jnp.dot(normed, qkv_held[:, :channels], preferred_element_type=F32).astype(BF16)
         * BF16(scale)
@@ -287,7 +320,7 @@
             queries[p * PATCH : (p + 1) * PATCH, :], both[:, :channels], both[:, channels:], masks
         )
     done = finish(
-        second, attended[...], gains_held[3:4, :], (proj_held, up_held, down_held), copies[2:]
+        second, attended[...], gains_held[3:4, :], (proj_held, up_held, down_held), copies[1:]
     )
     features[...] = done
     normals[...] = lax.dot_general(
@@ -344,7 +377,7 @@
     weights = (w_proj, w_up, w_down)
     kv_shape = jax.ShapeDtypeStruct((kept_rows, 2 * channels), BF16)
 
-    def project(keyed, blocks):
+    def project(keyed, blocks, keep=False):
         parts = [rows for _, block in blocks for rows in block]
         count = len(parts)
         rows = parts[0].shape[0]
@@ -352,30 +385,29 @@
             slot * rows_here + i * rows for slot, block in blocks for i in range(len(block))
         ]
         own = keyed is None
-        own_shapes = [jax.ShapeDtypeStruct((rows_here, channels), BF16)]
-        own_shapes += [jax.ShapeDtypeStruct(w.shape[1:], BF16) for w in weights]
+        shapes = [kv_shape]
+        shapes += [jax.ShapeDtypeStruct((rows_here, channels), BF16)] * own
+        shapes += [jax.ShapeDtypeStruct(w.shape[1:], BF16) for w in weights] * keep
         return pl.pallas_call(
-            functools.partial(own_kernel if own else project_kernel, first_rows),
-            out_shape=[kv_shape] + own_shapes if own else kv_shape,
-            in_specs=[ANY_SPEC] * (count + 1) + ([ANY_SPEC] * 3 if own else [VMEM_SPEC]),
-            out_specs=[VMEM_SPEC] * 5 if own else VMEM_SPEC,
+            functools.partial(project_kernel, first_rows, own, keep),
+            out_shape=shapes,
+            in_specs=[ANY_SPEC] * (count + 1 + 3 * keep) + [VMEM_SPEC] * (not own),
+            out_specs=[VMEM_SPEC] * len(shapes),
             scratch_shapes=[
                 pltpu.VMEM((count, rows, channels), BF16),
                 pltpu.VMEM((channels, (3 if own else 2) * channels), BF16),
                 pltpu.SemaphoreType.DMA((count + 1,)),
-            ]
-            + ([pltpu.SemaphoreType.DMA((3,))] if own else []),
-            input_output_aliases={} if own else {count + 1: 0},
+                pltpu.SemaphoreType.DMA((3,)),
+            ],
+            input_output_aliases={} if own else {count + 1 + 3 * keep: 0},
             cost_estimate=pl.CostEstimate(
                 flops=4 * count * rows * channels**2,
                 bytes_accessed=3 * count * rows * channels * 2 + 3 * channels**2 * 2,
                 transcendentals=0,
             ),
-            compiler_params=pltpu.CompilerParams(
-                vmem_limit_bytes=OWN_BYTES if own else PROJECT_BYTES
-            ),
+            compiler_params=pltpu.CompilerParams(vmem_limit_bytes=PROJECT_BYTES),
             name="project_own" if own else "project",
-        )(*parts, w_qkv, *(weights if own else [keyed]))
+        )(*parts, w_qkv, *(weights * keep), *([] if own else [keyed]))
 
     target = destination // rows_here
     place_at = destination % rows_here
@@ -387,15 +419,17 @@
     slot_index = target * capacity + send_rank
     slot_ids = jnp.arange(slot_total, dtype=jnp.int32)
     match_send = slot_index[None, :] == slot_ids[:, None]
-    out_places = jnp.sum(jnp.where(match_send, place_at[None, :] + 1, 0), axis=1) - 1
-    in_places = lax.all_to_all(
-        out_places.reshape(devices, capacity),
-        ("grp", "seq"),
-        split_axis=0,
-        concat_axis=0,
-        tiled=True,
-    ).reshape(1, slot_total)
+    codes = jnp.sum(jnp.where(match_send, place_at[None, :] + 1, 0), axis=1)
+    index = lax.axis_index("grp") * lax.axis_size("seq") + lax.axis_index("seq")
+    per_row = LANES // capacity
+    lane = jnp.arange(LANES, dtype=jnp.int32)
+    codes = jnp.where(
+        lane // capacity == index % per_row, jnp.tile(codes.reshape(devices, capacity), per_row), 0
+    )
+    digits = jnp.stack([codes % DIGIT, codes // DIGIT], axis=1).astype(BF16)
+    tail = jnp.concatenate([digits, jnp.zeros((devices, TAIL - 2, LANES), BF16)], axis=1)
     slot_index = slot_index.reshape(1, rows_here)
+    packed = capacity % 16 == 0
 
     pattern_second = pattern_second.reshape(-1)
     me = lax.axis_index("seq")
@@ -409,59 +443,61 @@
     if ring:
         beside = [lax.ppermute(rows, "seq", swap) for rows in column]
         waiting = [(0, column), (1, beside)]
-        keyed = None
         for step in range(1, chips):
             column = [lax.ppermute(rows, "seq", onward) for rows in column]
             if step == 1:
-                tied = (column, waiting[0][1], beside, pattern_slots, pattern_second, slot_index)
-                tied, in_places = lax.optimization_barrier((tied, in_places))
-                column, own, beside, pattern_slots, pattern_second, slot_index = tied
-                waiting = [(0, own), (1, beside)]
-            elif step == 2:
-                keyed, queries, *kept = project(None, waiting)
+                own = [rows for _, block in waiting for rows in block]
+                own, tail, slot_index, pattern_slots, pattern_second = lax.optimization_barrier(
+                    (own, tail, slot_index, pattern_slots, pattern_second)
+                )
+                waiting = [(0, own[:RING_PARTS]), (1, own[RING_PARTS:])]
+            else:
+                if step == 2:
+                    keyed, queries = project(None, waiting)
+                else:
+                    keyed, *kept = project(keyed, waiting, keep=step == 3)
+                column, keyed = lax.optimization_barrier((column, keyed))
                 waiting = []
-            else:
-                keyed = project(keyed, waiting)
-                waiting = []
-            if step > 1:
-                column, keyed = lax.optimization_barrier((column, keyed))
             beside = [lax.ppermute(rows, "seq", swap) for rows in column]
             waiting = waiting + [(2 * step, column), (2 * step + 1, beside)]
         for block in waiting:
-            keyed = project(keyed, [block])
+            (keyed,) = project(keyed, [block])
     else:
         group = lax.all_gather(jnp.concatenate(column), "seq", axis=0, tiled=True)
         picked = group.reshape(-1, PATCH, channels)[pattern_first].reshape(-1, channels)
-        keyed, queries, *kept = project(None, [(0, column)])
-        keyed = project(keyed, [(1, [picked])])
+        keyed, queries = project(None, [(0, column)])
+        keyed, *kept = project(keyed, [(1, [picked])], keep=True)
 
     held_weights = [pltpu.VMEM(w.shape[1:], BF16) for w in weights]
     held_rows = pltpu.VMEM((rows_here, channels), BF16)
+    pair_shape = (capacity, channels)
+    if packed:
+        pair_shape = (channels // LANES * capacity + TAIL, LANES)
+    held_slots = pltpu.VMEM((devices, capacity, channels), BF16)
     outgoing = pl.pallas_call(
         first_kernel,
-        out_shape=jax.ShapeDtypeStruct((slot_total, channels), BF16),
+        out_shape=jax.ShapeDtypeStruct((devices,) + pair_shape, BF16),
         in_specs=[SMEM_SPEC, ANY_SPEC, ANY_SPEC, VMEM_SPEC, VMEM_SPEC, ANY_SPEC]
-        + [VMEM_SPEC] * 3,
+        + [VMEM_SPEC] * 3
+        + [ANY_SPEC],
         out_specs=ANY_SPEC,
         scratch_shapes=[
             held_rows,
             held_rows,
             pltpu.VMEM(norm_gains.shape, F32),
             pltpu.VMEM(slot_index.shape, jnp.int32),
-            pltpu.VMEM((slot_total, channels), BF16),
-            pltpu.SemaphoreType.DMA((3 + SEND_PARTS,)),
+            held_slots,
+            pltpu.SemaphoreType.DMA((1 + SEND_PARTS, 4)),
         ],
         compiler_params=pltpu.CompilerParams(vmem_limit_bytes=FIRST_BYTES),
         name="block_first",
-    )(pattern_slots, slot_index, norm_gains, keyed, queries, points, *kept)
-
-    incoming = lax.all_to_all(
-        outgoing.reshape(devices, capacity, channels),
-        ("grp", "seq"),
-        split_axis=0,
-        concat_axis=0,
-        tiled=True,
-    ).reshape(slot_total, channels)
+    )(pattern_slots, slot_index, norm_gains, keyed, queries, points, *kept, tail)
+
+    def exchange(array):
+        return lax.all_to_all(array, ("grp", "seq"), split_axis=0, concat_axis=0, tiled=True)
+
+    incoming = exchange(outgoing)
+    tail = tail if packed else exchange(tail)
 
     return pl.pallas_call(
         second_kernel,
@@ -474,17 +510,17 @@
         scratch_shapes=[
             pltpu.VMEM((rows_here, 2 * channels), BF16),
             held_rows,
-            pltpu.VMEM((slot_total, channels), BF16),
+            held_slots,
             pltpu.VMEM(w_qkv.shape[1:], BF16),
             *held_weights,
             pltpu.VMEM(norm_gains.shape, F32),
-            pltpu.VMEM(in_places.shape, jnp.int32),
+            pltpu.VMEM(tail.shape, BF16),
             pltpu.VMEM(w_head.shape, BF16),
-            pltpu.SemaphoreType.DMA((2, 5)),
+            pltpu.SemaphoreType.DMA((3, 5)),
         ],
         compiler_params=pltpu.CompilerParams(vmem_limit_bytes=SECOND_BYTES),
         name="block_second",
-    )(pattern_second, in_places, norm_gains, incoming, w_qkv, *weights, w_head)
+    )(pattern_second, norm_gains, tail, incoming, w_qkv, *weights, w_head)
 
 
 def solution(mesh):

time: 107 us -> 106 us (level)
  waiting for transfers between devices: 16.8 us -> 26.5 us
  starting transfers between devices: 15.3 us -> 7.26 us
  local copies, waits for them, and re-layouts: 11.9 us -> 7.43 us
  blocking collectives: 29.3 us -> 31.8 us
    ppermute x6, waiting for transfers between devices: 10.8 us -> 24.9 us  [shards(): column = [lax.ppermute(rows, 'seq', onward) for rows in column]]
    all_to_all x1 -> x0, waiting for transfers between devices: 5.4 us -> none  [shards(): lax.all_to_all(out_places.reshape(devices, capacity), ('grp', 'seq'), spl...]
    all_to_all x1 -> x0, starting transfers between devices: 4.5 us -> none  [shards(): lax.all_to_all(out_places.reshape(devices, capacity), ('grp', 'seq'), spl...]
    unnamed x21 -> x19, local copies, waits for them, and re-layouts: 10.2 us -> 6.76 us
    ppermute x6, starting transfers between devices: 8.94 us -> 5.55 us  [shards(): column = [lax.ppermute(rows, 'seq', onward) for rows in column]]
    all_to_all x1, blocking collectives: 29.3 us -> 31.8 us  [exchange(): lax.all_to_all(array, ('grp', 'seq'), split_axis=0, concat_axis=0, tiled=...]
  transfers between devices with their start and end apart: 15 -> 14, of which waited for: 6 -> 9; matrix products, arithmetic and copies ran while one was open for 6% -> 4% of each run, Pallas kernels for 7% -> 7%
where the time goes in v5:
time: 106 us
  blocking collectives  31.8 us (30%)
  Pallas kernels  28.7 us (27%)
  waiting for transfers between devices  26.5 us (25%)
  local copies, waits for them, and re-layouts  7.43 us (7%)
  starting transfers between devices  7.26 us (7%)
  other arithmetic  3.23 us (3%)
    all_to_all x1, blocking collectives, exchange(): lax.all_to_all(array, ('grp', 'seq'), split_axis=0, concat_axis=0, tiled=...  31.8 us
    ppermute x6, waiting for transfers between devices, shards(): column = [lax.ppermute(rows, 'seq', onward) for rows in column]  24.9 us
    pallas_call x1, Pallas kernels, shards(): pl.pallas_call(second_kernel, out_shape=(jax.ShapeDtypeStruct((rows_here,...  9.63 us
    pallas_call x4, Pallas kernels, project(): pl.pallas_call(functools.partial(project_kernel, first_rows, own, keep),...  8.8 us
    pallas_call x1, Pallas kernels, shards(): pl.pallas_call(first_kernel, out_shape=jax.ShapeDtypeStruct((devices,) +...  8.12 us
    unnamed x19, local copies, waits for them, and re-layouts  6.76 us
    ppermute x6, starting transfers between devices, shards(): column = [lax.ppermute(rows, 'seq', onward) for rows in column]  5.55 us
    pallas_call x1, Pallas kernels, shards(): pl.pallas_call(normalize_kernel, out_shape=[jax.ShapeDtypeStruct((part, c...  2.17 us
  transfers between devices with their start and end apart: 14, of which 9 were waited for; matrix products, arithmetic and copies ran while one was open for 4% of the time, Pallas kernels for 7%

profile of v5, /device:TPU:0, one launch (start us, length us, event | category | flops | bytes accessed | tf_op | source)
XLA Modules:
  0.0 106.0 jit_solution(3910357280430463380)
XLA Ops:
  0.6 2.2 %normalize.1 = (bf16[256,512]{1,0:T(8,128)(2,1)}, bf16[256,512]{1,0:T(8,128)(2,1)}) custom-call(bf16[512,512]{1,0:T(8,128)(2,1)} %points.3, f32[4,512]{1,0:T(4,128)} %gains.5), custom_call_target="tpu_custom_call" | custom-call | tf_op jit(solution)/shard_map/normalize/pallas_call | solution.py:363
  2.8 0.5 collective-permute-start
  3.3 2.6 %collective-permute-start.2 = (bf16[256,512]{1,0:T(8,128)(2,1)}, bf16[256,512]{1,0:T(8,128)(2,1)S(1)}, u32[]{:S(2)}, u32[]{:S(2)}) collective-permute-start(bf16[256,512]{1,0:T(8,128)(2,1)} %get-tuple-element.30.refs_0_), channel_id=1, source_target_pairs={{0,2},{1,3},{2,4},{3,5},{4,6},{5,7},{6,0},{7,1},{8,10},{9,11},{10,... | collective-permute-start | bytes 786440 | tf_op jit(solution)/shard_map/ppermute | solution.py:447
  6.0 0.2 collective-permute-start.1
  6.1 1.6 %collective-permute-start.4 = (bf16[256,512]{1,0:T(8,128)(2,1)}, bf16[256,512]{1,0:T(8,128)(2,1)S(1)}, u32[]{:S(2)}, u32[]{:S(2)}) collective-permute-start(bf16[256,512]{1,0:T(8,128)(2,1)} %get-tuple-element.31.refs_1_), channel_id=1, source_target_pairs={{0,2},{1,3},{2,4},{3,5},{4,6},{5,7},{6,0},{7,1},{8,10},{9,11},{10,... | collective-permute-start | bytes 786440 | tf_op jit(solution)/shard_map/ppermute | solution.py:447
  7.7 0.7 add_select_fusion.6
  8.4 1.2 %reduce-window.6 = s32[32,4,128]{2,0,1:T(8,128)S(1)} reduce-window(s32[32,4,128]{2,0,1:T(8,128)S(1)} %fusion.6, s32[]{:T(128)} %constant.142.clone.1), window={size=1x1x128 pad=0_0x0_0x127_0}, to_apply=%region_0.1 | reduce-window | flops 2080768 | bytes 131076 | tf_op jit(solution)/shard_map/reduce-window
  9.6 0.2 slice_reduce_fusion
  9.8 0.1 fusion.5
  10.0 0.3 select_reduce_fusion
  10.3 0.1 tile.10
  10.4 0.1 tile.12
  10.5 0.1 fusion.7
  10.6 0.7 fusion.15
  11.3 0.1 copy.21
  11.4 0.1 reshape.150.pattern
  11.4 0.8 copy.22
  12.2 0.1 reshape.151.pattern
  12.3 3.1 %collective-permute-done.2.refs_4_ = bf16[256,512]{1,0:T(8,128)(2,1)S(1)} collective-permute-done((bf16[256,512]{1,0:T(8,128)(2,1)}, bf16[256,512]{1,0:T(8,128)(2,1)S(1)}, u32[]{:S(2)}, u32[]{:S(2)}) %collective-permute-start.2) | collective-permute-done | bytes 262176 | tf_op jit(solution)/shard_map/ppermute | solution.py:447
  15.4 5.4 %collective-permute-done.4.refs_5_ = bf16[256,512]{1,0:T(8,128)(2,1)S(1)} collective-permute-done((bf16[256,512]{1,0:T(8,128)(2,1)}, bf16[256,512]{1,0:T(8,128)(2,1)S(1)}, u32[]{:S(2)}, u32[]{:S(2)}) %collective-permute-start.4) | collective-permute-done | bytes 262176 | tf_op jit(solution)/shard_map/ppermute | solution.py:447
  20.7 0.1 fusion.8
  20.8 0.1 collective-permute-start.3
  20.9 1.3 %collective-permute-start.5 = (bf16[256,512]{1,0:T(8,128)(2,1)S(1)}, bf16[256,512]{1,0:T(8,128)(2,1)S(1)}, u32[]{:S(2)}, u32[]{:S(2)}) collective-permute-start(bf16[256,512]{1,0:T(8,128)(2,1)S(1)} %collective-permute-done.4.refs_5_), channel_id=1, source_target_pairs={{0,2},{1,3},{2,4},{3,5},{4,6},{5,7},{6,0},{7,1},{8,10},{9,11},{10,... | collective-permute-start | bytes 786440 | tf_op jit(solution)/shard_map/ppermute | solution.py:447
  22.2 0.0 collective-permute-done.7.refs_7_
  22.3 1.9 %copy-done = bf16[2,512,1536]{2,1,0:T(8,128)(2,1)S(1)} copy-done((bf16[2,512,1536]{2,1,0:T(8,128)(2,1)S(1)}, bf16[2,512,1536]{2,1,0:T(8,128)(2,1)}, u32[]{:S(2)}) %copy-start) | copy-done | bytes 3145752
  24.2 0.9 copy-done.7
  25.1 0.9 copy-done.8
  26.1 4.2 %project_own.1 = (bf16[4096,1024]{1,0:T(8,128)(2,1)S(1)}, bf16[512,512]{1,0:T(8,128)(2,1)S(1)}) custom-call(bf16[256,512]{1,0:T(8,128)(2,1)S(1)} %copy-done.7, bf16[256,512]{1,0:T(8,128)(2,1)S(1)} %copy-done.8, bf16[256,512]{1,0:T(8,128)(2,1)S(1)} %collective-permute-done.refs_2_, bf16[256,512]{1,0:T(8,128)(2,1)S(1)} %collective-permute-done.1.refs_3_, ...), custom_call_target="tpu_custom_call" | custom-call | flops 2147483648 | bytes 7864320 | tf_op jit(solution)/shard_map/project_own/pallas_call | solution.py:391
  30.2 1.5 %collective-permute-done.3.refs_0_ = bf16[256,512]{1,0:T(8,128)(2,1)S(1)} collective-permute-done((bf16[256,512]{1,0:T(8,128)(2,1)S(1)}, bf16[256,512]{1,0:T(8,128)(2,1)S(1)}, u32[]{:S(2)}, u32[]{:S(2)}) %collective-permute-start.3) | collective-permute-done | bytes 262176 | tf_op jit(solution)/shard_map/ppermute | solution.py:447
  31.8 5.2 %collective-permute-done.5.refs_1_ = bf16[256,512]{1,0:T(8,128)(2,1)S(1)} collective-permute-done((bf16[256,512]{1,0:T(8,128)(2,1)S(1)}, bf16[256,512]{1,0:T(8,128)(2,1)S(1)}, u32[]{:S(2)}, u32[]{:S(2)}) %collective-permute-start.5) | collective-permute-done | bytes 262176 | tf_op jit(solution)/shard_map/ppermute | solution.py:447
  37.0 0.5 collective-permute-start.11
  37.5 0.0 collective-permute-start.9
  37.5 1.0 collective-permute-done.10.refs_2_
  38.6 0.4 collective-permute-done.11.refs_3_
  38.9 2.2 %copy-done.2 = bf16[2,2048,512]{2,1,0:T(8,128)(2,1)S(1)} copy-done((bf16[2,2048,512]{2,1,0:T(8,128)(2,1)S(1)}, bf16[2,2048,512]{2,1,0:T(8,128)(2,1)}, u32[]{:S(2)}) %copy-start.2) | copy-done | bytes 4194328
  41.1 2.4 %project.3 = (bf16[4096,1024]{1,0:T(8,128)(2,1)S(1)}, bf16[512,512]{1,0:T(8,128)(2,1)S(1)}, bf16[512,2048]{1,0:T(8,128)(2,1)S(1)}, bf16[2048,512]{1,0:T(8,128)(2,1)S(1)}) custom-call(bf16[256,512]{1,0:T(8,128)(2,1)S(1)} %collective-permute-done.3.refs_0_, bf16[256,512]{1,0:T(8,128)(2,1)S(1)} %collective-permute-done.5.refs_1_, ...), custom_call_target="tpu_custom_call", output_to_operand_aliasing={{0}: (8, {})} | custom-call | flops 1073741824 | bytes 4718592 | tf_op jit(solution)/shard_map/project/pallas_call | solution.py:391
  43.5 5.0 %collective-permute-done.8.refs_0_ = bf16[256,512]{1,0:T(8,128)(2,1)S(1)} collective-permute-done((bf16[256,512]{1,0:T(8,128)(2,1)S(1)}, bf16[256,512]{1,0:T(8,128)(2,1)S(1)}, u32[]{:S(2)}, u32[]{:S(2)}) %collective-permute-start.8) | collective-permute-done | bytes 262176 | tf_op jit(solution)/shard_map/ppermute | solution.py:447
  48.5 4.7 %collective-permute-done.9.refs_1_ = bf16[256,512]{1,0:T(8,128)(2,1)S(1)} collective-permute-done((bf16[256,512]{1,0:T(8,128)(2,1)S(1)}, bf16[256,512]{1,0:T(8,128)(2,1)S(1)}, u32[]{:S(2)}, u32[]{:S(2)}) %collective-permute-start.9) | collective-permute-done | bytes 262176 | tf_op jit(solution)/shard_map/ppermute | solution.py:447
  53.2 0.5 collective-permute-start.13
  53.7 1.1 %project.4.refs_3_ = bf16[4096,1024]{1,0:T(8,128)(2,1)S(1)} custom-call(bf16[256,512]{1,0:T(8,128)(2,1)S(1)} %collective-permute-done.8.refs_0_, bf16[256,512]{1,0:T(8,128)(2,1)S(1)} %collective-permute-done.9.refs_1_, bf16[2,512,1536]{2,1,0:T(8,128)(2,1)S(1)} %copy-done, ...), custom_call_target="tpu_custom_call", output_to_operand_aliasing={{}: (3, {})} | custom-call | flops 536870912 | bytes 3145728 | tf_op jit(solution)/shard_map/project/pallas_call | solution.py:391
  54.8 0.0 copy-start.4
  54.8 0.0 copy-start.5
  54.8 0.2 collective-permute-done.13.refs_1_
  55.1 1.1 %project.5.keyed = bf16[4096,1024]{1,0:T(8,128)(2,1)S(1)} custom-call(bf16[256,512]{1,0:T(8,128)(2,1)S(1)} %collective-permute-done.12.refs_0_, bf16[256,512]{1,0:T(8,128)(2,1)S(1)} %collective-permute-done.13.refs_1_, bf16[2,512,1536]{2,1,0:T(8,128)(2,1)S(1)} %copy-done, bf16[4096,1024]{1,0:T(8,128)(2,1)S(1)} %project.4.refs_3_), custom_call_target="tpu_custom_call", output_to_operand_aliasing={{}: (3, {})} | custom-call | flops 536870912 | bytes 3145728 | tf_op jit(solution)/shard_map/project/pallas_call | solution.py:391
  56.2 8.1 %block_first.1 = bf16[32,136,128]{2,1,0:T(8,128)(2,1)S(1)} custom-call(s32[24]{0:T(128)S(1)} %reshape.150.pattern, s32[1,512]{1,0:T(1,128)S(1)} %bitcast.21, f32[4,512]{1,0:T(4,128)S(1)} %copy-done.5, bf16[4096,1024]{1,0:T(8,128)(2,1)S(1)} %project.5.keyed, bf16[512,512]{1,0:T(8,128)(2,1)S(1)} %get-tuple-element.42.queries, bf16[512,512]{1,0:T(8,128)(2,1)S(1)} %copy-done.4, ...), custom_call_target="tpu_custom_call" | custom-call | tf_op jit(solution)/shard_map/block_first/pallas_call | solution.py:477
  64.4 0.0 copy-start.6
  64.4 31.8 %all_to_all.5.incoming = bf16[32,136,128]{2,1,0:T(8,128)(2,1)S(1)} all-to-all(bf16[32,136,128]{2,1,0:T(8,128)(2,1)S(1)} %block_first.1), channel_id=1, replica_groups=mesh['grp'=4,'seq'=8] {'grp','seq'}, dimensions={0} | all-to-all | bytes 2228224 | tf_op jit(solution)/shard_map/all_to_all | solution.py:497
  96.2 9.6 %block_second.1 = (bf16[512,512]{1,0:T(8,128)(2,1)}, f32[3,512]{1,0:T(4,128)}) custom-call(s32[24]{0:T(128)S(1)} %reshape.151.pattern, f32[4,512]{1,0:T(4,128)S(1)} %copy-done.5, bf16[32,8,128]{2,1,0:T(8,128)(2,1)S(1)} %fusion.2.tail, bf16[32,136,128]{2,1,0:T(8,128)(2,1)S(1)} %all_to_all.5.incoming, bf16[2,512,1536]{2,1,0:T(8,128)(2,1)} %w_qkv.1, ...), custom_call_target="tpu_custom_call" | custom-call | tf_op jit(solution)/shard_map/block_second/pallas_call | solution.py:502
  (27 shorter events, 0.2 us)
Async XLA Ops:
  2.8 18.1 %collective-permute-start = (bf16[256,512]{1,0:T(8,128)(2,1)}, bf16[256,512]{1,0:T(8,128)(2,1)S(1)}, u32[]{:S(2)}, u32[]{:S(2)}) collective-permute-start(bf16[256,512]{1,0:T(8,128)(2,1)} %get-tuple-element.30.refs_0_), channel_id=1, source_target_pairs={{0,1},{1,0},{2,3},{3,2},{4,5},{5,4},{6,7},{7,6},{8,9},{9,8},{10,11... | collective-permute-start | bytes 786440 | tf_op jit(solution)/shard_map/ppermute | solution.py:444
  3.3 12.0 %collective-permute-start.2 = (bf16[256,512]{1,0:T(8,128)(2,1)}, bf16[256,512]{1,0:T(8,128)(2,1)S(1)}, u32[]{:S(2)}, u32[]{:S(2)}) collective-permute-start(bf16[256,512]{1,0:T(8,128)(2,1)} %get-tuple-element.30.refs_0_), channel_id=1, source_target_pairs={{0,2},{1,3},{2,4},{3,5},{4,6},{5,7},{6,0},{7,1},{8,10},{9,11},{10,... | collective-permute-start | bytes 786440 | tf_op jit(solution)/shard_map/ppermute | solution.py:447
  6.0 16.3 %collective-permute-start.1 = (bf16[256,512]{1,0:T(8,128)(2,1)}, bf16[256,512]{1,0:T(8,128)(2,1)S(1)}, u32[]{:S(2)}, u32[]{:S(2)}) collective-permute-start(bf16[256,512]{1,0:T(8,128)(2,1)} %get-tuple-element.31.refs_1_), channel_id=1, source_target_pairs={{0,1},{1,0},{2,3},{3,2},{4,5},{5,4},{6,7},{7,6},{8,9},{9,8},{10,11... | collective-permute-start | bytes 786440 | tf_op jit(solution)/shard_map/ppermute | solution.py:444
  6.1 14.6 %collective-permute-start.4 = (bf16[256,512]{1,0:T(8,128)(2,1)}, bf16[256,512]{1,0:T(8,128)(2,1)S(1)}, u32[]{:S(2)}, u32[]{:S(2)}) collective-permute-start(bf16[256,512]{1,0:T(8,128)(2,1)} %get-tuple-element.31.refs_1_), channel_id=1, source_target_pairs={{0,2},{1,3},{2,4},{3,5},{4,6},{5,7},{6,0},{7,1},{8,10},{9,11},{10,... | collective-permute-start | bytes 786440 | tf_op jit(solution)/shard_map/ppermute | solution.py:447
  15.4 6.9 %collective-permute-start.6 = (bf16[256,512]{1,0:T(8,128)(2,1)S(1)}, bf16[256,512]{1,0:T(8,128)(2,1)S(1)}, u32[]{:S(2)}, u32[]{:S(2)}) collective-permute-start(bf16[256,512]{1,0:T(8,128)(2,1)S(1)} %collective-permute-done.2.refs_4_), channel_id=1, source_target_pairs={{0,1},{1,0},{2,3},{3,2},{4,5},{5,4},{6,7},{7,6},{8,9},{9,8},{10,11... | collective-permute-start | bytes 786440 | tf_op jit(solution)/shard_map/ppermute | solution.py:461
  20.7 1.5 %collective-permute-start.7 = (bf16[256,512]{1,0:T(8,128)(2,1)S(1)}, bf16[256,512]{1,0:T(8,128)(2,1)S(1)}, u32[]{:S(2)}, u32[]{:S(2)}) collective-permute-start(bf16[256,512]{1,0:T(8,128)(2,1)S(1)} %collective-permute-done.4.refs_5_), channel_id=1, source_target_pairs={{0,1},{1,0},{2,3},{3,2},{4,5},{5,4},{6,7},{7,6},{8,9},{9,8},{10,11... | collective-permute-start | bytes 786440 | tf_op jit(solution)/shard_map/ppermute | solution.py:461
  20.8 10.9 %collective-permute-start.3 = (bf16[256,512]{1,0:T(8,128)(2,1)S(1)}, bf16[256,512]{1,0:T(8,128)(2,1)S(1)}, u32[]{:S(2)}, u32[]{:S(2)}) collective-permute-start(bf16[256,512]{1,0:T(8,128)(2,1)S(1)} %collective-permute-done.2.refs_4_), channel_id=1, source_target_pairs={{0,2},{1,3},{2,4},{3,5},{4,6},{5,7},{6,0},{7,1},{8,10},{9,11},{10,... | collective-permute-start | bytes 786440 | tf_op jit(solution)/shard_map/ppermute | solution.py:447
  20.9 16.1 %collective-permute-start.5 = (bf16[256,512]{1,0:T(8,128)(2,1)S(1)}, bf16[256,512]{1,0:T(8,128)(2,1)S(1)}, u32[]{:S(2)}, u32[]{:S(2)}) collective-permute-start(bf16[256,512]{1,0:T(8,128)(2,1)S(1)} %collective-permute-done.4.refs_5_), channel_id=1, source_target_pairs={{0,2},{1,3},{2,4},{3,5},{4,6},{5,7},{6,0},{7,1},{8,10},{9,11},{10,... | collective-permute-start | bytes 786440 | tf_op jit(solution)/shard_map/ppermute | solution.py:447
  22.3 1.9 %copy-start = (bf16[2,512,1536]{2,1,0:T(8,128)(2,1)S(1)}, bf16[2,512,1536]{2,1,0:T(8,128)(2,1)}, u32[]{:S(2)}) copy-start(bf16[2,512,1536]{2,1,0:T(8,128)(2,1)} %w_qkv.1) | copy-start | bytes 9437188
  24.2 0.9 copy-start.7
  25.1 0.9 copy-start.8
  26.1 12.9 %copy-start.1 = (bf16[2,512,2048]{2,1,0:T(8,128)(2,1)S(1)}, bf16[2,512,2048]{2,1,0:T(8,128)(2,1)}, u32[]{:S(2)}) copy-start(bf16[2,512,2048]{2,1,0:T(8,128)(2,1)} %w_up.1) | copy-start | bytes 12582916
  26.1 12.9 %copy-start.3 = (bf16[2,512,512]{2,1,0:T(8,128)(2,1)S(1)}, bf16[2,512,512]{2,1,0:T(8,128)(2,1)}, u32[]{:S(2)}) copy-start(bf16[2,512,512]{2,1,0:T(8,128)(2,1)} %w_proj.1) | copy-start | bytes 3145732
  37.0 1.5 %collective-permute-start.10 = (bf16[256,512]{1,0:T(8,128)(2,1)S(1)}, bf16[256,512]{1,0:T(8,128)(2,1)S(1)}, u32[]{:S(2)}, u32[]{:S(2)}) collective-permute-start(bf16[256,512]{1,0:T(8,128)(2,1)S(1)} %collective-permute-done.3.refs_0_), channel_id=1, source_target_pairs={{0,1},{1,0},{2,3},{3,2},{4,5},{5,4},{6,7},{7,6},{8,9},{9,8},{10,11... | collective-permute-start | bytes 786440 | tf_op jit(solution)/shard_map/ppermute | solution.py:461
  37.0 1.9 %collective-permute-start.11 = (bf16[256,512]{1,0:T(8,128)(2,1)S(1)}, bf16[256,512]{1,0:T(8,128)(2,1)S(1)}, u32[]{:S(2)}, u32[]{:S(2)}) collective-permute-start(bf16[256,512]{1,0:T(8,128)(2,1)S(1)} %collective-permute-done.5.refs_1_), channel_id=1, source_target_pairs={{0,1},{1,0},{2,3},{3,2},{4,5},{5,4},{6,7},{7,6},{8,9},{9,8},{10,11... | collective-permute-start | bytes 786440 | tf_op jit(solution)/shard_map/ppermute | solution.py:461
  37.5 11.0 %collective-permute-start.8 = (bf16[256,512]{1,0:T(8,128)(2,1)S(1)}, bf16[256,512]{1,0:T(8,128)(2,1)S(1)}, u32[]{:S(2)}, u32[]{:S(2)}) collective-permute-start(bf16[256,512]{1,0:T(8,128)(2,1)S(1)} %collective-permute-done.3.refs_0_), channel_id=1, source_target_pairs={{0,2},{1,3},{2,4},{3,5},{4,6},{5,7},{6,0},{7,1},{8,10},{9,11},{10,... | collective-permute-start | bytes 786440 | tf_op jit(solution)/shard_map/ppermute | solution.py:447
  37.5 15.6 %collective-permute-start.9 = (bf16[256,512]{1,0:T(8,128)(2,1)S(1)}, bf16[256,512]{1,0:T(8,128)(2,1)S(1)}, u32[]{:S(2)}, u32[]{:S(2)}) collective-permute-start(bf16[256,512]{1,0:T(8,128)(2,1)S(1)} %collective-permute-done.5.refs_1_), channel_id=1, source_target_pairs={{0,2},{1,3},{2,4},{3,5},{4,6},{5,7},{6,0},{7,1},{8,10},{9,11},{10,... | collective-permute-start | bytes 786440 | tf_op jit(solution)/shard_map/ppermute | solution.py:447
  38.9 2.2 %copy-start.2 = (bf16[2,2048,512]{2,1,0:T(8,128)(2,1)S(1)}, bf16[2,2048,512]{2,1,0:T(8,128)(2,1)}, u32[]{:S(2)}) copy-start(bf16[2,2048,512]{2,1,0:T(8,128)(2,1)} %w_down.1) | copy-start | bytes 12582916
  53.2 1.7 %collective-permute-start.12 = (bf16[256,512]{1,0:T(8,128)(2,1)S(1)}, bf16[256,512]{1,0:T(8,128)(2,1)S(1)}, u32[]{:S(2)}, u32[]{:S(2)}) collective-permute-start(bf16[256,512]{1,0:T(8,128)(2,1)S(1)} %collective-permute-done.8.refs_0_), channel_id=1, source_target_pairs={{0,1},{1,0},{2,3},{3,2},{4,5},{5,4},{6,7},{7,6},{8,9},{9,8},{10,11... | collective-permute-start | bytes 786440 | tf_op jit(solution)/shard_map/ppermute | solution.py:461
  53.2 1.9 %collective-permute-start.13 = (bf16[256,512]{1,0:T(8,128)(2,1)S(1)}, bf16[256,512]{1,0:T(8,128)(2,1)S(1)}, u32[]{:S(2)}, u32[]{:S(2)}) collective-permute-start(bf16[256,512]{1,0:T(8,128)(2,1)S(1)} %collective-permute-done.9.refs_1_), channel_id=1, source_target_pairs={{0,1},{1,0},{2,3},{3,2},{4,5},{5,4},{6,7},{7,6},{8,9},{9,8},{10,11... | collective-permute-start | bytes 786440 | tf_op jit(solution)/shard_map/ppermute | solution.py:461
  54.8 1.4 %copy-start.4 = (bf16[512,512]{1,0:T(8,128)(2,1)S(1)}, bf16[512,512]{1,0:T(8,128)(2,1)}, u32[]{:S(2)}) copy-start(bf16[512,512]{1,0:T(8,128)(2,1)} %points.3) | copy-start | bytes 1572868
  54.8 1.4 %copy-start.5 = (f32[4,512]{1,0:T(4,128)S(1)}, f32[4,512]{1,0:T(4,128)}, u32[]{:S(2)}) copy-start(f32[4,512]{1,0:T(4,128)} %gains.5) | copy-start | bytes 24580
  64.4 31.9 %copy-start.6 = (bf16[3,512]{1,0:T(4,128)(2,1)S(1)}, bf16[3,512]{1,0:T(4,128)(2,1)}, u32[]{:S(2)}) copy-start(bf16[3,512]{1,0:T(4,128)(2,1)} %w_head.1) | copy-start | bytes 9220

commit v6 on v5

--- a/solution.py
+++ b/solution.py
@@ -19,6 +19,7 @@
 SECOND_BYTES = 50 * 1024 * 1024
 PROJECT_BYTES = 16 * 1024 * 1024
 NORMALIZE_BYTES = 60 * 1024 * 1024
+PREPARE_BYTES = 46 * 1024 * 1024
 RING_BYTES = 16 * 1024 * 1024
 F32 = jnp.float32
 BF16 = jnp.bfloat16
@@ -117,44 +118,67 @@
         part[...] = layer_norm(held[i], gains_held[0:1, :])
 
 
-def project_kernel(first_rows, own, keep, *refs):
-    refs = list(refs)
-
-    def take(count):
-        taken = refs[:count]
-        del refs[:count]
-        return taken
-
+def prepare_kernel(capacity, destination, *refs):
+    count = (len(refs) - 4) // 2
+    weights, (slots, tail), kept = refs[:count], refs[count : count + 2], refs[count + 2 : -2]
+    held, sems = refs[-2:]
+    fetch, *copies = started(
+        [(destination, held)] + [(w.at[0], place) for w, place in zip(weights, kept)], sems
+    )
+    fetch.wait()
+    rows = held.shape[1]
+    devices = tail.shape[0]
+    shift = rows.bit_length() - 1
+    target = lax.shift_right_logical(held[...], shift)
+    place = held[...] & (rows - 1)
+    mine = lax.broadcasted_iota(jnp.int32, (devices, rows), 0) == target
+    mine = jnp.where(mine, 1.0, 0.0).astype(F32)
+    before = lax.broadcasted_iota(jnp.int32, (rows, rows), 0)
+    before = before < lax.broadcasted_iota(jnp.int32, (rows, rows), 1)
+    earlier = jnp.dot(
+        mine.astype(BF16),
+        jnp.where(before, 1.0, 0.0).astype(BF16),
+        preferred_element_type=F32,
+    )
+    rank = jnp.sum(mine * earlier, axis=0, keepdims=True).astype(jnp.int32)
+    slots[...] = target * capacity + rank
+
+    index = lax.axis_index("grp") * lax.axis_size("seq") + lax.axis_index("seq")
+    lane = rank + lax.rem(index, LANES // capacity) * capacity
+    by_lane = lax.broadcasted_iota(jnp.int32, (LANES, rows), 0) == lane
+    by_lane = jnp.where(by_lane, 1.0, 0.0).astype(BF16)
+    line = lax.broadcasted_iota(jnp.int32, (devices * TAIL, rows), 0)
+    code = place + 1
+    low = (code & (DIGIT - 1)).astype(F32)
+    high = lax.shift_right_logical(code, DIGIT.bit_length() - 1).astype(F32)
+    digit = line & (TAIL - 1)
+    digits = jnp.where(digit == 0, low, jnp.where(digit == 1, high, 0.0))
+    digits = jnp.where(lax.shift_right_logical(line, TAIL.bit_length() - 1) == target, digits, 0.0)
+    lines = lax.dot_general(
+        digits.astype(BF16), by_lane, (((1,), (1,)), ((), ())), preferred_element_type=F32
+    )
+    tail[...] = lines.reshape(devices, TAIL, LANES).astype(BF16)
+    for copy in copies:
+        copy.wait()
+
+
+def project_kernel(first_rows, own, *refs):
     count = len(first_rows)
-    parts = take(count)
-    (w_qkv,) = take(1)
-    others = take(3 * keep)
-    take(not own)
-    (whole,) = take(1)
-    queries = take(own)
-    kept = take(3 * keep)
-    held, held_w, sems, kept_sems = refs
-    channels = w_qkv.shape[1]
+    parts, w_qkv = refs[:count], refs[count]
+    refs = refs[count + 1 if own else count + 2 :]
+    whole, (held, sems) = refs[0], refs[-2:]
+    channels = w_qkv.shape[0]
     rows = held.shape[1]
-    first_column = 0 if own else channels
-    fetch, *copies = started(
-        [(w_qkv.at[0, :, pl.ds(first_column, held_w.shape[1])], held_w)]
-        + [(part, held.at[i]) for i, part in enumerate(parts)],
-        sems,
-    )
-    keeping = started([(w.at[0], place) for w, place in zip(others, kept)], kept_sems)
-    fetch.wait()
+    copies = started([(part, held.at[i]) for i, part in enumerate(parts)], sems)
     for i, first in enumerate(first_rows):
         copies[i].wait()
         whole[first : first + rows, :] = jnp.dot(
-            held[i], held_w[:, channels - first_column :], preferred_element_type=F32
+            held[i], w_qkv[:, channels:], preferred_element_type=F32
         ).astype(BF16)
-        if own and i * rows < queries[0].shape[0]:
+        if own and i * rows < refs[1].shape[0]:
             scale = BF16((channels // HEADS) ** (-0.5))
-            query = jnp.dot(held[i], held_w[:, :channels], preferred_element_type=F32).astype(BF16)
-            queries[0][i * rows : (i + 1) * rows, :] = (query * scale).astype(BF16)
-    for copy in keeping:
-        copy.wait()
+            query = jnp.dot(held[i], w_qkv[:, :channels], preferred_element_type=F32).astype(BF16)
+            refs[1][i * rows : (i + 1) * rows, :] = (query * scale).astype(BF16)
 
 
 def lane_tiles(packed, rows):
@@ -169,6 +193,7 @@
 
 
 def first_kernel(
+    ring_chips,
     pattern,
     slot_of_row,
     gains,
@@ -183,21 +208,20 @@
     attended,
     points_held,
     gains_held,
-    slots_held,
     outgoing_held,
     sems,
 ):
     rows, channels = points.shape
+    me = lax.axis_index("seq")
     devices, capacity, _ = outgoing_held.shape
     packed = outgoing.shape[2] == LANES
     row_tiles = channels // LANES * capacity
     patches = rows // PATCH
-    chosen = pattern.shape[0] // patches
+    chosen = pattern.shape[0]
     copies = started(
         [
             (points, points_held),
             (gains, gains_held),
-            (slot_of_row, slots_held),
         ]
         + ([(tail, outgoing.at[:, pl.ds(row_tiles, TAIL), :])] if packed else []),
         sems.at[0],
@@ -206,7 +230,15 @@
     for p in range(patches):
         pieces = [keyed[p * PATCH : (p + 1) * PATCH, :]]
         for j in range(chosen):
-            start = pl.multiple_of(pattern[p * chosen + j] * PATCH, PATCH)
+            patch = pattern[j, p]
+            if ring_chips:
+                owner, local = lax.div(patch, patches), lax.rem(patch, patches)
+                chip = lax.rem(lax.div(me, 2) - lax.div(owner, 2) + ring_chips, ring_chips)
+                slot = 2 * chip + jnp.where(lax.rem(me, 2) == lax.rem(owner, 2), 0, 1)
+                patch = slot * patches + local
+            else:
+                patch = patches + p * chosen + j
+            start = pl.multiple_of(patch * PATCH, PATCH)
             pieces.append(keyed[pl.ds(start, PATCH), :])
         both = jnp.concatenate(pieces, axis=0)
         attended[p * PATCH : (p + 1) * PATCH, :] = attend_patch(
@@ -220,7 +252,7 @@
     first = finish(
         points_held[...], attended[...], gains_held[1:2, :], (w_proj, w_up, w_down)
     )
-    slots = slots_held[...]
+    slots = slot_of_row[...]
     targets = devices // SEND_PARTS
     piece = targets * capacity
     leaving = []
@@ -270,7 +302,7 @@
         arriving = lane_tiles(incoming, incoming_held)
         tail = incoming.at[:, pl.ds(channels // LANES * capacity, TAIL), :]
     patches = rows // PATCH
-    chosen = pattern.shape[0] // patches
+    chosen = pattern.shape[0]
     small = started(
         [(tail, tail_held), (gains, gains_held), (w_head, head_held)], sems.at[0]
     )
@@ -313,7 +345,7 @@
     for p in range(patches):
         pieces = [kv[p * PATCH : (p + 1) * PATCH, :]]
         for j in range(chosen):
-            start = pl.multiple_of(pattern[p * chosen + j] * PATCH, PATCH)
+            start = pl.multiple_of(pattern[j, p] * PATCH, PATCH)
             pieces.append(kv[pl.ds(start, PATCH), :])
         both = jnp.concatenate(pieces, axis=0)
         attended[p * PATCH : (p + 1) * PATCH, :] = attend_patch(
@@ -376,8 +408,26 @@
 
     weights = (w_proj, w_up, w_down)
     kv_shape = jax.ShapeDtypeStruct((kept_rows, 2 * channels), BF16)
-
-    def project(keyed, blocks, keep=False):
+    own_shape = jax.ShapeDtypeStruct((rows_here, channels), BF16)
+
+    slot_index, tail, qkv_kept, *kept = pl.pallas_call(
+        functools.partial(prepare_kernel, capacity),
+        out_shape=[
+            jax.ShapeDtypeStruct((1, rows_here), jnp.int32),
+            jax.ShapeDtypeStruct((devices, TAIL, LANES), BF16),
+            *[jax.ShapeDtypeStruct(w.shape[1:], BF16) for w in (w_qkv,) + weights],
+        ],
+        in_specs=[ANY_SPEC] * 5,
+        out_specs=[VMEM_SPEC] * 6,
+        scratch_shapes=[
+            pltpu.VMEM((1, rows_here), jnp.int32),
+            pltpu.SemaphoreType.DMA((5,)),
+        ],
+        compiler_params=pltpu.CompilerParams(vmem_limit_bytes=PREPARE_BYTES),
+        name="prepare",
+    )(destination.reshape(1, rows_here), w_qkv, *weights)
+
+    def project(keyed, blocks):
         parts = [rows for _, block in blocks for rows in block]
         count = len(parts)
         rows = parts[0].shape[0]
@@ -385,21 +435,16 @@
             slot * rows_here + i * rows for slot, block in blocks for i in range(len(block))
         ]
         own = keyed is None
-        shapes = [kv_shape]
-        shapes += [jax.ShapeDtypeStruct((rows_here, channels), BF16)] * own
-        shapes += [jax.ShapeDtypeStruct(w.shape[1:], BF16) for w in weights] * keep
         return pl.pallas_call(
-            functools.partial(project_kernel, first_rows, own, keep),
-            out_shape=shapes,
-            in_specs=[ANY_SPEC] * (count + 1 + 3 * keep) + [VMEM_SPEC] * (not own),
-            out_specs=[VMEM_SPEC] * len(shapes),
+            functools.partial(project_kernel, first_rows, own),
+            out_shape=[kv_shape, own_shape] if own else kv_shape,
+            in_specs=[ANY_SPEC] * count + [VMEM_SPEC] * (1 if own else 2),
+            out_specs=[VMEM_SPEC] * 2 if own else VMEM_SPEC,
             scratch_shapes=[
                 pltpu.VMEM((count, rows, channels), BF16),
-                pltpu.VMEM((channels, (3 if own else 2) * channels), BF16),
-                pltpu.SemaphoreType.DMA((count + 1,)),
-                pltpu.SemaphoreType.DMA((3,)),
+                pltpu.SemaphoreType.DMA((count,)),
             ],
-            input_output_aliases={} if own else {count + 1 + 3 * keep: 0},
+            input_output_aliases={} if own else {count + 1: 0},
             cost_estimate=pl.CostEstimate(
                 flops=4 * count * rows * channels**2,
                 bytes_accessed=3 * count * rows * channels * 2 + 3 * channels**2 * 2,
@@ -407,66 +452,31 @@
             ),
             compiler_params=pltpu.CompilerParams(vmem_limit_bytes=PROJECT_BYTES),
             name="project_own" if own else "project",
-        )(*parts, w_qkv, *(weights * keep), *([] if own else [keyed]))
-
-    target = destination // rows_here
-    place_at = destination % rows_here
-    onehot_dev = (target[:, None] == jnp.arange(devices, dtype=jnp.int32)[None, :]).astype(
-        jnp.int32
-    )
-    earlier = jnp.cumsum(onehot_dev, axis=0) - onehot_dev
-    send_rank = jnp.sum(earlier * onehot_dev, axis=1)
-    slot_index = target * capacity + send_rank
-    slot_ids = jnp.arange(slot_total, dtype=jnp.int32)
-    match_send = slot_index[None, :] == slot_ids[:, None]
-    codes = jnp.sum(jnp.where(match_send, place_at[None, :] + 1, 0), axis=1)
-    index = lax.axis_index("grp") * lax.axis_size("seq") + lax.axis_index("seq")
-    per_row = LANES // capacity
-    lane = jnp.arange(LANES, dtype=jnp.int32)
-    codes = jnp.where(
-        lane // capacity == index % per_row, jnp.tile(codes.reshape(devices, capacity), per_row), 0
-    )
-    digits = jnp.stack([codes % DIGIT, codes // DIGIT], axis=1).astype(BF16)
-    tail = jnp.concatenate([digits, jnp.zeros((devices, TAIL - 2, LANES), BF16)], axis=1)
-    slot_index = slot_index.reshape(1, rows_here)
+        )(*parts, qkv_kept, *([] if own else [keyed]))
+
     packed = capacity % 16 == 0
-
-    pattern_second = pattern_second.reshape(-1)
-    me = lax.axis_index("seq")
-    if ring:
-        owner = pattern_first // patches
-        slot_of = 2 * ((me // 2 - owner // 2) % chips) + (me % 2 != owner % 2).astype(jnp.int32)
-        pattern_slots = (slot_of * patches + pattern_first % patches).reshape(-1)
-    else:
-        pattern_slots = patches + jnp.arange(patches * chosen, dtype=jnp.int32)
-
     if ring:
         beside = [lax.ppermute(rows, "seq", swap) for rows in column]
         waiting = [(0, column), (1, beside)]
         for step in range(1, chips):
             column = [lax.ppermute(rows, "seq", onward) for rows in column]
             if step == 1:
-                own = [rows for _, block in waiting for rows in block]
-                own, tail, slot_index, pattern_slots, pattern_second = lax.optimization_barrier(
-                    (own, tail, slot_index, pattern_slots, pattern_second)
-                )
-                waiting = [(0, own[:RING_PARTS]), (1, own[RING_PARTS:])]
+                column[0], slot_index = lax.optimization_barrier((column[0], slot_index))
+                keyed, queries = project(None, waiting)
+                column[1], keyed = lax.optimization_barrier((column[1], keyed))
             else:
-                if step == 2:
-                    keyed, queries = project(None, waiting)
-                else:
-                    keyed, *kept = project(keyed, waiting, keep=step == 3)
-                column, keyed = lax.optimization_barrier((column, keyed))
-                waiting = []
+                for i, block in enumerate(waiting):
+                    keyed = project(keyed, [block])
+                    column[i], keyed = lax.optimization_barrier((column[i], keyed))
             beside = [lax.ppermute(rows, "seq", swap) for rows in column]
-            waiting = waiting + [(2 * step, column), (2 * step + 1, beside)]
+            waiting = [(2 * step, column), (2 * step + 1, beside)]
         for block in waiting:
-            (keyed,) = project(keyed, [block])
+            keyed = project(keyed, [block])
     else:
         group = lax.all_gather(jnp.concatenate(column), "seq", axis=0, tiled=True)
         picked = group.reshape(-1, PATCH, channels)[pattern_first].reshape(-1, channels)
         keyed, queries = project(None, [(0, column)])
-        keyed, *kept = project(keyed, [(1, [picked])], keep=True)
+        keyed = project(keyed, [(1, [picked])])
 
     held_weights = [pltpu.VMEM(w.shape[1:], BF16) for w in weights]
     held_rows = pltpu.VMEM((rows_here, channels), BF16)
@@ -475,9 +485,9 @@
         pair_shape = (channels // LANES * capacity + TAIL, LANES)
     held_slots = pltpu.VMEM((devices, capacity, channels), BF16)
     outgoing = pl.pallas_call(
-        first_kernel,
+        functools.partial(first_kernel, chips if ring else 0),
         out_shape=jax.ShapeDtypeStruct((devices,) + pair_shape, BF16),
-        in_specs=[SMEM_SPEC, ANY_SPEC, ANY_SPEC, VMEM_SPEC, VMEM_SPEC, ANY_SPEC]
+        in_specs=[SMEM_SPEC, VMEM_SPEC, ANY_SPEC, VMEM_SPEC, VMEM_SPEC, ANY_SPEC]
         + [VMEM_SPEC] * 3
         + [ANY_SPEC],
         out_specs=ANY_SPEC,
@@ -485,13 +495,12 @@
             held_rows,
             held_rows,
             pltpu.VMEM(norm_gains.shape, F32),
-            pltpu.VMEM(slot_index.shape, jnp.int32),
             held_slots,
             pltpu.SemaphoreType.DMA((1 + SEND_PARTS, 4)),
         ],
         compiler_params=pltpu.CompilerParams(vmem_limit_bytes=FIRST_BYTES),
         name="block_first",
-    )(pattern_slots, slot_index, norm_gains, keyed, queries, points, *kept, tail)
+    )(pattern_first.T, slot_index, norm_gains, keyed, queries, points, *kept, tail)
 
     def exchange(array):
         return lax.all_to_all(array, ("grp", "seq"), split_axis=0, concat_axis=0, tiled=True)
@@ -520,7 +529,7 @@
         ],
         compiler_params=pltpu.CompilerParams(vmem_limit_bytes=SECOND_BYTES),
         name="block_second",
-    )(pattern_second, norm_gains, tail, incoming, w_qkv, *weights, w_head)
+    )(pattern_second.T, norm_gains, tail, incoming, w_qkv, *weights, w_head)
 
 
 def solution(mesh):

time: 106 us -> 96.7 us (0.912)
  local copies, waits for them, and re-layouts: 7.43 us -> 1.95 us
  waiting for transfers between devices: 26.5 us -> 22.8 us
  other arithmetic: 3.23 us -> 0 us
  Pallas kernels: 28.7 us -> 30.5 us
    unnamed x19 -> x20, local copies, waits for them, and re-layouts: 6.76 us -> 1.95 us
    ppermute x6, waiting for transfers between devices: 24.9 us -> 22.4 us  [shards(): column = [lax.ppermute(rows, 'seq', onward) for rows in column]]
    pallas_call x5 -> x9, Pallas kernels: 16.9 us -> 18.7 us  [the longest x1 8.12 us: shards(): pl.pallas_call(functools.partial(first_kernel, chips if ring else 0), out...]
    another operation x5 -> x0, other arithmetic: 1.4 us -> none
    ppermute x8, waiting for transfers between devices: 1.65 us -> 0.44 us  [shards(): beside = [lax.ppermute(rows, 'seq', swap) for rows in column]]
  transfers between devices with their start and end apart: 14 -> 14, of which waited for: 9 -> 7; matrix products, arithmetic and copies ran while one was open for 4% -> 0% of each run, Pallas kernels for 7% -> 10%
where the time goes in v6:
time: 96.7 us; the launch traced here: 96.4 us
  blocking collectives  32.7 us (34%)
  Pallas kernels  30.5 us (32%)
  waiting for transfers between devices  22.8 us (24%)
  starting transfers between devices  7.52 us (8%)
  local copies, waits for them, and re-layouts  1.95 us (2%)
  between operations  0.99 us (1%)
    all_to_all x1, blocking collectives, exchange(): lax.all_to_all(array, ('grp', 'seq'), split_axis=0, concat_axis=0, tiled=...  32.7 us
    ppermute x6, waiting for transfers between devices, shards(): column = [lax.ppermute(rows, 'seq', onward) for rows in column]  22.4 us
    pallas_call x1, Pallas kernels, shards(): pl.pallas_call(second_kernel, out_shape=(jax.ShapeDtypeStruct((rows_here,...  9.65 us
    pallas_call x1, Pallas kernels, shards(): pl.pallas_call(functools.partial(first_kernel, chips if ring else 0), out...  8.12 us
    pallas_call x7, Pallas kernels, project(): pl.pallas_call(functools.partial(project_kernel, first_rows, own), out_sh...  7.76 us
    ppermute x6, starting transfers between devices, shards(): column = [lax.ppermute(rows, 'seq', onward) for rows in column]  5.48 us
    pallas_call x1, Pallas kernels, shards(): pl.pallas_call(functools.partial(prepare_kernel, capacity), out_shape=[ja...  2.8 us
    pallas_call x1, Pallas kernels, shards(): pl.pallas_call(normalize_kernel, out_shape=[jax.ShapeDtypeStruct((part, c...  2.18 us
  transfers between devices with their start and end apart: 14, of which 7 were waited for; matrix products, arithmetic and copies ran while one was open for 0% of the time, Pallas kernels for 10%

profile of v6, /device:TPU:0, one launch (start us, length us, event | category | flops | bytes accessed | tf_op | source)
XLA Modules:
  0.0 96.4 jit_solution(11920009609914100752)
XLA Ops:
  0.6 2.2 %normalize.1 = (bf16[256,512]{1,0:T(8,128)(2,1)}, bf16[256,512]{1,0:T(8,128)(2,1)}) custom-call(bf16[512,512]{1,0:T(8,128)(2,1)} %points.3, f32[4,512]{1,0:T(4,128)} %gains.5), custom_call_target="tpu_custom_call" | custom-call | tf_op jit(solution)/shard_map/normalize/pallas_call | solution.py:395
  2.8 3.1 %collective-permute-start = (bf16[256,512]{1,0:T(8,128)(2,1)}, bf16[256,512]{1,0:T(8,128)(2,1)S(1)}, u32[]{:S(2)}, u32[]{:S(2)}) collective-permute-start(bf16[256,512]{1,0:T(8,128)(2,1)} %get-tuple-element.25.refs_0_), channel_id=1, source_target_pairs={{0,2},{1,3},{2,4},{3,5},{4,6},{5,7},{6,0},{7,1},{8,10},{9,11},{10,... | collective-permute-start | bytes 786440 | tf_op jit(solution)/shard_map/ppermute | solution.py:462
  5.9 0.0 collective-permute-start.3
  5.9 0.5 collective-permute-start.4
  6.4 1.6 %collective-permute-start.2 = (bf16[256,512]{1,0:T(8,128)(2,1)}, bf16[256,512]{1,0:T(8,128)(2,1)S(1)}, u32[]{:S(2)}, u32[]{:S(2)}) collective-permute-start(bf16[256,512]{1,0:T(8,128)(2,1)} %get-tuple-element.29.refs_1_), channel_id=1, source_target_pairs={{0,2},{1,3},{2,4},{3,5},{4,6},{5,7},{6,0},{7,1},{8,10},{9,11},{10,... | collective-permute-start | bytes 786440 | tf_op jit(solution)/shard_map/ppermute | solution.py:462
  8.0 1.2 %copy-done = bf16[2,512,512]{2,1,0:T(8,128)(2,1)S(1)} copy-done((bf16[2,512,512]{2,1,0:T(8,128)(2,1)S(1)}, bf16[2,512,512]{2,1,0:T(8,128)(2,1)}, u32[]{:S(2)}) %copy-start) | copy-done | bytes 1048600
  9.2 0.7 copy-done.6
  9.9 2.8 %prepare.1 = (s32[1,512]{1,0:T(1,128)S(1)}, bf16[32,8,128]{2,1,0:T(8,128)(2,1)S(1)}, bf16[512,1536]{1,0:T(8,128)(2,1)S(1)}, bf16[512,512]{1,0:T(8,128)(2,1)S(1)}...) custom-call(s32[1,512]{1,0:T(1,128)S(1)} %bitcast.4, bf16[2,512,1536]{2,1,0:T(8,128)(2,1)} %w_qkv.1, ...), custom_call_target="tpu_custom_call" | custom-call | tf_op jit(solution)/shard_map/prepare/pallas_call | solution.py:413
  12.7 2.6 %collective-permute-done.refs_0_ = bf16[256,512]{1,0:T(8,128)(2,1)S(1)} collective-permute-done((bf16[256,512]{1,0:T(8,128)(2,1)}, bf16[256,512]{1,0:T(8,128)(2,1)S(1)}, u32[]{:S(2)}, u32[]{:S(2)}) %collective-permute-start) | collective-permute-done | bytes 262176 | tf_op jit(solution)/shard_map/ppermute | solution.py:462
  15.3 0.0 collective-permute-start.1
  15.3 0.0 collective-permute-done.3.refs_2_
  15.3 0.0 collective-permute-done.4.refs_3_
  15.3 2.1 %project_own.1 = (bf16[4096,1024]{1,0:T(8,128)(2,1)S(1)}, bf16[512,512]{1,0:T(8,128)(2,1)S(1)}) custom-call(bf16[256,512]{1,0:T(8,128)(2,1)S(1)} %copy-done.9, bf16[256,512]{1,0:T(8,128)(2,1)S(1)} %copy-done.8, bf16[256,512]{1,0:T(8,128)(2,1)S(1)} %collective-permute-done.3.refs_2_, bf16[256,512]{1,0:T(8,128)(2,1)S(1)} %collective-permute-done.4.refs_3_, ...), custom_call_target="tpu_custom_call" | custom-call | flops 1073741824 | bytes 4718592 | tf_op jit(solution)/shard_map/project_own/pallas_call | solution.py:438
  17.5 3.4 %collective-permute-done.2.refs_1_ = bf16[256,512]{1,0:T(8,128)(2,1)S(1)} collective-permute-done((bf16[256,512]{1,0:T(8,128)(2,1)}, bf16[256,512]{1,0:T(8,128)(2,1)S(1)}, u32[]{:S(2)}, u32[]{:S(2)}) %collective-permute-start.2) | collective-permute-done | bytes 262176 | tf_op jit(solution)/shard_map/ppermute | solution.py:462
  20.9 0.0 collective-permute-start.8
  20.9 0.5 collective-permute-start.7
  21.4 0.0 collective-permute-start.6
  21.4 0.9 project.6.refs_3_
  22.4 3.3 %collective-permute-done.1.refs_0_ = bf16[256,512]{1,0:T(8,128)(2,1)S(1)} collective-permute-done((bf16[256,512]{1,0:T(8,128)(2,1)S(1)}, bf16[256,512]{1,0:T(8,128)(2,1)S(1)}, u32[]{:S(2)}, u32[]{:S(2)}) %collective-permute-start.1) | collective-permute-done | bytes 262176 | tf_op jit(solution)/shard_map/ppermute | solution.py:462
  25.7 0.8 collective-permute-start.5
  26.4 0.0 collective-permute-done.8.refs_1_
  26.4 0.0 collective-permute-done.7.refs_0_
  26.4 0.9 project.7.refs_3_
  27.4 5.0 %collective-permute-done.6.refs_1_ = bf16[256,512]{1,0:T(8,128)(2,1)S(1)} collective-permute-done((bf16[256,512]{1,0:T(8,128)(2,1)S(1)}, bf16[256,512]{1,0:T(8,128)(2,1)S(1)}, u32[]{:S(2)}, u32[]{:S(2)}) %collective-permute-start.6) | collective-permute-done | bytes 262176 | tf_op jit(solution)/shard_map/ppermute | solution.py:462
  32.4 0.0 collective-permute-start.12
  32.4 0.5 collective-permute-start.11
  32.9 0.0 collective-permute-start.10
  32.9 0.9 project.8.refs_3_
  33.8 3.2 %collective-permute-done.5.refs_0_ = bf16[256,512]{1,0:T(8,128)(2,1)S(1)} collective-permute-done((bf16[256,512]{1,0:T(8,128)(2,1)S(1)}, bf16[256,512]{1,0:T(8,128)(2,1)S(1)}, u32[]{:S(2)}, u32[]{:S(2)}) %collective-permute-start.5) | collective-permute-done | bytes 262176 | tf_op jit(solution)/shard_map/ppermute | solution.py:462
  37.0 0.0 collective-permute-done.12.refs_1_
  37.0 0.0 collective-permute-done.11.refs_0_
  37.0 0.9 project.9.refs_3_
  38.0 4.9 %collective-permute-done.10.refs_1_ = bf16[256,512]{1,0:T(8,128)(2,1)S(1)} collective-permute-done((bf16[256,512]{1,0:T(8,128)(2,1)S(1)}, bf16[256,512]{1,0:T(8,128)(2,1)S(1)}, u32[]{:S(2)}, u32[]{:S(2)}) %collective-permute-start.10) | collective-permute-done | bytes 262176 | tf_op jit(solution)/shard_map/ppermute | solution.py:462
  42.9 0.0 collective-permute-start.13
  42.9 0.5 collective-permute-start.9
  43.4 0.9 project.10.refs_3_
  44.3 0.0 copy-start.2
  44.4 0.0 copy-start.3
  44.4 0.0 copy-start.7
  44.4 0.0 collective-permute-done.13.refs_1_
  44.4 0.4 collective-permute-done.9.refs_0_
  44.8 0.9 project.11.keyed
  45.8 0.0 copy-start.1
  45.8 0.0 copy-start.4
  45.8 0.0 copy-start.5
  45.8 8.1 %block_first.1 = bf16[32,136,128]{2,1,0:T(8,128)(2,1)S(1)} custom-call(s32[3,8]{1,0:T(4,128)S(1)} %bitcast.5, s32[1,512]{1,0:T(1,128)S(1)} %get-tuple-element.27.slot_of_row, f32[4,512]{1,0:T(4,128)S(1)} %copy-done.3, bf16[4096,1024]{1,0:T(8,128)(2,1)S(1)} %project.11.keyed, bf16[512,512]{1,0:T(8,128)(2,1)S(1)} %get-tuple-element.42.queries, ...), custom_call_target="tpu_custom_call" | custom-call | tf_op jit(solution)/shard_map/block_first/pallas_call | solution.py:487
  53.9 32.7 %all_to_all.5.incoming = bf16[32,136,128]{2,1,0:T(8,128)(2,1)S(1)} all-to-all(bf16[32,136,128]{2,1,0:T(8,128)(2,1)S(1)} %block_first.1), channel_id=1, replica_groups=mesh['grp'=4,'seq'=8] {'grp','seq'}, dimensions={0} | all-to-all | bytes 2228224 | tf_op jit(solution)/shard_map/all_to_all | solution.py:506
  86.6 9.7 %block_second.1 = (bf16[512,512]{1,0:T(8,128)(2,1)}, f32[3,512]{1,0:T(4,128)}) custom-call(s32[3,8]{1,0:T(4,128)S(1)} %bitcast.3, f32[4,512]{1,0:T(4,128)S(1)} %copy-done.3, bf16[32,8,128]{2,1,0:T(8,128)(2,1)S(1)} %get-tuple-element.24.tail, bf16[32,136,128]{2,1,0:T(8,128)(2,1)S(1)} %all_to_all.5.incoming, bf16[2,512,1536]{2,1,0:T(8,128)(2,1)} %w_qkv.1, ...), custom_call_target="tpu_custom_call" | custom-call | tf_op jit(solution)/shard_map/block_second/pallas_call | solution.py:511
  (12 shorter events, 0.0 us)
Async XLA Ops:
  2.8 12.4 %collective-permute-start = (bf16[256,512]{1,0:T(8,128)(2,1)}, bf16[256,512]{1,0:T(8,128)(2,1)S(1)}, u32[]{:S(2)}, u32[]{:S(2)}) collective-permute-start(bf16[256,512]{1,0:T(8,128)(2,1)} %get-tuple-element.25.refs_0_), channel_id=1, source_target_pairs={{0,2},{1,3},{2,4},{3,5},{4,6},{5,7},{6,0},{7,1},{8,10},{9,11},{10,... | collective-permute-start | bytes 786440 | tf_op jit(solution)/shard_map/ppermute | solution.py:462
  5.9 9.4 %collective-permute-start.3 = (bf16[256,512]{1,0:T(8,128)(2,1)}, bf16[256,512]{1,0:T(8,128)(2,1)S(1)}, u32[]{:S(2)}, u32[]{:S(2)}) collective-permute-start(bf16[256,512]{1,0:T(8,128)(2,1)} %get-tuple-element.25.refs_0_), channel_id=1, source_target_pairs={{0,1},{1,0},{2,3},{3,2},{4,5},{5,4},{6,7},{7,6},{8,9},{9,8},{10,11... | collective-permute-start | bytes 786440 | tf_op jit(solution)/shard_map/ppermute | solution.py:459
  5.9 9.4 %collective-permute-start.4 = (bf16[256,512]{1,0:T(8,128)(2,1)}, bf16[256,512]{1,0:T(8,128)(2,1)S(1)}, u32[]{:S(2)}, u32[]{:S(2)}) collective-permute-start(bf16[256,512]{1,0:T(8,128)(2,1)} %get-tuple-element.29.refs_1_), channel_id=1, source_target_pairs={{0,1},{1,0},{2,3},{3,2},{4,5},{5,4},{6,7},{7,6},{8,9},{9,8},{10,11... | collective-permute-start | bytes 786440 | tf_op jit(solution)/shard_map/ppermute | solution.py:459
  6.4 14.5 %collective-permute-start.2 = (bf16[256,512]{1,0:T(8,128)(2,1)}, bf16[256,512]{1,0:T(8,128)(2,1)S(1)}, u32[]{:S(2)}, u32[]{:S(2)}) collective-permute-start(bf16[256,512]{1,0:T(8,128)(2,1)} %get-tuple-element.29.refs_1_), channel_id=1, source_target_pairs={{0,2},{1,3},{2,4},{3,5},{4,6},{5,7},{6,0},{7,1},{8,10},{9,11},{10,... | collective-permute-start | bytes 786440 | tf_op jit(solution)/shard_map/ppermute | solution.py:462
  8.0 1.2 %copy-start = (bf16[2,512,512]{2,1,0:T(8,128)(2,1)S(1)}, bf16[2,512,512]{2,1,0:T(8,128)(2,1)}, u32[]{:S(2)}) copy-start(bf16[2,512,512]{2,1,0:T(8,128)(2,1)} %w_proj.1) | copy-start | bytes 3145732
  9.2 0.7 copy-start.6
  9.9 5.4 %copy-start.8 = (bf16[256,512]{1,0:T(8,128)(2,1)S(1)}, bf16[256,512]{1,0:T(8,128)(2,1)}, u32[]{:S(2)}) copy-start(bf16[256,512]{1,0:T(8,128)(2,1)} %get-tuple-element.29.refs_1_) | copy-start | bytes 786436
  9.9 5.4 %copy-start.9 = (bf16[256,512]{1,0:T(8,128)(2,1)S(1)}, bf16[256,512]{1,0:T(8,128)(2,1)}, u32[]{:S(2)}) copy-start(bf16[256,512]{1,0:T(8,128)(2,1)} %get-tuple-element.25.refs_0_) | copy-start | bytes 786436
  15.3 10.4 %collective-permute-start.1 = (bf16[256,512]{1,0:T(8,128)(2,1)S(1)}, bf16[256,512]{1,0:T(8,128)(2,1)S(1)}, u32[]{:S(2)}, u32[]{:S(2)}) collective-permute-start(bf16[256,512]{1,0:T(8,128)(2,1)S(1)} %collective-permute-done.refs_0_), channel_id=1, source_target_pairs={{0,2},{1,3},{2,4},{3,5},{4,6},{5,7},{6,0},{7,1},{8,10},{9,11},{10,... | collective-permute-start | bytes 786440 | tf_op jit(solution)/shard_map/ppermute | solution.py:462
  20.9 5.5 %collective-permute-start.8 = (bf16[256,512]{1,0:T(8,128)(2,1)S(1)}, bf16[256,512]{1,0:T(8,128)(2,1)S(1)}, u32[]{:S(2)}, u32[]{:S(2)}) collective-permute-start(bf16[256,512]{1,0:T(8,128)(2,1)S(1)} %collective-permute-done.2.refs_1_), channel_id=1, source_target_pairs={{0,1},{1,0},{2,3},{3,2},{4,5},{5,4},{6,7},{7,6},{8,9},{9,8},{10,11... | collective-permute-start | bytes 786440 | tf_op jit(solution)/shard_map/ppermute | solution.py:471
  20.9 5.5 %collective-permute-start.7 = (bf16[256,512]{1,0:T(8,128)(2,1)S(1)}, bf16[256,512]{1,0:T(8,128)(2,1)S(1)}, u32[]{:S(2)}, u32[]{:S(2)}) collective-permute-start(bf16[256,512]{1,0:T(8,128)(2,1)S(1)} %collective-permute-done.refs_0_), channel_id=1, source_target_pairs={{0,1},{1,0},{2,3},{3,2},{4,5},{5,4},{6,7},{7,6},{8,9},{9,8},{10,11... | collective-permute-start | bytes 786440 | tf_op jit(solution)/shard_map/ppermute | solution.py:471
  21.4 11.0 %collective-permute-start.6 = (bf16[256,512]{1,0:T(8,128)(2,1)S(1)}, bf16[256,512]{1,0:T(8,128)(2,1)S(1)}, u32[]{:S(2)}, u32[]{:S(2)}) collective-permute-start(bf16[256,512]{1,0:T(8,128)(2,1)S(1)} %collective-permute-done.2.refs_1_), channel_id=1, source_target_pairs={{0,2},{1,3},{2,4},{3,5},{4,6},{5,7},{6,0},{7,1},{8,10},{9,11},{10,... | collective-permute-start | bytes 786440 | tf_op jit(solution)/shard_map/ppermute | solution.py:462
  25.7 11.4 %collective-permute-start.5 = (bf16[256,512]{1,0:T(8,128)(2,1)S(1)}, bf16[256,512]{1,0:T(8,128)(2,1)S(1)}, u32[]{:S(2)}, u32[]{:S(2)}) collective-permute-start(bf16[256,512]{1,0:T(8,128)(2,1)S(1)} %collective-permute-done.1.refs_0_), channel_id=1, source_target_pairs={{0,2},{1,3},{2,4},{3,5},{4,6},{5,7},{6,0},{7,1},{8,10},{9,11},{10,... | collective-permute-start | bytes 786440 | tf_op jit(solution)/shard_map/ppermute | solution.py:462
  32.4 4.7 %collective-permute-start.12 = (bf16[256,512]{1,0:T(8,128)(2,1)S(1)}, bf16[256,512]{1,0:T(8,128)(2,1)S(1)}, u32[]{:S(2)}, u32[]{:S(2)}) collective-permute-start(bf16[256,512]{1,0:T(8,128)(2,1)S(1)} %collective-permute-done.6.refs_1_), channel_id=1, source_target_pairs={{0,1},{1,0},{2,3},{3,2},{4,5},{5,4},{6,7},{7,6},{8,9},{9,8},{10,11... | collective-permute-start | bytes 786440 | tf_op jit(solution)/shard_map/ppermute | solution.py:471
  32.4 4.7 %collective-permute-start.11 = (bf16[256,512]{1,0:T(8,128)(2,1)S(1)}, bf16[256,512]{1,0:T(8,128)(2,1)S(1)}, u32[]{:S(2)}, u32[]{:S(2)}) collective-permute-start(bf16[256,512]{1,0:T(8,128)(2,1)S(1)} %collective-permute-done.1.refs_0_), channel_id=1, source_target_pairs={{0,1},{1,0},{2,3},{3,2},{4,5},{5,4},{6,7},{7,6},{8,9},{9,8},{10,11... | collective-permute-start | bytes 786440 | tf_op jit(solution)/shard_map/ppermute | solution.py:471
  32.9 10.0 %collective-permute-start.10 = (bf16[256,512]{1,0:T(8,128)(2,1)S(1)}, bf16[256,512]{1,0:T(8,128)(2,1)S(1)}, u32[]{:S(2)}, u32[]{:S(2)}) collective-permute-start(bf16[256,512]{1,0:T(8,128)(2,1)S(1)} %collective-permute-done.6.refs_1_), channel_id=1, source_target_pairs={{0,2},{1,3},{2,4},{3,5},{4,6},{5,7},{6,0},{7,1},{8,10},{9,11},{10,... | collective-permute-start | bytes 786440 | tf_op jit(solution)/shard_map/ppermute | solution.py:462
  42.9 1.5 %collective-permute-start.13 = (bf16[256,512]{1,0:T(8,128)(2,1)S(1)}, bf16[256,512]{1,0:T(8,128)(2,1)S(1)}, u32[]{:S(2)}, u32[]{:S(2)}) collective-permute-start(bf16[256,512]{1,0:T(8,128)(2,1)S(1)} %collective-permute-done.10.refs_1_), channel_id=1, source_target_pairs={{0,1},{1,0},{2,3},{3,2},{4,5},{5,4},{6,7},{7,6},{8,9},{9,8},{10,11... | collective-permute-start | bytes 786440 | tf_op jit(solution)/shard_map/ppermute | solution.py:471
  42.9 1.9 %collective-permute-start.9 = (bf16[256,512]{1,0:T(8,128)(2,1)S(1)}, bf16[256,512]{1,0:T(8,128)(2,1)S(1)}, u32[]{:S(2)}, u32[]{:S(2)}) collective-permute-start(bf16[256,512]{1,0:T(8,128)(2,1)S(1)} %collective-permute-done.5.refs_0_), channel_id=1, source_target_pairs={{0,1},{1,0},{2,3},{3,2},{4,5},{5,4},{6,7},{7,6},{8,9},{9,8},{10,11... | collective-permute-start | bytes 786440 | tf_op jit(solution)/shard_map/ppermute | solution.py:471
  44.3 1.4 %copy-start.2 = (bf16[512,512]{1,0:T(8,128)(2,1)S(1)}, bf16[512,512]{1,0:T(8,128)(2,1)}, u32[]{:S(2)}) copy-start(bf16[512,512]{1,0:T(8,128)(2,1)} %points.3) | copy-start | bytes 1572868
  44.4 1.4 %copy-start.3 = (f32[4,512]{1,0:T(4,128)S(1)}, f32[4,512]{1,0:T(4,128)}, u32[]{:S(2)}) copy-start(f32[4,512]{1,0:T(4,128)} %gains.5) | copy-start | bytes 24580
  44.4 1.4 %copy-start.7 = (s32[8,3]{0,1:T(4,128)S(1)}, s32[8,3]{0,1:T(4,128)}, u32[]{:S(2)}) copy-start(s32[8,3]{0,1:T(4,128)} %param.11) | copy-start | bytes 292
  45.8 40.8 %copy-start.1 = (bf16[2,512,512]{2,1,0:T(8,128)(2,1)S(1)}, bf16[2,512,512]{2,1,0:T(8,128)(2,1)}, u32[]{:S(2)}) copy-start(bf16[2,512,512]{2,1,0:T(8,128)(2,1)} %w_proj.1) | copy-start | bytes 3145732
  45.8 40.8 %copy-start.4 = (bf16[3,512]{1,0:T(4,128)(2,1)S(1)}, bf16[3,512]{1,0:T(4,128)(2,1)}, u32[]{:S(2)}) copy-start(bf16[3,512]{1,0:T(4,128)(2,1)} %w_head.1) | copy-start | bytes 9220
  45.8 40.8 %copy-start.5 = (s32[8,3]{0,1:T(4,128)S(1)}, s32[8,3]{0,1:T(4,128)}, u32[]{:S(2)}) copy-start(s32[8,3]{0,1:T(4,128)} %param.12) | copy-start | bytes 292

commit v7 on v6

v7 whole, which is shorter than its diff:
```python
import functools

import jax
import jax.numpy as jnp
from jax import lax
from jax.experimental import pallas as pl
from jax.experimental.pallas import tpu as pltpu
from jax.sharding import Mesh, PartitionSpec as P

HEADS = 8
PATCH = 64
HEADS_TOGETHER = 4
GROUP = ("half", "seq")
RING_PARTS = 2
SEND_PARTS = 4
LANES = 128
TAIL = 8
DIGIT = 256
FIRST_BYTES = 28 * 1024 * 1024
SECOND_BYTES = 50 * 1024 * 1024
PROJECT_BYTES = 16 * 1024 * 1024
SPLIT_BYTES = 60 * 1024 * 1024
PREPARE_BYTES = 46 * 1024 * 1024
RING_BYTES = 16 * 1024 * 1024
F32 = jnp.float32
BF16 = jnp.bfloat16


def layer_norm(rows, gains):
    values = rows.astype(F32)
    average = jnp.mean(values, axis=-1, keepdims=True)
    spread = jnp.mean((values - average) ** 2, axis=-1, keepdims=True)
    return ((values - average) * lax.rsqrt(spread + 1e-05) * gains).astype(BF16)


def gelu(x):
    half = 0.5 * x
    return half + half * lax.erf(x * 0.5**0.5)


def head_masks(head_dim):
    lane = lax.broadcasted_iota(jnp.int32, (PATCH, HEADS_TOGETHER * head_dim), 1)
    return [
        jnp.where((lane >= h * head_dim) & (lane < (h + 1) * head_dim), 1.0, 0.0).astype(F32)
        for h in range(HEADS_TOGETHER)
    ]


def attend_patch(queries, key_rows, value_rows, masks):
    channels = queries.shape[1]
    width = HEADS_TOGETHER * (channels // HEADS)
    sides = []
    for at in range(0, channels, width):
        q = queries[:, at : at + width]
        stacked = jnp.concatenate([q * mask.astype(BF16) for mask in masks], axis=0)
        scores = lax.dot_general(
            stacked,
            key_rows[:, at : at + width],
            (((1,), (1,)), ((), ())),
            preferred_element_type=F32,
        )
        top = jnp.max(scores, axis=-1, keepdims=True)
        grown = jnp.exp(scores - top)
        total = jnp.sum(grown, axis=-1, keepdims=True)
        weights = (grown * (1.0 / total)).astype(BF16)
        mixed = jnp.dot(weights, value_rows[:, at : at + width], preferred_element_type=F32)
        side = mixed[:PATCH] * masks[0]
        for h in range(1, HEADS_TOGETHER):
            side = side + mixed[h * PATCH : (h + 1) * PATCH] * masks[h]
        sides.append(side.astype(BF16))
    return jnp.concatenate(sides, axis=1)


def one_hot_rows(places, rows):
    row = lax.broadcasted_iota(jnp.int32, (rows, places.shape[1]), 0)
    return jnp.where(row == places, 1.0, 0.0).astype(BF16)


def started(pairs, sems):
    copies = [
        pltpu.make_async_copy(source, place, sems.at[at])
        for at, (source, place) in enumerate(pairs)
    ]
    for copy in copies:
        copy.start()
    return copies


def finish(rows, attended, gain, held, copies=()):
    w_proj, w_up, w_down = held
    for copy in copies[:1]:
        copy.wait()
    first = (
        rows.astype(F32) + jnp.dot(attended, w_proj[...], preferred_element_type=F32)
    ).astype(BF16)
    hidden = layer_norm(first, gain)
    total = first.astype(F32)
    for copy in copies[1:]:
        copy.wait()
    piece = 512
    for at in range(0, w_up.shape[1], piece):
        upper = jnp.dot(hidden, w_up[:, at : at + piece], preferred_element_type=F32)
        act = gelu(upper).astype(BF16)
        total = total + jnp.dot(act, w_down[at : at + piece, :], preferred_element_type=F32)
    return total.astype(BF16)


def split_kernel(points, *refs):
    *parts, sems = refs
    rows = parts[0].shape[0]
    for copy in started(
        [(points.at[pl.ds(i * rows, rows), :], part) for i, part in enumerate(parts)], sems
    ):
        copy.wait()


def prepare_kernel(capacity, destination, beyond, *refs):
    count = (len(refs) - 4) // 2
    sources, (slots, tail), kept = refs[:count], refs[count : count + 2], refs[count + 2 : -2]
    held, sems = refs[-2:]
    fetches = started([(destination, held.at[0]), (beyond, held.at[1])], sems.at[0])
    copies = started(
        [
            (source.at[0] if len(source.shape) == 3 else source, place)
            for source, place in zip(sources, kept)
        ],
        sems.at[1],
    )
    for fetch in fetches:
        fetch.wait()
    rows = held.shape[2]
    devices = tail.shape[0]
    in_half = lax.axis_size("seq")
    seq_bits = in_half.bit_length() - 1
    index = lax.axis_index(("grp", "seq"))
    offset = lax.rem(index, LANES // (2 * capacity)) * 2 * capacity
    before = lax.broadcasted_iota(jnp.int32, (rows, rows), 0)
    before = before < lax.broadcasted_iota(jnp.int32, (rows, rows), 1)
    before = jnp.where(before, 1.0, 0.0).astype(BF16)
    lines = jnp.zeros((devices * TAIL, LANES), F32)
    for b in range(2):
        target = lax.shift_right_logical(held[b], rows.bit_length() - 1)
        place = held[b] & (rows - 1)
        half = lax.shift_right_logical(target, seq_bits) & 1
        group = lax.shift_right_logical(target, seq_bits + 1)
        target = group * in_half + (target & (in_half - 1))
        target = jnp.where(half == lax.axis_index("half"), target, -1)
        mine = lax.broadcasted_iota(jnp.int32, (devices, rows), 0) == target
        mine = jnp.where(mine, 1.0, 0.0).astype(F32)
        earlier = jnp.dot(mine.astype(BF16), before, preferred_element_type=F32)
        rank = jnp.sum(mine * earlier, axis=0, keepdims=True).astype(jnp.int32) + b * capacity
        slots[:, b * rows : (b + 1) * rows] = jnp.where(
            target >= 0, target * 2 * capacity + rank, -1
        )
        by_lane = lax.broadcasted_iota(jnp.int32, (LANES, rows), 0) == rank + offset
        by_lane = jnp.where(by_lane, 1.0, 0.0).astype(BF16)
        line = lax.broadcasted_iota(jnp.int32, (devices * TAIL, rows), 0)
        code = place + 1
        low = (code & (DIGIT - 1)).astype(F32)
        high = lax.shift_right_logical(code, DIGIT.bit_length() - 1).astype(F32)
        digit = line & (TAIL - 1)
        digits = jnp.where(digit == 0, low, jnp.where(digit == 1, high, 0.0))
        line = lax.shift_right_logical(line, TAIL.bit_length() - 1)
        digits = jnp.where(line == target, digits, 0.0)
        lines = lines + lax.dot_general(
            digits.astype(BF16), by_lane, (((1,), (1,)), ((), ())), preferred_element_type=F32
        )
    tail[...] = lines.reshape(devices, TAIL, LANES).astype(BF16)
    for copy in copies:
        copy.wait()


def project_kernel(first_rows, new, ask, *refs):
    count = len(first_rows)
    parts, gains, w_qkv = refs[:count], refs[count], refs[count + 1]
    refs = refs[count + 2 if new else count + 3 :]
    whole, (held, sems) = refs[0], refs[-2:]
    channels = w_qkv.shape[0]
    rows = held.shape[1]
    copies = started([(part, held.at[i]) for i, part in enumerate(parts)], sems)
    for i, first in enumerate(first_rows):
        copies[i].wait()
        normed = layer_norm(held[i], gains[0:1, :])
        whole[first : first + rows, :] = jnp.dot(
            normed, w_qkv[:, channels:], preferred_element_type=F32
        ).astype(BF16)
        if ask and i * rows < refs[1].shape[0]:
            scale = BF16((channels // HEADS) ** (-0.5))
            query = jnp.dot(normed, w_qkv[:, :channels], preferred_element_type=F32).astype(BF16)
            refs[1][i * rows : (i + 1) * rows, :] = (query * scale).astype(BF16)


def lane_tiles(packed, rows):
    capacity, channels = rows.shape[1:]
    return [
        (
            packed.at[:, pl.ds(j * capacity, capacity), :],
            rows.at[:, :, pl.ds(j * LANES, LANES)],
        )
        for j in range(channels // LANES)
    ]


def first_kernel(
    ring_chips,
    pattern,
    pattern_beyond,
    slot_of_row,
    gains,
    keyed,
    queries,
    queries_beyond,
    w_proj,
    w_up,
    w_down,
    tail,
    points,
    *refs,
):
    *points_beyond, outgoing, attended, points_held, first_held, outgoing_held, sems = refs
    rows, channels = points.shape
    devices, capacity, _ = outgoing_held.shape
    row_tiles = channels // LANES * capacity
    patches = rows // PATCH
    chosen = pattern.shape[0]
    me = lax.axis_index(GROUP)
    part = rows // len(points_beyond)
    copies = started(
        [(tail, outgoing.at[:, pl.ds(row_tiles, TAIL), :]), (points, points_held.at[:rows])]
        + [
            (piece, points_held.at[pl.ds(rows + i * part, part), :])
            for i, piece in enumerate(points_beyond)
        ],
        sems.at[0],
    )
    masks = head_masks(channels // HEADS)
    blocks = ((pattern, queries, 0), (pattern_beyond, queries_beyond, ring_chips or 1))
    for b, (picked, asking, own_slot) in enumerate(blocks):
        for p in range(patches):
            start = own_slot * rows + p * PATCH
            pieces = [keyed[start : start + PATCH, :]]
            for j in range(chosen):
                if ring_chips:
                    patch = picked[j, p]
                    owner, local = lax.div(patch, patches), lax.rem(patch, patches)
                    chip = lax.rem(lax.div(me, 2) - lax.div(owner, 2) + ring_chips, ring_chips)
                    slot = 2 * chip + jnp.where(lax.rem(me, 2) == lax.rem(owner, 2), 0, 1)
                    patch = slot * patches + local
                else:
                    patch = 2 * patches + (b * patches + p) * chosen + j
                start = patch * PATCH
                if ring_chips:
                    start = pl.multiple_of(start, PATCH)
                pieces.append(keyed[pl.ds(start, PATCH), :])
            both = jnp.concatenate(pieces, axis=0)
            attended[b * rows + p * PATCH : b * rows + (p + 1) * PATCH, :] = attend_patch(
                asking[p * PATCH : (p + 1) * PATCH, :], both[:, :channels], both[:, channels:], masks
            )
    for copy in copies[1:]:
        copy.wait()

    @pl.loop(0, 2)
    def _(b):
        here = pl.ds(pl.multiple_of(b * rows, rows), rows)
        first_held[here, :] = finish(
            points_held[here, :], attended[here, :], gains[1:2, :], (w_proj, w_up, w_down)
        )

    copies[0].wait()
    slots = slot_of_row[...]
    targets = devices // SEND_PARTS
    piece = targets * capacity
    leaving = []
    for i in range(SEND_PARTS):
        here = pl.ds(i * targets, targets)
        send = one_hot_rows(slots - i * piece, piece)
        moved = jnp.dot(send, first_held[...], preferred_element_type=F32).astype(BF16)
        outgoing_held[here] = moved.reshape(targets, capacity, channels)
        pairs = lane_tiles(outgoing.at[here], outgoing_held.at[here])
        leaving += started([(source, place) for place, source in pairs], sems.at[1 + i])
    for copy in leaving:
        copy.wait()


def second_kernel(
    pattern,
    gains,
    incoming,
    w_qkv,
    w_proj,
    w_up,
    w_down,
    w_head,
    features,
    normals,
    kv,
    attended,
    incoming_held,
    qkv_held,
    proj_held,
    up_held,
    down_held,
    gains_held,
    tail_held,
    head_held,
    sems,
):
    rows, channels = features.shape
    devices, capacity, _ = incoming_held.shape
    patches = rows // PATCH
    chosen = pattern.shape[0]
    tail = incoming.at[:, pl.ds(channels // LANES * capacity, TAIL), :]
    small = started(
        [(tail, tail_held), (gains, gains_held), (w_head, head_held)], sems.at[0]
    )
    landing = started(lane_tiles(incoming, incoming_held), sems.at[1])
    copies = started(
        [
            (w_qkv.at[1], qkv_held),
            (w_proj.at[1], proj_held),
            (w_up.at[1], up_held),
            (w_down.at[1], down_held),
        ],
        sems.at[2],
    )
    for copy in small:
        copy.wait()
    per_row = LANES // capacity
    digits = tail_held[...].astype(F32)
    codes = digits[:, 0:1, :] + DIGIT * digits[:, 1:2, :]
    pieces = []
    for at in range(0, devices, per_row):
        code = codes[at]
        for i in range(1, per_row):
            code = code + codes[at + i]
        pieces.append(code)
    places = jnp.concatenate(pieces, axis=1).astype(jnp.int32) - 1
    place = one_hot_rows(places, rows)
    for copy in landing:
        copy.wait()
    moved = incoming_held[...].reshape(devices * capacity, channels)
    second = jnp.dot(place, moved, preferred_element_type=F32).astype(BF16)
    normed = layer_norm(second, gains_held[2:3, :])
    scale = (channels // HEADS) ** (-0.5)
    copies[0].wait()
    queries = (
        jnp.dot(normed, qkv_held[:, :channels], preferred_element_type=F32).astype(BF16)
        * BF16(scale)
    ).astype(BF16)
    kv[...] = jnp.dot(normed, qkv_held[:, channels:], preferred_element_type=F32).astype(BF16)
    masks = head_masks(channels // HEADS)
    for p in range(patches):
        pieces = [kv[p * PATCH : (p + 1) * PATCH, :]]
        for j in range(chosen):
            start = pl.multiple_of(pattern[j, p] * PATCH, PATCH)
            pieces.append(kv[pl.ds(start, PATCH), :])
        both = jnp.concatenate(pieces, axis=0)
        attended[p * PATCH : (p + 1) * PATCH, :] = attend_patch(
            queries[p * PATCH : (p + 1) * PATCH, :], both[:, :channels], both[:, channels:], masks
        )
    done = finish(
        second, attended[...], gains_held[3:4, :], (proj_held, up_held, down_held), copies[1:]
    )
    features[...] = done
    normals[...] = lax.dot_general(
        head_held[...], done, (((1,), (1,)), ((), ())), preferred_element_type=F32
    )


VMEM_SPEC = pl.BlockSpec(memory_space=pltpu.VMEM)
SMEM_SPEC = pl.BlockSpec(memory_space=pltpu.SMEM)
ANY_SPEC = pl.BlockSpec(memory_space=pl.ANY)


def shards(
    points,
    pattern_first,
    pattern_second,
    destination,
    norm_gains,
    w_qkv,
    w_proj,
    w_up,
    w_down,
    w_head,
):
    rows_here, channels = points.shape
    patches, chosen = pattern_first.shape
    devices = lax.axis_size("grp") * lax.axis_size("seq")
    capacity = 2 * rows_here // (2 * devices)
    pair_slots = 2 * capacity

    shards_in_group = lax.axis_size(GROUP)
    chips = shards_in_group // 2
    onward = [(i, (i + 2) % shards_in_group) for i in range(shards_in_group)]
    swap = [(i, i ^ 1) for i in range(shards_in_group)]
    across = [(i, (i + chips) % shards_in_group) for i in range(shards_in_group)]
    ring = shards_in_group * rows_here * 2 * channels * 2 <= RING_BYTES
    kept_rows = shards_in_group * rows_here if ring else 2 * patches * (1 + chosen) * PATCH
    part = rows_here // RING_PARTS

    column = pl.pallas_call(
        split_kernel,
        out_shape=[jax.ShapeDtypeStruct((part, channels), BF16)] * RING_PARTS,
        in_specs=[ANY_SPEC],
        out_specs=[ANY_SPEC] * RING_PARTS,
        scratch_shapes=[pltpu.SemaphoreType.DMA((RING_PARTS,))],
        compiler_params=pltpu.CompilerParams(vmem_limit_bytes=SPLIT_BYTES),
        name="split",
    )(points)

    weights = (w_proj, w_up, w_down)
    kv_shape = jax.ShapeDtypeStruct((kept_rows, 2 * channels), BF16)
    own_shape = jax.ShapeDtypeStruct((rows_here, channels), BF16)

    destination = destination.reshape(1, rows_here)
    pattern_first = pattern_first.T
    pattern_beyond = lax.ppermute(pattern_first, GROUP, across)
    slot_index, tail, qkv_kept, *kept, gains_kept = pl.pallas_call(
        functools.partial(prepare_kernel, capacity),
        out_shape=[
            jax.ShapeDtypeStruct((1, 2 * rows_here), jnp.int32),
            jax.ShapeDtypeStruct((devices, TAIL, LANES), BF16),
            *[jax.ShapeDtypeStruct(w.shape[1:], BF16) for w in (w_qkv,) + weights],
            jax.ShapeDtypeStruct(norm_gains.shape, F32),
        ],
        in_specs=[ANY_SPEC] * 7,
        out_specs=[VMEM_SPEC] * 7,
        scratch_shapes=[
            pltpu.VMEM((2, 1, rows_here), jnp.int32),
            pltpu.SemaphoreType.DMA((2, 5)),
        ],
        compiler_params=pltpu.CompilerParams(vmem_limit_bytes=PREPARE_BYTES),
        name="prepare",
    )(destination, lax.ppermute(destination, GROUP, across), w_qkv, *weights, norm_gains)

    def project(keyed, blocks, ask=False):
        parts = [rows for _, block in blocks for rows in block]
        count = len(parts)
        rows = parts[0].shape[0]
        first_rows = [
            slot * rows_here + i * rows for slot, block in blocks for i in range(len(block))
        ]
        new = keyed is None
        return pl.pallas_call(
            functools.partial(project_kernel, first_rows, new, ask),
            out_shape=[kv_shape] + [own_shape] * ask,
            in_specs=[ANY_SPEC] * count + [VMEM_SPEC] * (2 if new else 3),
            out_specs=[VMEM_SPEC] * (1 + ask),
            scratch_shapes=[
                pltpu.VMEM((count, rows, channels), BF16),
                pltpu.SemaphoreType.DMA((count,)),
            ],
            input_output_aliases={} if new else {count + 2: 0},
            cost_estimate=pl.CostEstimate(
                flops=4 * count * rows * channels**2,
                bytes_accessed=3 * count * rows * channels * 2 + 3 * channels**2 * 2,
                transcendentals=0,
            ),
            compiler_params=pltpu.CompilerParams(vmem_limit_bytes=PROJECT_BYTES),
            name="project_own" if new else "project",
        )(*parts, gains_kept, qkv_kept, *([] if new else [keyed]))

    if ring:
        beside = [lax.ppermute(rows, GROUP, swap) for rows in column]
        waiting = [(0, column), (1, beside)]
        for step in range(1, chips):
            column = [lax.ppermute(rows, GROUP, onward) for rows in column]
            if step == 1:
                column[0], slot_index = lax.optimization_barrier((column[0], slot_index))
                keyed, queries = project(None, waiting, ask=True)
                column[1], keyed = lax.optimization_barrier((column[1], keyed))
            else:
                for i, block in enumerate(waiting):
                    if block[0] == chips:
                        keyed, queries_beyond = project(keyed, [block], ask=True)
                    else:
                        (keyed,) = project(keyed, [block])
                    column[i], keyed = lax.optimization_barrier((column[i], keyed))
            if step == chips // 2:
                points_beyond = column
            beside = [lax.ppermute(rows, GROUP, swap) for rows in column]
            waiting = [(2 * step, column), (2 * step + 1, beside)]
        for block in waiting:
            (keyed,) = project(keyed, [block])
    else:
        group = lax.all_gather(points, GROUP, axis=0, tiled=True)
        partner = lax.rem(lax.axis_index(GROUP) + chips, shards_in_group)
        points_beyond = [lax.dynamic_slice_in_dim(group, partner * rows_here, rows_here)]
        group = group.reshape(-1, PATCH, channels)
        picked = [
            group[pattern.T].reshape(-1, channels) for pattern in (pattern_first, pattern_beyond)
        ]
        keyed, queries = project(None, [(0, column)], ask=True)
        keyed, queries_beyond = project(keyed, [(1, points_beyond)], ask=True)
        (keyed,) = project(keyed, [(2, [picked[0]])])
        (keyed,) = project(keyed, [(2 + chosen, [picked[1]])])

    held_weights = [pltpu.VMEM(w.shape[1:], BF16) for w in weights]
    held_rows = pltpu.VMEM((rows_here, channels), BF16)
    held_slots = pltpu.VMEM((devices, pair_slots, channels), BF16)
    held_both = pltpu.VMEM((2 * rows_here, channels), BF16)
    pair_rows = channels // LANES * pair_slots + TAIL
    outgoing = pl.pallas_call(
        functools.partial(first_kernel, chips if ring else 0),
        out_shape=jax.ShapeDtypeStruct((devices, pair_rows, LANES), BF16),
        in_specs=[SMEM_SPEC] * 2 + [VMEM_SPEC] * 8 + [ANY_SPEC] * (2 + len(points_beyond)),
        out_specs=ANY_SPEC,
        scratch_shapes=[
            held_both,
            held_both,
            held_both,
            held_slots,
            pltpu.SemaphoreType.DMA((1 + SEND_PARTS, 4)),
        ],
        compiler_params=pltpu.CompilerParams(vmem_limit_bytes=FIRST_BYTES),
        name="block_first",
    )(
        pattern_first,
        pattern_beyond,
        slot_index,
        gains_kept,
        keyed,
        queries,
        queries_beyond,
        *kept,
        tail,
        points,
        *points_beyond,
    )
    incoming = lax.all_to_all(outgoing, ("grp", "seq"), split_axis=0, concat_axis=0, tiled=True)

    return pl.pallas_call(
        second_kernel,
        out_shape=(
            jax.ShapeDtypeStruct((rows_here, channels), BF16),
            jax.ShapeDtypeStruct((w_head.shape[0], rows_here), F32),
        ),
        in_specs=[SMEM_SPEC] + [ANY_SPEC] * 7,
        out_specs=(VMEM_SPEC, VMEM_SPEC),
        scratch_shapes=[
            pltpu.VMEM((rows_here, 2 * channels), BF16),
            held_rows,
            held_slots,
            pltpu.VMEM(w_qkv.shape[1:], BF16),
            *held_weights,
            pltpu.VMEM(norm_gains.shape, F32),
            pltpu.VMEM(tail.shape, BF16),
            pltpu.VMEM(w_head.shape, BF16),
            pltpu.SemaphoreType.DMA((3, 5)),
        ],
        compiler_params=pltpu.CompilerParams(vmem_limit_bytes=SECOND_BYTES),
        name="block_second",
    )(pattern_second.T, norm_gains, incoming, w_qkv, *weights, w_head)


def solution(mesh):
    groups, shards_in_group = mesh.devices.shape
    halves = Mesh(
        mesh.devices.reshape(groups, 2, shards_in_group // 2), ("grp",) + GROUP
    )
    everywhere = ("grp",) + GROUP
    placed = (
        P(everywhere, None),
        P(everywhere, None),
        P(everywhere, None),
        P(everywhere),
        P(),
        P(),
        P(),
        P(),
        P(),
        P(),
    )
    return jax.shard_map(
        shards,
        mesh=halves,
        in_specs=placed,
        out_specs=(P(everywhere, None), P(None, everywhere)),
        check_vma=False,
    )
```

time: 96.7 us -> 115 us (1.19)
  Pallas kernels: 30.5 us -> 53.9 us
  blocking collectives: 32.7 us -> 20.1 us
  starting transfers between devices: 7.52 us -> 13.1 us
    pallas_call x8, Pallas kernels: 9.94 us -> 28.2 us  [the longest x1 17 us: shards(): pl.pallas_call(split_kernel, out_shape=[jax.ShapeDtypeStruct((part, chann...]
    all_to_all x1, blocking collectives: 32.7 us -> 20.1 us  [shards(): lax.all_to_all(outgoing, ('grp', 'seq'), split_axis=0, concat_axis=0, til...]
    ppermute x14 -> x16, starting transfers between devices: 7.52 us -> 13.1 us  [the longest x6 9.92 us: shards(): column = [lax.ppermute(rows, GROUP, onward) for rows in column]]
    pallas_call x1, Pallas kernels: 8.12 us -> 13.2 us  [shards(): pl.pallas_call(functools.partial(first_kernel, chips if ring else 0), out...]
    ppermute x14 -> x16, waiting for transfers between devices: 22.8 us -> 23.6 us  [the longest x6 13.4 us: shards(): column = [lax.ppermute(rows, GROUP, onward) for rows in column]]
    unnamed x20 -> x22, local copies, waits for them, and re-layouts: 1.95 us -> 2.64 us
  transfers between devices with their start and end apart: 14 -> 16, of which waited for: 7 -> 6; matrix products, arithmetic and copies ran while one was open for 0% -> 0% of each run, Pallas kernels for 10% -> 12%
where the time goes in v7:
time: 115 us; the launch traced here: 114 us
  Pallas kernels  53.9 us (47%)
  waiting for transfers between devices  23.6 us (21%)
  blocking collectives  20.1 us (17%)
  starting transfers between devices  13.1 us (11%)
  local copies, waits for them, and re-layouts  2.64 us (2%)
    all_to_all x1, blocking collectives, shards(): lax.all_to_all(outgoing, ('grp', 'seq'), split_axis=0, concat_axis=0, til...  20.1 us
    pallas_call x1, Pallas kernels, shards(): pl.pallas_call(split_kernel, out_shape=[jax.ShapeDtypeStruct((part, chann...  17 us
    ppermute x6, waiting for transfers between devices, shards(): column = [lax.ppermute(rows, GROUP, onward) for rows in column]  13.4 us
    pallas_call x1, Pallas kernels, shards(): pl.pallas_call(functools.partial(first_kernel, chips if ring else 0), out...  13.2 us
    pallas_call x7, Pallas kernels, project(): pl.pallas_call(functools.partial(project_kernel, first_rows, new, ask), o...  11.2 us
    ppermute x6, starting transfers between devices, shards(): column = [lax.ppermute(rows, GROUP, onward) for rows in column]  9.92 us
    pallas_call x1, Pallas kernels, shards(): pl.pallas_call(second_kernel, out_shape=(jax.ShapeDtypeStruct((rows_here,...  9.65 us
    ppermute x1, waiting for transfers between devices, shards(): lax.ppermute(destination, GROUP, across)  8.34 us
  transfers between devices with their start and end apart: 16, of which 6 were waited for; matrix products, arithmetic and copies ran while one was open for 0% of the time, Pallas kernels for 12%

profile of v7, /device:TPU:0, one launch (start us, length us, event | category | flops | bytes accessed | tf_op | source)
XLA Modules:
  0.0 114.3 jit_solution(13909389503035265317)
XLA Ops:
  0.6 17.0 %split.1 = (bf16[256,512]{1,0:T(8,128)(2,1)}, bf16[256,512]{1,0:T(8,128)(2,1)}) custom-call(bf16[512,512]{1,0:T(8,128)(2,1)} %points.3), custom_call_target="tpu_custom_call" | custom-call | tf_op jit(solution)/shard_map/split/pallas_call | solution.py:402
  17.6 3.1 %collective-permute-start.1 = (bf16[256,512]{1,0:T(8,128)(2,1)}, bf16[256,512]{1,0:T(8,128)(2,1)S(1)}, u32[]{:S(2)}, u32[]{:S(2)}) collective-permute-start(bf16[256,512]{1,0:T(8,128)(2,1)} %get-tuple-element.27.refs_0_), channel_id=1, source_target_pairs={{0,2},{1,3},{2,4},{3,5},{4,6},{5,7},{6,0},{7,1},{8,10},{9,11},{10,... | collective-permute-start | bytes 786440 | tf_op jit(solution)/shard_map/ppermute | solution.py:468
  20.7 0.0 collective-permute-start.5
  20.7 0.5 collective-permute-start.6
  21.2 1.6 %collective-permute-start.4 = (bf16[256,512]{1,0:T(8,128)(2,1)}, bf16[256,512]{1,0:T(8,128)(2,1)S(1)}, u32[]{:S(2)}, u32[]{:S(2)}) collective-permute-start(bf16[256,512]{1,0:T(8,128)(2,1)} %get-tuple-element.32.refs_1_), channel_id=1, source_target_pairs={{0,2},{1,3},{2,4},{3,5},{4,6},{5,7},{6,0},{7,1},{8,10},{9,11},{10,... | collective-permute-start | bytes 786440 | tf_op jit(solution)/shard_map/ppermute | solution.py:468
  22.8 1.1 collective-permute-start.2
  23.9 8.3 %collective-permute-done.2.beyond = s32[1,512]{1,0:T(1,128)S(1)} collective-permute-done((s32[1,512]{1,0:T(1,128)}, s32[1,512]{1,0:T(1,128)S(1)}, u32[]{:S(2)}, u32[]{:S(2)}) %collective-permute-start.2) | collective-permute-done | bytes 2080 | tf_op jit(solution)/shard_map/ppermute | solution.py:435
  32.2 1.2 %copy-done = bf16[2,512,512]{2,1,0:T(8,128)(2,1)S(1)} copy-done((bf16[2,512,512]{2,1,0:T(8,128)(2,1)S(1)}, bf16[2,512,512]{2,1,0:T(8,128)(2,1)}, u32[]{:S(2)}) %copy-start) | copy-done | bytes 1048600
  33.5 0.7 copy-done.3
  34.2 0.7 copy-done.6
  34.8 2.8 %prepare.1 = (s32[1,1024]{1,0:T(1,128)S(1)}, bf16[16,8,128]{2,1,0:T(8,128)(2,1)S(1)}, bf16[512,1536]{1,0:T(8,128)(2,1)S(1)}, bf16[512,512]{1,0:T(8,128)(2,1)S(1)...) custom-call(s32[1,512]{1,0:T(1,128)S(1)} %bitcast.4, ...), custom_call_target="tpu_custom_call" | custom-call | tf_op jit(solution)/shard_map/prepare/pallas_call | solution.py:419
  37.7 0.0 collective-permute-done.1.refs_0_
  37.7 3.3 %collective-permute-start.3 = (bf16[256,512]{1,0:T(8,128)(2,1)S(1)}, bf16[256,512]{1,0:T(8,128)(2,1)S(1)}, u32[]{:S(2)}, u32[]{:S(2)}) collective-permute-start(bf16[256,512]{1,0:T(8,128)(2,1)S(1)} %collective-permute-done.1.refs_0_), channel_id=1, source_target_pairs={{0,2},{1,3},{2,4},{3,5},{4,6},{5,7},{6,0},{7,1},{8,10},{9,11},{10,... | collective-permute-start | bytes 786440 | tf_op jit(solution)/shard_map/ppermute | solution.py:468
  41.1 0.0 collective-permute-done.5.refs_2_
  41.1 0.0 collective-permute-done.6.refs_3_
  41.1 2.9 %project_own.1 = (bf16[4096,1024]{1,0:T(8,128)(2,1)S(1)}, bf16[512,512]{1,0:T(8,128)(2,1)S(1)}) custom-call(bf16[256,512]{1,0:T(8,128)(2,1)S(1)} %copy-done.10, bf16[256,512]{1,0:T(8,128)(2,1)S(1)} %copy-done.9, bf16[256,512]{1,0:T(8,128)(2,1)S(1)} %collective-permute-done.5.refs_2_, bf16[256,512]{1,0:T(8,128)(2,1)S(1)} %collective-permute-done.6.refs_3_, ...), custom_call_target="tpu_custom_call" | custom-call | flops 1073741824 | bytes 4718592 | tf_op jit(solution)/shard_map/project_own/pallas_call | solution.py:445
  44.0 0.0 collective-permute-done.4.refs_1_
  44.0 0.1 collective-permute-start.10
  44.1 0.5 collective-permute-start.9
  44.6 0.7 collective-permute-start.8
  45.3 1.3 %project.6.refs_4_ = bf16[4096,1024]{1,0:T(8,128)(2,1)S(1)} custom-call(bf16[256,512]{1,0:T(8,128)(2,1)S(1)} %collective-permute-done.1.refs_0_, bf16[256,512]{1,0:T(8,128)(2,1)S(1)} %collective-permute-done.4.refs_1_, f32[4,512]{1,0:T(4,128)S(1)} %get-tuple-element.30.refs_4_.refs_2_.gains, ...), custom_call_target="tpu_custom_call", output_to_operand_aliasing={{}: (4, {})} | custom-call | flops 536870912 | bytes 3145728 | tf_op jit(solution)/shard_map/project/pallas_call | solution.py:445
  46.6 0.7 collective-permute-done.3.refs_0_
  47.2 1.3 %collective-permute-start.7 = (bf16[256,512]{1,0:T(8,128)(2,1)S(1)}, bf16[256,512]{1,0:T(8,128)(2,1)S(1)}, u32[]{:S(2)}, u32[]{:S(2)}) collective-permute-start(bf16[256,512]{1,0:T(8,128)(2,1)S(1)} %collective-permute-done.3.refs_0_), channel_id=1, source_target_pairs={{0,2},{1,3},{2,4},{3,5},{4,6},{5,7},{6,0},{7,1},{8,10},{9,11},{10,... | collective-permute-start | bytes 786440 | tf_op jit(solution)/shard_map/ppermute | solution.py:468
  48.5 0.0 collective-permute-done.10.refs_1_
  48.5 0.0 collective-permute-done.9.refs_0_
  48.5 1.3 %project.7.refs_4_ = bf16[4096,1024]{1,0:T(8,128)(2,1)S(1)} custom-call(bf16[256,512]{1,0:T(8,128)(2,1)S(1)} %collective-permute-done.9.refs_0_, bf16[256,512]{1,0:T(8,128)(2,1)S(1)} %collective-permute-done.10.refs_1_, f32[4,512]{1,0:T(4,128)S(1)} %get-tuple-element.30.refs_4_.refs_2_.gains, ...), custom_call_target="tpu_custom_call", output_to_operand_aliasing={{}: (4, {})} | custom-call | flops 536870912 | bytes 3145728 | tf_op jit(solution)/shard_map/project/pallas_call | solution.py:445
  49.8 5.7 %collective-permute-done.8.refs_1_ = bf16[256,512]{1,0:T(8,128)(2,1)S(1)} collective-permute-done((bf16[256,512]{1,0:T(8,128)(2,1)S(1)}, bf16[256,512]{1,0:T(8,128)(2,1)S(1)}, u32[]{:S(2)}, u32[]{:S(2)}) %collective-permute-start.8) | collective-permute-done | bytes 262176 | tf_op jit(solution)/shard_map/ppermute | solution.py:468
  55.6 0.0 collective-permute-start.14
  55.6 0.5 collective-permute-start.13
  56.1 0.0 collective-permute-start.12
  56.1 1.6 %project.8 = (bf16[4096,1024]{1,0:T(8,128)(2,1)S(1)}, bf16[512,512]{1,0:T(8,128)(2,1)S(1)}) custom-call(bf16[256,512]{1,0:T(8,128)(2,1)S(1)} %collective-permute-done.3.refs_0_, bf16[256,512]{1,0:T(8,128)(2,1)S(1)} %collective-permute-done.8.refs_1_, f32[4,512]{1,0:T(4,128)S(1)} %get-tuple-element.30.refs_4_.refs_2_.gains, ...), custom_call_target="tpu_custom_call", output_to_operand_aliasing={{0}: (4, {})} | custom-call | flops 536870912 | bytes 3145728 | tf_op jit(solution)/shard_map/project/pallas_call | solution.py:445
  57.7 2.6 %collective-permute-done.7.refs_0_ = bf16[256,512]{1,0:T(8,128)(2,1)S(1)} collective-permute-done((bf16[256,512]{1,0:T(8,128)(2,1)S(1)}, bf16[256,512]{1,0:T(8,128)(2,1)S(1)}, u32[]{:S(2)}, u32[]{:S(2)}) %collective-permute-start.7) | collective-permute-done | bytes 262176 | tf_op jit(solution)/shard_map/ppermute | solution.py:468
  60.3 0.0 collective-permute-done.14.refs_1_
  60.3 0.0 collective-permute-done.13.refs_0_
  60.3 1.3 %project.9.refs_4_ = bf16[4096,1024]{1,0:T(8,128)(2,1)S(1)} custom-call(bf16[256,512]{1,0:T(8,128)(2,1)S(1)} %collective-permute-done.13.refs_0_, bf16[256,512]{1,0:T(8,128)(2,1)S(1)} %collective-permute-done.14.refs_1_, f32[4,512]{1,0:T(4,128)S(1)} %get-tuple-element.30.refs_4_.refs_2_.gains, ...), custom_call_target="tpu_custom_call", output_to_operand_aliasing={{}: (4, {})} | custom-call | flops 536870912 | bytes 3145728 | tf_op jit(solution)/shard_map/project/pallas_call | solution.py:445
  61.7 4.4 %collective-permute-done.12.refs_1_ = bf16[256,512]{1,0:T(8,128)(2,1)S(1)} collective-permute-done((bf16[256,512]{1,0:T(8,128)(2,1)S(1)}, bf16[256,512]{1,0:T(8,128)(2,1)S(1)}, u32[]{:S(2)}, u32[]{:S(2)}) %collective-permute-start.12) | collective-permute-done | bytes 262176 | tf_op jit(solution)/shard_map/ppermute | solution.py:468
  66.1 0.0 collective-permute-start.15
  66.1 0.5 collective-permute-start.11
  66.6 1.3 %project.10.refs_4_ = bf16[4096,1024]{1,0:T(8,128)(2,1)S(1)} custom-call(bf16[256,512]{1,0:T(8,128)(2,1)S(1)} %collective-permute-done.7.refs_0_, bf16[256,512]{1,0:T(8,128)(2,1)S(1)} %collective-permute-done.12.refs_1_, f32[4,512]{1,0:T(4,128)S(1)} %get-tuple-element.30.refs_4_.refs_2_.gains, ...), custom_call_target="tpu_custom_call", output_to_operand_aliasing={{}: (4, {})} | custom-call | flops 536870912 | bytes 3145728 | tf_op jit(solution)/shard_map/project/pallas_call | solution.py:445
  67.9 0.0 copy-start.2
  67.9 0.0 collective-permute-done.15.refs_1_
  68.0 0.0 collective-permute-done.11.refs_0_
  68.0 1.3 %project.11.keyed = bf16[4096,1024]{1,0:T(8,128)(2,1)S(1)} custom-call(bf16[256,512]{1,0:T(8,128)(2,1)S(1)} %collective-permute-done.11.refs_0_, bf16[256,512]{1,0:T(8,128)(2,1)S(1)} %collective-permute-done.15.refs_1_, f32[4,512]{1,0:T(4,128)S(1)} %get-tuple-element.30.refs_4_.refs_2_.gains, ...), custom_call_target="tpu_custom_call", output_to_operand_aliasing={{}: (4, {})} | custom-call | flops 536870912 | bytes 3145728 | tf_op jit(solution)/shard_map/project/pallas_call | solution.py:445
  69.3 1.8 %collective-permute-done.pattern_beyond = s32[3,8]{1,0:T(4,128)S(1)} collective-permute-done((s32[3,8]{1,0:T(4,128)S(1)}, s32[3,8]{1,0:T(4,128)S(1)}, u32[]{:S(2)}, u32[]{:S(2)}) %collective-permute-start) | collective-permute-done | bytes 128 | tf_op jit(solution)/shard_map/ppermute | solution.py:418
  71.1 0.0 copy-start.8
  71.1 13.2 %block_first.1 = bf16[16,264,128]{2,1,0:T(8,128)(2,1)S(1)} custom-call(s32[3,8]{1,0:T(4,128)S(1)} %bitcast.6, s32[3,8]{1,0:T(4,128)S(1)} %collective-permute-done.pattern_beyond, s32[1,1024]{1,0:T(1,128)S(1)} %get-tuple-element.29.slot_of_row, f32[4,512]{1,0:T(4,128)S(1)} %get-tuple-element.30.refs_4_.refs_2_.gains, bf16[4096,1024]{1,0:T(8,128)(2,1)S(1)} %project.11.keyed, ...), custom_call_target="tpu_custom_call" | custom-call | tf_op jit(solution)/shard_map/block_first/pallas_call | solution.py:504
  84.3 20.1 %all_to_all.5.incoming = bf16[16,264,128]{2,1,0:T(8,128)(2,1)S(1)} all-to-all(bf16[16,264,128]{2,1,0:T(8,128)(2,1)S(1)} %block_first.1), channel_id=1, replica_groups=mesh['grp'=4,'half'=2,'seq'=4] {'grp','seq'}, dimensions={0} | all-to-all | bytes 2162688 | tf_op jit(solution)/shard_map/all_to_all | solution.py:531
  104.5 9.6 %block_second.1 = (bf16[512,512]{1,0:T(8,128)(2,1)}, f32[3,512]{1,0:T(4,128)}) custom-call(s32[3,8]{1,0:T(4,128)S(1)} %bitcast.7, f32[4,512]{1,0:T(4,128)S(1)} %copy-done.4, bf16[16,264,128]{2,1,0:T(8,128)(2,1)S(1)} %all_to_all.5.incoming, bf16[2,512,1536]{2,1,0:T(8,128)(2,1)} %w_qkv.1, bf16[2,512,512]{2,1,0:T(8,128)(2,1)S(1)} %copy-done.1, ...), custom_call_target="tpu_custom_call" | custom-call | tf_op jit(solution)/shard_map/block_second/pallas_call | solution.py:533
  (18 shorter events, 0.0 us)
Async XLA Ops:
  17.6 20.1 %collective-permute-start.1 = (bf16[256,512]{1,0:T(8,128)(2,1)}, bf16[256,512]{1,0:T(8,128)(2,1)S(1)}, u32[]{:S(2)}, u32[]{:S(2)}) collective-permute-start(bf16[256,512]{1,0:T(8,128)(2,1)} %get-tuple-element.27.refs_0_), channel_id=1, source_target_pairs={{0,2},{1,3},{2,4},{3,5},{4,6},{5,7},{6,0},{7,1},{8,10},{9,11},{10,... | collective-permute-start | bytes 786440 | tf_op jit(solution)/shard_map/ppermute | solution.py:468
  20.7 20.3 %collective-permute-start.5 = (bf16[256,512]{1,0:T(8,128)(2,1)}, bf16[256,512]{1,0:T(8,128)(2,1)S(1)}, u32[]{:S(2)}, u32[]{:S(2)}) collective-permute-start(bf16[256,512]{1,0:T(8,128)(2,1)} %get-tuple-element.27.refs_0_), channel_id=1, source_target_pairs={{0,1},{1,0},{2,3},{3,2},{4,5},{5,4},{6,7},{7,6},{8,9},{9,8},{10,11... | collective-permute-start | bytes 786440 | tf_op jit(solution)/shard_map/ppermute | solution.py:465
  20.7 20.3 %collective-permute-start.6 = (bf16[256,512]{1,0:T(8,128)(2,1)}, bf16[256,512]{1,0:T(8,128)(2,1)S(1)}, u32[]{:S(2)}, u32[]{:S(2)}) collective-permute-start(bf16[256,512]{1,0:T(8,128)(2,1)} %get-tuple-element.32.refs_1_), channel_id=1, source_target_pairs={{0,1},{1,0},{2,3},{3,2},{4,5},{5,4},{6,7},{7,6},{8,9},{9,8},{10,11... | collective-permute-start | bytes 786440 | tf_op jit(solution)/shard_map/ppermute | solution.py:465
  21.2 22.8 %collective-permute-start.4 = (bf16[256,512]{1,0:T(8,128)(2,1)}, bf16[256,512]{1,0:T(8,128)(2,1)S(1)}, u32[]{:S(2)}, u32[]{:S(2)}) collective-permute-start(bf16[256,512]{1,0:T(8,128)(2,1)} %get-tuple-element.32.refs_1_), channel_id=1, source_target_pairs={{0,2},{1,3},{2,4},{3,5},{4,6},{5,7},{6,0},{7,1},{8,10},{9,11},{10,... | collective-permute-start | bytes 786440 | tf_op jit(solution)/shard_map/ppermute | solution.py:468
  22.8 9.4 %collective-permute-start.2 = (s32[1,512]{1,0:T(1,128)}, s32[1,512]{1,0:T(1,128)S(1)}, u32[]{:S(2)}, u32[]{:S(2)}) collective-permute-start(s32[1,512]{1,0:T(1,128)} %bitcast.3), channel_id=1, source_target_pairs={{0,4},{1,5},{2,6},{3,7},{4,0},{5,1},{6,2},{7,3},{8,12},{9,13},{10,... | collective-permute-start | bytes 6152 | tf_op jit(solution)/shard_map/ppermute | solution.py:435
  32.2 1.2 %copy-start = (bf16[2,512,512]{2,1,0:T(8,128)(2,1)S(1)}, bf16[2,512,512]{2,1,0:T(8,128)(2,1)}, u32[]{:S(2)}) copy-start(bf16[2,512,512]{2,1,0:T(8,128)(2,1)} %w_proj.1) | copy-start | bytes 3145732
  33.5 0.7 copy-start.3
  34.2 0.7 copy-start.6
  34.8 6.2 %copy-start.9 = (bf16[256,512]{1,0:T(8,128)(2,1)S(1)}, bf16[256,512]{1,0:T(8,128)(2,1)}, u32[]{:S(2)}) copy-start(bf16[256,512]{1,0:T(8,128)(2,1)} %get-tuple-element.32.refs_1_) | copy-start | bytes 786436
  34.8 6.2 %copy-start.10 = (bf16[256,512]{1,0:T(8,128)(2,1)S(1)}, bf16[256,512]{1,0:T(8,128)(2,1)}, u32[]{:S(2)}) copy-start(bf16[256,512]{1,0:T(8,128)(2,1)} %get-tuple-element.27.refs_0_) | copy-start | bytes 786436
  37.7 9.5 %collective-permute-start.3 = (bf16[256,512]{1,0:T(8,128)(2,1)S(1)}, bf16[256,512]{1,0:T(8,128)(2,1)S(1)}, u32[]{:S(2)}, u32[]{:S(2)}) collective-permute-start(bf16[256,512]{1,0:T(8,128)(2,1)S(1)} %collective-permute-done.1.refs_0_), channel_id=1, source_target_pairs={{0,2},{1,3},{2,4},{3,5},{4,6},{5,7},{6,0},{7,1},{8,10},{9,11},{10,... | collective-permute-start | bytes 786440 | tf_op jit(solution)/shard_map/ppermute | solution.py:468
  44.0 4.5 %collective-permute-start.10 = (bf16[256,512]{1,0:T(8,128)(2,1)S(1)}, bf16[256,512]{1,0:T(8,128)(2,1)S(1)}, u32[]{:S(2)}, u32[]{:S(2)}) collective-permute-start(bf16[256,512]{1,0:T(8,128)(2,1)S(1)} %collective-permute-done.4.refs_1_), channel_id=1, source_target_pairs={{0,1},{1,0},{2,3},{3,2},{4,5},{5,4},{6,7},{7,6},{8,9},{9,8},{10,11... | collective-permute-start | bytes 786440 | tf_op jit(solution)/shard_map/ppermute | solution.py:482
  44.1 4.4 %collective-permute-start.9 = (bf16[256,512]{1,0:T(8,128)(2,1)S(1)}, bf16[256,512]{1,0:T(8,128)(2,1)S(1)}, u32[]{:S(2)}, u32[]{:S(2)}) collective-permute-start(bf16[256,512]{1,0:T(8,128)(2,1)S(1)} %collective-permute-done.1.refs_0_), channel_id=1, source_target_pairs={{0,1},{1,0},{2,3},{3,2},{4,5},{5,4},{6,7},{7,6},{8,9},{9,8},{10,11... | collective-permute-start | bytes 786440 | tf_op jit(solution)/shard_map/ppermute | solution.py:482
  44.6 11.0 %collective-permute-start.8 = (bf16[256,512]{1,0:T(8,128)(2,1)S(1)}, bf16[256,512]{1,0:T(8,128)(2,1)S(1)}, u32[]{:S(2)}, u32[]{:S(2)}) collective-permute-start(bf16[256,512]{1,0:T(8,128)(2,1)S(1)} %collective-permute-done.4.refs_1_), channel_id=1, source_target_pairs={{0,2},{1,3},{2,4},{3,5},{4,6},{5,7},{6,0},{7,1},{8,10},{9,11},{10,... | collective-permute-start | bytes 786440 | tf_op jit(solution)/shard_map/ppermute | solution.py:468
  47.2 13.1 %collective-permute-start.7 = (bf16[256,512]{1,0:T(8,128)(2,1)S(1)}, bf16[256,512]{1,0:T(8,128)(2,1)S(1)}, u32[]{:S(2)}, u32[]{:S(2)}) collective-permute-start(bf16[256,512]{1,0:T(8,128)(2,1)S(1)} %collective-permute-done.3.refs_0_), channel_id=1, source_target_pairs={{0,2},{1,3},{2,4},{3,5},{4,6},{5,7},{6,0},{7,1},{8,10},{9,11},{10,... | collective-permute-start | bytes 786440 | tf_op jit(solution)/shard_map/ppermute | solution.py:468
  55.6 4.8 %collective-permute-start.14 = (bf16[256,512]{1,0:T(8,128)(2,1)S(1)}, bf16[256,512]{1,0:T(8,128)(2,1)S(1)}, u32[]{:S(2)}, u32[]{:S(2)}) collective-permute-start(bf16[256,512]{1,0:T(8,128)(2,1)S(1)} %collective-permute-done.8.refs_1_), channel_id=1, source_target_pairs={{0,1},{1,0},{2,3},{3,2},{4,5},{5,4},{6,7},{7,6},{8,9},{9,8},{10,11... | collective-permute-start | bytes 786440 | tf_op jit(solution)/shard_map/ppermute | solution.py:482
  55.6 4.8 %collective-permute-start.13 = (bf16[256,512]{1,0:T(8,128)(2,1)S(1)}, bf16[256,512]{1,0:T(8,128)(2,1)S(1)}, u32[]{:S(2)}, u32[]{:S(2)}) collective-permute-start(bf16[256,512]{1,0:T(8,128)(2,1)S(1)} %collective-permute-done.3.refs_0_), channel_id=1, source_target_pairs={{0,1},{1,0},{2,3},{3,2},{4,5},{5,4},{6,7},{7,6},{8,9},{9,8},{10,11... | collective-permute-start | bytes 786440 | tf_op jit(solution)/shard_map/ppermute | solution.py:482
  56.1 10.0 %collective-permute-start.12 = (bf16[256,512]{1,0:T(8,128)(2,1)S(1)}, bf16[256,512]{1,0:T(8,128)(2,1)S(1)}, u32[]{:S(2)}, u32[]{:S(2)}) collective-permute-start(bf16[256,512]{1,0:T(8,128)(2,1)S(1)} %collective-permute-done.8.refs_1_), channel_id=1, source_target_pairs={{0,2},{1,3},{2,4},{3,5},{4,6},{5,7},{6,0},{7,1},{8,10},{9,11},{10,... | collective-permute-start | bytes 786440 | tf_op jit(solution)/shard_map/ppermute | solution.py:468
  60.3 6.3 %copy-start.7 = (s32[8,3]{0,1:T(4,128)S(1)}, s32[8,3]{0,1:T(4,128)}, u32[]{:S(2)}) copy-start(s32[8,3]{0,1:T(4,128)} %param.11) | copy-start | bytes 292
  66.1 1.9 %collective-permute-start.15 = (bf16[256,512]{1,0:T(8,128)(2,1)S(1)}, bf16[256,512]{1,0:T(8,128)(2,1)S(1)}, u32[]{:S(2)}, u32[]{:S(2)}) collective-permute-start(bf16[256,512]{1,0:T(8,128)(2,1)S(1)} %collective-permute-done.12.refs_1_), channel_id=1, source_target_pairs={{0,1},{1,0},{2,3},{3,2},{4,5},{5,4},{6,7},{7,6},{8,9},{9,8},{10,11... | collective-permute-start | bytes 786440 | tf_op jit(solution)/shard_map/ppermute | solution.py:482
  66.1 1.9 %collective-permute-start.11 = (bf16[256,512]{1,0:T(8,128)(2,1)S(1)}, bf16[256,512]{1,0:T(8,128)(2,1)S(1)}, u32[]{:S(2)}, u32[]{:S(2)}) collective-permute-start(bf16[256,512]{1,0:T(8,128)(2,1)S(1)} %collective-permute-done.7.refs_0_), channel_id=1, source_target_pairs={{0,1},{1,0},{2,3},{3,2},{4,5},{5,4},{6,7},{7,6},{8,9},{9,8},{10,11... | collective-permute-start | bytes 786440 | tf_op jit(solution)/shard_map/ppermute | solution.py:482
  66.6 4.5 %collective-permute-start = (s32[3,8]{1,0:T(4,128)S(1)}, s32[3,8]{1,0:T(4,128)S(1)}, u32[]{:S(2)}, u32[]{:S(2)}) collective-permute-start(s32[3,8]{1,0:T(4,128)S(1)} %bitcast.5), channel_id=1, source_target_pairs={{0,4},{1,5},{2,6},{3,7},{4,0},{5,1},{6,2},{7,3},{8,12},{9,13},{10,... | collective-permute-start | bytes 296 | tf_op jit(solution)/shard_map/ppermute | solution.py:418
  67.9 3.2 %copy-start.2 = (bf16[512,512]{1,0:T(8,128)(2,1)S(1)}, bf16[512,512]{1,0:T(8,128)(2,1)}, u32[]{:S(2)}) copy-start(bf16[512,512]{1,0:T(8,128)(2,1)} %points.3) | copy-start | bytes 1572868
  71.1 33.4 %copy-start.1 = (bf16[2,512,512]{2,1,0:T(8,128)(2,1)S(1)}, bf16[2,512,512]{2,1,0:T(8,128)(2,1)}, u32[]{:S(2)}) copy-start(bf16[2,512,512]{2,1,0:T(8,128)(2,1)} %w_proj.1) | copy-start | bytes 3145732
  71.1 33.4 %copy-start.4 = (f32[4,512]{1,0:T(4,128)S(1)}, f32[4,512]{1,0:T(4,128)}, u32[]{:S(2)}) copy-start(f32[4,512]{1,0:T(4,128)} %gains.1) | copy-start | bytes 24580
  71.1 33.4 %copy-start.5 = (bf16[3,512]{1,0:T(4,128)(2,1)S(1)}, bf16[3,512]{1,0:T(4,128)(2,1)}, u32[]{:S(2)}) copy-start(bf16[3,512]{1,0:T(4,128)(2,1)} %w_head.1) | copy-start | bytes 9220
  71.1 33.4 %copy-start.8 = (s32[8,3]{0,1:T(4,128)S(1)}, s32[8,3]{0,1:T(4,128)}, u32[]{:S(2)}) copy-start(s32[8,3]{0,1:T(4,128)} %param.12) | copy-start | bytes 292

commit v8 on v7

--- a/solution.py
+++ b/solution.py
@@ -105,29 +105,53 @@
     return total.astype(BF16)
 
 
-def split_kernel(points, *refs):
-    *parts, sems = refs
-    rows = parts[0].shape[0]
-    for copy in started(
-        [(points.at[pl.ds(i * rows, rows), :], part) for i, part in enumerate(parts)], sems
-    ):
-        copy.wait()
-
-
-def prepare_kernel(capacity, destination, beyond, *refs):
-    count = (len(refs) - 4) // 2
-    sources, (slots, tail), kept = refs[:count], refs[count : count + 2], refs[count + 2 : -2]
-    held, sems = refs[-2:]
-    fetches = started([(destination, held.at[0]), (beyond, held.at[1])], sems.at[0])
+def split_kernel(points, destination, pattern, *refs):
+    *parts, destination_held, pattern_held, notes, sems = refs
+    rows = points.shape[0] // len(parts)
+    fetches = started([(destination, destination_held), (pattern, pattern_held)], sems.at[0])
     copies = started(
         [
-            (source.at[0] if len(source.shape) == 3 else source, place)
-            for source, place in zip(sources, kept)
+            (points.at[pl.ds(i * rows, rows), :], part.at[pl.ds(0, rows), :])
+            for i, part in enumerate(parts)
         ],
         sems.at[1],
     )
     for fetch in fetches:
         fetch.wait()
+    chosen, patches = pattern.shape
+    row = lax.broadcasted_iota(jnp.int32, notes.shape, 0)
+    low = destination_held[...] & (DIGIT - 1)
+    high = lax.shift_right_logical(destination_held[...], DIGIT.bit_length() - 1)
+    values = jnp.where(row == chosen, low, jnp.where(row == chosen + 1, high, 0))
+    notes[...] = values.astype(F32)
+    notes[0:chosen, 0:patches] = pattern_held[...].astype(F32)
+    parts[0][rows : rows + TAIL, :] = notes[...].astype(BF16)
+    for copy in copies:
+        copy.wait()
+
+
+def keep_kernel(*refs):
+    *refs, sems = refs
+    count = len(refs) // 2
+    for copy in started(
+        [
+            (source.at[0] if len(source.shape) == 3 else source, place)
+            for source, place in zip(refs[:count], refs[count:])
+        ],
+        sems,
+    ):
+        copy.wait()
+
+
+def index_kernel(capacity, destination, beyond, slots, tail, pattern, held, notes, sems):
+    added = beyond.at[pl.ds(beyond.shape[0] - TAIL, TAIL), :]
+    for fetch in started([(destination, held.at[0]), (added, notes)], sems):
+        fetch.wait()
+    chosen, patches = pattern.shape
+    noted = notes[...].astype(F32)
+    pattern[...] = noted[0:chosen, 0:patches].astype(jnp.int32)
+    low, high = noted[chosen : chosen + 1, :], noted[chosen + 1 : chosen + 2, :]
+    held[1] = (low + DIGIT * high).astype(jnp.int32)
     rows = held.shape[2]
     devices = tail.shape[0]
     in_half = lax.axis_size("seq")
@@ -166,8 +190,6 @@
             digits.astype(BF16), by_lane, (((1,), (1,)), ((), ())), preferred_element_type=F32
         )
     tail[...] = lines.reshape(devices, TAIL, LANES).astype(BF16)
-    for copy in copies:
-        copy.wait()
 
 
 def project_kernel(first_rows, new, ask, *refs):
@@ -177,7 +199,9 @@
     whole, (held, sems) = refs[0], refs[-2:]
     channels = w_qkv.shape[0]
     rows = held.shape[1]
-    copies = started([(part, held.at[i]) for i, part in enumerate(parts)], sems)
+    copies = started(
+        [(part.at[pl.ds(0, rows), :], held.at[i]) for i, part in enumerate(parts)], sems
+    )
     for i, first in enumerate(first_rows):
         copies[i].wait()
         normed = layer_norm(held[i], gains[0:1, :])
@@ -228,7 +252,7 @@
     copies = started(
         [(tail, outgoing.at[:, pl.ds(row_tiles, TAIL), :]), (points, points_held.at[:rows])]
         + [
-            (piece, points_held.at[pl.ds(rows + i * part, part), :])
+            (piece.at[pl.ds(0, part), :], points_held.at[pl.ds(rows + i * part, part), :])
             for i, piece in enumerate(points_beyond)
         ],
         sems.at[0],
@@ -399,45 +423,62 @@
     kept_rows = shards_in_group * rows_here if ring else 2 * patches * (1 + chosen) * PATCH
     part = rows_here // RING_PARTS
 
+    destination = destination.reshape(1, rows_here)
+    pattern_first = pattern_first.T
+    part_rows = [part + TAIL] + [part] * (RING_PARTS - 1)
     column = pl.pallas_call(
         split_kernel,
-        out_shape=[jax.ShapeDtypeStruct((part, channels), BF16)] * RING_PARTS,
-        in_specs=[ANY_SPEC],
-        out_specs=[ANY_SPEC] * RING_PARTS,
-        scratch_shapes=[pltpu.SemaphoreType.DMA((RING_PARTS,))],
+        out_shape=[jax.ShapeDtypeStruct((rows, channels), BF16) for rows in part_rows],
+        in_specs=[ANY_SPEC] * 3,
+        out_specs=[VMEM_SPEC] * RING_PARTS,
+        scratch_shapes=[
+            pltpu.VMEM((1, rows_here), jnp.int32),
+            pltpu.VMEM(pattern_first.shape, jnp.int32),
+            pltpu.VMEM((TAIL, channels), F32),
+            pltpu.SemaphoreType.DMA((2, RING_PARTS)),
+        ],
         compiler_params=pltpu.CompilerParams(vmem_limit_bytes=SPLIT_BYTES),
         name="split",
-    )(points)
+    )(points, destination, pattern_first)
 
     weights = (w_proj, w_up, w_down)
     kv_shape = jax.ShapeDtypeStruct((kept_rows, 2 * channels), BF16)
     own_shape = jax.ShapeDtypeStruct((rows_here, channels), BF16)
 
-    destination = destination.reshape(1, rows_here)
-    pattern_first = pattern_first.T
-    pattern_beyond = lax.ppermute(pattern_first, GROUP, across)
-    slot_index, tail, qkv_kept, *kept, gains_kept = pl.pallas_call(
-        functools.partial(prepare_kernel, capacity),
+    qkv_kept, *kept, gains_kept = pl.pallas_call(
+        keep_kernel,
         out_shape=[
-            jax.ShapeDtypeStruct((1, 2 * rows_here), jnp.int32),
-            jax.ShapeDtypeStruct((devices, TAIL, LANES), BF16),
             *[jax.ShapeDtypeStruct(w.shape[1:], BF16) for w in (w_qkv,) + weights],
             jax.ShapeDtypeStruct(norm_gains.shape, F32),
         ],
-        in_specs=[ANY_SPEC] * 7,
-        out_specs=[VMEM_SPEC] * 7,
-        scratch_shapes=[
-            pltpu.VMEM((2, 1, rows_here), jnp.int32),
-            pltpu.SemaphoreType.DMA((2, 5)),
-        ],
+        in_specs=[ANY_SPEC] * 5,
+        out_specs=[VMEM_SPEC] * 5,
+        scratch_shapes=[pltpu.SemaphoreType.DMA((5,))],
         compiler_params=pltpu.CompilerParams(vmem_limit_bytes=PREPARE_BYTES),
-        name="prepare",
-    )(destination, lax.ppermute(destination, GROUP, across), w_qkv, *weights, norm_gains)
-
-    def project(keyed, blocks, ask=False):
-        parts = [rows for _, block in blocks for rows in block]
+        name="keep",
+    )(w_qkv, *weights, norm_gains)
+    def index(beyond):
+        return pl.pallas_call(
+            functools.partial(index_kernel, capacity),
+            out_shape=[
+                jax.ShapeDtypeStruct((1, 2 * rows_here), jnp.int32),
+                jax.ShapeDtypeStruct((devices, TAIL, LANES), BF16),
+                jax.ShapeDtypeStruct(pattern_first.shape, jnp.int32),
+            ],
+            in_specs=[ANY_SPEC] * 2,
+            out_specs=[VMEM_SPEC] * 3,
+            scratch_shapes=[
+                pltpu.VMEM((2, 1, rows_here), jnp.int32),
+                pltpu.VMEM((TAIL, channels), BF16),
+                pltpu.SemaphoreType.DMA((2,)),
+            ],
+            compiler_params=pltpu.CompilerParams(vmem_limit_bytes=PROJECT_BYTES),
+            name="index",
+        )(destination, beyond)
+
+    def project(keyed, blocks, ask=False, rows=part):
+        parts = [piece for _, block in blocks for piece in block]
         count = len(parts)
-        rows = parts[0].shape[0]
         first_rows = [
             slot * rows_here + i * rows for slot, block in blocks for i in range(len(block))
         ]
@@ -467,7 +508,7 @@
         for step in range(1, chips):
             column = [lax.ppermute(rows, GROUP, onward) for rows in column]
             if step == 1:
-                column[0], slot_index = lax.optimization_barrier((column[0], slot_index))
+                column[0], gains_kept = lax.optimization_barrier((column[0], gains_kept))
                 keyed, queries = project(None, waiting, ask=True)
                 column[1], keyed = lax.optimization_barrier((column[1], keyed))
             else:
@@ -479,6 +520,9 @@
                     column[i], keyed = lax.optimization_barrier((column[i], keyed))
             if step == chips // 2:
                 points_beyond = column
+                slot_index, tail, pattern_beyond = index(column[0])
+            if step == chips - 1:
+                column[0], slot_index = lax.optimization_barrier((column[0], slot_index))
             beside = [lax.ppermute(rows, GROUP, swap) for rows in column]
             waiting = [(2 * step, column), (2 * step + 1, beside)]
         for block in waiting:
@@ -488,13 +532,15 @@
         partner = lax.rem(lax.axis_index(GROUP) + chips, shards_in_group)
         points_beyond = [lax.dynamic_slice_in_dim(group, partner * rows_here, rows_here)]
         group = group.reshape(-1, PATCH, channels)
+        slot_index, tail, pattern_beyond = index(lax.ppermute(column[0], GROUP, across))
         picked = [
             group[pattern.T].reshape(-1, channels) for pattern in (pattern_first, pattern_beyond)
         ]
+        wide = picked[0].shape[0]
         keyed, queries = project(None, [(0, column)], ask=True)
-        keyed, queries_beyond = project(keyed, [(1, points_beyond)], ask=True)
-        (keyed,) = project(keyed, [(2, [picked[0]])])
-        (keyed,) = project(keyed, [(2 + chosen, [picked[1]])])
+        keyed, queries_beyond = project(keyed, [(1, points_beyond)], ask=True, rows=rows_here)
+        (keyed,) = project(keyed, [(2, [picked[0]])], rows=wide)
+        (keyed,) = project(keyed, [(2 + chosen, [picked[1]])], rows=wide)
 
     held_weights = [pltpu.VMEM(w.shape[1:], BF16) for w in weights]
     held_rows = pltpu.VMEM((rows_here, channels), BF16)

time: 115 us -> 89.3 us (0.78)
  Pallas kernels: 53.9 us -> 39.2 us
  starting transfers between devices: 13.1 us -> 6.65 us
  waiting for transfers between devices: 23.6 us -> 19.9 us
    pallas_call x2 -> x3, Pallas kernels: 19.9 us -> 5.28 us  [the longest x1 2.8 us: shards(): pl.pallas_call(keep_kernel, out_shape=[*[jax.ShapeDtypeStruct(w.shape[1:]...]
    ppermute x2 -> x0, waiting for transfers between devices: 10.1 us -> none  [the longest x1 8.34 us: shards(): lax.ppermute(destination, GROUP, across)]
    ppermute x6, waiting for transfers between devices: 13.4 us -> 19.7 us  [shards(): column = [lax.ppermute(rows, GROUP, onward) for rows in column]]
    ppermute x6, starting transfers between devices: 9.92 us -> 6.12 us  [shards(): column = [lax.ppermute(rows, GROUP, onward) for rows in column]]
    ppermute x8, starting transfers between devices: 2.1 us -> 0.53 us  [shards(): beside = [lax.ppermute(rows, GROUP, swap) for rows in column]]
  transfers between devices with their start and end apart: 16 -> 14, of which waited for: 6 -> 7; matrix products, arithmetic and copies ran while one was open for 0% -> 0% of each run, Pallas kernels for 12% -> 15%
where the time goes in v8:
time: 89.3 us; the launch traced here: 89.1 us
  Pallas kernels  39.2 us (44%)
  blocking collectives  20.3 us (23%)
  waiting for transfers between devices  19.9 us (22%)
  starting transfers between devices  6.65 us (7%)
  local copies, waits for them, and re-layouts  1.97 us (2%)
  between operations  1.02 us (1%)
    all_to_all x1, blocking collectives, shards(): lax.all_to_all(outgoing, ('grp', 'seq'), split_axis=0, concat_axis=0, til...  20.3 us
    ppermute x6, waiting for transfers between devices, shards(): column = [lax.ppermute(rows, GROUP, onward) for rows in column]  19.7 us
    pallas_call x1, Pallas kernels, shards(): pl.pallas_call(functools.partial(first_kernel, chips if ring else 0), out...  13.2 us
    pallas_call x7, Pallas kernels, project(): pl.pallas_call(functools.partial(project_kernel, first_rows, new, ask), o...  11.1 us
    pallas_call x1, Pallas kernels, shards(): pl.pallas_call(second_kernel, out_shape=(jax.ShapeDtypeStruct((rows_here,...  9.65 us
    ppermute x6, starting transfers between devices, shards(): column = [lax.ppermute(rows, GROUP, onward) for rows in column]  6.12 us
    pallas_call x1, Pallas kernels, shards(): pl.pallas_call(keep_kernel, out_shape=[*[jax.ShapeDtypeStruct(w.shape[1:]...  2.8 us
    unnamed x22, local copies, waits for them, and re-layouts  1.97 us
  transfers between devices with their start and end apart: 14, of which 7 were waited for; matrix products, arithmetic and copies ran while one was open for 0% of the time, Pallas kernels for 15%

profile of v8, /device:TPU:0, one launch (start us, length us, event | category | flops | bytes accessed | tf_op | source)
XLA Modules:
  0.0 89.1 jit_solution(14635628912500464456)
XLA Ops:
  0.6 1.9 %split.1 = (bf16[264,512]{1,0:T(8,128)(2,1)}, bf16[256,512]{1,0:T(8,128)(2,1)}) custom-call(bf16[512,512]{1,0:T(8,128)(2,1)} %points.3, s32[1,512]{1,0:T(1,128)} %bitcast.3, s32[3,8]{1,0:T(4,128)} %bitcast.5), custom_call_target="tpu_custom_call" | custom-call | tf_op jit(solution)/shard_map/split/pallas_call | solution.py:429
  2.5 3.1 %collective-permute-start = (bf16[264,512]{1,0:T(8,128)(2,1)}, bf16[264,512]{1,0:T(8,128)(2,1)S(1)}, u32[]{:S(2)}, u32[]{:S(2)}) collective-permute-start(bf16[264,512]{1,0:T(8,128)(2,1)} %get-tuple-element.30.refs_0_), channel_id=1, source_target_pairs={{0,2},{1,3},{2,4},{3,5},{4,6},{5,7},{6,0},{7,1},{8,10},{9,11},{10,... | collective-permute-start | bytes 811016 | tf_op jit(solution)/shard_map/ppermute | solution.py:509
  5.6 0.0 collective-permute-start.3
  5.6 0.5 collective-permute-start.4
  6.1 1.6 %collective-permute-start.2 = (bf16[256,512]{1,0:T(8,128)(2,1)}, bf16[256,512]{1,0:T(8,128)(2,1)S(1)}, u32[]{:S(2)}, u32[]{:S(2)}) collective-permute-start(bf16[256,512]{1,0:T(8,128)(2,1)} %get-tuple-element.33.refs_1_), channel_id=1, source_target_pairs={{0,2},{1,3},{2,4},{3,5},{4,6},{5,7},{6,0},{7,1},{8,10},{9,11},{10,... | collective-permute-start | bytes 786440 | tf_op jit(solution)/shard_map/ppermute | solution.py:509
  7.7 1.2 %copy-done = bf16[2,512,512]{2,1,0:T(8,128)(2,1)S(1)} copy-done((bf16[2,512,512]{2,1,0:T(8,128)(2,1)S(1)}, bf16[2,512,512]{2,1,0:T(8,128)(2,1)}, u32[]{:S(2)}) %copy-start) | copy-done | bytes 1048600
  8.9 0.7 copy-done.3
  9.6 2.8 %keep.1 = (bf16[512,1536]{1,0:T(8,128)(2,1)S(1)}, bf16[512,512]{1,0:T(8,128)(2,1)S(1)}, bf16[512,2048]{1,0:T(8,128)(2,1)S(1)}, bf16[2048,512]{1,0:T(8,128)(2,1)S(1)}, f32[4,512]{1,0:T(4,128)S(1)}) custom-call(bf16[2,512,1536]{2,1,0:T(8,128)(2,1)} %w_qkv.1, bf16[2,512,512]{2,1,0:T(8,128)(2,1)S(1)} %copy-done, bf16[2,512,2048]{2,1,0:T(8,128)(2,1)} %w_up.1, ...), custom_call_target="tpu_custom_call" | custom-call | tf_op jit(solution)/shard_map/keep/pallas_call | solution.py:448
  12.4 2.7 %collective-permute-done.refs_0_ = bf16[264,512]{1,0:T(8,128)(2,1)S(1)} collective-permute-done((bf16[264,512]{1,0:T(8,128)(2,1)}, bf16[264,512]{1,0:T(8,128)(2,1)S(1)}, u32[]{:S(2)}, u32[]{:S(2)}) %collective-permute-start) | collective-permute-done | bytes 270368 | tf_op jit(solution)/shard_map/ppermute | solution.py:509
  15.1 0.0 collective-permute-start.1
  15.2 0.0 collective-permute-start.7
  15.2 0.0 collective-permute-done.4.refs_3_
  15.2 0.0 collective-permute-done.3.refs_2_
  15.2 2.9 %project_own.1 = (bf16[4096,1024]{1,0:T(8,128)(2,1)S(1)}, bf16[512,512]{1,0:T(8,128)(2,1)S(1)}) custom-call(bf16[264,512]{1,0:T(8,128)(2,1)S(1)} %copy-done.9, bf16[256,512]{1,0:T(8,128)(2,1)S(1)} %copy-done.10, bf16[264,512]{1,0:T(8,128)(2,1)S(1)} %collective-permute-done.3.refs_2_, bf16[256,512]{1,0:T(8,128)(2,1)S(1)} %collective-permute-done.4.refs_3_, ...), custom_call_target="tpu_custom_call" | custom-call | flops 1073741824 | bytes 4718592 | tf_op jit(solution)/shard_map/project_own/pallas_call | solution.py:486
  18.1 2.6 %collective-permute-done.2.refs_1_ = bf16[256,512]{1,0:T(8,128)(2,1)S(1)} collective-permute-done((bf16[256,512]{1,0:T(8,128)(2,1)}, bf16[256,512]{1,0:T(8,128)(2,1)S(1)}, u32[]{:S(2)}, u32[]{:S(2)}) %collective-permute-start.2) | collective-permute-done | bytes 262176 | tf_op jit(solution)/shard_map/ppermute | solution.py:509
  20.8 0.0 collective-permute-start.8
  20.8 0.0 collective-permute-start.6
  20.8 1.3 %project.6.refs_4_ = bf16[4096,1024]{1,0:T(8,128)(2,1)S(1)} custom-call(bf16[264,512]{1,0:T(8,128)(2,1)S(1)} %collective-permute-done.refs_0_, bf16[256,512]{1,0:T(8,128)(2,1)S(1)} %collective-permute-done.2.refs_1_, f32[4,512]{1,0:T(4,128)S(1)} %get-tuple-element.34.refs_4_.refs_2_.gains, ...), custom_call_target="tpu_custom_call", output_to_operand_aliasing={{}: (4, {})} | custom-call | flops 536870912 | bytes 3145728 | tf_op jit(solution)/shard_map/project/pallas_call | solution.py:486
  22.1 0.0 copy-start.5
  22.1 3.6 %collective-permute-done.1.beyond.refs_0_ = bf16[264,512]{1,0:T(8,128)(2,1)S(1)} collective-permute-done((bf16[264,512]{1,0:T(8,128)(2,1)S(1)}, bf16[264,512]{1,0:T(8,128)(2,1)S(1)}, u32[]{:S(2)}, u32[]{:S(2)}) %collective-permute-start.1) | collective-permute-done | bytes 270368 | tf_op jit(solution)/shard_map/ppermute | solution.py:509
  25.7 0.9 collective-permute-start.5
  26.6 0.0 collective-permute-start.11
  26.6 0.0 collective-permute-done.8.refs_1_
  26.6 0.0 collective-permute-done.7.refs_0_
  26.6 1.3 %project.7.refs_4_ = bf16[4096,1024]{1,0:T(8,128)(2,1)S(1)} custom-call(bf16[264,512]{1,0:T(8,128)(2,1)S(1)} %collective-permute-done.7.refs_0_, bf16[256,512]{1,0:T(8,128)(2,1)S(1)} %collective-permute-done.8.refs_1_, f32[4,512]{1,0:T(4,128)S(1)} %get-tuple-element.34.refs_4_.refs_2_.gains, ...), custom_call_target="tpu_custom_call", output_to_operand_aliasing={{}: (4, {})} | custom-call | flops 536870912 | bytes 3145728 | tf_op jit(solution)/shard_map/project/pallas_call | solution.py:486
  27.9 3.8 %collective-permute-done.6.refs_1_ = bf16[256,512]{1,0:T(8,128)(2,1)S(1)} collective-permute-done((bf16[256,512]{1,0:T(8,128)(2,1)S(1)}, bf16[256,512]{1,0:T(8,128)(2,1)S(1)}, u32[]{:S(2)}, u32[]{:S(2)}) %collective-permute-start.6) | collective-permute-done | bytes 262176 | tf_op jit(solution)/shard_map/ppermute | solution.py:509
  31.7 0.0 collective-permute-start.12
  31.7 0.5 collective-permute-start.10
  32.2 0.6 index.1
  32.8 1.6 %project.8 = (bf16[4096,1024]{1,0:T(8,128)(2,1)S(1)}, bf16[512,512]{1,0:T(8,128)(2,1)S(1)}) custom-call(bf16[264,512]{1,0:T(8,128)(2,1)S(1)} %collective-permute-done.1.beyond.refs_0_, bf16[256,512]{1,0:T(8,128)(2,1)S(1)} %collective-permute-done.6.refs_1_, f32[4,512]{1,0:T(4,128)S(1)} %get-tuple-element.34.refs_4_.refs_2_.gains, ...), custom_call_target="tpu_custom_call", output_to_operand_aliasing={{0}: (4, {})} | custom-call | flops 536870912 | bytes 3145728 | tf_op jit(solution)/shard_map/project/pallas_call | solution.py:486
  34.4 3.0 %collective-permute-done.5.refs_0_ = bf16[264,512]{1,0:T(8,128)(2,1)S(1)} collective-permute-done((bf16[264,512]{1,0:T(8,128)(2,1)S(1)}, bf16[264,512]{1,0:T(8,128)(2,1)S(1)}, u32[]{:S(2)}, u32[]{:S(2)}) %collective-permute-start.5) | collective-permute-done | bytes 270368 | tf_op jit(solution)/shard_map/ppermute | solution.py:509
  37.5 0.0 collective-permute-start.9
  37.5 0.0 collective-permute-done.12.refs_1_
  37.5 0.0 collective-permute-done.11.refs_0_
  37.5 1.3 %project.9.refs_4_ = bf16[4096,1024]{1,0:T(8,128)(2,1)S(1)} custom-call(bf16[264,512]{1,0:T(8,128)(2,1)S(1)} %collective-permute-done.11.refs_0_, bf16[256,512]{1,0:T(8,128)(2,1)S(1)} %collective-permute-done.12.refs_1_, f32[4,512]{1,0:T(4,128)S(1)} %get-tuple-element.34.refs_4_.refs_2_.gains, ...), custom_call_target="tpu_custom_call", output_to_operand_aliasing={{}: (4, {})} | custom-call | flops 536870912 | bytes 3145728 | tf_op jit(solution)/shard_map/project/pallas_call | solution.py:486
  38.8 4.0 %collective-permute-done.10.refs_1_ = bf16[256,512]{1,0:T(8,128)(2,1)S(1)} collective-permute-done((bf16[256,512]{1,0:T(8,128)(2,1)S(1)}, bf16[256,512]{1,0:T(8,128)(2,1)S(1)}, u32[]{:S(2)}, u32[]{:S(2)}) %collective-permute-start.10) | collective-permute-done | bytes 262176 | tf_op jit(solution)/shard_map/ppermute | solution.py:509
  42.8 1.3 %project.10.refs_4_ = bf16[4096,1024]{1,0:T(8,128)(2,1)S(1)} custom-call(bf16[264,512]{1,0:T(8,128)(2,1)S(1)} %collective-permute-done.5.refs_0_, bf16[256,512]{1,0:T(8,128)(2,1)S(1)} %collective-permute-done.10.refs_1_, f32[4,512]{1,0:T(4,128)S(1)} %get-tuple-element.34.refs_4_.refs_2_.gains, ...), custom_call_target="tpu_custom_call", output_to_operand_aliasing={{}: (4, {})} | custom-call | flops 536870912 | bytes 3145728 | tf_op jit(solution)/shard_map/project/pallas_call | solution.py:486
  44.1 0.0 copy-start.2
  44.1 0.0 copy-start.6
  44.1 0.2 collective-permute-done.13.refs_1_
  44.3 1.3 %project.11.keyed = bf16[4096,1024]{1,0:T(8,128)(2,1)S(1)} custom-call(bf16[264,512]{1,0:T(8,128)(2,1)S(1)} %collective-permute-done.9.refs_0_, bf16[256,512]{1,0:T(8,128)(2,1)S(1)} %collective-permute-done.13.refs_1_, f32[4,512]{1,0:T(4,128)S(1)} %get-tuple-element.34.refs_4_.refs_2_.gains, ...), custom_call_target="tpu_custom_call", output_to_operand_aliasing={{}: (4, {})} | custom-call | flops 536870912 | bytes 3145728 | tf_op jit(solution)/shard_map/project/pallas_call | solution.py:486
  45.6 0.0 copy-start.1
  45.6 0.0 copy-start.4
  45.7 0.0 copy-start.7
  45.7 0.0 copy-start.8
  45.7 13.2 %block_first.1 = bf16[16,264,128]{2,1,0:T(8,128)(2,1)S(1)} custom-call(s32[3,8]{1,0:T(4,128)S(1)} %bitcast.6, s32[3,8]{1,0:T(4,128)S(1)} %get-tuple-element.40.pattern_beyond, s32[1,1024]{1,0:T(1,128)S(1)} %get-tuple-element.47.slot_of_row, f32[4,512]{1,0:T(4,128)S(1)} %get-tuple-element.34.refs_4_.refs_2_.gains, bf16[4096,1024]{1,0:T(8,128)(2,1)S(1)} %project.11.keyed, ...), custom_call_target="tpu_custom_call" | custom-call | tf_op jit(solution)/shard_map/block_first/pallas_call | solution.py:550
  58.9 20.3 %all_to_all.5.incoming = bf16[16,264,128]{2,1,0:T(8,128)(2,1)S(1)} all-to-all(bf16[16,264,128]{2,1,0:T(8,128)(2,1)S(1)} %block_first.1), channel_id=1, replica_groups=mesh['grp'=4,'half'=2,'seq'=4] {'grp','seq'}, dimensions={0} | all-to-all | bytes 2162688 | tf_op jit(solution)/shard_map/all_to_all | solution.py:577
  79.2 9.6 %block_second.1 = (bf16[512,512]{1,0:T(8,128)(2,1)}, f32[3,512]{1,0:T(4,128)}) custom-call(s32[3,8]{1,0:T(4,128)S(1)} %bitcast.7, f32[4,512]{1,0:T(4,128)S(1)} %copy-done.4, bf16[16,264,128]{2,1,0:T(8,128)(2,1)S(1)} %all_to_all.5.incoming, bf16[2,512,1536]{2,1,0:T(8,128)(2,1)} %w_qkv.1, bf16[2,512,512]{2,1,0:T(8,128)(2,1)S(1)} %copy-done.1, ...), custom_call_target="tpu_custom_call" | custom-call | tf_op jit(solution)/shard_map/block_second/pallas_call | solution.py:579
  (15 shorter events, 0.0 us)
Async XLA Ops:
  2.5 12.6 %collective-permute-start = (bf16[264,512]{1,0:T(8,128)(2,1)}, bf16[264,512]{1,0:T(8,128)(2,1)S(1)}, u32[]{:S(2)}, u32[]{:S(2)}) collective-permute-start(bf16[264,512]{1,0:T(8,128)(2,1)} %get-tuple-element.30.refs_0_), channel_id=1, source_target_pairs={{0,2},{1,3},{2,4},{3,5},{4,6},{5,7},{6,0},{7,1},{8,10},{9,11},{10,... | collective-permute-start | bytes 811016 | tf_op jit(solution)/shard_map/ppermute | solution.py:509
  5.6 9.6 %collective-permute-start.3 = (bf16[264,512]{1,0:T(8,128)(2,1)}, bf16[264,512]{1,0:T(8,128)(2,1)S(1)}, u32[]{:S(2)}, u32[]{:S(2)}) collective-permute-start(bf16[264,512]{1,0:T(8,128)(2,1)} %get-tuple-element.30.refs_0_), channel_id=1, source_target_pairs={{0,1},{1,0},{2,3},{3,2},{4,5},{5,4},{6,7},{7,6},{8,9},{9,8},{10,11... | collective-permute-start | bytes 811016 | tf_op jit(solution)/shard_map/ppermute | solution.py:506
  5.6 9.6 %collective-permute-start.4 = (bf16[256,512]{1,0:T(8,128)(2,1)}, bf16[256,512]{1,0:T(8,128)(2,1)S(1)}, u32[]{:S(2)}, u32[]{:S(2)}) collective-permute-start(bf16[256,512]{1,0:T(8,128)(2,1)} %get-tuple-element.33.refs_1_), channel_id=1, source_target_pairs={{0,1},{1,0},{2,3},{3,2},{4,5},{5,4},{6,7},{7,6},{8,9},{9,8},{10,11... | collective-permute-start | bytes 786440 | tf_op jit(solution)/shard_map/ppermute | solution.py:506
  6.1 14.7 %collective-permute-start.2 = (bf16[256,512]{1,0:T(8,128)(2,1)}, bf16[256,512]{1,0:T(8,128)(2,1)S(1)}, u32[]{:S(2)}, u32[]{:S(2)}) collective-permute-start(bf16[256,512]{1,0:T(8,128)(2,1)} %get-tuple-element.33.refs_1_), channel_id=1, source_target_pairs={{0,2},{1,3},{2,4},{3,5},{4,6},{5,7},{6,0},{7,1},{8,10},{9,11},{10,... | collective-permute-start | bytes 786440 | tf_op jit(solution)/shard_map/ppermute | solution.py:509
  7.7 1.2 %copy-start = (bf16[2,512,512]{2,1,0:T(8,128)(2,1)S(1)}, bf16[2,512,512]{2,1,0:T(8,128)(2,1)}, u32[]{:S(2)}) copy-start(bf16[2,512,512]{2,1,0:T(8,128)(2,1)} %w_proj.1) | copy-start | bytes 3145732
  8.9 0.7 copy-start.3
  9.6 5.6 %copy-start.9 = (bf16[264,512]{1,0:T(8,128)(2,1)S(1)}, bf16[264,512]{1,0:T(8,128)(2,1)}, u32[]{:S(2)}) copy-start(bf16[264,512]{1,0:T(8,128)(2,1)} %get-tuple-element.30.refs_0_) | copy-start | bytes 811012
  9.6 5.6 %copy-start.10 = (bf16[256,512]{1,0:T(8,128)(2,1)S(1)}, bf16[256,512]{1,0:T(8,128)(2,1)}, u32[]{:S(2)}) copy-start(bf16[256,512]{1,0:T(8,128)(2,1)} %get-tuple-element.33.refs_1_) | copy-start | bytes 786436
  15.1 10.6 %collective-permute-start.1 = (bf16[264,512]{1,0:T(8,128)(2,1)S(1)}, bf16[264,512]{1,0:T(8,128)(2,1)S(1)}, u32[]{:S(2)}, u32[]{:S(2)}) collective-permute-start(bf16[264,512]{1,0:T(8,128)(2,1)S(1)} %collective-permute-done.refs_0_), channel_id=1, source_target_pairs={{0,2},{1,3},{2,4},{3,5},{4,6},{5,7},{6,0},{7,1},{8,10},{9,11},{10,... | collective-permute-start | bytes 811016 | tf_op jit(solution)/shard_map/ppermute | solution.py:509
  15.2 11.4 %collective-permute-start.7 = (bf16[264,512]{1,0:T(8,128)(2,1)S(1)}, bf16[264,512]{1,0:T(8,128)(2,1)S(1)}, u32[]{:S(2)}, u32[]{:S(2)}) collective-permute-start(bf16[264,512]{1,0:T(8,128)(2,1)S(1)} %collective-permute-done.refs_0_), channel_id=1, source_target_pairs={{0,1},{1,0},{2,3},{3,2},{4,5},{5,4},{6,7},{7,6},{8,9},{9,8},{10,11... | collective-permute-start | bytes 811016 | tf_op jit(solution)/shard_map/ppermute | solution.py:526
  20.8 5.8 %collective-permute-start.8 = (bf16[256,512]{1,0:T(8,128)(2,1)S(1)}, bf16[256,512]{1,0:T(8,128)(2,1)S(1)}, u32[]{:S(2)}, u32[]{:S(2)}) collective-permute-start(bf16[256,512]{1,0:T(8,128)(2,1)S(1)} %collective-permute-done.2.refs_1_), channel_id=1, source_target_pairs={{0,1},{1,0},{2,3},{3,2},{4,5},{5,4},{6,7},{7,6},{8,9},{9,8},{10,11... | collective-permute-start | bytes 786440 | tf_op jit(solution)/shard_map/ppermute | solution.py:526
  20.8 10.9 %collective-permute-start.6 = (bf16[256,512]{1,0:T(8,128)(2,1)S(1)}, bf16[256,512]{1,0:T(8,128)(2,1)S(1)}, u32[]{:S(2)}, u32[]{:S(2)}) collective-permute-start(bf16[256,512]{1,0:T(8,128)(2,1)S(1)} %collective-permute-done.2.refs_1_), channel_id=1, source_target_pairs={{0,2},{1,3},{2,4},{3,5},{4,6},{5,7},{6,0},{7,1},{8,10},{9,11},{10,... | collective-permute-start | bytes 786440 | tf_op jit(solution)/shard_map/ppermute | solution.py:509
  22.1 10.1 %copy-start.5 = (s32[512]{0:T(512)S(1)}, s32[512]{0:T(512)}, u32[]{:S(2)}) copy-start(s32[512]{0:T(512)} %param.13) | copy-start | bytes 6148
  25.7 11.7 %collective-permute-start.5 = (bf16[264,512]{1,0:T(8,128)(2,1)S(1)}, bf16[264,512]{1,0:T(8,128)(2,1)S(1)}, u32[]{:S(2)}, u32[]{:S(2)}) collective-permute-start(bf16[264,512]{1,0:T(8,128)(2,1)S(1)} %collective-permute-done.1.beyond.refs_0_), channel_id=1, source_target_pairs={{0,2},{1,3},{2,4},{3,5},{4,6},{5,7},{6,0},{7,1},{8,10},{9,11},{10,... | collective-permute-start | bytes 811016 | tf_op jit(solution)/shard_map/ppermute | solution.py:509
  26.6 10.9 %collective-permute-start.11 = (bf16[264,512]{1,0:T(8,128)(2,1)S(1)}, bf16[264,512]{1,0:T(8,128)(2,1)S(1)}, u32[]{:S(2)}, u32[]{:S(2)}) collective-permute-start(bf16[264,512]{1,0:T(8,128)(2,1)S(1)} %collective-permute-done.1.beyond.refs_0_), channel_id=1, source_target_pairs={{0,1},{1,0},{2,3},{3,2},{4,5},{5,4},{6,7},{7,6},{8,9},{9,8},{10,11... | collective-permute-start | bytes 811016 | tf_op jit(solution)/shard_map/ppermute | solution.py:526
  31.7 5.8 %collective-permute-start.12 = (bf16[256,512]{1,0:T(8,128)(2,1)S(1)}, bf16[256,512]{1,0:T(8,128)(2,1)S(1)}, u32[]{:S(2)}, u32[]{:S(2)}) collective-permute-start(bf16[256,512]{1,0:T(8,128)(2,1)S(1)} %collective-permute-done.6.refs_1_), channel_id=1, source_target_pairs={{0,1},{1,0},{2,3},{3,2},{4,5},{5,4},{6,7},{7,6},{8,9},{9,8},{10,11... | collective-permute-start | bytes 786440 | tf_op jit(solution)/shard_map/ppermute | solution.py:526
  31.7 11.1 %collective-permute-start.10 = (bf16[256,512]{1,0:T(8,128)(2,1)S(1)}, bf16[256,512]{1,0:T(8,128)(2,1)S(1)}, u32[]{:S(2)}, u32[]{:S(2)}) collective-permute-start(bf16[256,512]{1,0:T(8,128)(2,1)S(1)} %collective-permute-done.6.refs_1_), channel_id=1, source_target_pairs={{0,2},{1,3},{2,4},{3,5},{4,6},{5,7},{6,0},{7,1},{8,10},{9,11},{10,... | collective-permute-start | bytes 786440 | tf_op jit(solution)/shard_map/ppermute | solution.py:509
  37.5 6.8 %collective-permute-start.9 = (bf16[264,512]{1,0:T(8,128)(2,1)S(1)}, bf16[264,512]{1,0:T(8,128)(2,1)S(1)}, u32[]{:S(2)}, u32[]{:S(2)}) collective-permute-start(bf16[264,512]{1,0:T(8,128)(2,1)S(1)} %collective-permute-done.5.refs_0_), channel_id=1, source_target_pairs={{0,1},{1,0},{2,3},{3,2},{4,5},{5,4},{6,7},{7,6},{8,9},{9,8},{10,11... | collective-permute-start | bytes 811016 | tf_op jit(solution)/shard_map/ppermute | solution.py:526
  42.8 1.5 %collective-permute-start.13 = (bf16[256,512]{1,0:T(8,128)(2,1)S(1)}, bf16[256,512]{1,0:T(8,128)(2,1)S(1)}, u32[]{:S(2)}, u32[]{:S(2)}) collective-permute-start(bf16[256,512]{1,0:T(8,128)(2,1)S(1)} %collective-permute-done.10.refs_1_), channel_id=1, source_target_pairs={{0,1},{1,0},{2,3},{3,2},{4,5},{5,4},{6,7},{7,6},{8,9},{9,8},{10,11... | collective-permute-start | bytes 786440 | tf_op jit(solution)/shard_map/ppermute | solution.py:526
  44.1 1.5 %copy-start.2 = (bf16[512,512]{1,0:T(8,128)(2,1)S(1)}, bf16[512,512]{1,0:T(8,128)(2,1)}, u32[]{:S(2)}) copy-start(bf16[512,512]{1,0:T(8,128)(2,1)} %points.3) | copy-start | bytes 1572868
  44.1 1.5 %copy-start.6 = (s32[8,3]{0,1:T(4,128)S(1)}, s32[8,3]{0,1:T(4,128)}, u32[]{:S(2)}) copy-start(s32[8,3]{0,1:T(4,128)} %param.11) | copy-start | bytes 292
  45.6 33.6 %copy-start.1 = (bf16[2,512,512]{2,1,0:T(8,128)(2,1)S(1)}, bf16[2,512,512]{2,1,0:T(8,128)(2,1)}, u32[]{:S(2)}) copy-start(bf16[2,512,512]{2,1,0:T(8,128)(2,1)} %w_proj.1) | copy-start | bytes 3145732
  45.6 33.6 %copy-start.4 = (f32[4,512]{1,0:T(4,128)S(1)}, f32[4,512]{1,0:T(4,128)}, u32[]{:S(2)}) copy-start(f32[4,512]{1,0:T(4,128)} %gains.1) | copy-start | bytes 24580
  45.7 33.5 %copy-start.7 = (bf16[3,512]{1,0:T(4,128)(2,1)S(1)}, bf16[3,512]{1,0:T(4,128)(2,1)}, u32[]{:S(2)}) copy-start(bf16[3,512]{1,0:T(4,128)(2,1)} %w_head.1) | copy-start | bytes 9220
  45.7 33.5 %copy-start.8 = (s32[8,3]{0,1:T(4,128)S(1)}, s32[8,3]{0,1:T(4,128)}, u32[]{:S(2)}) copy-start(s32[8,3]{0,1:T(4,128)} %param.12) | copy-start | bytes 292

commit v9 on v8

--- a/solution.py
+++ b/solution.py
@@ -41,34 +41,44 @@
 def head_masks(head_dim):
     lane = lax.broadcasted_iota(jnp.int32, (PATCH, HEADS_TOGETHER * head_dim), 1)
     return [
-        jnp.where((lane >= h * head_dim) & (lane < (h + 1) * head_dim), 1.0, 0.0).astype(F32)
+        jnp.where((lane >= h * head_dim) & (lane < (h + 1) * head_dim), 1.0, 0.0).astype(BF16)
         for h in range(HEADS_TOGETHER)
     ]
 
 
-def attend_patch(queries, key_rows, value_rows, masks):
-    channels = queries.shape[1]
-    width = HEADS_TOGETHER * (channels // HEADS)
-    sides = []
-    for at in range(0, channels, width):
-        q = queries[:, at : at + width]
-        stacked = jnp.concatenate([q * mask.astype(BF16) for mask in masks], axis=0)
-        scores = lax.dot_general(
-            stacked,
-            key_rows[:, at : at + width],
-            (((1,), (1,)), ((), ())),
-            preferred_element_type=F32,
+def attend(patches, head_dim):
+    masks = head_masks(head_dim)
+    width = HEADS_TOGETHER * head_dim
+    heads_per_tile = LANES // head_dim
+    lane = lax.broadcasted_iota(jnp.int32, (PATCH, LANES), 1)
+    steps = [(p, g) for p in range(len(patches)) for g in range(HEADS // HEADS_TOGETHER)]
+
+    def scores_of(step):
+        p, g = step
+        queries, keys, _ = patches[p]
+        q = queries(g * width, width)
+        stacked = jnp.concatenate([q * mask for mask in masks], axis=0)
+        return lax.dot_general(
+            stacked, keys(g * width, width), (((1,), (1,)), ((), ())), preferred_element_type=F32
         )
-        top = jnp.max(scores, axis=-1, keepdims=True)
-        grown = jnp.exp(scores - top)
-        total = jnp.sum(grown, axis=-1, keepdims=True)
-        weights = (grown * (1.0 / total)).astype(BF16)
-        mixed = jnp.dot(weights, value_rows[:, at : at + width], preferred_element_type=F32)
-        side = mixed[:PATCH] * masks[0]
-        for h in range(1, HEADS_TOGETHER):
-            side = side + mixed[h * PATCH : (h + 1) * PATCH] * masks[h]
-        sides.append(side.astype(BF16))
-    return jnp.concatenate(sides, axis=1)
+
+    scores = scores_of(steps[0])
+    for i, (p, g) in enumerate(steps):
+        later = scores_of(steps[i + 1]) if i + 1 < len(steps) else None
+        grown = jnp.exp(scores - jnp.max(scores, axis=-1, keepdims=True))
+        scale = 1.0 / jnp.sum(grown, axis=-1, keepdims=True)
+        values = patches[p][2](g * width, width)
+        mixed = jnp.dot(grown.astype(BF16), values, preferred_element_type=F32)
+        tiles = []
+        for t in range(width // LANES):
+            tile = None
+            for h in range(heads_per_tile):
+                rows = slice((t * heads_per_tile + h) * PATCH, (t * heads_per_tile + h + 1) * PATCH)
+                head = mixed[rows, t * LANES : (t + 1) * LANES] * scale[rows]
+                tile = head if tile is None else jnp.where(lane < h * head_dim, tile, head)
+            tiles.append(tile)
+        yield p, g * width, jnp.concatenate(tiles, axis=1).astype(BF16)
+        scores = later
 
 
 def one_hot_rows(places, rows):
@@ -98,10 +108,17 @@
     for copy in copies[1:]:
         copy.wait()
     piece = 512
-    for at in range(0, w_up.shape[1], piece):
-        upper = jnp.dot(hidden, w_up[:, at : at + piece], preferred_element_type=F32)
+    pieces = range(0, w_up.shape[1], piece)
+    upper = jnp.dot(hidden, w_up[:, :piece], preferred_element_type=F32)
+    for at in pieces:
+        later = None
+        if at + piece < w_up.shape[1]:
+            later = jnp.dot(
+                hidden, w_up[:, at + piece : at + 2 * piece], preferred_element_type=F32
+            )
         act = gelu(upper).astype(BF16)
         total = total + jnp.dot(act, w_down[at : at + piece, :], preferred_element_type=F32)
+        upper = later
     return total.astype(BF16)
 
 
@@ -214,6 +231,19 @@
             refs[1][i * rows : (i + 1) * rows, :] = (query * scale).astype(BF16)
 
 
+def loads(queries, p, keyed, starts):
+    channels = queries.shape[1]
+
+    def asked(at, width):
+        return queries[p * PATCH : (p + 1) * PATCH, at : at + width]
+
+    def keys(at, width):
+        pieces = [keyed[pl.ds(start, PATCH), at : at + width] for start in starts]
+        return jnp.concatenate(pieces, axis=0)
+
+    return asked, keys, lambda at, width: keys(channels + at, width)
+
+
 def lane_tiles(packed, rows):
     capacity, channels = rows.shape[1:]
     return [
@@ -257,29 +287,23 @@
         ],
         sems.at[0],
     )
-    masks = head_masks(channels // HEADS)
     blocks = ((pattern, queries, 0), (pattern_beyond, queries_beyond, ring_chips or 1))
+    loaded = []
     for b, (picked, asking, own_slot) in enumerate(blocks):
         for p in range(patches):
-            start = own_slot * rows + p * PATCH
-            pieces = [keyed[start : start + PATCH, :]]
+            starts = [own_slot * rows + p * PATCH]
             for j in range(chosen):
                 if ring_chips:
                     patch = picked[j, p]
                     owner, local = lax.div(patch, patches), lax.rem(patch, patches)
                     chip = lax.rem(lax.div(me, 2) - lax.div(owner, 2) + ring_chips, ring_chips)
                     slot = 2 * chip + jnp.where(lax.rem(me, 2) == lax.rem(owner, 2), 0, 1)
-                    patch = slot * patches + local
+                    starts.append(pl.multiple_of((slot * patches + local) * PATCH, PATCH))
                 else:
-                    patch = 2 * patches + (b * patches + p) * chosen + j
-                start = patch * PATCH
-                if ring_chips:
-                    start = pl.multiple_of(start, PATCH)
-                pieces.append(keyed[pl.ds(start, PATCH), :])
-            both = jnp.concatenate(pieces, axis=0)
-            attended[b * rows + p * PATCH : b * rows + (p + 1) * PATCH, :] = attend_patch(
-                asking[p * PATCH : (p + 1) * PATCH, :], both[:, :channels], both[:, channels:], masks
-            )
+                    starts.append((2 * patches + (b * patches + p) * chosen + j) * PATCH)
+            loaded.append(loads(asking, p, keyed, starts))
+    for p, at, rows_done in attend(loaded, channels // HEADS):
+        attended[p * PATCH : (p + 1) * PATCH, at : at + rows_done.shape[1]] = rows_done
     for copy in copies[1:]:
         copy.wait()
 
@@ -318,6 +342,7 @@
     features,
     normals,
     kv,
+    queries,
     attended,
     incoming_held,
     qkv_held,
@@ -360,28 +385,26 @@
         pieces.append(code)
     places = jnp.concatenate(pieces, axis=1).astype(jnp.int32) - 1
     place = one_hot_rows(places, rows)
-    for copy in landing:
-        copy.wait()
-    moved = incoming_held[...].reshape(devices * capacity, channels)
-    second = jnp.dot(place, moved, preferred_element_type=F32).astype(BF16)
+    sides = []
+    for at in range(0, len(landing), 2):
+        for copy in landing[at : at + 2]:
+            copy.wait()
+        moved = incoming_held[:, :, at * LANES : (at + 2) * LANES]
+        moved = moved.reshape(devices * capacity, 2 * LANES)
+        sides.append(jnp.dot(place, moved, preferred_element_type=F32).astype(BF16))
+    second = jnp.concatenate(sides, axis=1)
     normed = layer_norm(second, gains_held[2:3, :])
     scale = (channels // HEADS) ** (-0.5)
     copies[0].wait()
-    queries = (
-        jnp.dot(normed, qkv_held[:, :channels], preferred_element_type=F32).astype(BF16)
-        * BF16(scale)
-    ).astype(BF16)
+    asked = jnp.dot(normed, qkv_held[:, :channels], preferred_element_type=F32).astype(BF16)
+    queries[...] = (asked * BF16(scale)).astype(BF16)
     kv[...] = jnp.dot(normed, qkv_held[:, channels:], preferred_element_type=F32).astype(BF16)
-    masks = head_masks(channels // HEADS)
+    loaded = []
     for p in range(patches):
-        pieces = [kv[p * PATCH : (p + 1) * PATCH, :]]
-        for j in range(chosen):
-            start = pl.multiple_of(pattern[j, p] * PATCH, PATCH)
-            pieces.append(kv[pl.ds(start, PATCH), :])
-        both = jnp.concatenate(pieces, axis=0)
-        attended[p * PATCH : (p + 1) * PATCH, :] = attend_patch(
-            queries[p * PATCH : (p + 1) * PATCH, :], both[:, :channels], both[:, channels:], masks
-        )
+        starts = [pl.multiple_of(pattern[j, p] * PATCH, PATCH) for j in range(chosen)]
+        loaded.append(loads(queries, p, kv, [p * PATCH] + starts))
+    for p, at, rows_done in attend(loaded, channels // HEADS):
+        attended[p * PATCH : (p + 1) * PATCH, at : at + rows_done.shape[1]] = rows_done
     done = finish(
         second, attended[...], gains_held[3:4, :], (proj_held, up_held, down_held), copies[1:]
     )
@@ -477,10 +500,12 @@
         )(destination, beyond)
 
     def project(keyed, blocks, ask=False, rows=part):
-        parts = [piece for _, block in blocks for piece in block]
+        parts = [piece for _, _, block in blocks for piece in block]
         count = len(parts)
         first_rows = [
-            slot * rows_here + i * rows for slot, block in blocks for i in range(len(block))
+            slot * rows_here + first + i * rows
+            for slot, first, block in blocks
+            for i in range(len(block))
         ]
         new = keyed is None
         return pl.pallas_call(
@@ -504,7 +529,7 @@
 
     if ring:
         beside = [lax.ppermute(rows, GROUP, swap) for rows in column]
-        waiting = [(0, column), (1, beside)]
+        waiting = [(0, 0, column), (1, 0, beside)]
         for step in range(1, chips):
             column = [lax.ppermute(rows, GROUP, onward) for rows in column]
             if step == 1:
@@ -524,9 +549,14 @@
             if step == chips - 1:
                 column[0], slot_index = lax.optimization_barrier((column[0], slot_index))
             beside = [lax.ppermute(rows, GROUP, swap) for rows in column]
-            waiting = [(2 * step, column), (2 * step + 1, beside)]
-        for block in waiting:
-            (keyed,) = project(keyed, [block])
+            waiting = [(2 * step, 0, column), (2 * step + 1, 0, beside)]
+        for i in range(RING_PARTS):
+            halves = [(slot, i * part, block[i : i + 1]) for slot, _, block in waiting]
+            if i + 1 < RING_PARTS:
+                (keyed,) = project(keyed, halves)
+            else:
+                for half in halves:
+                    (keyed,) = project(keyed, [half])
     else:
         group = lax.all_gather(points, GROUP, axis=0, tiled=True)
         partner = lax.rem(lax.axis_index(GROUP) + chips, shards_in_group)
@@ -537,10 +567,10 @@
             group[pattern.T].reshape(-1, channels) for pattern in (pattern_first, pattern_beyond)
         ]
         wide = picked[0].shape[0]
-        keyed, queries = project(None, [(0, column)], ask=True)
-        keyed, queries_beyond = project(keyed, [(1, points_beyond)], ask=True, rows=rows_here)
-        (keyed,) = project(keyed, [(2, [picked[0]])], rows=wide)
-        (keyed,) = project(keyed, [(2 + chosen, [picked[1]])], rows=wide)
+        keyed, queries = project(None, [(0, 0, column)], ask=True)
+        keyed, queries_beyond = project(keyed, [(1, 0, points_beyond)], ask=True, rows=rows_here)
+        (keyed,) = project(keyed, [(2, 0, [picked[0]])], rows=wide)
+        (keyed,) = project(keyed, [(2 + chosen, 0, [picked[1]])], rows=wide)
 
     held_weights = [pltpu.VMEM(w.shape[1:], BF16) for w in weights]
     held_rows = pltpu.VMEM((rows_here, channels), BF16)
@@ -587,6 +617,7 @@
         scratch_shapes=[
             pltpu.VMEM((rows_here, 2 * channels), BF16),
             held_rows,
+            held_rows,
             held_slots,
             pltpu.VMEM(w_qkv.shape[1:], BF16),
             *held_weights,

time: 89.3 us -> 88 us (0.985)
  Pallas kernels: 39.2 us -> 37.6 us
    pallas_call x1, Pallas kernels: 13.2 us -> 12 us  [shards(): pl.pallas_call(functools.partial(first_kernel, chips if ring else 0), out...]
    pallas_call x7 -> x8, Pallas kernels: 11.1 us -> 11.1 us  [project(): pl.pallas_call(functools.partial(project_kernel, first_rows, new, ask), o...]
  transfers between devices with their start and end apart: 14 -> 14, of which waited for: 7 -> 6; matrix products, arithmetic and copies ran while one was open for 0% -> 0% of each run, Pallas kernels for 15% -> 16%
where the time goes in v9:
time: 88 us; the launch traced here: 87.7 us
  Pallas kernels  37.6 us (43%)
  blocking collectives  20.4 us (23%)
  waiting for transfers between devices  19.7 us (22%)
  starting transfers between devices  6.65 us (8%)
  local copies, waits for them, and re-layouts  2.31 us (3%)
  between operations  1 us (1%)
    all_to_all x1, blocking collectives, shards(): lax.all_to_all(outgoing, ('grp', 'seq'), split_axis=0, concat_axis=0, til...  20.4 us
    ppermute x6, waiting for transfers between devices, shards(): column = [lax.ppermute(rows, GROUP, onward) for rows in column]  19.7 us
    pallas_call x1, Pallas kernels, shards(): pl.pallas_call(functools.partial(first_kernel, chips if ring else 0), out...  12 us
    pallas_call x8, Pallas kernels, project(): pl.pallas_call(functools.partial(project_kernel, first_rows, new, ask), o...  11.1 us
    pallas_call x1, Pallas kernels, shards(): pl.pallas_call(second_kernel, out_shape=(jax.ShapeDtypeStruct((rows_here,...  9.26 us
    ppermute x6, starting transfers between devices, shards(): column = [lax.ppermute(rows, GROUP, onward) for rows in column]  6.12 us
    pallas_call x1, Pallas kernels, shards(): pl.pallas_call(keep_kernel, out_shape=[*[jax.ShapeDtypeStruct(w.shape[1:]...  2.8 us
    unnamed x22, local copies, waits for them, and re-layouts  2.31 us
  transfers between devices with their start and end apart: 14, of which 6 were waited for; matrix products, arithmetic and copies ran while one was open for 0% of the time, Pallas kernels for 16%

profile of v9, /device:TPU:0, one launch (start us, length us, event | category | flops | bytes accessed | tf_op | source)
XLA Modules:
  0.0 87.7 jit_solution(9123449717276197766)
XLA Ops:
  0.6 1.9 %split.1 = (bf16[264,512]{1,0:T(8,128)(2,1)}, bf16[256,512]{1,0:T(8,128)(2,1)}) custom-call(bf16[512,512]{1,0:T(8,128)(2,1)} %points.3, s32[1,512]{1,0:T(1,128)} %bitcast.3, s32[3,8]{1,0:T(4,128)} %bitcast.5), custom_call_target="tpu_custom_call" | custom-call | tf_op jit(solution)/shard_map/split/pallas_call | solution.py:452
  2.5 3.1 %collective-permute-start = (bf16[264,512]{1,0:T(8,128)(2,1)}, bf16[264,512]{1,0:T(8,128)(2,1)S(1)}, u32[]{:S(2)}, u32[]{:S(2)}) collective-permute-start(bf16[264,512]{1,0:T(8,128)(2,1)} %get-tuple-element.30.refs_0_), channel_id=1, source_target_pairs={{0,2},{1,3},{2,4},{3,5},{4,6},{5,7},{6,0},{7,1},{8,10},{9,11},{10,... | collective-permute-start | bytes 811016 | tf_op jit(solution)/shard_map/ppermute | solution.py:534
  5.6 0.0 collective-permute-start.3
  5.6 0.5 collective-permute-start.4
  6.1 1.6 %collective-permute-start.2 = (bf16[256,512]{1,0:T(8,128)(2,1)}, bf16[256,512]{1,0:T(8,128)(2,1)S(1)}, u32[]{:S(2)}, u32[]{:S(2)}) collective-permute-start(bf16[256,512]{1,0:T(8,128)(2,1)} %get-tuple-element.33.refs_1_), channel_id=1, source_target_pairs={{0,2},{1,3},{2,4},{3,5},{4,6},{5,7},{6,0},{7,1},{8,10},{9,11},{10,... | collective-permute-start | bytes 786440 | tf_op jit(solution)/shard_map/ppermute | solution.py:534
  7.7 1.2 %copy-done = bf16[2,512,512]{2,1,0:T(8,128)(2,1)S(1)} copy-done((bf16[2,512,512]{2,1,0:T(8,128)(2,1)S(1)}, bf16[2,512,512]{2,1,0:T(8,128)(2,1)}, u32[]{:S(2)}) %copy-start) | copy-done | bytes 1048600
  8.9 0.7 copy-done.3
  9.6 2.8 %keep.1 = (bf16[512,1536]{1,0:T(8,128)(2,1)S(1)}, bf16[512,512]{1,0:T(8,128)(2,1)S(1)}, bf16[512,2048]{1,0:T(8,128)(2,1)S(1)}, bf16[2048,512]{1,0:T(8,128)(2,1)S(1)}, f32[4,512]{1,0:T(4,128)S(1)}) custom-call(bf16[2,512,1536]{2,1,0:T(8,128)(2,1)} %w_qkv.1, bf16[2,512,512]{2,1,0:T(8,128)(2,1)S(1)} %copy-done, bf16[2,512,2048]{2,1,0:T(8,128)(2,1)} %w_up.1, ...), custom_call_target="tpu_custom_call" | custom-call | tf_op jit(solution)/shard_map/keep/pallas_call | solution.py:471
  12.4 2.7 %collective-permute-done.refs_0_ = bf16[264,512]{1,0:T(8,128)(2,1)S(1)} collective-permute-done((bf16[264,512]{1,0:T(8,128)(2,1)}, bf16[264,512]{1,0:T(8,128)(2,1)S(1)}, u32[]{:S(2)}, u32[]{:S(2)}) %collective-permute-start) | collective-permute-done | bytes 270368 | tf_op jit(solution)/shard_map/ppermute | solution.py:534
  15.1 0.0 collective-permute-start.1
  15.2 0.0 collective-permute-start.7
  15.2 0.0 collective-permute-done.4.refs_3_
  15.2 0.0 collective-permute-done.3.refs_2_
  15.2 2.9 %project_own.1 = (bf16[4096,1024]{1,0:T(8,128)(2,1)S(1)}, bf16[512,512]{1,0:T(8,128)(2,1)S(1)}) custom-call(bf16[264,512]{1,0:T(8,128)(2,1)S(1)} %copy-done.9, bf16[256,512]{1,0:T(8,128)(2,1)S(1)} %copy-done.10, bf16[264,512]{1,0:T(8,128)(2,1)S(1)} %collective-permute-done.3.refs_2_, bf16[256,512]{1,0:T(8,128)(2,1)S(1)} %collective-permute-done.4.refs_3_, ...), custom_call_target="tpu_custom_call" | custom-call | flops 1073741824 | bytes 4718592 | tf_op jit(solution)/shard_map/project_own/pallas_call | solution.py:511
  18.1 2.6 %collective-permute-done.2.refs_1_ = bf16[256,512]{1,0:T(8,128)(2,1)S(1)} collective-permute-done((bf16[256,512]{1,0:T(8,128)(2,1)}, bf16[256,512]{1,0:T(8,128)(2,1)S(1)}, u32[]{:S(2)}, u32[]{:S(2)}) %collective-permute-start.2) | collective-permute-done | bytes 262176 | tf_op jit(solution)/shard_map/ppermute | solution.py:534
  20.8 0.0 collective-permute-start.8
  20.8 0.0 collective-permute-start.6
  20.8 1.3 %project.7.refs_4_ = bf16[4096,1024]{1,0:T(8,128)(2,1)S(1)} custom-call(bf16[264,512]{1,0:T(8,128)(2,1)S(1)} %collective-permute-done.refs_0_, bf16[256,512]{1,0:T(8,128)(2,1)S(1)} %collective-permute-done.2.refs_1_, f32[4,512]{1,0:T(4,128)S(1)} %get-tuple-element.34.refs_4_.refs_2_.refs_1_.gains, ...), custom_call_target="tpu_custom_call", output_to_operand_aliasing={{}: (4, {})} | custom-call | flops 536870912 | bytes 3145728 | tf_op jit(solution)/shard_map/project/pallas_call | solution.py:511
  22.1 0.0 copy-start.5
  22.1 3.6 %collective-permute-done.1.beyond.refs_0_ = bf16[264,512]{1,0:T(8,128)(2,1)S(1)} collective-permute-done((bf16[264,512]{1,0:T(8,128)(2,1)S(1)}, bf16[264,512]{1,0:T(8,128)(2,1)S(1)}, u32[]{:S(2)}, u32[]{:S(2)}) %collective-permute-start.1) | collective-permute-done | bytes 270368 | tf_op jit(solution)/shard_map/ppermute | solution.py:534
  25.7 0.9 collective-permute-start.5
  26.6 0.0 collective-permute-start.10
  26.6 0.0 collective-permute-done.8.refs_1_
  26.6 0.0 collective-permute-done.7.refs_0_
  26.6 1.3 %project.8.refs_4_ = bf16[4096,1024]{1,0:T(8,128)(2,1)S(1)} custom-call(bf16[264,512]{1,0:T(8,128)(2,1)S(1)} %collective-permute-done.7.refs_0_, bf16[256,512]{1,0:T(8,128)(2,1)S(1)} %collective-permute-done.8.refs_1_, f32[4,512]{1,0:T(4,128)S(1)} %get-tuple-element.34.refs_4_.refs_2_.refs_1_.gains, ...), custom_call_target="tpu_custom_call", output_to_operand_aliasing={{}: (4, {})} | custom-call | flops 536870912 | bytes 3145728 | tf_op jit(solution)/shard_map/project/pallas_call | solution.py:511
  27.9 3.8 %collective-permute-done.6.refs_1_ = bf16[256,512]{1,0:T(8,128)(2,1)S(1)} collective-permute-done((bf16[256,512]{1,0:T(8,128)(2,1)S(1)}, bf16[256,512]{1,0:T(8,128)(2,1)S(1)}, u32[]{:S(2)}, u32[]{:S(2)}) %collective-permute-start.6) | collective-permute-done | bytes 262176 | tf_op jit(solution)/shard_map/ppermute | solution.py:534
  31.7 0.0 collective-permute-start.11
  31.7 0.5 collective-permute-start.9
  32.2 0.6 index.1
  32.8 1.6 %project.9 = (bf16[4096,1024]{1,0:T(8,128)(2,1)S(1)}, bf16[512,512]{1,0:T(8,128)(2,1)S(1)}) custom-call(bf16[264,512]{1,0:T(8,128)(2,1)S(1)} %collective-permute-done.1.beyond.refs_0_, bf16[256,512]{1,0:T(8,128)(2,1)S(1)} %collective-permute-done.6.refs_1_, ...), custom_call_target="tpu_custom_call", output_to_operand_aliasing={{0}: (4, {})} | custom-call | flops 536870912 | bytes 3145728 | tf_op jit(solution)/shard_map/project/pallas_call | solution.py:511
  34.4 3.0 %collective-permute-done.5.refs_0_ = bf16[264,512]{1,0:T(8,128)(2,1)S(1)} collective-permute-done((bf16[264,512]{1,0:T(8,128)(2,1)S(1)}, bf16[264,512]{1,0:T(8,128)(2,1)S(1)}, u32[]{:S(2)}, u32[]{:S(2)}) %collective-permute-start.5) | collective-permute-done | bytes 270368 | tf_op jit(solution)/shard_map/ppermute | solution.py:534
  37.5 0.0 collective-permute-start.13
  37.5 0.0 collective-permute-done.11.refs_1_
  37.5 0.0 collective-permute-done.10.refs_0_
  37.5 1.3 %project.10.refs_4_ = bf16[4096,1024]{1,0:T(8,128)(2,1)S(1)} custom-call(bf16[264,512]{1,0:T(8,128)(2,1)S(1)} %collective-permute-done.10.refs_0_, bf16[256,512]{1,0:T(8,128)(2,1)S(1)} %collective-permute-done.11.refs_1_, f32[4,512]{1,0:T(4,128)S(1)} %get-tuple-element.34.refs_4_.refs_2_.refs_1_.gains, ...), custom_call_target="tpu_custom_call", output_to_operand_aliasing={{}: (4, {})} | custom-call | flops 536870912 | bytes 3145728 | tf_op jit(solution)/shard_map/project/pallas_call | solution.py:511
  38.8 4.0 %collective-permute-done.9.refs_0_ = bf16[256,512]{1,0:T(8,128)(2,1)S(1)} collective-permute-done((bf16[256,512]{1,0:T(8,128)(2,1)S(1)}, bf16[256,512]{1,0:T(8,128)(2,1)S(1)}, u32[]{:S(2)}, u32[]{:S(2)}) %collective-permute-start.9) | collective-permute-done | bytes 262176 | tf_op jit(solution)/shard_map/ppermute | solution.py:534
  42.8 0.0 collective-permute-start.12
  42.8 1.3 %project.11.refs_3_ = bf16[4096,1024]{1,0:T(8,128)(2,1)S(1)} custom-call(bf16[264,512]{1,0:T(8,128)(2,1)S(1)} %collective-permute-done.5.refs_0_, bf16[264,512]{1,0:T(8,128)(2,1)S(1)} %collective-permute-done.13.refs_1_, f32[4,512]{1,0:T(4,128)S(1)} %get-tuple-element.34.refs_4_.refs_2_.refs_1_.gains, ...), custom_call_target="tpu_custom_call", output_to_operand_aliasing={{}: (4, {})} | custom-call | flops 536870912 | bytes 3145728 | tf_op jit(solution)/shard_map/project/pallas_call | solution.py:511
  44.1 0.7 project.12.refs_3_
  44.7 0.0 copy-start.2
  44.8 0.0 copy-start.6
  44.8 0.0 collective-permute-done.12.refs_0_
  44.8 0.7 project.13.keyed
  45.4 0.3 copy-done.2
  45.8 0.0 copy-start.8
  45.8 12.0 %block_first.1 = bf16[16,264,128]{2,1,0:T(8,128)(2,1)S(1)} custom-call(s32[3,8]{1,0:T(4,128)S(1)} %bitcast.6, s32[3,8]{1,0:T(4,128)S(1)} %get-tuple-element.40.pattern_beyond, s32[1,1024]{1,0:T(1,128)S(1)} %get-tuple-element.47.slot_of_row, f32[4,512]{1,0:T(4,128)S(1)} %get-tuple-element.34.refs_4_.refs_2_.refs_1_.gains, ...), custom_call_target="tpu_custom_call" | custom-call | tf_op jit(solution)/shard_map/block_first/pallas_call | solution.py:580
  57.8 20.4 %all_to_all.5.incoming = bf16[16,264,128]{2,1,0:T(8,128)(2,1)S(1)} all-to-all(bf16[16,264,128]{2,1,0:T(8,128)(2,1)S(1)} %block_first.1), channel_id=1, replica_groups=mesh['grp'=4,'half'=2,'seq'=4] {'grp','seq'}, dimensions={0} | all-to-all | bytes 2162688 | tf_op jit(solution)/shard_map/all_to_all | solution.py:607
  78.2 9.3 %block_second.1 = (bf16[512,512]{1,0:T(8,128)(2,1)}, f32[3,512]{1,0:T(4,128)}) custom-call(s32[3,8]{1,0:T(4,128)S(1)} %bitcast.7, f32[4,512]{1,0:T(4,128)S(1)} %copy-done.4, bf16[16,264,128]{2,1,0:T(8,128)(2,1)S(1)} %all_to_all.5.incoming, bf16[2,512,1536]{2,1,0:T(8,128)(2,1)} %w_qkv.1, bf16[2,512,512]{2,1,0:T(8,128)(2,1)S(1)} %copy-done.1, ...), custom_call_target="tpu_custom_call" | custom-call | tf_op jit(solution)/shard_map/block_second/pallas_call | solution.py:609
  (16 shorter events, 0.0 us)
Async XLA Ops:
  2.5 12.6 %collective-permute-start = (bf16[264,512]{1,0:T(8,128)(2,1)}, bf16[264,512]{1,0:T(8,128)(2,1)S(1)}, u32[]{:S(2)}, u32[]{:S(2)}) collective-permute-start(bf16[264,512]{1,0:T(8,128)(2,1)} %get-tuple-element.30.refs_0_), channel_id=1, source_target_pairs={{0,2},{1,3},{2,4},{3,5},{4,6},{5,7},{6,0},{7,1},{8,10},{9,11},{10,... | collective-permute-start | bytes 811016 | tf_op jit(solution)/shard_map/ppermute | solution.py:534
  5.6 9.6 %collective-permute-start.3 = (bf16[264,512]{1,0:T(8,128)(2,1)}, bf16[264,512]{1,0:T(8,128)(2,1)S(1)}, u32[]{:S(2)}, u32[]{:S(2)}) collective-permute-start(bf16[264,512]{1,0:T(8,128)(2,1)} %get-tuple-element.30.refs_0_), channel_id=1, source_target_pairs={{0,1},{1,0},{2,3},{3,2},{4,5},{5,4},{6,7},{7,6},{8,9},{9,8},{10,11... | collective-permute-start | bytes 811016 | tf_op jit(solution)/shard_map/ppermute | solution.py:531
  5.6 9.6 %collective-permute-start.4 = (bf16[256,512]{1,0:T(8,128)(2,1)}, bf16[256,512]{1,0:T(8,128)(2,1)S(1)}, u32[]{:S(2)}, u32[]{:S(2)}) collective-permute-start(bf16[256,512]{1,0:T(8,128)(2,1)} %get-tuple-element.33.refs_1_), channel_id=1, source_target_pairs={{0,1},{1,0},{2,3},{3,2},{4,5},{5,4},{6,7},{7,6},{8,9},{9,8},{10,11... | collective-permute-start | bytes 786440 | tf_op jit(solution)/shard_map/ppermute | solution.py:531
  6.1 14.7 %collective-permute-start.2 = (bf16[256,512]{1,0:T(8,128)(2,1)}, bf16[256,512]{1,0:T(8,128)(2,1)S(1)}, u32[]{:S(2)}, u32[]{:S(2)}) collective-permute-start(bf16[256,512]{1,0:T(8,128)(2,1)} %get-tuple-element.33.refs_1_), channel_id=1, source_target_pairs={{0,2},{1,3},{2,4},{3,5},{4,6},{5,7},{6,0},{7,1},{8,10},{9,11},{10,... | collective-permute-start | bytes 786440 | tf_op jit(solution)/shard_map/ppermute | solution.py:534
  7.7 1.2 %copy-start = (bf16[2,512,512]{2,1,0:T(8,128)(2,1)S(1)}, bf16[2,512,512]{2,1,0:T(8,128)(2,1)}, u32[]{:S(2)}) copy-start(bf16[2,512,512]{2,1,0:T(8,128)(2,1)} %w_proj.1) | copy-start | bytes 3145732
  8.9 0.7 copy-start.3
  9.6 5.6 %copy-start.9 = (bf16[264,512]{1,0:T(8,128)(2,1)S(1)}, bf16[264,512]{1,0:T(8,128)(2,1)}, u32[]{:S(2)}) copy-start(bf16[264,512]{1,0:T(8,128)(2,1)} %get-tuple-element.30.refs_0_) | copy-start | bytes 811012
  9.6 5.6 %copy-start.10 = (bf16[256,512]{1,0:T(8,128)(2,1)S(1)}, bf16[256,512]{1,0:T(8,128)(2,1)}, u32[]{:S(2)}) copy-start(bf16[256,512]{1,0:T(8,128)(2,1)} %get-tuple-element.33.refs_1_) | copy-start | bytes 786436
  15.1 10.6 %collective-permute-start.1 = (bf16[264,512]{1,0:T(8,128)(2,1)S(1)}, bf16[264,512]{1,0:T(8,128)(2,1)S(1)}, u32[]{:S(2)}, u32[]{:S(2)}) collective-permute-start(bf16[264,512]{1,0:T(8,128)(2,1)S(1)} %collective-permute-done.refs_0_), channel_id=1, source_target_pairs={{0,2},{1,3},{2,4},{3,5},{4,6},{5,7},{6,0},{7,1},{8,10},{9,11},{10,... | collective-permute-start | bytes 811016 | tf_op jit(solution)/shard_map/ppermute | solution.py:534
  15.2 11.4 %collective-permute-start.7 = (bf16[264,512]{1,0:T(8,128)(2,1)S(1)}, bf16[264,512]{1,0:T(8,128)(2,1)S(1)}, u32[]{:S(2)}, u32[]{:S(2)}) collective-permute-start(bf16[264,512]{1,0:T(8,128)(2,1)S(1)} %collective-permute-done.refs_0_), channel_id=1, source_target_pairs={{0,1},{1,0},{2,3},{3,2},{4,5},{5,4},{6,7},{7,6},{8,9},{9,8},{10,11... | collective-permute-start | bytes 811016 | tf_op jit(solution)/shard_map/ppermute | solution.py:551
  20.8 5.8 %collective-permute-start.8 = (bf16[256,512]{1,0:T(8,128)(2,1)S(1)}, bf16[256,512]{1,0:T(8,128)(2,1)S(1)}, u32[]{:S(2)}, u32[]{:S(2)}) collective-permute-start(bf16[256,512]{1,0:T(8,128)(2,1)S(1)} %collective-permute-done.2.refs_1_), channel_id=1, source_target_pairs={{0,1},{1,0},{2,3},{3,2},{4,5},{5,4},{6,7},{7,6},{8,9},{9,8},{10,11... | collective-permute-start | bytes 786440 | tf_op jit(solution)/shard_map/ppermute | solution.py:551
  20.8 10.9 %collective-permute-start.6 = (bf16[256,512]{1,0:T(8,128)(2,1)S(1)}, bf16[256,512]{1,0:T(8,128)(2,1)S(1)}, u32[]{:S(2)}, u32[]{:S(2)}) collective-permute-start(bf16[256,512]{1,0:T(8,128)(2,1)S(1)} %collective-permute-done.2.refs_1_), channel_id=1, source_target_pairs={{0,2},{1,3},{2,4},{3,5},{4,6},{5,7},{6,0},{7,1},{8,10},{9,11},{10,... | collective-permute-start | bytes 786440 | tf_op jit(solution)/shard_map/ppermute | solution.py:534
  22.1 10.1 %copy-start.5 = (s32[512]{0:T(512)S(1)}, s32[512]{0:T(512)}, u32[]{:S(2)}) copy-start(s32[512]{0:T(512)} %param.13) | copy-start | bytes 6148
  25.7 11.7 %collective-permute-start.5 = (bf16[264,512]{1,0:T(8,128)(2,1)S(1)}, bf16[264,512]{1,0:T(8,128)(2,1)S(1)}, u32[]{:S(2)}, u32[]{:S(2)}) collective-permute-start(bf16[264,512]{1,0:T(8,128)(2,1)S(1)} %collective-permute-done.1.beyond.refs_0_), channel_id=1, source_target_pairs={{0,2},{1,3},{2,4},{3,5},{4,6},{5,7},{6,0},{7,1},{8,10},{9,11},{10,... | collective-permute-start | bytes 811016 | tf_op jit(solution)/shard_map/ppermute | solution.py:534
  26.6 10.9 %collective-permute-start.10 = (bf16[264,512]{1,0:T(8,128)(2,1)S(1)}, bf16[264,512]{1,0:T(8,128)(2,1)S(1)}, u32[]{:S(2)}, u32[]{:S(2)}) collective-permute-start(bf16[264,512]{1,0:T(8,128)(2,1)S(1)} %collective-permute-done.1.beyond.refs_0_), channel_id=1, source_target_pairs={{0,1},{1,0},{2,3},{3,2},{4,5},{5,4},{6,7},{7,6},{8,9},{9,8},{10,11... | collective-permute-start | bytes 811016 | tf_op jit(solution)/shard_map/ppermute | solution.py:551
  31.7 5.8 %collective-permute-start.11 = (bf16[256,512]{1,0:T(8,128)(2,1)S(1)}, bf16[256,512]{1,0:T(8,128)(2,1)S(1)}, u32[]{:S(2)}, u32[]{:S(2)}) collective-permute-start(bf16[256,512]{1,0:T(8,128)(2,1)S(1)} %collective-permute-done.6.refs_1_), channel_id=1, source_target_pairs={{0,1},{1,0},{2,3},{3,2},{4,5},{5,4},{6,7},{7,6},{8,9},{9,8},{10,11... | collective-permute-start | bytes 786440 | tf_op jit(solution)/shard_map/ppermute | solution.py:551
  31.7 11.1 %collective-permute-start.9 = (bf16[256,512]{1,0:T(8,128)(2,1)S(1)}, bf16[256,512]{1,0:T(8,128)(2,1)S(1)}, u32[]{:S(2)}, u32[]{:S(2)}) collective-permute-start(bf16[256,512]{1,0:T(8,128)(2,1)S(1)} %collective-permute-done.6.refs_1_), channel_id=1, source_target_pairs={{0,2},{1,3},{2,4},{3,5},{4,6},{5,7},{6,0},{7,1},{8,10},{9,11},{10,... | collective-permute-start | bytes 786440 | tf_op jit(solution)/shard_map/ppermute | solution.py:534
  37.5 5.3 %collective-permute-start.13 = (bf16[264,512]{1,0:T(8,128)(2,1)S(1)}, bf16[264,512]{1,0:T(8,128)(2,1)S(1)}, u32[]{:S(2)}, u32[]{:S(2)}) collective-permute-start(bf16[264,512]{1,0:T(8,128)(2,1)S(1)} %collective-permute-done.5.refs_0_), channel_id=1, source_target_pairs={{0,1},{1,0},{2,3},{3,2},{4,5},{5,4},{6,7},{7,6},{8,9},{9,8},{10,11... | collective-permute-start | bytes 811016 | tf_op jit(solution)/shard_map/ppermute | solution.py:551
  42.8 2.0 %collective-permute-start.12 = (bf16[256,512]{1,0:T(8,128)(2,1)S(1)}, bf16[256,512]{1,0:T(8,128)(2,1)S(1)}, u32[]{:S(2)}, u32[]{:S(2)}) collective-permute-start(bf16[256,512]{1,0:T(8,128)(2,1)S(1)} %collective-permute-done.9.refs_0_), channel_id=1, source_target_pairs={{0,1},{1,0},{2,3},{3,2},{4,5},{5,4},{6,7},{7,6},{8,9},{9,8},{10,11... | collective-permute-start | bytes 786440 | tf_op jit(solution)/shard_map/ppermute | solution.py:551
  44.7 1.0 %copy-start.2 = (bf16[512,512]{1,0:T(8,128)(2,1)S(1)}, bf16[512,512]{1,0:T(8,128)(2,1)}, u32[]{:S(2)}) copy-start(bf16[512,512]{1,0:T(8,128)(2,1)} %points.3) | copy-start | bytes 1572868
  44.8 1.0 %copy-start.6 = (s32[8,3]{0,1:T(4,128)S(1)}, s32[8,3]{0,1:T(4,128)}, u32[]{:S(2)}) copy-start(s32[8,3]{0,1:T(4,128)} %param.11) | copy-start | bytes 292
  45.8 32.4 %copy-start.1 = (bf16[2,512,512]{2,1,0:T(8,128)(2,1)S(1)}, bf16[2,512,512]{2,1,0:T(8,128)(2,1)}, u32[]{:S(2)}) copy-start(bf16[2,512,512]{2,1,0:T(8,128)(2,1)} %w_proj.1) | copy-start | bytes 3145732
  45.8 32.4 %copy-start.4 = (f32[4,512]{1,0:T(4,128)S(1)}, f32[4,512]{1,0:T(4,128)}, u32[]{:S(2)}) copy-start(f32[4,512]{1,0:T(4,128)} %gains.1) | copy-start | bytes 24580
  45.8 32.4 %copy-start.7 = (bf16[3,512]{1,0:T(4,128)(2,1)S(1)}, bf16[3,512]{1,0:T(4,128)(2,1)}, u32[]{:S(2)}) copy-start(bf16[3,512]{1,0:T(4,128)(2,1)} %w_head.1) | copy-start | bytes 9220
  45.8 32.4 %copy-start.8 = (s32[8,3]{0,1:T(4,128)S(1)}, s32[8,3]{0,1:T(4,128)}, u32[]{:S(2)}) copy-start(s32[8,3]{0,1:T(4,128)} %param.12) | copy-start | bytes 292

commit v10 on v9

--- a/solution.py
+++ b/solution.py
@@ -189,11 +189,10 @@
         mine = lax.broadcasted_iota(jnp.int32, (devices, rows), 0) == target
         mine = jnp.where(mine, 1.0, 0.0).astype(F32)
         earlier = jnp.dot(mine.astype(BF16), before, preferred_element_type=F32)
-        rank = jnp.sum(mine * earlier, axis=0, keepdims=True).astype(jnp.int32) + b * capacity
-        slots[:, b * rows : (b + 1) * rows] = jnp.where(
-            target >= 0, target * 2 * capacity + rank, -1
-        )
-        by_lane = lax.broadcasted_iota(jnp.int32, (LANES, rows), 0) == rank + offset
+        rank = jnp.sum(mine * earlier, axis=0, keepdims=True).astype(jnp.int32)
+        slots[:, b * rows : (b + 1) * rows] = jnp.where(target >= 0, target * capacity + rank, -1)
+        rank = rank + b * capacity + offset
+        by_lane = lax.broadcasted_iota(jnp.int32, (LANES, rows), 0) == rank
         by_lane = jnp.where(by_lane, 1.0, 0.0).astype(BF16)
         line = lax.broadcasted_iota(jnp.int32, (devices * TAIL, rows), 0)
         code = place + 1
@@ -307,23 +306,25 @@
     for copy in copies[1:]:
         copy.wait()
 
-    @pl.loop(0, 2)
-    def _(b):
-        here = pl.ds(pl.multiple_of(b * rows, rows), rows)
-        first_held[here, :] = finish(
-            points_held[here, :], attended[here, :], gains[1:2, :], (w_proj, w_up, w_down)
-        )
-
+    first_held[...] = finish(
+        points_held[...], attended[...], gains[1:2, :], (w_proj, w_up, w_down)
+    )
     copies[0].wait()
-    slots = slot_of_row[...]
     targets = devices // SEND_PARTS
-    piece = targets * capacity
+    block_slots = capacity // 2
     leaving = []
     for i in range(SEND_PARTS):
         here = pl.ds(i * targets, targets)
-        send = one_hot_rows(slots - i * piece, piece)
-        moved = jnp.dot(send, first_held[...], preferred_element_type=F32).astype(BF16)
-        outgoing_held[here] = moved.reshape(targets, capacity, channels)
+        for b in range(2):
+            mine = pl.ds(b * block_slots, block_slots)
+            slots = slot_of_row[:, b * rows : (b + 1) * rows] - i * targets * block_slots
+            send = one_hot_rows(slots, targets * block_slots)
+            moved = jnp.dot(
+                send, first_held[b * rows : (b + 1) * rows, :], preferred_element_type=F32
+            )
+            outgoing_held[here, mine, :] = moved.astype(BF16).reshape(
+                targets, block_slots, channels
+            )
         pairs = lane_tiles(outgoing.at[here], outgoing_held.at[here])
         leaving += started([(source, place) for place, source in pairs], sems.at[1 + i])
     for copy in leaving:
@@ -352,6 +353,7 @@
     gains_held,
     tail_held,
     head_held,
+    features_held,
     sems,
 ):
     rows, channels = features.shape
@@ -408,10 +410,12 @@
     done = finish(
         second, attended[...], gains_held[3:4, :], (proj_held, up_held, down_held), copies[1:]
     )
-    features[...] = done
+    features_held[...] = done
+    (leaving,) = started([(features_held, features)], sems.at[0])
     normals[...] = lax.dot_general(
         head_held[...], done, (((1,), (1,)), ((), ())), preferred_element_type=F32
     )
+    leaving.wait()
 
 
 VMEM_SPEC = pl.BlockSpec(memory_space=pltpu.VMEM)
@@ -613,7 +617,7 @@
             jax.ShapeDtypeStruct((w_head.shape[0], rows_here), F32),
         ),
         in_specs=[SMEM_SPEC] + [ANY_SPEC] * 7,
-        out_specs=(VMEM_SPEC, VMEM_SPEC),
+        out_specs=(ANY_SPEC, VMEM_SPEC),
         scratch_shapes=[
             pltpu.VMEM((rows_here, 2 * channels), BF16),
             held_rows,
@@ -624,6 +628,7 @@
             pltpu.VMEM(norm_gains.shape, F32),
             pltpu.VMEM(tail.shape, BF16),
             pltpu.VMEM(w_head.shape, BF16),
+            held_rows,
             pltpu.SemaphoreType.DMA((3, 5)),
         ],
         compiler_params=pltpu.CompilerParams(vmem_limit_bytes=SECOND_BYTES),

time: 88 us -> 87.9 us (level)
  no operation moved by 1% of the time
where the time goes in v10:
time: 87.9 us; the launch traced here: 87.6 us
  Pallas kernels  37.5 us (43%)
  blocking collectives  20.4 us (23%)
  waiting for transfers between devices  19.7 us (22%)
  starting transfers between devices  6.65 us (8%)
  local copies, waits for them, and re-layouts  2.31 us (3%)
  between operations  1 us (1%)
    all_to_all x1, blocking collectives, shards(): lax.all_to_all(outgoing, ('grp', 'seq'), split_axis=0, concat_axis=0, til...  20.4 us
    ppermute x6, waiting for transfers between devices, shards(): column = [lax.ppermute(rows, GROUP, onward) for rows in column]  19.7 us
    pallas_call x1, Pallas kernels, shards(): pl.pallas_call(functools.partial(first_kernel, chips if ring else 0), out...  11.3 us
    pallas_call x8, Pallas kernels, project(): pl.pallas_call(functools.partial(project_kernel, first_rows, new, ask), o...  11.1 us
    pallas_call x1, Pallas kernels, shards(): pl.pallas_call(second_kernel, out_shape=(jax.ShapeDtypeStruct((rows_here,...  9.87 us
    ppermute x6, starting transfers between devices, shards(): column = [lax.ppermute(rows, GROUP, onward) for rows in column]  6.12 us
    pallas_call x1, Pallas kernels, shards(): pl.pallas_call(keep_kernel, out_shape=[*[jax.ShapeDtypeStruct(w.shape[1:]...  2.8 us
    unnamed x22, local copies, waits for them, and re-layouts  2.31 us
  transfers between devices with their start and end apart: 14, of which 6 were waited for; matrix products, arithmetic and copies ran while one was open for 0% of the time, Pallas kernels for 16%

profile of v10, /device:TPU:0, one launch (start us, length us, event | category | flops | bytes accessed | tf_op | source)
XLA Modules:
  0.0 87.6 jit_solution(3378194994353469652)
XLA Ops:
  0.6 1.9 %split.1 = (bf16[264,512]{1,0:T(8,128)(2,1)}, bf16[256,512]{1,0:T(8,128)(2,1)}) custom-call(bf16[512,512]{1,0:T(8,128)(2,1)} %points.3, s32[1,512]{1,0:T(1,128)} %bitcast.3, s32[3,8]{1,0:T(4,128)} %bitcast.5), custom_call_target="tpu_custom_call" | custom-call | tf_op jit(solution)/shard_map/split/pallas_call | solution.py:456
  2.5 3.1 %collective-permute-start = (bf16[264,512]{1,0:T(8,128)(2,1)}, bf16[264,512]{1,0:T(8,128)(2,1)S(1)}, u32[]{:S(2)}, u32[]{:S(2)}) collective-permute-start(bf16[264,512]{1,0:T(8,128)(2,1)} %get-tuple-element.30.refs_0_), channel_id=1, source_target_pairs={{0,2},{1,3},{2,4},{3,5},{4,6},{5,7},{6,0},{7,1},{8,10},{9,11},{10,... | collective-permute-start | bytes 811016 | tf_op jit(solution)/shard_map/ppermute | solution.py:538
  5.6 0.0 collective-permute-start.3
  5.6 0.5 collective-permute-start.4
  6.1 1.6 %collective-permute-start.2 = (bf16[256,512]{1,0:T(8,128)(2,1)}, bf16[256,512]{1,0:T(8,128)(2,1)S(1)}, u32[]{:S(2)}, u32[]{:S(2)}) collective-permute-start(bf16[256,512]{1,0:T(8,128)(2,1)} %get-tuple-element.33.refs_1_), channel_id=1, source_target_pairs={{0,2},{1,3},{2,4},{3,5},{4,6},{5,7},{6,0},{7,1},{8,10},{9,11},{10,... | collective-permute-start | bytes 786440 | tf_op jit(solution)/shard_map/ppermute | solution.py:538
  7.7 1.2 %copy-done = bf16[2,512,512]{2,1,0:T(8,128)(2,1)S(1)} copy-done((bf16[2,512,512]{2,1,0:T(8,128)(2,1)S(1)}, bf16[2,512,512]{2,1,0:T(8,128)(2,1)}, u32[]{:S(2)}) %copy-start) | copy-done | bytes 1048600
  8.9 0.7 copy-done.3
  9.6 2.8 %keep.1 = (bf16[512,1536]{1,0:T(8,128)(2,1)S(1)}, bf16[512,512]{1,0:T(8,128)(2,1)S(1)}, bf16[512,2048]{1,0:T(8,128)(2,1)S(1)}, bf16[2048,512]{1,0:T(8,128)(2,1)S(1)}, f32[4,512]{1,0:T(4,128)S(1)}) custom-call(bf16[2,512,1536]{2,1,0:T(8,128)(2,1)} %w_qkv.1, bf16[2,512,512]{2,1,0:T(8,128)(2,1)S(1)} %copy-done, bf16[2,512,2048]{2,1,0:T(8,128)(2,1)} %w_up.1, ...), custom_call_target="tpu_custom_call" | custom-call | tf_op jit(solution)/shard_map/keep/pallas_call | solution.py:475
  12.4 2.7 %collective-permute-done.refs_0_ = bf16[264,512]{1,0:T(8,128)(2,1)S(1)} collective-permute-done((bf16[264,512]{1,0:T(8,128)(2,1)}, bf16[264,512]{1,0:T(8,128)(2,1)S(1)}, u32[]{:S(2)}, u32[]{:S(2)}) %collective-permute-start) | collective-permute-done | bytes 270368 | tf_op jit(solution)/shard_map/ppermute | solution.py:538
  15.1 0.0 collective-permute-start.1
  15.2 0.0 collective-permute-start.7
  15.2 0.0 collective-permute-done.4.refs_3_
  15.2 0.0 collective-permute-done.3.refs_2_
  15.2 2.9 %project_own.1 = (bf16[4096,1024]{1,0:T(8,128)(2,1)S(1)}, bf16[512,512]{1,0:T(8,128)(2,1)S(1)}) custom-call(bf16[264,512]{1,0:T(8,128)(2,1)S(1)} %copy-done.9, bf16[256,512]{1,0:T(8,128)(2,1)S(1)} %copy-done.10, bf16[264,512]{1,0:T(8,128)(2,1)S(1)} %collective-permute-done.3.refs_2_, bf16[256,512]{1,0:T(8,128)(2,1)S(1)} %collective-permute-done.4.refs_3_, ...), custom_call_target="tpu_custom_call" | custom-call | flops 1073741824 | bytes 4718592 | tf_op jit(solution)/shard_map/project_own/pallas_call | solution.py:515
  18.1 2.6 %collective-permute-done.2.refs_1_ = bf16[256,512]{1,0:T(8,128)(2,1)S(1)} collective-permute-done((bf16[256,512]{1,0:T(8,128)(2,1)}, bf16[256,512]{1,0:T(8,128)(2,1)S(1)}, u32[]{:S(2)}, u32[]{:S(2)}) %collective-permute-start.2) | collective-permute-done | bytes 262176 | tf_op jit(solution)/shard_map/ppermute | solution.py:538
  20.8 0.0 collective-permute-start.8
  20.8 0.0 collective-permute-start.6
  20.8 1.3 %project.7.refs_4_ = bf16[4096,1024]{1,0:T(8,128)(2,1)S(1)} custom-call(bf16[264,512]{1,0:T(8,128)(2,1)S(1)} %collective-permute-done.refs_0_, bf16[256,512]{1,0:T(8,128)(2,1)S(1)} %collective-permute-done.2.refs_1_, f32[4,512]{1,0:T(4,128)S(1)} %get-tuple-element.34.refs_4_.refs_2_.refs_1_.gains, ...), custom_call_target="tpu_custom_call", output_to_operand_aliasing={{}: (4, {})} | custom-call | flops 536870912 | bytes 3145728 | tf_op jit(solution)/shard_map/project/pallas_call | solution.py:515
  22.1 0.0 copy-start.5
  22.1 3.6 %collective-permute-done.1.beyond.refs_0_ = bf16[264,512]{1,0:T(8,128)(2,1)S(1)} collective-permute-done((bf16[264,512]{1,0:T(8,128)(2,1)S(1)}, bf16[264,512]{1,0:T(8,128)(2,1)S(1)}, u32[]{:S(2)}, u32[]{:S(2)}) %collective-permute-start.1) | collective-permute-done | bytes 270368 | tf_op jit(solution)/shard_map/ppermute | solution.py:538
  25.7 0.9 collective-permute-start.5
  26.6 0.0 collective-permute-start.10
  26.6 0.0 collective-permute-done.8.refs_1_
  26.6 0.0 collective-permute-done.7.refs_0_
  26.6 1.3 %project.8.refs_4_ = bf16[4096,1024]{1,0:T(8,128)(2,1)S(1)} custom-call(bf16[264,512]{1,0:T(8,128)(2,1)S(1)} %collective-permute-done.7.refs_0_, bf16[256,512]{1,0:T(8,128)(2,1)S(1)} %collective-permute-done.8.refs_1_, f32[4,512]{1,0:T(4,128)S(1)} %get-tuple-element.34.refs_4_.refs_2_.refs_1_.gains, ...), custom_call_target="tpu_custom_call", output_to_operand_aliasing={{}: (4, {})} | custom-call | flops 536870912 | bytes 3145728 | tf_op jit(solution)/shard_map/project/pallas_call | solution.py:515
  27.9 3.8 %collective-permute-done.6.refs_1_ = bf16[256,512]{1,0:T(8,128)(2,1)S(1)} collective-permute-done((bf16[256,512]{1,0:T(8,128)(2,1)S(1)}, bf16[256,512]{1,0:T(8,128)(2,1)S(1)}, u32[]{:S(2)}, u32[]{:S(2)}) %collective-permute-start.6) | collective-permute-done | bytes 262176 | tf_op jit(solution)/shard_map/ppermute | solution.py:538
  31.7 0.0 collective-permute-start.11
  31.7 0.5 collective-permute-start.9
  32.2 0.6 index.1
  32.8 1.6 %project.9 = (bf16[4096,1024]{1,0:T(8,128)(2,1)S(1)}, bf16[512,512]{1,0:T(8,128)(2,1)S(1)}) custom-call(bf16[264,512]{1,0:T(8,128)(2,1)S(1)} %collective-permute-done.1.beyond.refs_0_, bf16[256,512]{1,0:T(8,128)(2,1)S(1)} %collective-permute-done.6.refs_1_, ...), custom_call_target="tpu_custom_call", output_to_operand_aliasing={{0}: (4, {})} | custom-call | flops 536870912 | bytes 3145728 | tf_op jit(solution)/shard_map/project/pallas_call | solution.py:515
  34.4 3.0 %collective-permute-done.5.refs_0_ = bf16[264,512]{1,0:T(8,128)(2,1)S(1)} collective-permute-done((bf16[264,512]{1,0:T(8,128)(2,1)S(1)}, bf16[264,512]{1,0:T(8,128)(2,1)S(1)}, u32[]{:S(2)}, u32[]{:S(2)}) %collective-permute-start.5) | collective-permute-done | bytes 270368 | tf_op jit(solution)/shard_map/ppermute | solution.py:538
  37.5 0.0 collective-permute-start.13
  37.5 0.0 collective-permute-done.11.refs_1_
  37.5 0.0 collective-permute-done.10.refs_0_
  37.5 1.3 %project.10.refs_4_ = bf16[4096,1024]{1,0:T(8,128)(2,1)S(1)} custom-call(bf16[264,512]{1,0:T(8,128)(2,1)S(1)} %collective-permute-done.10.refs_0_, bf16[256,512]{1,0:T(8,128)(2,1)S(1)} %collective-permute-done.11.refs_1_, f32[4,512]{1,0:T(4,128)S(1)} %get-tuple-element.34.refs_4_.refs_2_.refs_1_.gains, ...), custom_call_target="tpu_custom_call", output_to_operand_aliasing={{}: (4, {})} | custom-call | flops 536870912 | bytes 3145728 | tf_op jit(solution)/shard_map/project/pallas_call | solution.py:515
  38.8 4.0 %collective-permute-done.9.refs_0_ = bf16[256,512]{1,0:T(8,128)(2,1)S(1)} collective-permute-done((bf16[256,512]{1,0:T(8,128)(2,1)S(1)}, bf16[256,512]{1,0:T(8,128)(2,1)S(1)}, u32[]{:S(2)}, u32[]{:S(2)}) %collective-permute-start.9) | collective-permute-done | bytes 262176 | tf_op jit(solution)/shard_map/ppermute | solution.py:538
  42.8 0.0 collective-permute-start.12
  42.8 0.0 collective-permute-done.13.refs_1_
  42.8 1.3 %project.11.refs_3_ = bf16[4096,1024]{1,0:T(8,128)(2,1)S(1)} custom-call(bf16[264,512]{1,0:T(8,128)(2,1)S(1)} %collective-permute-done.5.refs_0_, bf16[264,512]{1,0:T(8,128)(2,1)S(1)} %collective-permute-done.13.refs_1_, f32[4,512]{1,0:T(4,128)S(1)} %get-tuple-element.34.refs_4_.refs_2_.refs_1_.gains, ...), custom_call_target="tpu_custom_call", output_to_operand_aliasing={{}: (4, {})} | custom-call | flops 536870912 | bytes 3145728 | tf_op jit(solution)/shard_map/project/pallas_call | solution.py:515
  44.1 0.7 project.12.refs_3_
  44.7 0.0 copy-start.2
  44.8 0.0 copy-start.6
  44.8 0.7 project.13.keyed
  45.4 0.3 copy-done.2
  45.8 0.0 copy-start.8
  45.8 11.3 %block_first.1 = bf16[16,264,128]{2,1,0:T(8,128)(2,1)S(1)} custom-call(s32[3,8]{1,0:T(4,128)S(1)} %bitcast.6, s32[3,8]{1,0:T(4,128)S(1)} %get-tuple-element.40.pattern_beyond, s32[1,1024]{1,0:T(1,128)S(1)} %get-tuple-element.47.slot_of_row, f32[4,512]{1,0:T(4,128)S(1)} %get-tuple-element.34.refs_4_.refs_2_.refs_1_.gains, ...), custom_call_target="tpu_custom_call" | custom-call | tf_op jit(solution)/shard_map/block_first/pallas_call | solution.py:584
  57.1 20.4 %all_to_all.5.incoming = bf16[16,264,128]{2,1,0:T(8,128)(2,1)S(1)} all-to-all(bf16[16,264,128]{2,1,0:T(8,128)(2,1)S(1)} %block_first.1), channel_id=1, replica_groups=mesh['grp'=4,'half'=2,'seq'=4] {'grp','seq'}, dimensions={0} | all-to-all | bytes 2162688 | tf_op jit(solution)/shard_map/all_to_all | solution.py:611
  77.5 9.9 %block_second.1 = (bf16[512,512]{1,0:T(8,128)(2,1)}, f32[3,512]{1,0:T(4,128)}) custom-call(s32[3,8]{1,0:T(4,128)S(1)} %bitcast.7, f32[4,512]{1,0:T(4,128)S(1)} %copy-done.4, bf16[16,264,128]{2,1,0:T(8,128)(2,1)S(1)} %all_to_all.5.incoming, bf16[2,512,1536]{2,1,0:T(8,128)(2,1)} %w_qkv.1, bf16[2,512,512]{2,1,0:T(8,128)(2,1)S(1)} %copy-done.1, ...), custom_call_target="tpu_custom_call" | custom-call | tf_op jit(solution)/shard_map/block_second/pallas_call | solution.py:613
  (16 shorter events, 0.0 us)
Async XLA Ops:
  2.5 12.6 %collective-permute-start = (bf16[264,512]{1,0:T(8,128)(2,1)}, bf16[264,512]{1,0:T(8,128)(2,1)S(1)}, u32[]{:S(2)}, u32[]{:S(2)}) collective-permute-start(bf16[264,512]{1,0:T(8,128)(2,1)} %get-tuple-element.30.refs_0_), channel_id=1, source_target_pairs={{0,2},{1,3},{2,4},{3,5},{4,6},{5,7},{6,0},{7,1},{8,10},{9,11},{10,... | collective-permute-start | bytes 811016 | tf_op jit(solution)/shard_map/ppermute | solution.py:538
  5.6 9.6 %collective-permute-start.3 = (bf16[264,512]{1,0:T(8,128)(2,1)}, bf16[264,512]{1,0:T(8,128)(2,1)S(1)}, u32[]{:S(2)}, u32[]{:S(2)}) collective-permute-start(bf16[264,512]{1,0:T(8,128)(2,1)} %get-tuple-element.30.refs_0_), channel_id=1, source_target_pairs={{0,1},{1,0},{2,3},{3,2},{4,5},{5,4},{6,7},{7,6},{8,9},{9,8},{10,11... | collective-permute-start | bytes 811016 | tf_op jit(solution)/shard_map/ppermute | solution.py:535
  5.6 9.6 %collective-permute-start.4 = (bf16[256,512]{1,0:T(8,128)(2,1)}, bf16[256,512]{1,0:T(8,128)(2,1)S(1)}, u32[]{:S(2)}, u32[]{:S(2)}) collective-permute-start(bf16[256,512]{1,0:T(8,128)(2,1)} %get-tuple-element.33.refs_1_), channel_id=1, source_target_pairs={{0,1},{1,0},{2,3},{3,2},{4,5},{5,4},{6,7},{7,6},{8,9},{9,8},{10,11... | collective-permute-start | bytes 786440 | tf_op jit(solution)/shard_map/ppermute | solution.py:535
  6.1 14.7 %collective-permute-start.2 = (bf16[256,512]{1,0:T(8,128)(2,1)}, bf16[256,512]{1,0:T(8,128)(2,1)S(1)}, u32[]{:S(2)}, u32[]{:S(2)}) collective-permute-start(bf16[256,512]{1,0:T(8,128)(2,1)} %get-tuple-element.33.refs_1_), channel_id=1, source_target_pairs={{0,2},{1,3},{2,4},{3,5},{4,6},{5,7},{6,0},{7,1},{8,10},{9,11},{10,... | collective-permute-start | bytes 786440 | tf_op jit(solution)/shard_map/ppermute | solution.py:538
  7.7 1.2 %copy-start = (bf16[2,512,512]{2,1,0:T(8,128)(2,1)S(1)}, bf16[2,512,512]{2,1,0:T(8,128)(2,1)}, u32[]{:S(2)}) copy-start(bf16[2,512,512]{2,1,0:T(8,128)(2,1)} %w_proj.1) | copy-start | bytes 3145732
  8.9 0.7 copy-start.3
  9.6 5.6 %copy-start.9 = (bf16[264,512]{1,0:T(8,128)(2,1)S(1)}, bf16[264,512]{1,0:T(8,128)(2,1)}, u32[]{:S(2)}) copy-start(bf16[264,512]{1,0:T(8,128)(2,1)} %get-tuple-element.30.refs_0_) | copy-start | bytes 811012
  9.6 5.6 %copy-start.10 = (bf16[256,512]{1,0:T(8,128)(2,1)S(1)}, bf16[256,512]{1,0:T(8,128)(2,1)}, u32[]{:S(2)}) copy-start(bf16[256,512]{1,0:T(8,128)(2,1)} %get-tuple-element.33.refs_1_) | copy-start | bytes 786436
  15.1 10.6 %collective-permute-start.1 = (bf16[264,512]{1,0:T(8,128)(2,1)S(1)}, bf16[264,512]{1,0:T(8,128)(2,1)S(1)}, u32[]{:S(2)}, u32[]{:S(2)}) collective-permute-start(bf16[264,512]{1,0:T(8,128)(2,1)S(1)} %collective-permute-done.refs_0_), channel_id=1, source_target_pairs={{0,2},{1,3},{2,4},{3,5},{4,6},{5,7},{6,0},{7,1},{8,10},{9,11},{10,... | collective-permute-start | bytes 811016 | tf_op jit(solution)/shard_map/ppermute | solution.py:538
  15.2 11.4 %collective-permute-start.7 = (bf16[264,512]{1,0:T(8,128)(2,1)S(1)}, bf16[264,512]{1,0:T(8,128)(2,1)S(1)}, u32[]{:S(2)}, u32[]{:S(2)}) collective-permute-start(bf16[264,512]{1,0:T(8,128)(2,1)S(1)} %collective-permute-done.refs_0_), channel_id=1, source_target_pairs={{0,1},{1,0},{2,3},{3,2},{4,5},{5,4},{6,7},{7,6},{8,9},{9,8},{10,11... | collective-permute-start | bytes 811016 | tf_op jit(solution)/shard_map/ppermute | solution.py:555
  20.8 5.8 %collective-permute-start.8 = (bf16[256,512]{1,0:T(8,128)(2,1)S(1)}, bf16[256,512]{1,0:T(8,128)(2,1)S(1)}, u32[]{:S(2)}, u32[]{:S(2)}) collective-permute-start(bf16[256,512]{1,0:T(8,128)(2,1)S(1)} %collective-permute-done.2.refs_1_), channel_id=1, source_target_pairs={{0,1},{1,0},{2,3},{3,2},{4,5},{5,4},{6,7},{7,6},{8,9},{9,8},{10,11... | collective-permute-start | bytes 786440 | tf_op jit(solution)/shard_map/ppermute | solution.py:555
  20.8 10.9 %collective-permute-start.6 = (bf16[256,512]{1,0:T(8,128)(2,1)S(1)}, bf16[256,512]{1,0:T(8,128)(2,1)S(1)}, u32[]{:S(2)}, u32[]{:S(2)}) collective-permute-start(bf16[256,512]{1,0:T(8,128)(2,1)S(1)} %collective-permute-done.2.refs_1_), channel_id=1, source_target_pairs={{0,2},{1,3},{2,4},{3,5},{4,6},{5,7},{6,0},{7,1},{8,10},{9,11},{10,... | collective-permute-start | bytes 786440 | tf_op jit(solution)/shard_map/ppermute | solution.py:538
  22.1 10.1 %copy-start.5 = (s32[512]{0:T(512)S(1)}, s32[512]{0:T(512)}, u32[]{:S(2)}) copy-start(s32[512]{0:T(512)} %param.13) | copy-start | bytes 6148
  25.7 11.7 %collective-permute-start.5 = (bf16[264,512]{1,0:T(8,128)(2,1)S(1)}, bf16[264,512]{1,0:T(8,128)(2,1)S(1)}, u32[]{:S(2)}, u32[]{:S(2)}) collective-permute-start(bf16[264,512]{1,0:T(8,128)(2,1)S(1)} %collective-permute-done.1.beyond.refs_0_), channel_id=1, source_target_pairs={{0,2},{1,3},{2,4},{3,5},{4,6},{5,7},{6,0},{7,1},{8,10},{9,11},{10,... | collective-permute-start | bytes 811016 | tf_op jit(solution)/shard_map/ppermute | solution.py:538
  26.6 10.9 %collective-permute-start.10 = (bf16[264,512]{1,0:T(8,128)(2,1)S(1)}, bf16[264,512]{1,0:T(8,128)(2,1)S(1)}, u32[]{:S(2)}, u32[]{:S(2)}) collective-permute-start(bf16[264,512]{1,0:T(8,128)(2,1)S(1)} %collective-permute-done.1.beyond.refs_0_), channel_id=1, source_target_pairs={{0,1},{1,0},{2,3},{3,2},{4,5},{5,4},{6,7},{7,6},{8,9},{9,8},{10,11... | collective-permute-start | bytes 811016 | tf_op jit(solution)/shard_map/ppermute | solution.py:555
  31.7 5.8 %collective-permute-start.11 = (bf16[256,512]{1,0:T(8,128)(2,1)S(1)}, bf16[256,512]{1,0:T(8,128)(2,1)S(1)}, u32[]{:S(2)}, u32[]{:S(2)}) collective-permute-start(bf16[256,512]{1,0:T(8,128)(2,1)S(1)} %collective-permute-done.6.refs_1_), channel_id=1, source_target_pairs={{0,1},{1,0},{2,3},{3,2},{4,5},{5,4},{6,7},{7,6},{8,9},{9,8},{10,11... | collective-permute-start | bytes 786440 | tf_op jit(solution)/shard_map/ppermute | solution.py:555
  31.7 11.1 %collective-permute-start.9 = (bf16[256,512]{1,0:T(8,128)(2,1)S(1)}, bf16[256,512]{1,0:T(8,128)(2,1)S(1)}, u32[]{:S(2)}, u32[]{:S(2)}) collective-permute-start(bf16[256,512]{1,0:T(8,128)(2,1)S(1)} %collective-permute-done.6.refs_1_), channel_id=1, source_target_pairs={{0,2},{1,3},{2,4},{3,5},{4,6},{5,7},{6,0},{7,1},{8,10},{9,11},{10,... | collective-permute-start | bytes 786440 | tf_op jit(solution)/shard_map/ppermute | solution.py:538
  37.5 5.3 %collective-permute-start.13 = (bf16[264,512]{1,0:T(8,128)(2,1)S(1)}, bf16[264,512]{1,0:T(8,128)(2,1)S(1)}, u32[]{:S(2)}, u32[]{:S(2)}) collective-permute-start(bf16[264,512]{1,0:T(8,128)(2,1)S(1)} %collective-permute-done.5.refs_0_), channel_id=1, source_target_pairs={{0,1},{1,0},{2,3},{3,2},{4,5},{5,4},{6,7},{7,6},{8,9},{9,8},{10,11... | collective-permute-start | bytes 811016 | tf_op jit(solution)/shard_map/ppermute | solution.py:555
  42.8 2.0 %collective-permute-start.12 = (bf16[256,512]{1,0:T(8,128)(2,1)S(1)}, bf16[256,512]{1,0:T(8,128)(2,1)S(1)}, u32[]{:S(2)}, u32[]{:S(2)}) collective-permute-start(bf16[256,512]{1,0:T(8,128)(2,1)S(1)} %collective-permute-done.9.refs_0_), channel_id=1, source_target_pairs={{0,1},{1,0},{2,3},{3,2},{4,5},{5,4},{6,7},{7,6},{8,9},{9,8},{10,11... | collective-permute-start | bytes 786440 | tf_op jit(solution)/shard_map/ppermute | solution.py:555
  44.7 1.0 %copy-start.2 = (bf16[512,512]{1,0:T(8,128)(2,1)S(1)}, bf16[512,512]{1,0:T(8,128)(2,1)}, u32[]{:S(2)}) copy-start(bf16[512,512]{1,0:T(8,128)(2,1)} %points.3) | copy-start | bytes 1572868
  44.8 1.0 %copy-start.6 = (s32[8,3]{0,1:T(4,128)S(1)}, s32[8,3]{0,1:T(4,128)}, u32[]{:S(2)}) copy-start(s32[8,3]{0,1:T(4,128)} %param.11) | copy-start | bytes 292
  45.8 31.7 %copy-start.1 = (bf16[2,512,512]{2,1,0:T(8,128)(2,1)S(1)}, bf16[2,512,512]{2,1,0:T(8,128)(2,1)}, u32[]{:S(2)}) copy-start(bf16[2,512,512]{2,1,0:T(8,128)(2,1)} %w_proj.1) | copy-start | bytes 3145732
  45.8 31.7 %copy-start.4 = (f32[4,512]{1,0:T(4,128)S(1)}, f32[4,512]{1,0:T(4,128)}, u32[]{:S(2)}) copy-start(f32[4,512]{1,0:T(4,128)} %gains.1) | copy-start | bytes 24580
  45.8 31.7 %copy-start.7 = (bf16[3,512]{1,0:T(4,128)(2,1)S(1)}, bf16[3,512]{1,0:T(4,128)(2,1)}, u32[]{:S(2)}) copy-start(bf16[3,512]{1,0:T(4,128)(2,1)} %w_head.1) | copy-start | bytes 9220
  45.8 31.7 %copy-start.8 = (s32[8,3]{0,1:T(4,128)S(1)}, s32[8,3]{0,1:T(4,128)}, u32[]{:S(2)}) copy-start(s32[8,3]{0,1:T(4,128)} %param.12) | copy-start | bytes 292

commit v11 on v10

--- a/solution.py
+++ b/solution.py
@@ -14,6 +14,8 @@
 RING_PARTS = 2
 SEND_PARTS = 4
 LANES = 128
+SECOND_SCRATCH = 13
+PERMUTED_DEVICES = 16
 TAIL = 8
 DIGIT = 256
 FIRST_BYTES = 28 * 1024 * 1024
@@ -243,19 +245,19 @@
     return asked, keys, lambda at, width: keys(channels + at, width)
 
 
-def lane_tiles(packed, rows):
-    capacity, channels = rows.shape[1:]
+def part_pairs(arrays, mask, partner, rows, tail):
+    part = arrays[mask] if len(arrays) > 1 else arrays[0].at[partner]
+    capacity, channels = rows.shape
+    tiles = channels // LANES
     return [
-        (
-            packed.at[:, pl.ds(j * capacity, capacity), :],
-            rows.at[:, :, pl.ds(j * LANES, LANES)],
-        )
-        for j in range(channels // LANES)
-    ]
+        (part.at[pl.ds(j * capacity, capacity), :], rows.at[:, pl.ds(j * LANES, LANES)])
+        for j in range(tiles)
+    ] + [(part.at[pl.ds(tiles * capacity, TAIL), :], tail)]
 
 
 def first_kernel(
     ring_chips,
+    beyond_parts,
     pattern,
     pattern_beyond,
     slot_of_row,
@@ -270,21 +272,22 @@
     points,
     *refs,
 ):
-    *points_beyond, outgoing, attended, points_held, first_held, outgoing_held, sems = refs
+    points_beyond, refs = refs[:beyond_parts], refs[beyond_parts:]
+    *outgoing, attended, points_held, first_held, outgoing_held, sems, part_sems = refs
     rows, channels = points.shape
     devices, capacity, _ = outgoing_held.shape
-    row_tiles = channels // LANES * capacity
+    index = lax.axis_index(("grp", "seq"))
     patches = rows // PATCH
     chosen = pattern.shape[0]
     me = lax.axis_index(GROUP)
     part = rows // len(points_beyond)
     copies = started(
-        [(tail, outgoing.at[:, pl.ds(row_tiles, TAIL), :]), (points, points_held.at[:rows])]
+        [(points, points_held.at[:rows])]
         + [
             (piece.at[pl.ds(0, part), :], points_held.at[pl.ds(rows + i * part, part), :])
             for i, piece in enumerate(points_beyond)
         ],
-        sems.at[0],
+        sems,
     )
     blocks = ((pattern, queries, 0), (pattern_beyond, queries_beyond, ring_chips or 1))
     loaded = []
@@ -303,30 +306,32 @@
             loaded.append(loads(asking, p, keyed, starts))
     for p, at, rows_done in attend(loaded, channels // HEADS):
         attended[p * PATCH : (p + 1) * PATCH, at : at + rows_done.shape[1]] = rows_done
-    for copy in copies[1:]:
+    for copy in copies:
         copy.wait()
-
     first_held[...] = finish(
         points_held[...], attended[...], gains[1:2, :], (w_proj, w_up, w_down)
     )
-    copies[0].wait()
     targets = devices // SEND_PARTS
     block_slots = capacity // 2
     leaving = []
     for i in range(SEND_PARTS):
-        here = pl.ds(i * targets, targets)
+        masks = range(i * targets, (i + 1) * targets)
+        start = (lax.div(index, targets) ^ i) * targets * block_slots
         for b in range(2):
             mine = pl.ds(b * block_slots, block_slots)
-            slots = slot_of_row[:, b * rows : (b + 1) * rows] - i * targets * block_slots
+            slots = slot_of_row[:, b * rows : (b + 1) * rows] - start
             send = one_hot_rows(slots, targets * block_slots)
             moved = jnp.dot(
                 send, first_held[b * rows : (b + 1) * rows, :], preferred_element_type=F32
             )
-            outgoing_held[here, mine, :] = moved.astype(BF16).reshape(
+            outgoing_held[pl.ds(i * targets, targets), mine, :] = moved.astype(BF16).reshape(
                 targets, block_slots, channels
             )
-        pairs = lane_tiles(outgoing.at[here], outgoing_held.at[here])
-        leaving += started([(source, place) for place, source in pairs], sems.at[1 + i])
+        for mask in masks:
+            partner = index ^ mask
+            rows_out = outgoing_held.at[i * targets + lax.rem(partner, targets)]
+            pairs = part_pairs(outgoing, mask, partner, rows_out, tail.at[partner])
+            leaving += started([(source, place) for place, source in pairs], part_sems.at[mask])
     for copy in leaving:
         copy.wait()
 
@@ -334,37 +339,43 @@
 def second_kernel(
     pattern,
     gains,
-    incoming,
     w_qkv,
     w_proj,
     w_up,
     w_down,
     w_head,
-    features,
-    normals,
-    kv,
-    queries,
-    attended,
-    incoming_held,
-    qkv_held,
-    proj_held,
-    up_held,
-    down_held,
-    gains_held,
-    tail_held,
-    head_held,
-    features_held,
-    sems,
+    *refs,
 ):
+    *incoming, features, normals = refs[:-SECOND_SCRATCH]
+    (
+        kv,
+        queries,
+        attended,
+        incoming_held,
+        qkv_held,
+        proj_held,
+        up_held,
+        down_held,
+        gains_held,
+        tail_held,
+        head_held,
+        sems,
+        part_sems,
+    ) = refs[-SECOND_SCRATCH:]
     rows, channels = features.shape
     devices, capacity, _ = incoming_held.shape
     patches = rows // PATCH
     chosen = pattern.shape[0]
-    tail = incoming.at[:, pl.ds(channels // LANES * capacity, TAIL), :]
-    small = started(
-        [(tail, tail_held), (gains, gains_held), (w_head, head_held)], sems.at[0]
-    )
-    landing = started(lane_tiles(incoming, incoming_held), sems.at[1])
+    small = started([(gains, gains_held), (w_head, head_held)], sems.at[0])
+    per_row = LANES // capacity
+    index = lax.axis_index(("grp", "seq"))
+    landing = []
+    for mask in range(devices):
+        at = mask ^ lax.rem(index, per_row)
+        pairs = part_pairs(
+            incoming, mask, index ^ mask, incoming_held.at[at], tail_held.at[at]
+        )
+        landing.append(started(pairs, part_sems.at[mask]))
     copies = started(
         [
             (w_qkv.at[1], qkv_held),
@@ -372,11 +383,10 @@
             (w_up.at[1], up_held),
             (w_down.at[1], down_held),
         ],
-        sems.at[2],
-    )
-    for copy in small:
+        sems.at[1],
+    )
+    for copy in small + [part[-1] for part in landing]:
         copy.wait()
-    per_row = LANES // capacity
     digits = tail_held[...].astype(F32)
     codes = digits[:, 0:1, :] + DIGIT * digits[:, 1:2, :]
     pieces = []
@@ -388,9 +398,10 @@
     places = jnp.concatenate(pieces, axis=1).astype(jnp.int32) - 1
     place = one_hot_rows(places, rows)
     sides = []
-    for at in range(0, len(landing), 2):
-        for copy in landing[at : at + 2]:
-            copy.wait()
+    for at in range(0, channels // LANES, 2):
+        for part in landing:
+            for copy in part[at : at + 2]:
+                copy.wait()
         moved = incoming_held[:, :, at * LANES : (at + 2) * LANES]
         moved = moved.reshape(devices * capacity, 2 * LANES)
         sides.append(jnp.dot(place, moved, preferred_element_type=F32).astype(BF16))
@@ -410,12 +421,10 @@
     done = finish(
         second, attended[...], gains_held[3:4, :], (proj_held, up_held, down_held), copies[1:]
     )
-    features_held[...] = done
-    (leaving,) = started([(features_held, features)], sems.at[0])
+    features[...] = done
     normals[...] = lax.dot_general(
         head_held[...], done, (((1,), (1,)), ((), ())), preferred_element_type=F32
     )
-    leaving.wait()
 
 
 VMEM_SPEC = pl.BlockSpec(memory_space=pltpu.VMEM)
@@ -581,17 +590,21 @@
     held_slots = pltpu.VMEM((devices, pair_slots, channels), BF16)
     held_both = pltpu.VMEM((2 * rows_here, channels), BF16)
     pair_rows = channels // LANES * pair_slots + TAIL
+    permuted = devices <= PERMUTED_DEVICES
+    part_shape = jax.ShapeDtypeStruct((pair_rows, LANES), BF16)
+    whole_shape = jax.ShapeDtypeStruct((devices, pair_rows, LANES), BF16)
     outgoing = pl.pallas_call(
-        functools.partial(first_kernel, chips if ring else 0),
-        out_shape=jax.ShapeDtypeStruct((devices, pair_rows, LANES), BF16),
+        functools.partial(first_kernel, chips if ring else 0, len(points_beyond)),
+        out_shape=[part_shape] * devices if permuted else [whole_shape],
         in_specs=[SMEM_SPEC] * 2 + [VMEM_SPEC] * 8 + [ANY_SPEC] * (2 + len(points_beyond)),
-        out_specs=ANY_SPEC,
+        out_specs=[ANY_SPEC] * (devices if permuted else 1),
         scratch_shapes=[
             held_both,
             held_both,
             held_both,
             held_slots,
-            pltpu.SemaphoreType.DMA((1 + SEND_PARTS, 4)),
+            pltpu.SemaphoreType.DMA((1 + len(points_beyond),)),
+            pltpu.SemaphoreType.DMA((devices, channels // LANES + 1)),
         ],
         compiler_params=pltpu.CompilerParams(vmem_limit_bytes=FIRST_BYTES),
         name="block_first",
@@ -608,7 +621,14 @@
         points,
         *points_beyond,
     )
-    incoming = lax.all_to_all(outgoing, ("grp", "seq"), split_axis=0, concat_axis=0, tiled=True)
+    inside = ("grp", "seq")
+    if permuted:
+        incoming = [outgoing[0]] + [
+            lax.ppermute(outgoing[mask], inside, [(i, i ^ mask) for i in range(devices)])
+            for mask in range(1, devices)
+        ]
+    else:
+        incoming = [lax.all_to_all(outgoing[0], inside, split_axis=0, concat_axis=0, tiled=True)]
 
     return pl.pallas_call(
         second_kernel,
@@ -616,8 +636,8 @@
             jax.ShapeDtypeStruct((rows_here, channels), BF16),
             jax.ShapeDtypeStruct((w_head.shape[0], rows_here), F32),
         ),
-        in_specs=[SMEM_SPEC] + [ANY_SPEC] * 7,
-        out_specs=(ANY_SPEC, VMEM_SPEC),
+        in_specs=[SMEM_SPEC] + [ANY_SPEC] * (6 + len(incoming)),
+        out_specs=(VMEM_SPEC, VMEM_SPEC),
         scratch_shapes=[
             pltpu.VMEM((rows_here, 2 * channels), BF16),
             held_rows,
@@ -628,12 +648,12 @@
             pltpu.VMEM(norm_gains.shape, F32),
             pltpu.VMEM(tail.shape, BF16),
             pltpu.VMEM(w_head.shape, BF16),
-            held_rows,
-            pltpu.SemaphoreType.DMA((3, 5)),
+            pltpu.SemaphoreType.DMA((2, 5)),
+            pltpu.SemaphoreType.DMA((devices, channels // LANES + 1)),
         ],
         compiler_params=pltpu.CompilerParams(vmem_limit_bytes=SECOND_BYTES),
         name="block_second",
-    )(pattern_second.T, norm_gains, incoming, w_qkv, *weights, w_head)
+    )(pattern_second.T, norm_gains, w_qkv, *weights, w_head, *incoming)
 
 
 def solution(mesh):

time: 87.9 us -> 92.5 us (1.052)
  blocking collectives: 20.4 us -> 0 us
  starting transfers between devices: 6.65 us -> 24.3 us
  waiting for transfers between devices: 19.7 us -> 26.1 us
  Pallas kernels: 37.5 us -> 38.6 us
    all_to_all x1 -> x0, blocking collectives: 20.4 us -> none  [shards(): lax.all_to_all(outgoing, ('grp', 'seq'), split_axis=0, concat_axis=0, til...]
    ppermute x0 -> x15, starting transfers between devices: none -> 17.6 us  [shards(): lax.ppermute(outgoing[mask], inside, [(i, i ^ mask) for i in range(device...]
    ppermute x0 -> x15, waiting for transfers between devices: none -> 6.43 us  [shards(): lax.ppermute(outgoing[mask], inside, [(i, i ^ mask) for i in range(device...]
  transfers between devices with their start and end apart: 14 -> 29, of which waited for: 6 -> 9; matrix products, arithmetic and copies ran while one was open for 0% -> 0% of each run, Pallas kernels for 16% -> 15%
where the time goes in v11:
time: 92.5 us; the launch traced here: 92.3 us
  Pallas kernels  38.6 us (42%)
  waiting for transfers between devices  26.1 us (28%)
  starting transfers between devices  24.3 us (26%)
  local copies, waits for them, and re-layouts  2.26 us (2%)
  between operations  1.05 us (1%)
    ppermute x6, waiting for transfers between devices, shards(): column = [lax.ppermute(rows, GROUP, onward) for rows in column]  19.7 us
    ppermute x15, starting transfers between devices, shards(): lax.ppermute(outgoing[mask], inside, [(i, i ^ mask) for i in range(device...  17.6 us
    pallas_call x1, Pallas kernels, shards(): pl.pallas_call(functools.partial(first_kernel, chips if ring else 0, len(...  11.8 us
    pallas_call x8, Pallas kernels, project(): pl.pallas_call(functools.partial(project_kernel, first_rows, new, ask), o...  11.1 us
    pallas_call x1, Pallas kernels, shards(): pl.pallas_call(second_kernel, out_shape=(jax.ShapeDtypeStruct((rows_here,...  10.4 us
    ppermute x15, waiting for transfers between devices, shards(): lax.ppermute(outgoing[mask], inside, [(i, i ^ mask) for i in range(device...  6.43 us
    ppermute x6, starting transfers between devices, shards(): column = [lax.ppermute(rows, GROUP, onward) for rows in column]  6.12 us
    pallas_call x1, Pallas kernels, shards(): pl.pallas_call(keep_kernel, out_shape=[*[jax.ShapeDtypeStruct(w.shape[1:]...  2.8 us
  transfers between devices with their start and end apart: 29, of which 9 were waited for; matrix products, arithmetic and copies ran while one was open for 0% of the time, Pallas kernels for 15%

profile of v11, /device:TPU:0, one launch (start us, length us, event | category | flops | bytes accessed | tf_op | source)
XLA Modules:
  0.0 92.3 jit_solution(14498334609809995972)
XLA Ops:
  0.6 1.9 %split.1 = (bf16[264,512]{1,0:T(8,128)(2,1)}, bf16[256,512]{1,0:T(8,128)(2,1)}) custom-call(bf16[512,512]{1,0:T(8,128)(2,1)} %points.3, s32[1,512]{1,0:T(1,128)} %bitcast.3, s32[3,8]{1,0:T(4,128)} %bitcast.5), custom_call_target="tpu_custom_call" | custom-call | tf_op jit(solution)/shard_map/split/pallas_call | solution.py:465
  2.5 3.1 %collective-permute-start = (bf16[264,512]{1,0:T(8,128)(2,1)}, bf16[264,512]{1,0:T(8,128)(2,1)S(1)}, u32[]{:S(2)}, u32[]{:S(2)}) collective-permute-start(bf16[264,512]{1,0:T(8,128)(2,1)} %get-tuple-element.46.refs_0_), channel_id=1, source_target_pairs={{0,2},{1,3},{2,4},{3,5},{4,6},{5,7},{6,0},{7,1},{8,10},{9,11},{10,... | collective-permute-start | bytes 811016 | tf_op jit(solution)/shard_map/ppermute | solution.py:547
  5.6 0.5 collective-permute-start.4
  6.1 1.6 %collective-permute-start.2 = (bf16[256,512]{1,0:T(8,128)(2,1)}, bf16[256,512]{1,0:T(8,128)(2,1)S(1)}, u32[]{:S(2)}, u32[]{:S(2)}) collective-permute-start(bf16[256,512]{1,0:T(8,128)(2,1)} %get-tuple-element.49.refs_1_), channel_id=1, source_target_pairs={{0,2},{1,3},{2,4},{3,5},{4,6},{5,7},{6,0},{7,1},{8,10},{9,11},{10,... | collective-permute-start | bytes 786440 | tf_op jit(solution)/shard_map/ppermute | solution.py:547
  7.7 1.2 %copy-done = bf16[2,512,512]{2,1,0:T(8,128)(2,1)S(1)} copy-done((bf16[2,512,512]{2,1,0:T(8,128)(2,1)S(1)}, bf16[2,512,512]{2,1,0:T(8,128)(2,1)}, u32[]{:S(2)}) %copy-start) | copy-done | bytes 1048600
  8.9 0.7 copy-done.3
  9.6 2.8 %keep.1 = (bf16[512,1536]{1,0:T(8,128)(2,1)S(1)}, bf16[512,512]{1,0:T(8,128)(2,1)S(1)}, bf16[512,2048]{1,0:T(8,128)(2,1)S(1)}, bf16[2048,512]{1,0:T(8,128)(2,1)S(1)}, f32[4,512]{1,0:T(4,128)S(1)}) custom-call(bf16[2,512,1536]{2,1,0:T(8,128)(2,1)} %w_qkv.1, bf16[2,512,512]{2,1,0:T(8,128)(2,1)S(1)} %copy-done, bf16[2,512,2048]{2,1,0:T(8,128)(2,1)} %w_up.1, ...), custom_call_target="tpu_custom_call" | custom-call | tf_op jit(solution)/shard_map/keep/pallas_call | solution.py:484
  12.4 2.7 %collective-permute-done.refs_0_ = bf16[264,512]{1,0:T(8,128)(2,1)S(1)} collective-permute-done((bf16[264,512]{1,0:T(8,128)(2,1)}, bf16[264,512]{1,0:T(8,128)(2,1)S(1)}, u32[]{:S(2)}, u32[]{:S(2)}) %collective-permute-start) | collective-permute-done | bytes 270368 | tf_op jit(solution)/shard_map/ppermute | solution.py:547
  15.1 0.0 collective-permute-start.1
  15.2 2.9 %project_own.1 = (bf16[4096,1024]{1,0:T(8,128)(2,1)S(1)}, bf16[512,512]{1,0:T(8,128)(2,1)S(1)}) custom-call(bf16[264,512]{1,0:T(8,128)(2,1)S(1)} %copy-done.9, bf16[256,512]{1,0:T(8,128)(2,1)S(1)} %copy-done.10, bf16[264,512]{1,0:T(8,128)(2,1)S(1)} %collective-permute-done.3.refs_2_, bf16[256,512]{1,0:T(8,128)(2,1)S(1)} %collective-permute-done.4.refs_3_, ...), custom_call_target="tpu_custom_call" | custom-call | flops 1073741824 | bytes 4718592 | tf_op jit(solution)/shard_map/project_own/pallas_call | solution.py:524
  18.1 2.6 %collective-permute-done.2.refs_1_ = bf16[256,512]{1,0:T(8,128)(2,1)S(1)} collective-permute-done((bf16[256,512]{1,0:T(8,128)(2,1)}, bf16[256,512]{1,0:T(8,128)(2,1)S(1)}, u32[]{:S(2)}, u32[]{:S(2)}) %collective-permute-start.2) | collective-permute-done | bytes 262176 | tf_op jit(solution)/shard_map/ppermute | solution.py:547
  20.8 0.0 collective-permute-start.6
  20.8 1.3 %project.7.refs_4_ = bf16[4096,1024]{1,0:T(8,128)(2,1)S(1)} custom-call(bf16[264,512]{1,0:T(8,128)(2,1)S(1)} %collective-permute-done.refs_0_, bf16[256,512]{1,0:T(8,128)(2,1)S(1)} %collective-permute-done.2.refs_1_, f32[4,512]{1,0:T(4,128)S(1)} %get-tuple-element.50.refs_4_.refs_2_.refs_1_.gains, ...), custom_call_target="tpu_custom_call", output_to_operand_aliasing={{}: (4, {})} | custom-call | flops 536870912 | bytes 3145728 | tf_op jit(solution)/shard_map/project/pallas_call | solution.py:524
  22.1 3.6 %collective-permute-done.1.beyond.refs_0_ = bf16[264,512]{1,0:T(8,128)(2,1)S(1)} collective-permute-done((bf16[264,512]{1,0:T(8,128)(2,1)S(1)}, bf16[264,512]{1,0:T(8,128)(2,1)S(1)}, u32[]{:S(2)}, u32[]{:S(2)}) %collective-permute-start.1) | collective-permute-done | bytes 270368 | tf_op jit(solution)/shard_map/ppermute | solution.py:547
  25.7 0.9 collective-permute-start.5
  26.6 1.3 %project.8.refs_4_ = bf16[4096,1024]{1,0:T(8,128)(2,1)S(1)} custom-call(bf16[264,512]{1,0:T(8,128)(2,1)S(1)} %collective-permute-done.7.refs_0_, bf16[256,512]{1,0:T(8,128)(2,1)S(1)} %collective-permute-done.8.refs_1_, f32[4,512]{1,0:T(4,128)S(1)} %get-tuple-element.50.refs_4_.refs_2_.refs_1_.gains, ...), custom_call_target="tpu_custom_call", output_to_operand_aliasing={{}: (4, {})} | custom-call | flops 536870912 | bytes 3145728 | tf_op jit(solution)/shard_map/project/pallas_call | solution.py:524
  27.9 3.7 %collective-permute-done.6.refs_1_ = bf16[256,512]{1,0:T(8,128)(2,1)S(1)} collective-permute-done((bf16[256,512]{1,0:T(8,128)(2,1)S(1)}, bf16[256,512]{1,0:T(8,128)(2,1)S(1)}, u32[]{:S(2)}, u32[]{:S(2)}) %collective-permute-start.6) | collective-permute-done | bytes 262176 | tf_op jit(solution)/shard_map/ppermute | solution.py:547
  31.7 0.5 collective-permute-start.9
  32.2 0.6 index.1
  32.8 1.6 %project.9 = (bf16[4096,1024]{1,0:T(8,128)(2,1)S(1)}, bf16[512,512]{1,0:T(8,128)(2,1)S(1)}) custom-call(bf16[264,512]{1,0:T(8,128)(2,1)S(1)} %collective-permute-done.1.beyond.refs_0_, bf16[256,512]{1,0:T(8,128)(2,1)S(1)} %collective-permute-done.6.refs_1_, ...), custom_call_target="tpu_custom_call", output_to_operand_aliasing={{0}: (4, {})} | custom-call | flops 536870912 | bytes 3145728 | tf_op jit(solution)/shard_map/project/pallas_call | solution.py:524
  34.4 3.0 %collective-permute-done.5.refs_0_ = bf16[264,512]{1,0:T(8,128)(2,1)S(1)} collective-permute-done((bf16[264,512]{1,0:T(8,128)(2,1)S(1)}, bf16[264,512]{1,0:T(8,128)(2,1)S(1)}, u32[]{:S(2)}, u32[]{:S(2)}) %collective-permute-start.5) | collective-permute-done | bytes 270368 | tf_op jit(solution)/shard_map/ppermute | solution.py:547
  37.5 1.3 %project.10.refs_4_ = bf16[4096,1024]{1,0:T(8,128)(2,1)S(1)} custom-call(bf16[264,512]{1,0:T(8,128)(2,1)S(1)} %collective-permute-done.10.refs_0_, bf16[256,512]{1,0:T(8,128)(2,1)S(1)} %collective-permute-done.11.refs_1_, f32[4,512]{1,0:T(4,128)S(1)} %get-tuple-element.50.refs_4_.refs_2_.refs_1_.gains, ...), custom_call_target="tpu_custom_call", output_to_operand_aliasing={{}: (4, {})} | custom-call | flops 536870912 | bytes 3145728 | tf_op jit(solution)/shard_map/project/pallas_call | solution.py:524
  38.8 4.0 %collective-permute-done.9.refs_0_ = bf16[256,512]{1,0:T(8,128)(2,1)S(1)} collective-permute-done((bf16[256,512]{1,0:T(8,128)(2,1)S(1)}, bf16[256,512]{1,0:T(8,128)(2,1)S(1)}, u32[]{:S(2)}, u32[]{:S(2)}) %collective-permute-start.9) | collective-permute-done | bytes 262176 | tf_op jit(solution)/shard_map/ppermute | solution.py:547
  42.8 1.3 %project.11.refs_3_ = bf16[4096,1024]{1,0:T(8,128)(2,1)S(1)} custom-call(bf16[264,512]{1,0:T(8,128)(2,1)S(1)} %collective-permute-done.5.refs_0_, bf16[264,512]{1,0:T(8,128)(2,1)S(1)} %collective-permute-done.13.refs_1_, f32[4,512]{1,0:T(4,128)S(1)} %get-tuple-element.50.refs_4_.refs_2_.refs_1_.gains, ...), custom_call_target="tpu_custom_call", output_to_operand_aliasing={{}: (4, {})} | custom-call | flops 536870912 | bytes 3145728 | tf_op jit(solution)/shard_map/project/pallas_call | solution.py:524
  44.1 0.7 project.12.refs_3_
  44.8 0.0 copy-start.2
  44.8 0.7 project.13.keyed
  45.5 0.0 copy-start.1
  45.5 0.3 copy-done.2
  45.8 11.8 %block_first.1 = (bf16[264,128]{1,0:T(8,128)(2,1)S(1)}, bf16[264,128]{1,0:T(8,128)(2,1)S(1)}, bf16[264,128]{1,0:T(8,128)(2,1)S(1)}, bf16[264,128]{1,0:T(8,128)(2...) custom-call(s32[3,8]{1,0:T(4,128)S(1)} %bitcast.6, ...), custom_call_target="tpu_custom_call" | custom-call | tf_op jit(solution)/shard_map/block_first/pallas_call | solution.py:596
  57.6 0.6 collective-permute-start.14
  58.2 1.4 %collective-permute-start.16 = (bf16[264,128]{1,0:T(8,128)(2,1)S(1)}, bf16[264,128]{1,0:T(8,128)(2,1)S(1)}, u32[]{:S(2)}, u32[]{:S(2)}) collective-permute-start(bf16[264,128]{1,0:T(8,128)(2,1)S(1)} %get-tuple-element.77), channel_id=1, source_target_pairs={{0,3},{1,2},{2,1},{3,0},{8,11},{9,10},{10,9},{11,8},{16,19},{17,18... | collective-permute-start | bytes 202760 | tf_op jit(solution)/shard_map/ppermute | solution.py:627
  59.6 1.7 %collective-permute-start.17 = (bf16[264,128]{1,0:T(8,128)(2,1)S(1)}, bf16[264,128]{1,0:T(8,128)(2,1)S(1)}, u32[]{:S(2)}, u32[]{:S(2)}) collective-permute-start(bf16[264,128]{1,0:T(8,128)(2,1)S(1)} %get-tuple-element.78), channel_id=1, source_target_pairs={{0,8},{1,9},{2,10},{3,11},{8,0},{9,1},{10,2},{11,3},{16,24},{17,25... | collective-permute-start | bytes 202760 | tf_op jit(solution)/shard_map/ppermute | solution.py:627
  61.3 0.4 collective-permute-start.18
  61.7 1.1 %collective-permute-start.19 = (bf16[264,128]{1,0:T(8,128)(2,1)S(1)}, bf16[264,128]{1,0:T(8,128)(2,1)S(1)}, u32[]{:S(2)}, u32[]{:S(2)}) collective-permute-start(bf16[264,128]{1,0:T(8,128)(2,1)S(1)} %get-tuple-element.80), channel_id=1, source_target_pairs={{0,10},{1,11},{2,8},{3,9},{8,2},{9,3},{10,0},{11,1},{16,26},{17,27... | collective-permute-start | bytes 202760 | tf_op jit(solution)/shard_map/ppermute | solution.py:627
  62.8 0.2 collective-permute-done.15.refs_2_
  63.0 1.0 %collective-permute-start.20 = (bf16[264,128]{1,0:T(8,128)(2,1)S(1)}, bf16[264,128]{1,0:T(8,128)(2,1)S(1)}, u32[]{:S(2)}, u32[]{:S(2)}) collective-permute-start(bf16[264,128]{1,0:T(8,128)(2,1)S(1)} %get-tuple-element.81), channel_id=1, source_target_pairs={{0,11},{1,10},{2,9},{3,8},{8,3},{9,2},{10,1},{11,0},{16,27},{17,26... | collective-permute-start | bytes 202760 | tf_op jit(solution)/shard_map/ppermute | solution.py:627
  64.0 1.7 %collective-permute-start.21 = (bf16[264,128]{1,0:T(8,128)(2,1)S(1)}, bf16[264,128]{1,0:T(8,128)(2,1)S(1)}, u32[]{:S(2)}, u32[]{:S(2)}) collective-permute-start(bf16[264,128]{1,0:T(8,128)(2,1)S(1)} %get-tuple-element.82), channel_id=1, source_target_pairs={{0,16},{1,17},{2,18},{3,19},{8,24},{9,25},{10,26},{11,27},{16,0},{... | collective-permute-start | bytes 202760 | tf_op jit(solution)/shard_map/ppermute | solution.py:627
  65.7 0.4 collective-permute-start.22
  66.1 1.8 %collective-permute-done.18.refs_5_ = bf16[264,128]{1,0:T(8,128)(2,1)S(1)} collective-permute-done((bf16[264,128]{1,0:T(8,128)(2,1)S(1)}, bf16[264,128]{1,0:T(8,128)(2,1)S(1)}, u32[]{:S(2)}, u32[]{:S(2)}) %collective-permute-start.18) | collective-permute-done | bytes 67616 | tf_op jit(solution)/shard_map/ppermute | solution.py:627
  67.9 0.7 collective-permute-start.23
  68.7 2.4 %collective-permute-start.24 = (bf16[264,128]{1,0:T(8,128)(2,1)S(1)}, bf16[264,128]{1,0:T(8,128)(2,1)S(1)}, u32[]{:S(2)}, u32[]{:S(2)}) collective-permute-start(bf16[264,128]{1,0:T(8,128)(2,1)S(1)} %get-tuple-element.85), channel_id=1, source_target_pairs={{0,19},{1,18},{2,17},{3,16},{8,27},{9,26},{10,25},{11,24},{16,3},{... | collective-permute-start | bytes 202760 | tf_op jit(solution)/shard_map/ppermute | solution.py:627
  71.1 2.6 %collective-permute-start.25 = (bf16[264,128]{1,0:T(8,128)(2,1)S(1)}, bf16[264,128]{1,0:T(8,128)(2,1)S(1)}, u32[]{:S(2)}, u32[]{:S(2)}) collective-permute-start(bf16[264,128]{1,0:T(8,128)(2,1)S(1)} %get-tuple-element.86), channel_id=1, source_target_pairs={{0,24},{1,25},{2,26},{3,27},{8,16},{9,17},{10,18},{11,19},{16,8},{... | collective-permute-start | bytes 202760 | tf_op jit(solution)/shard_map/ppermute | solution.py:627
  73.7 0.1 collective-permute-start.26
  73.8 1.1 %collective-permute-start.27 = (bf16[264,128]{1,0:T(8,128)(2,1)S(1)}, bf16[264,128]{1,0:T(8,128)(2,1)S(1)}, u32[]{:S(2)}, u32[]{:S(2)}) collective-permute-start(bf16[264,128]{1,0:T(8,128)(2,1)S(1)} %get-tuple-element.88), channel_id=1, source_target_pairs={{0,26},{1,27},{2,24},{3,25},{8,18},{9,19},{10,16},{11,17},{16,10},... | collective-permute-start | bytes 202760 | tf_op jit(solution)/shard_map/ppermute | solution.py:627
  74.9 2.4 %collective-permute-start.28 = (bf16[264,128]{1,0:T(8,128)(2,1)S(1)}, bf16[264,128]{1,0:T(8,128)(2,1)S(1)}, u32[]{:S(2)}, u32[]{:S(2)}) collective-permute-start(bf16[264,128]{1,0:T(8,128)(2,1)S(1)} %get-tuple-element.89), channel_id=1, source_target_pairs={{0,27},{1,26},{2,25},{3,24},{8,19},{9,18},{10,17},{11,16},{16,11},... | collective-permute-start | bytes 202760 | tf_op jit(solution)/shard_map/ppermute | solution.py:627
  77.3 4.4 %collective-permute-done.26.refs_13_ = bf16[264,128]{1,0:T(8,128)(2,1)S(1)} collective-permute-done((bf16[264,128]{1,0:T(8,128)(2,1)S(1)}, bf16[264,128]{1,0:T(8,128)(2,1)S(1)}, u32[]{:S(2)}, u32[]{:S(2)}) %collective-permute-start.26) | collective-permute-done | bytes 67616 | tf_op jit(solution)/shard_map/ppermute | solution.py:627
  81.7 10.4 %block_second.1 = (bf16[512,512]{1,0:T(8,128)(2,1)}, f32[3,512]{1,0:T(4,128)}) custom-call(s32[3,8]{1,0:T(4,128)S(1)} %bitcast.7, f32[4,512]{1,0:T(4,128)S(1)} %copy-done.4, bf16[2,512,1536]{2,1,0:T(8,128)(2,1)} %w_qkv.1, bf16[2,512,512]{2,1,0:T(8,128)(2,1)S(1)} %copy-done.1, bf16[2,512,2048]{2,1,0:T(8,128)(2,1)} %w_up.1, bf16[2,2048,512]{2,1,0:T(8,128)(2,1)} %w_down.1, ...), custom_call_target="tpu_custom_call" | custom-call | tf_op jit(solution)/shard_map/block_second/pallas_call | solution.py:633
  (45 shorter events, 0.1 us)
Async XLA Ops:
  2.5 12.6 %collective-permute-start = (bf16[264,512]{1,0:T(8,128)(2,1)}, bf16[264,512]{1,0:T(8,128)(2,1)S(1)}, u32[]{:S(2)}, u32[]{:S(2)}) collective-permute-start(bf16[264,512]{1,0:T(8,128)(2,1)} %get-tuple-element.46.refs_0_), channel_id=1, source_target_pairs={{0,2},{1,3},{2,4},{3,5},{4,6},{5,7},{6,0},{7,1},{8,10},{9,11},{10,... | collective-permute-start | bytes 811016 | tf_op jit(solution)/shard_map/ppermute | solution.py:547
  5.6 9.6 %collective-permute-start.3 = (bf16[264,512]{1,0:T(8,128)(2,1)}, bf16[264,512]{1,0:T(8,128)(2,1)S(1)}, u32[]{:S(2)}, u32[]{:S(2)}) collective-permute-start(bf16[264,512]{1,0:T(8,128)(2,1)} %get-tuple-element.46.refs_0_), channel_id=1, source_target_pairs={{0,1},{1,0},{2,3},{3,2},{4,5},{5,4},{6,7},{7,6},{8,9},{9,8},{10,11... | collective-permute-start | bytes 811016 | tf_op jit(solution)/shard_map/ppermute | solution.py:544
  5.6 9.6 %collective-permute-start.4 = (bf16[256,512]{1,0:T(8,128)(2,1)}, bf16[256,512]{1,0:T(8,128)(2,1)S(1)}, u32[]{:S(2)}, u32[]{:S(2)}) collective-permute-start(bf16[256,512]{1,0:T(8,128)(2,1)} %get-tuple-element.49.refs_1_), channel_id=1, source_target_pairs={{0,1},{1,0},{2,3},{3,2},{4,5},{5,4},{6,7},{7,6},{8,9},{9,8},{10,11... | collective-permute-start | bytes 786440 | tf_op jit(solution)/shard_map/ppermute | solution.py:544
  6.1 14.7 %collective-permute-start.2 = (bf16[256,512]{1,0:T(8,128)(2,1)}, bf16[256,512]{1,0:T(8,128)(2,1)S(1)}, u32[]{:S(2)}, u32[]{:S(2)}) collective-permute-start(bf16[256,512]{1,0:T(8,128)(2,1)} %get-tuple-element.49.refs_1_), channel_id=1, source_target_pairs={{0,2},{1,3},{2,4},{3,5},{4,6},{5,7},{6,0},{7,1},{8,10},{9,11},{10,... | collective-permute-start | bytes 786440 | tf_op jit(solution)/shard_map/ppermute | solution.py:547
  7.7 1.2 %copy-start = (bf16[2,512,512]{2,1,0:T(8,128)(2,1)S(1)}, bf16[2,512,512]{2,1,0:T(8,128)(2,1)}, u32[]{:S(2)}) copy-start(bf16[2,512,512]{2,1,0:T(8,128)(2,1)} %w_proj.1) | copy-start | bytes 3145732
  8.9 0.7 copy-start.3
  9.6 5.6 %copy-start.9 = (bf16[264,512]{1,0:T(8,128)(2,1)S(1)}, bf16[264,512]{1,0:T(8,128)(2,1)}, u32[]{:S(2)}) copy-start(bf16[264,512]{1,0:T(8,128)(2,1)} %get-tuple-element.46.refs_0_) | copy-start | bytes 811012
  9.6 5.6 %copy-start.10 = (bf16[256,512]{1,0:T(8,128)(2,1)S(1)}, bf16[256,512]{1,0:T(8,128)(2,1)}, u32[]{:S(2)}) copy-start(bf16[256,512]{1,0:T(8,128)(2,1)} %get-tuple-element.49.refs_1_) | copy-start | bytes 786436
  15.1 10.6 %collective-permute-start.1 = (bf16[264,512]{1,0:T(8,128)(2,1)S(1)}, bf16[264,512]{1,0:T(8,128)(2,1)S(1)}, u32[]{:S(2)}, u32[]{:S(2)}) collective-permute-start(bf16[264,512]{1,0:T(8,128)(2,1)S(1)} %collective-permute-done.refs_0_), channel_id=1, source_target_pairs={{0,2},{1,3},{2,4},{3,5},{4,6},{5,7},{6,0},{7,1},{8,10},{9,11},{10,... | collective-permute-start | bytes 811016 | tf_op jit(solution)/shard_map/ppermute | solution.py:547
  15.2 11.4 %collective-permute-start.7 = (bf16[264,512]{1,0:T(8,128)(2,1)S(1)}, bf16[264,512]{1,0:T(8,128)(2,1)S(1)}, u32[]{:S(2)}, u32[]{:S(2)}) collective-permute-start(bf16[264,512]{1,0:T(8,128)(2,1)S(1)} %collective-permute-done.refs_0_), channel_id=1, source_target_pairs={{0,1},{1,0},{2,3},{3,2},{4,5},{5,4},{6,7},{7,6},{8,9},{9,8},{10,11... | collective-permute-start | bytes 811016 | tf_op jit(solution)/shard_map/ppermute | solution.py:564
  20.8 5.8 %collective-permute-start.8 = (bf16[256,512]{1,0:T(8,128)(2,1)S(1)}, bf16[256,512]{1,0:T(8,128)(2,1)S(1)}, u32[]{:S(2)}, u32[]{:S(2)}) collective-permute-start(bf16[256,512]{1,0:T(8,128)(2,1)S(1)} %collective-permute-done.2.refs_1_), channel_id=1, source_target_pairs={{0,1},{1,0},{2,3},{3,2},{4,5},{5,4},{6,7},{7,6},{8,9},{9,8},{10,11... | collective-permute-start | bytes 786440 | tf_op jit(solution)/shard_map/ppermute | solution.py:564
  20.8 10.9 %collective-permute-start.6 = (bf16[256,512]{1,0:T(8,128)(2,1)S(1)}, bf16[256,512]{1,0:T(8,128)(2,1)S(1)}, u32[]{:S(2)}, u32[]{:S(2)}) collective-permute-start(bf16[256,512]{1,0:T(8,128)(2,1)S(1)} %collective-permute-done.2.refs_1_), channel_id=1, source_target_pairs={{0,2},{1,3},{2,4},{3,5},{4,6},{5,7},{6,0},{7,1},{8,10},{9,11},{10,... | collective-permute-start | bytes 786440 | tf_op jit(solution)/shard_map/ppermute | solution.py:547
  22.1 10.1 %copy-start.5 = (s32[512]{0:T(512)S(1)}, s32[512]{0:T(512)}, u32[]{:S(2)}) copy-start(s32[512]{0:T(512)} %param.13) | copy-start | bytes 6148
  25.7 11.7 %collective-permute-start.5 = (bf16[264,512]{1,0:T(8,128)(2,1)S(1)}, bf16[264,512]{1,0:T(8,128)(2,1)S(1)}, u32[]{:S(2)}, u32[]{:S(2)}) collective-permute-start(bf16[264,512]{1,0:T(8,128)(2,1)S(1)} %collective-permute-done.1.beyond.refs_0_), channel_id=1, source_target_pairs={{0,2},{1,3},{2,4},{3,5},{4,6},{5,7},{6,0},{7,1},{8,10},{9,11},{10,... | collective-permute-start | bytes 811016 | tf_op jit(solution)/shard_map/ppermute | solution.py:547
  26.6 10.9 %collective-permute-start.10 = (bf16[264,512]{1,0:T(8,128)(2,1)S(1)}, bf16[264,512]{1,0:T(8,128)(2,1)S(1)}, u32[]{:S(2)}, u32[]{:S(2)}) collective-permute-start(bf16[264,512]{1,0:T(8,128)(2,1)S(1)} %collective-permute-done.1.beyond.refs_0_), channel_id=1, source_target_pairs={{0,1},{1,0},{2,3},{3,2},{4,5},{5,4},{6,7},{7,6},{8,9},{9,8},{10,11... | collective-permute-start | bytes 811016 | tf_op jit(solution)/shard_map/ppermute | solution.py:564
  31.7 5.8 %collective-permute-start.11 = (bf16[256,512]{1,0:T(8,128)(2,1)S(1)}, bf16[256,512]{1,0:T(8,128)(2,1)S(1)}, u32[]{:S(2)}, u32[]{:S(2)}) collective-permute-start(bf16[256,512]{1,0:T(8,128)(2,1)S(1)} %collective-permute-done.6.refs_1_), channel_id=1, source_target_pairs={{0,1},{1,0},{2,3},{3,2},{4,5},{5,4},{6,7},{7,6},{8,9},{9,8},{10,11... | collective-permute-start | bytes 786440 | tf_op jit(solution)/shard_map/ppermute | solution.py:564
  31.7 11.1 %collective-permute-start.9 = (bf16[256,512]{1,0:T(8,128)(2,1)S(1)}, bf16[256,512]{1,0:T(8,128)(2,1)S(1)}, u32[]{:S(2)}, u32[]{:S(2)}) collective-permute-start(bf16[256,512]{1,0:T(8,128)(2,1)S(1)} %collective-permute-done.6.refs_1_), channel_id=1, source_target_pairs={{0,2},{1,3},{2,4},{3,5},{4,6},{5,7},{6,0},{7,1},{8,10},{9,11},{10,... | collective-permute-start | bytes 786440 | tf_op jit(solution)/shard_map/ppermute | solution.py:547
  37.5 5.3 %collective-permute-start.13 = (bf16[264,512]{1,0:T(8,128)(2,1)S(1)}, bf16[264,512]{1,0:T(8,128)(2,1)S(1)}, u32[]{:S(2)}, u32[]{:S(2)}) collective-permute-start(bf16[264,512]{1,0:T(8,128)(2,1)S(1)} %collective-permute-done.5.refs_0_), channel_id=1, source_target_pairs={{0,1},{1,0},{2,3},{3,2},{4,5},{5,4},{6,7},{7,6},{8,9},{9,8},{10,11... | collective-permute-start | bytes 811016 | tf_op jit(solution)/shard_map/ppermute | solution.py:564
  42.8 2.0 %collective-permute-start.12 = (bf16[256,512]{1,0:T(8,128)(2,1)S(1)}, bf16[256,512]{1,0:T(8,128)(2,1)S(1)}, u32[]{:S(2)}, u32[]{:S(2)}) collective-permute-start(bf16[256,512]{1,0:T(8,128)(2,1)S(1)} %collective-permute-done.9.refs_0_), channel_id=1, source_target_pairs={{0,1},{1,0},{2,3},{3,2},{4,5},{5,4},{6,7},{7,6},{8,9},{9,8},{10,11... | collective-permute-start | bytes 786440 | tf_op jit(solution)/shard_map/ppermute | solution.py:564
  44.8 1.0 %copy-start.2 = (bf16[512,512]{1,0:T(8,128)(2,1)S(1)}, bf16[512,512]{1,0:T(8,128)(2,1)}, u32[]{:S(2)}) copy-start(bf16[512,512]{1,0:T(8,128)(2,1)} %points.3) | copy-start | bytes 1572868
  44.8 1.0 %copy-start.6 = (s32[8,3]{0,1:T(4,128)S(1)}, s32[8,3]{0,1:T(4,128)}, u32[]{:S(2)}) copy-start(s32[8,3]{0,1:T(4,128)} %param.11) | copy-start | bytes 292
  45.5 36.2 %copy-start.1 = (bf16[2,512,512]{2,1,0:T(8,128)(2,1)S(1)}, bf16[2,512,512]{2,1,0:T(8,128)(2,1)}, u32[]{:S(2)}) copy-start(bf16[2,512,512]{2,1,0:T(8,128)(2,1)} %w_proj.1) | copy-start | bytes 3145732
  45.5 36.2 %copy-start.4 = (f32[4,512]{1,0:T(4,128)S(1)}, f32[4,512]{1,0:T(4,128)}, u32[]{:S(2)}) copy-start(f32[4,512]{1,0:T(4,128)} %gains.1) | copy-start | bytes 24580
  45.5 36.2 %copy-start.7 = (bf16[3,512]{1,0:T(4,128)(2,1)S(1)}, bf16[3,512]{1,0:T(4,128)(2,1)}, u32[]{:S(2)}) copy-start(bf16[3,512]{1,0:T(4,128)(2,1)} %w_head.1) | copy-start | bytes 9220
  45.5 36.2 %copy-start.8 = (s32[8,3]{0,1:T(4,128)S(1)}, s32[8,3]{0,1:T(4,128)}, u32[]{:S(2)}) copy-start(s32[8,3]{0,1:T(4,128)} %param.12) | copy-start | bytes 292
  57.6 4.1 %collective-permute-start.14 = (bf16[264,128]{1,0:T(8,128)(2,1)S(1)}, bf16[264,128]{1,0:T(8,128)(2,1)S(1)}, u32[]{:S(2)}, u32[]{:S(2)}) collective-permute-start(bf16[264,128]{1,0:T(8,128)(2,1)S(1)} %get-tuple-element.75), channel_id=1, source_target_pairs={{0,1},{1,0},{2,3},{3,2},{8,9},{9,8},{10,11},{11,10},{16,17},{17,16... | collective-permute-start | bytes 202760 | tf_op jit(solution)/shard_map/ppermute | solution.py:627
  58.2 4.8 %collective-permute-start.15 = (bf16[264,128]{1,0:T(8,128)(2,1)S(1)}, bf16[264,128]{1,0:T(8,128)(2,1)S(1)}, u32[]{:S(2)}, u32[]{:S(2)}) collective-permute-start(bf16[264,128]{1,0:T(8,128)(2,1)S(1)} %get-tuple-element.76), channel_id=1, source_target_pairs={{0,2},{1,3},{2,0},{3,1},{8,10},{9,11},{10,8},{11,9},{16,18},{17,19... | collective-permute-start | bytes 202760 | tf_op jit(solution)/shard_map/ppermute | solution.py:627
  58.2 5.8 %collective-permute-start.16 = (bf16[264,128]{1,0:T(8,128)(2,1)S(1)}, bf16[264,128]{1,0:T(8,128)(2,1)S(1)}, u32[]{:S(2)}, u32[]{:S(2)}) collective-permute-start(bf16[264,128]{1,0:T(8,128)(2,1)S(1)} %get-tuple-element.77), channel_id=1, source_target_pairs={{0,3},{1,2},{2,1},{3,0},{8,11},{9,10},{10,9},{11,8},{16,19},{17,18... | collective-permute-start | bytes 202760 | tf_op jit(solution)/shard_map/ppermute | solution.py:627
  59.6 6.1 %collective-permute-start.17 = (bf16[264,128]{1,0:T(8,128)(2,1)S(1)}, bf16[264,128]{1,0:T(8,128)(2,1)S(1)}, u32[]{:S(2)}, u32[]{:S(2)}) collective-permute-start(bf16[264,128]{1,0:T(8,128)(2,1)S(1)} %get-tuple-element.78), channel_id=1, source_target_pairs={{0,8},{1,9},{2,10},{3,11},{8,0},{9,1},{10,2},{11,3},{16,24},{17,25... | collective-permute-start | bytes 202760 | tf_op jit(solution)/shard_map/ppermute | solution.py:627
  61.3 6.7 %collective-permute-start.18 = (bf16[264,128]{1,0:T(8,128)(2,1)S(1)}, bf16[264,128]{1,0:T(8,128)(2,1)S(1)}, u32[]{:S(2)}, u32[]{:S(2)}) collective-permute-start(bf16[264,128]{1,0:T(8,128)(2,1)S(1)} %get-tuple-element.79), channel_id=1, source_target_pairs={{0,9},{1,8},{2,11},{3,10},{8,1},{9,0},{10,3},{11,2},{16,25},{17,24... | collective-permute-start | bytes 202760 | tf_op jit(solution)/shard_map/ppermute | solution.py:627
  61.7 7.0 %collective-permute-start.19 = (bf16[264,128]{1,0:T(8,128)(2,1)S(1)}, bf16[264,128]{1,0:T(8,128)(2,1)S(1)}, u32[]{:S(2)}, u32[]{:S(2)}) collective-permute-start(bf16[264,128]{1,0:T(8,128)(2,1)S(1)} %get-tuple-element.80), channel_id=1, source_target_pairs={{0,10},{1,11},{2,8},{3,9},{8,2},{9,3},{10,0},{11,1},{16,26},{17,27... | collective-permute-start | bytes 202760 | tf_op jit(solution)/shard_map/ppermute | solution.py:627
  63.0 8.1 %collective-permute-start.20 = (bf16[264,128]{1,0:T(8,128)(2,1)S(1)}, bf16[264,128]{1,0:T(8,128)(2,1)S(1)}, u32[]{:S(2)}, u32[]{:S(2)}) collective-permute-start(bf16[264,128]{1,0:T(8,128)(2,1)S(1)} %get-tuple-element.81), channel_id=1, source_target_pairs={{0,11},{1,10},{2,9},{3,8},{8,3},{9,2},{10,1},{11,0},{16,27},{17,26... | collective-permute-start | bytes 202760 | tf_op jit(solution)/shard_map/ppermute | solution.py:627
  64.0 9.7 %collective-permute-start.21 = (bf16[264,128]{1,0:T(8,128)(2,1)S(1)}, bf16[264,128]{1,0:T(8,128)(2,1)S(1)}, u32[]{:S(2)}, u32[]{:S(2)}) collective-permute-start(bf16[264,128]{1,0:T(8,128)(2,1)S(1)} %get-tuple-element.82), channel_id=1, source_target_pairs={{0,16},{1,17},{2,18},{3,19},{8,24},{9,25},{10,26},{11,27},{16,0},{... | collective-permute-start | bytes 202760 | tf_op jit(solution)/shard_map/ppermute | solution.py:627
  65.7 8.1 %collective-permute-start.22 = (bf16[264,128]{1,0:T(8,128)(2,1)S(1)}, bf16[264,128]{1,0:T(8,128)(2,1)S(1)}, u32[]{:S(2)}, u32[]{:S(2)}) collective-permute-start(bf16[264,128]{1,0:T(8,128)(2,1)S(1)} %get-tuple-element.83), channel_id=1, source_target_pairs={{0,17},{1,16},{2,19},{3,18},{8,25},{9,24},{10,27},{11,26},{16,1},{... | collective-permute-start | bytes 202760 | tf_op jit(solution)/shard_map/ppermute | solution.py:627
  67.9 7.0 %collective-permute-start.23 = (bf16[264,128]{1,0:T(8,128)(2,1)S(1)}, bf16[264,128]{1,0:T(8,128)(2,1)S(1)}, u32[]{:S(2)}, u32[]{:S(2)}) collective-permute-start(bf16[264,128]{1,0:T(8,128)(2,1)S(1)} %get-tuple-element.84), channel_id=1, source_target_pairs={{0,18},{1,19},{2,16},{3,17},{8,26},{9,27},{10,24},{11,25},{16,2},{... | collective-permute-start | bytes 202760 | tf_op jit(solution)/shard_map/ppermute | solution.py:627
  68.7 8.6 %collective-permute-start.24 = (bf16[264,128]{1,0:T(8,128)(2,1)S(1)}, bf16[264,128]{1,0:T(8,128)(2,1)S(1)}, u32[]{:S(2)}, u32[]{:S(2)}) collective-permute-start(bf16[264,128]{1,0:T(8,128)(2,1)S(1)} %get-tuple-element.85), channel_id=1, source_target_pairs={{0,19},{1,18},{2,17},{3,16},{8,27},{9,26},{10,25},{11,24},{16,3},{... | collective-permute-start | bytes 202760 | tf_op jit(solution)/shard_map/ppermute | solution.py:627
  71.1 6.2 %collective-permute-start.25 = (bf16[264,128]{1,0:T(8,128)(2,1)S(1)}, bf16[264,128]{1,0:T(8,128)(2,1)S(1)}, u32[]{:S(2)}, u32[]{:S(2)}) collective-permute-start(bf16[264,128]{1,0:T(8,128)(2,1)S(1)} %get-tuple-element.86), channel_id=1, source_target_pairs={{0,24},{1,25},{2,26},{3,27},{8,16},{9,17},{10,18},{11,19},{16,8},{... | collective-permute-start | bytes 202760 | tf_op jit(solution)/shard_map/ppermute | solution.py:627
  73.7 8.0 %collective-permute-start.26 = (bf16[264,128]{1,0:T(8,128)(2,1)S(1)}, bf16[264,128]{1,0:T(8,128)(2,1)S(1)}, u32[]{:S(2)}, u32[]{:S(2)}) collective-permute-start(bf16[264,128]{1,0:T(8,128)(2,1)S(1)} %get-tuple-element.87), channel_id=1, source_target_pairs={{0,25},{1,24},{2,27},{3,26},{8,17},{9,16},{10,19},{11,18},{16,9},{... | collective-permute-start | bytes 202760 | tf_op jit(solution)/shard_map/ppermute | solution.py:627
  73.8 7.9 %collective-permute-start.27 = (bf16[264,128]{1,0:T(8,128)(2,1)S(1)}, bf16[264,128]{1,0:T(8,128)(2,1)S(1)}, u32[]{:S(2)}, u32[]{:S(2)}) collective-permute-start(bf16[264,128]{1,0:T(8,128)(2,1)S(1)} %get-tuple-element.88), channel_id=1, source_target_pairs={{0,26},{1,27},{2,24},{3,25},{8,18},{9,19},{10,16},{11,17},{16,10},... | collective-permute-start | bytes 202760 | tf_op jit(solution)/shard_map/ppermute | solution.py:627
  74.9 6.8 %collective-permute-start.28 = (bf16[264,128]{1,0:T(8,128)(2,1)S(1)}, bf16[264,128]{1,0:T(8,128)(2,1)S(1)}, u32[]{:S(2)}, u32[]{:S(2)}) collective-permute-start(bf16[264,128]{1,0:T(8,128)(2,1)S(1)} %get-tuple-element.89), channel_id=1, source_target_pairs={{0,27},{1,26},{2,25},{3,24},{8,19},{9,18},{10,17},{11,16},{16,11},... | collective-permute-start | bytes 202760 | tf_op jit(solution)/shard_map/ppermute | solution.py:627

commit v12 on v10

--- a/solution.py
+++ b/solution.py
@@ -96,16 +96,15 @@
     return copies
 
 
-def finish(rows, attended, gain, held, copies=()):
-    w_proj, w_up, w_down = held
-    for copy in copies[:1]:
-        copy.wait()
-    first = (
-        rows.astype(F32) + jnp.dot(attended, w_proj[...], preferred_element_type=F32)
-    ).astype(BF16)
+def mix(rows, attended, w_proj):
+    mixed = jnp.dot(attended, w_proj[...], preferred_element_type=F32)
+    return (rows.astype(F32) + mixed).astype(BF16)
+
+
+def feed(first, gain, w_up, w_down, copies=()):
     hidden = layer_norm(first, gain)
     total = first.astype(F32)
-    for copy in copies[1:]:
+    for copy in copies:
         copy.wait()
     piece = 512
     pieces = range(0, w_up.shape[1], piece)
@@ -259,13 +258,10 @@
     pattern,
     pattern_beyond,
     slot_of_row,
-    gains,
     keyed,
     queries,
     queries_beyond,
     w_proj,
-    w_up,
-    w_down,
     tail,
     points,
     *refs,
@@ -306,9 +302,7 @@
     for copy in copies[1:]:
         copy.wait()
 
-    first_held[...] = finish(
-        points_held[...], attended[...], gains[1:2, :], (w_proj, w_up, w_down)
-    )
+    first_held[...] = mix(points_held[...], attended[...], w_proj)
     copies[0].wait()
     targets = devices // SEND_PARTS
     block_slots = capacity // 2
@@ -346,6 +340,8 @@
     queries,
     attended,
     incoming_held,
+    first_up_held,
+    first_down_held,
     qkv_held,
     proj_held,
     up_held,
@@ -353,7 +349,6 @@
     gains_held,
     tail_held,
     head_held,
-    features_held,
     sems,
 ):
     rows, channels = features.shape
@@ -367,6 +362,8 @@
     landing = started(lane_tiles(incoming, incoming_held), sems.at[1])
     copies = started(
         [
+            (w_up.at[0], first_up_held),
+            (w_down.at[0], first_down_held),
             (w_qkv.at[1], qkv_held),
             (w_proj.at[1], proj_held),
             (w_up.at[1], up_held),
@@ -394,10 +391,11 @@
         moved = incoming_held[:, :, at * LANES : (at + 2) * LANES]
         moved = moved.reshape(devices * capacity, 2 * LANES)
         sides.append(jnp.dot(place, moved, preferred_element_type=F32).astype(BF16))
-    second = jnp.concatenate(sides, axis=1)
+    first = jnp.concatenate(sides, axis=1)
+    second = feed(first, gains_held[1:2, :], first_up_held, first_down_held, copies[:2])
     normed = layer_norm(second, gains_held[2:3, :])
     scale = (channels // HEADS) ** (-0.5)
-    copies[0].wait()
+    copies[2].wait()
     asked = jnp.dot(normed, qkv_held[:, :channels], preferred_element_type=F32).astype(BF16)
     queries[...] = (asked * BF16(scale)).astype(BF16)
     kv[...] = jnp.dot(normed, qkv_held[:, channels:], preferred_element_type=F32).astype(BF16)
@@ -407,15 +405,13 @@
         loaded.append(loads(queries, p, kv, [p * PATCH] + starts))
     for p, at, rows_done in attend(loaded, channels // HEADS):
         attended[p * PATCH : (p + 1) * PATCH, at : at + rows_done.shape[1]] = rows_done
-    done = finish(
-        second, attended[...], gains_held[3:4, :], (proj_held, up_held, down_held), copies[1:]
-    )
-    features_held[...] = done
-    (leaving,) = started([(features_held, features)], sems.at[0])
+    copies[3].wait()
+    mixed = mix(second, attended[...], proj_held)
+    done = feed(mixed, gains_held[3:4, :], up_held, down_held, copies[4:])
+    features[...] = done
     normals[...] = lax.dot_general(
         head_held[...], done, (((1,), (1,)), ((), ())), preferred_element_type=F32
     )
-    leaving.wait()
 
 
 VMEM_SPEC = pl.BlockSpec(memory_space=pltpu.VMEM)
@@ -472,18 +468,18 @@
     kv_shape = jax.ShapeDtypeStruct((kept_rows, 2 * channels), BF16)
     own_shape = jax.ShapeDtypeStruct((rows_here, channels), BF16)
 
-    qkv_kept, *kept, gains_kept = pl.pallas_call(
+    qkv_kept, proj_kept, gains_kept = pl.pallas_call(
         keep_kernel,
         out_shape=[
-            *[jax.ShapeDtypeStruct(w.shape[1:], BF16) for w in (w_qkv,) + weights],
+            *[jax.ShapeDtypeStruct(w.shape[1:], BF16) for w in (w_qkv, w_proj)],
             jax.ShapeDtypeStruct(norm_gains.shape, F32),
         ],
-        in_specs=[ANY_SPEC] * 5,
-        out_specs=[VMEM_SPEC] * 5,
-        scratch_shapes=[pltpu.SemaphoreType.DMA((5,))],
+        in_specs=[ANY_SPEC] * 3,
+        out_specs=[VMEM_SPEC] * 3,
+        scratch_shapes=[pltpu.SemaphoreType.DMA((3,))],
         compiler_params=pltpu.CompilerParams(vmem_limit_bytes=PREPARE_BYTES),
         name="keep",
-    )(w_qkv, *weights, norm_gains)
+    )(w_qkv, w_proj, norm_gains)
     def index(beyond):
         return pl.pallas_call(
             functools.partial(index_kernel, capacity),
@@ -584,7 +580,7 @@
     outgoing = pl.pallas_call(
         functools.partial(first_kernel, chips if ring else 0),
         out_shape=jax.ShapeDtypeStruct((devices, pair_rows, LANES), BF16),
-        in_specs=[SMEM_SPEC] * 2 + [VMEM_SPEC] * 8 + [ANY_SPEC] * (2 + len(points_beyond)),
+        in_specs=[SMEM_SPEC] * 2 + [VMEM_SPEC] * 5 + [ANY_SPEC] * (2 + len(points_beyond)),
         out_specs=ANY_SPEC,
         scratch_shapes=[
             held_both,
@@ -599,11 +595,10 @@
         pattern_first,
         pattern_beyond,
         slot_index,
-        gains_kept,
         keyed,
         queries,
         queries_beyond,
-        *kept,
+        proj_kept,
         tail,
         points,
         *points_beyond,
@@ -617,19 +612,19 @@
             jax.ShapeDtypeStruct((w_head.shape[0], rows_here), F32),
         ),
         in_specs=[SMEM_SPEC] + [ANY_SPEC] * 7,
-        out_specs=(ANY_SPEC, VMEM_SPEC),
+        out_specs=(VMEM_SPEC, VMEM_SPEC),
         scratch_shapes=[
             pltpu.VMEM((rows_here, 2 * channels), BF16),
             held_rows,
             held_rows,
             held_slots,
+            *held_weights[1:],
             pltpu.VMEM(w_qkv.shape[1:], BF16),
             *held_weights,
             pltpu.VMEM(norm_gains.shape, F32),
             pltpu.VMEM(tail.shape, BF16),
             pltpu.VMEM(w_head.shape, BF16),
-            held_rows,
-            pltpu.SemaphoreType.DMA((3, 5)),
+            pltpu.SemaphoreType.DMA((3, 6)),
         ],
         compiler_params=pltpu.CompilerParams(vmem_limit_bytes=SECOND_BYTES),
         name="block_second",

time: 87.9 us -> 85.3 us (0.970)
  Pallas kernels: 37.5 us -> 32.3 us
  local copies, waits for them, and re-layouts: 2.31 us -> 6.04 us
  waiting for transfers between devices: 19.7 us -> 18.3 us
    pallas_call x1, Pallas kernels: 11.3 us -> 6.28 us  [shards(): pl.pallas_call(functools.partial(first_kernel, chips if ring else 0), out...]
    unnamed x22 -> x24, local copies, waits for them, and re-layouts: 2.31 us -> 6.04 us
    pallas_call x1, Pallas kernels: 2.8 us -> 0.18 us  [shards(): pl.pallas_call(keep_kernel, out_shape=[*[jax.ShapeDtypeStruct(w.shape[1:]...]
    pallas_call x1, Pallas kernels: 9.87 us -> 12.2 us  [shards(): pl.pallas_call(second_kernel, out_shape=(jax.ShapeDtypeStruct((rows_here,...]
    ppermute x6, waiting for transfers between devices: 19.7 us -> 18.3 us  [shards(): column = [lax.ppermute(rows, GROUP, onward) for rows in column]]
  transfers between devices with their start and end apart: 14 -> 14, of which waited for: 6 -> 6; matrix products, arithmetic and copies ran while one was open for 0% -> 0% of each run, Pallas kernels for 16% -> 13%
where the time goes in v12:
time: 85.3 us; the launch traced here: 85 us
  Pallas kernels  32.3 us (38%)
  blocking collectives  20.5 us (24%)
  waiting for transfers between devices  18.3 us (21%)
  starting transfers between devices  6.88 us (8%)
  local copies, waits for them, and re-layouts  6.04 us (7%)
  between operations  1.02 us (1%)
    all_to_all x1, blocking collectives, shards(): lax.all_to_all(outgoing, ('grp', 'seq'), split_axis=0, concat_axis=0, til...  20.5 us
    ppermute x6, waiting for transfers between devices, shards(): column = [lax.ppermute(rows, GROUP, onward) for rows in column]  18.3 us
    pallas_call x1, Pallas kernels, shards(): pl.pallas_call(second_kernel, out_shape=(jax.ShapeDtypeStruct((rows_here,...  12.2 us
    pallas_call x8, Pallas kernels, project(): pl.pallas_call(functools.partial(project_kernel, first_rows, new, ask), o...  11.1 us
    ppermute x6, starting transfers between devices, shards(): column = [lax.ppermute(rows, GROUP, onward) for rows in column]  6.35 us
    pallas_call x1, Pallas kernels, shards(): pl.pallas_call(functools.partial(first_kernel, chips if ring else 0), out...  6.28 us
    unnamed x24, local copies, waits for them, and re-layouts  6.04 us
    pallas_call x1, Pallas kernels, shards(): pl.pallas_call(split_kernel, out_shape=[jax.ShapeDtypeStruct((rows, chann...  1.89 us
  transfers between devices with their start and end apart: 14, of which 6 were waited for; matrix products, arithmetic and copies ran while one was open for 0% of the time, Pallas kernels for 13%

profile of v12, /device:TPU:0, one launch (start us, length us, event | category | flops | bytes accessed | tf_op | source)
XLA Modules:
  0.0 85.0 jit_solution(13928014471027486620)
XLA Ops:
  0.6 1.9 %split.1 = (bf16[264,512]{1,0:T(8,128)(2,1)}, bf16[256,512]{1,0:T(8,128)(2,1)}) custom-call(bf16[512,512]{1,0:T(8,128)(2,1)} %points.3, s32[1,512]{1,0:T(1,128)} %bitcast.3, s32[3,8]{1,0:T(4,128)} %bitcast.5), custom_call_target="tpu_custom_call" | custom-call | tf_op jit(solution)/shard_map/split/pallas_call | solution.py:452
  2.5 3.1 %collective-permute-start = (bf16[264,512]{1,0:T(8,128)(2,1)}, bf16[264,512]{1,0:T(8,128)(2,1)S(1)}, u32[]{:S(2)}, u32[]{:S(2)}) collective-permute-start(bf16[264,512]{1,0:T(8,128)(2,1)} %get-tuple-element.28.refs_0_), channel_id=1, source_target_pairs={{0,2},{1,3},{2,4},{3,5},{4,6},{5,7},{6,0},{7,1},{8,10},{9,11},{10,... | collective-permute-start | bytes 811016 | tf_op jit(solution)/shard_map/ppermute | solution.py:534
  5.6 0.0 collective-permute-start.3
  5.6 0.5 collective-permute-start.4
  6.1 1.6 %collective-permute-start.2 = (bf16[256,512]{1,0:T(8,128)(2,1)}, bf16[256,512]{1,0:T(8,128)(2,1)S(1)}, u32[]{:S(2)}, u32[]{:S(2)}) collective-permute-start(bf16[256,512]{1,0:T(8,128)(2,1)} %get-tuple-element.31.refs_1_), channel_id=1, source_target_pairs={{0,2},{1,3},{2,4},{3,5},{4,6},{5,7},{6,0},{7,1},{8,10},{9,11},{10,... | collective-permute-start | bytes 786440 | tf_op jit(solution)/shard_map/ppermute | solution.py:534
  7.7 1.9 %copy-done = bf16[2,512,1536]{2,1,0:T(8,128)(2,1)S(1)} copy-done((bf16[2,512,1536]{2,1,0:T(8,128)(2,1)S(1)}, bf16[2,512,1536]{2,1,0:T(8,128)(2,1)}, u32[]{:S(2)}) %copy-start) | copy-done | bytes 3145752
  9.6 1.2 %copy-done.1 = bf16[2,512,512]{2,1,0:T(8,128)(2,1)S(1)} copy-done((bf16[2,512,512]{2,1,0:T(8,128)(2,1)S(1)}, bf16[2,512,512]{2,1,0:T(8,128)(2,1)}, u32[]{:S(2)}) %copy-start.1) | copy-done | bytes 1048600
  10.8 0.7 copy-done.4
  11.5 0.2 keep.1
  11.7 3.5 %collective-permute-done.refs_0_ = bf16[264,512]{1,0:T(8,128)(2,1)S(1)} collective-permute-done((bf16[264,512]{1,0:T(8,128)(2,1)}, bf16[264,512]{1,0:T(8,128)(2,1)S(1)}, u32[]{:S(2)}, u32[]{:S(2)}) %collective-permute-start) | collective-permute-done | bytes 270368 | tf_op jit(solution)/shard_map/ppermute | solution.py:534
  15.1 0.0 collective-permute-start.1
  15.2 0.0 collective-permute-start.7
  15.2 0.0 copy-start.10
  15.2 0.9 %copy-done.10 = bf16[264,512]{1,0:T(8,128)(2,1)S(1)} copy-done((bf16[264,512]{1,0:T(8,128)(2,1)S(1)}, bf16[264,512]{1,0:T(8,128)(2,1)}, u32[]{:S(2)}) %copy-start.10) | copy-done | bytes 270360
  16.2 0.9 %copy-done.11 = bf16[256,512]{1,0:T(8,128)(2,1)S(1)} copy-done((bf16[256,512]{1,0:T(8,128)(2,1)S(1)}, bf16[256,512]{1,0:T(8,128)(2,1)}, u32[]{:S(2)}) %copy-start.11) | copy-done | bytes 262168
  17.1 2.9 %project_own.1 = (bf16[4096,1024]{1,0:T(8,128)(2,1)S(1)}, bf16[512,512]{1,0:T(8,128)(2,1)S(1)}) custom-call(bf16[264,512]{1,0:T(8,128)(2,1)S(1)} %copy-done.10, bf16[256,512]{1,0:T(8,128)(2,1)S(1)} %copy-done.11, bf16[264,512]{1,0:T(8,128)(2,1)S(1)} %collective-permute-done.3.refs_2_, bf16[256,512]{1,0:T(8,128)(2,1)S(1)} %collective-permute-done.4.refs_3_, ...), custom_call_target="tpu_custom_call" | custom-call | flops 1073741824 | bytes 4718592 | tf_op jit(solution)/shard_map/project_own/pallas_call | solution.py:511
  20.0 0.7 collective-permute-done.2.refs_1_
  20.8 0.0 collective-permute-start.8
  20.8 1.4 %collective-permute-start.6 = (bf16[256,512]{1,0:T(8,128)(2,1)S(1)}, bf16[256,512]{1,0:T(8,128)(2,1)S(1)}, u32[]{:S(2)}, u32[]{:S(2)}) collective-permute-start(bf16[256,512]{1,0:T(8,128)(2,1)S(1)} %collective-permute-done.2.refs_1_), channel_id=1, source_target_pairs={{0,2},{1,3},{2,4},{3,5},{4,6},{5,7},{6,0},{7,1},{8,10},{9,11},{10,... | collective-permute-start | bytes 786440 | tf_op jit(solution)/shard_map/ppermute | solution.py:534
  22.2 1.3 %project.7.refs_4_ = bf16[4096,1024]{1,0:T(8,128)(2,1)S(1)} custom-call(bf16[264,512]{1,0:T(8,128)(2,1)S(1)} %collective-permute-done.refs_0_, bf16[256,512]{1,0:T(8,128)(2,1)S(1)} %collective-permute-done.2.refs_1_, f32[4,512]{1,0:T(4,128)S(1)} %get-tuple-element.32.refs_4_.refs_2_.refs_1_, ...), custom_call_target="tpu_custom_call", output_to_operand_aliasing={{}: (4, {})} | custom-call | flops 536870912 | bytes 3145728 | tf_op jit(solution)/shard_map/project/pallas_call | solution.py:511
  23.5 0.0 copy-start.6
  23.5 2.2 %collective-permute-done.1.beyond.refs_0_ = bf16[264,512]{1,0:T(8,128)(2,1)S(1)} collective-permute-done((bf16[264,512]{1,0:T(8,128)(2,1)S(1)}, bf16[264,512]{1,0:T(8,128)(2,1)S(1)}, u32[]{:S(2)}, u32[]{:S(2)}) %collective-permute-start.1) | collective-permute-done | bytes 270368 | tf_op jit(solution)/shard_map/ppermute | solution.py:534
  25.7 0.3 collective-permute-start.5
  26.0 0.0 collective-permute-done.7.refs_0_
  26.0 1.3 %project.8.refs_4_ = bf16[4096,1024]{1,0:T(8,128)(2,1)S(1)} custom-call(bf16[264,512]{1,0:T(8,128)(2,1)S(1)} %collective-permute-done.7.refs_0_, bf16[256,512]{1,0:T(8,128)(2,1)S(1)} %collective-permute-done.8.refs_1_, f32[4,512]{1,0:T(4,128)S(1)} %get-tuple-element.32.refs_4_.refs_2_.refs_1_, ...), custom_call_target="tpu_custom_call", output_to_operand_aliasing={{}: (4, {})} | custom-call | flops 536870912 | bytes 3145728 | tf_op jit(solution)/shard_map/project/pallas_call | solution.py:511
  27.3 4.3 %collective-permute-done.6.refs_1_ = bf16[256,512]{1,0:T(8,128)(2,1)S(1)} collective-permute-done((bf16[256,512]{1,0:T(8,128)(2,1)S(1)}, bf16[256,512]{1,0:T(8,128)(2,1)S(1)}, u32[]{:S(2)}, u32[]{:S(2)}) %collective-permute-start.6) | collective-permute-done | bytes 262176 | tf_op jit(solution)/shard_map/ppermute | solution.py:534
  31.7 0.0 collective-permute-start.9
  31.7 0.6 index.1
  32.3 1.6 %project.9 = (bf16[4096,1024]{1,0:T(8,128)(2,1)S(1)}, bf16[512,512]{1,0:T(8,128)(2,1)S(1)}) custom-call(bf16[264,512]{1,0:T(8,128)(2,1)S(1)} %collective-permute-done.1.beyond.refs_0_, bf16[256,512]{1,0:T(8,128)(2,1)S(1)} %collective-permute-done.6.refs_1_, f32[4,512]{1,0:T(4,128)S(1)} %get-tuple-element.32.refs_4_.refs_2_.refs_1_, ...), custom_call_target="tpu_custom_call", output_to_operand_aliasing={{0}: (4, {})} | custom-call | flops 536870912 | bytes 3145728 | tf_op jit(solution)/shard_map/project/pallas_call | solution.py:511
  33.9 3.6 %collective-permute-done.5.refs_0_ = bf16[264,512]{1,0:T(8,128)(2,1)S(1)} collective-permute-done((bf16[264,512]{1,0:T(8,128)(2,1)S(1)}, bf16[264,512]{1,0:T(8,128)(2,1)S(1)}, u32[]{:S(2)}, u32[]{:S(2)}) %collective-permute-start.5) | collective-permute-done | bytes 270368 | tf_op jit(solution)/shard_map/ppermute | solution.py:534
  37.5 0.0 collective-permute-done.10.refs_0_
  37.5 1.3 %project.10.refs_4_ = bf16[4096,1024]{1,0:T(8,128)(2,1)S(1)} custom-call(bf16[264,512]{1,0:T(8,128)(2,1)S(1)} %collective-permute-done.10.refs_0_, bf16[256,512]{1,0:T(8,128)(2,1)S(1)} %collective-permute-done.11.refs_1_, f32[4,512]{1,0:T(4,128)S(1)} %get-tuple-element.32.refs_4_.refs_2_.refs_1_, ...), custom_call_target="tpu_custom_call", output_to_operand_aliasing={{}: (4, {})} | custom-call | flops 536870912 | bytes 3145728 | tf_op jit(solution)/shard_map/project/pallas_call | solution.py:511
  38.8 4.0 %collective-permute-done.9.refs_0_ = bf16[256,512]{1,0:T(8,128)(2,1)S(1)} collective-permute-done((bf16[256,512]{1,0:T(8,128)(2,1)S(1)}, bf16[256,512]{1,0:T(8,128)(2,1)S(1)}, u32[]{:S(2)}, u32[]{:S(2)}) %collective-permute-start.9) | collective-permute-done | bytes 262176 | tf_op jit(solution)/shard_map/ppermute | solution.py:534
  42.8 0.0 collective-permute-start.12
  42.8 0.0 collective-permute-done.13.refs_1_
  42.8 1.3 %project.11.refs_3_ = bf16[4096,1024]{1,0:T(8,128)(2,1)S(1)} custom-call(bf16[264,512]{1,0:T(8,128)(2,1)S(1)} %collective-permute-done.5.refs_0_, bf16[264,512]{1,0:T(8,128)(2,1)S(1)} %collective-permute-done.13.refs_1_, f32[4,512]{1,0:T(4,128)S(1)} %get-tuple-element.32.refs_4_.refs_2_.refs_1_, ...), custom_call_target="tpu_custom_call", output_to_operand_aliasing={{}: (4, {})} | custom-call | flops 536870912 | bytes 3145728 | tf_op jit(solution)/shard_map/project/pallas_call | solution.py:511
  44.1 0.7 project.12.refs_3_
  44.8 0.0 copy-start.3
  44.8 0.0 copy-start.7
  44.8 0.7 project.13.keyed
  45.5 0.0 copy-start.2
  45.5 0.0 copy-start.5
  45.5 0.0 copy-start.8
  45.5 0.0 copy-start.9
  45.5 0.3 copy-done.3
  45.8 6.3 %block_first.1 = bf16[16,264,128]{2,1,0:T(8,128)(2,1)S(1)} custom-call(s32[3,8]{1,0:T(4,128)S(1)} %bitcast.6, s32[3,8]{1,0:T(4,128)S(1)} %get-tuple-element.38.pattern_beyond, s32[1,1024]{1,0:T(1,128)S(1)} %get-tuple-element.45.slot_of_row, bf16[4096,1024]{1,0:T(8,128)(2,1)S(1)} %project.13.keyed, bf16[512,512]{1,0:T(8,128)(2,1)S(1)} %get-tuple-element.50.queries, ...), custom_call_target="tpu_custom_call" | custom-call | tf_op jit(solution)/shard_map/block_first/pallas_call | solution.py:580
  52.1 20.5 %all_to_all.5.incoming = bf16[16,264,128]{2,1,0:T(8,128)(2,1)S(1)} all-to-all(bf16[16,264,128]{2,1,0:T(8,128)(2,1)S(1)} %block_first.1), channel_id=1, replica_groups=mesh['grp'=4,'half'=2,'seq'=4] {'grp','seq'}, dimensions={0} | all-to-all | bytes 2162688 | tf_op jit(solution)/shard_map/all_to_all | solution.py:606
  72.6 12.2 %block_second.1 = (bf16[512,512]{1,0:T(8,128)(2,1)}, f32[3,512]{1,0:T(4,128)}) custom-call(s32[3,8]{1,0:T(4,128)S(1)} %bitcast.7, f32[4,512]{1,0:T(4,128)S(1)} %copy-done.5, bf16[16,264,128]{2,1,0:T(8,128)(2,1)S(1)} %all_to_all.5.incoming, bf16[2,512,1536]{2,1,0:T(8,128)(2,1)} %w_qkv.1, bf16[2,512,512]{2,1,0:T(8,128)(2,1)S(1)} %copy-done.2, ...), custom_call_target="tpu_custom_call" | custom-call | tf_op jit(solution)/shard_map/block_second/pallas_call | solution.py:608
  (18 shorter events, 0.0 us)
Async XLA Ops:
  2.5 12.6 %collective-permute-start = (bf16[264,512]{1,0:T(8,128)(2,1)}, bf16[264,512]{1,0:T(8,128)(2,1)S(1)}, u32[]{:S(2)}, u32[]{:S(2)}) collective-permute-start(bf16[264,512]{1,0:T(8,128)(2,1)} %get-tuple-element.28.refs_0_), channel_id=1, source_target_pairs={{0,2},{1,3},{2,4},{3,5},{4,6},{5,7},{6,0},{7,1},{8,10},{9,11},{10,... | collective-permute-start | bytes 811016 | tf_op jit(solution)/shard_map/ppermute | solution.py:534
  5.6 9.6 %collective-permute-start.3 = (bf16[264,512]{1,0:T(8,128)(2,1)}, bf16[264,512]{1,0:T(8,128)(2,1)S(1)}, u32[]{:S(2)}, u32[]{:S(2)}) collective-permute-start(bf16[264,512]{1,0:T(8,128)(2,1)} %get-tuple-element.28.refs_0_), channel_id=1, source_target_pairs={{0,1},{1,0},{2,3},{3,2},{4,5},{5,4},{6,7},{7,6},{8,9},{9,8},{10,11... | collective-permute-start | bytes 811016 | tf_op jit(solution)/shard_map/ppermute | solution.py:531
  5.6 9.6 %collective-permute-start.4 = (bf16[256,512]{1,0:T(8,128)(2,1)}, bf16[256,512]{1,0:T(8,128)(2,1)S(1)}, u32[]{:S(2)}, u32[]{:S(2)}) collective-permute-start(bf16[256,512]{1,0:T(8,128)(2,1)} %get-tuple-element.31.refs_1_), channel_id=1, source_target_pairs={{0,1},{1,0},{2,3},{3,2},{4,5},{5,4},{6,7},{7,6},{8,9},{9,8},{10,11... | collective-permute-start | bytes 786440 | tf_op jit(solution)/shard_map/ppermute | solution.py:531
  6.1 14.7 %collective-permute-start.2 = (bf16[256,512]{1,0:T(8,128)(2,1)}, bf16[256,512]{1,0:T(8,128)(2,1)S(1)}, u32[]{:S(2)}, u32[]{:S(2)}) collective-permute-start(bf16[256,512]{1,0:T(8,128)(2,1)} %get-tuple-element.31.refs_1_), channel_id=1, source_target_pairs={{0,2},{1,3},{2,4},{3,5},{4,6},{5,7},{6,0},{7,1},{8,10},{9,11},{10,... | collective-permute-start | bytes 786440 | tf_op jit(solution)/shard_map/ppermute | solution.py:534
  7.7 1.9 %copy-start = (bf16[2,512,1536]{2,1,0:T(8,128)(2,1)S(1)}, bf16[2,512,1536]{2,1,0:T(8,128)(2,1)}, u32[]{:S(2)}) copy-start(bf16[2,512,1536]{2,1,0:T(8,128)(2,1)} %w_qkv.1) | copy-start | bytes 9437188
  9.6 1.2 %copy-start.1 = (bf16[2,512,512]{2,1,0:T(8,128)(2,1)S(1)}, bf16[2,512,512]{2,1,0:T(8,128)(2,1)}, u32[]{:S(2)}) copy-start(bf16[2,512,512]{2,1,0:T(8,128)(2,1)} %w_proj.1) | copy-start | bytes 3145732
  10.8 0.7 copy-start.4
  15.1 10.6 %collective-permute-start.1 = (bf16[264,512]{1,0:T(8,128)(2,1)S(1)}, bf16[264,512]{1,0:T(8,128)(2,1)S(1)}, u32[]{:S(2)}, u32[]{:S(2)}) collective-permute-start(bf16[264,512]{1,0:T(8,128)(2,1)S(1)} %collective-permute-done.refs_0_), channel_id=1, source_target_pairs={{0,2},{1,3},{2,4},{3,5},{4,6},{5,7},{6,0},{7,1},{8,10},{9,11},{10,... | collective-permute-start | bytes 811016 | tf_op jit(solution)/shard_map/ppermute | solution.py:534
  15.2 10.8 %collective-permute-start.7 = (bf16[264,512]{1,0:T(8,128)(2,1)S(1)}, bf16[264,512]{1,0:T(8,128)(2,1)S(1)}, u32[]{:S(2)}, u32[]{:S(2)}) collective-permute-start(bf16[264,512]{1,0:T(8,128)(2,1)S(1)} %collective-permute-done.refs_0_), channel_id=1, source_target_pairs={{0,1},{1,0},{2,3},{3,2},{4,5},{5,4},{6,7},{7,6},{8,9},{9,8},{10,11... | collective-permute-start | bytes 811016 | tf_op jit(solution)/shard_map/ppermute | solution.py:551
  15.2 1.0 %copy-start.10 = (bf16[264,512]{1,0:T(8,128)(2,1)S(1)}, bf16[264,512]{1,0:T(8,128)(2,1)}, u32[]{:S(2)}) copy-start(bf16[264,512]{1,0:T(8,128)(2,1)} %get-tuple-element.28.refs_0_) | copy-start | bytes 811012
  16.2 0.9 %copy-start.11 = (bf16[256,512]{1,0:T(8,128)(2,1)S(1)}, bf16[256,512]{1,0:T(8,128)(2,1)}, u32[]{:S(2)}) copy-start(bf16[256,512]{1,0:T(8,128)(2,1)} %get-tuple-element.31.refs_1_) | copy-start | bytes 786436
  20.8 5.2 %collective-permute-start.8 = (bf16[256,512]{1,0:T(8,128)(2,1)S(1)}, bf16[256,512]{1,0:T(8,128)(2,1)S(1)}, u32[]{:S(2)}, u32[]{:S(2)}) collective-permute-start(bf16[256,512]{1,0:T(8,128)(2,1)S(1)} %collective-permute-done.2.refs_1_), channel_id=1, source_target_pairs={{0,1},{1,0},{2,3},{3,2},{4,5},{5,4},{6,7},{7,6},{8,9},{9,8},{10,11... | collective-permute-start | bytes 786440 | tf_op jit(solution)/shard_map/ppermute | solution.py:551
  20.8 10.9 %collective-permute-start.6 = (bf16[256,512]{1,0:T(8,128)(2,1)S(1)}, bf16[256,512]{1,0:T(8,128)(2,1)S(1)}, u32[]{:S(2)}, u32[]{:S(2)}) collective-permute-start(bf16[256,512]{1,0:T(8,128)(2,1)S(1)} %collective-permute-done.2.refs_1_), channel_id=1, source_target_pairs={{0,2},{1,3},{2,4},{3,5},{4,6},{5,7},{6,0},{7,1},{8,10},{9,11},{10,... | collective-permute-start | bytes 786440 | tf_op jit(solution)/shard_map/ppermute | solution.py:534
  23.5 8.2 %copy-start.6 = (s32[512]{0:T(512)S(1)}, s32[512]{0:T(512)}, u32[]{:S(2)}) copy-start(s32[512]{0:T(512)} %param.13) | copy-start | bytes 6148
  25.7 11.7 %collective-permute-start.5 = (bf16[264,512]{1,0:T(8,128)(2,1)S(1)}, bf16[264,512]{1,0:T(8,128)(2,1)S(1)}, u32[]{:S(2)}, u32[]{:S(2)}) collective-permute-start(bf16[264,512]{1,0:T(8,128)(2,1)S(1)} %collective-permute-done.1.beyond.refs_0_), channel_id=1, source_target_pairs={{0,2},{1,3},{2,4},{3,5},{4,6},{5,7},{6,0},{7,1},{8,10},{9,11},{10,... | collective-permute-start | bytes 811016 | tf_op jit(solution)/shard_map/ppermute | solution.py:534
  26.0 11.5 %collective-permute-start.10 = (bf16[264,512]{1,0:T(8,128)(2,1)S(1)}, bf16[264,512]{1,0:T(8,128)(2,1)S(1)}, u32[]{:S(2)}, u32[]{:S(2)}) collective-permute-start(bf16[264,512]{1,0:T(8,128)(2,1)S(1)} %collective-permute-done.1.beyond.refs_0_), channel_id=1, source_target_pairs={{0,1},{1,0},{2,3},{3,2},{4,5},{5,4},{6,7},{7,6},{8,9},{9,8},{10,11... | collective-permute-start | bytes 811016 | tf_op jit(solution)/shard_map/ppermute | solution.py:551
  31.7 5.8 %collective-permute-start.11 = (bf16[256,512]{1,0:T(8,128)(2,1)S(1)}, bf16[256,512]{1,0:T(8,128)(2,1)S(1)}, u32[]{:S(2)}, u32[]{:S(2)}) collective-permute-start(bf16[256,512]{1,0:T(8,128)(2,1)S(1)} %collective-permute-done.6.refs_1_), channel_id=1, source_target_pairs={{0,1},{1,0},{2,3},{3,2},{4,5},{5,4},{6,7},{7,6},{8,9},{9,8},{10,11... | collective-permute-start | bytes 786440 | tf_op jit(solution)/shard_map/ppermute | solution.py:551
  31.7 11.1 %collective-permute-start.9 = (bf16[256,512]{1,0:T(8,128)(2,1)S(1)}, bf16[256,512]{1,0:T(8,128)(2,1)S(1)}, u32[]{:S(2)}, u32[]{:S(2)}) collective-permute-start(bf16[256,512]{1,0:T(8,128)(2,1)S(1)} %collective-permute-done.6.refs_1_), channel_id=1, source_target_pairs={{0,2},{1,3},{2,4},{3,5},{4,6},{5,7},{6,0},{7,1},{8,10},{9,11},{10,... | collective-permute-start | bytes 786440 | tf_op jit(solution)/shard_map/ppermute | solution.py:534
  37.5 5.3 %collective-permute-start.13 = (bf16[264,512]{1,0:T(8,128)(2,1)S(1)}, bf16[264,512]{1,0:T(8,128)(2,1)S(1)}, u32[]{:S(2)}, u32[]{:S(2)}) collective-permute-start(bf16[264,512]{1,0:T(8,128)(2,1)S(1)} %collective-permute-done.5.refs_0_), channel_id=1, source_target_pairs={{0,1},{1,0},{2,3},{3,2},{4,5},{5,4},{6,7},{7,6},{8,9},{9,8},{10,11... | collective-permute-start | bytes 811016 | tf_op jit(solution)/shard_map/ppermute | solution.py:551
  42.8 2.0 %collective-permute-start.12 = (bf16[256,512]{1,0:T(8,128)(2,1)S(1)}, bf16[256,512]{1,0:T(8,128)(2,1)S(1)}, u32[]{:S(2)}, u32[]{:S(2)}) collective-permute-start(bf16[256,512]{1,0:T(8,128)(2,1)S(1)} %collective-permute-done.9.refs_0_), channel_id=1, source_target_pairs={{0,1},{1,0},{2,3},{3,2},{4,5},{5,4},{6,7},{7,6},{8,9},{9,8},{10,11... | collective-permute-start | bytes 786440 | tf_op jit(solution)/shard_map/ppermute | solution.py:551
  44.8 1.0 %copy-start.3 = (bf16[512,512]{1,0:T(8,128)(2,1)S(1)}, bf16[512,512]{1,0:T(8,128)(2,1)}, u32[]{:S(2)}) copy-start(bf16[512,512]{1,0:T(8,128)(2,1)} %points.3) | copy-start | bytes 1572868
  44.8 1.0 %copy-start.7 = (s32[8,3]{0,1:T(4,128)S(1)}, s32[8,3]{0,1:T(4,128)}, u32[]{:S(2)}) copy-start(s32[8,3]{0,1:T(4,128)} %param.11) | copy-start | bytes 292
  45.5 27.1 %copy-start.2 = (bf16[2,512,512]{2,1,0:T(8,128)(2,1)S(1)}, bf16[2,512,512]{2,1,0:T(8,128)(2,1)}, u32[]{:S(2)}) copy-start(bf16[2,512,512]{2,1,0:T(8,128)(2,1)} %w_proj.1) | copy-start | bytes 3145732
  45.5 27.1 %copy-start.5 = (f32[4,512]{1,0:T(4,128)S(1)}, f32[4,512]{1,0:T(4,128)}, u32[]{:S(2)}) copy-start(f32[4,512]{1,0:T(4,128)} %gains.1) | copy-start | bytes 24580
  45.5 27.1 %copy-start.8 = (bf16[3,512]{1,0:T(4,128)(2,1)S(1)}, bf16[3,512]{1,0:T(4,128)(2,1)}, u32[]{:S(2)}) copy-start(bf16[3,512]{1,0:T(4,128)(2,1)} %w_head.1) | copy-start | bytes 9220
  45.5 27.1 %copy-start.9 = (s32[8,3]{0,1:T(4,128)S(1)}, s32[8,3]{0,1:T(4,128)}, u32[]{:S(2)}) copy-start(s32[8,3]{0,1:T(4,128)} %param.12) | copy-start | bytes 292

commit v13 on v12

--- a/solution.py
+++ b/solution.py
@@ -104,7 +104,7 @@
 def feed(first, gain, w_up, w_down, copies=()):
     hidden = layer_norm(first, gain)
     total = first.astype(F32)
-    for copy in copies:
+    for copy in copies[:1]:
         copy.wait()
     piece = 512
     pieces = range(0, w_up.shape[1], piece)
@@ -116,6 +116,9 @@
                 hidden, w_up[:, at + piece : at + 2 * piece], preferred_element_type=F32
             )
         act = gelu(upper).astype(BF16)
+        if at == 0:
+            for copy in copies[1:]:
+                copy.wait()
         total = total + jnp.dot(act, w_down[at : at + piece, :], preferred_element_type=F32)
         upper = later
     return total.astype(BF16)
@@ -255,10 +258,13 @@
 
 def first_kernel(
     ring_chips,
+    late_rows,
     pattern,
     pattern_beyond,
     slot_of_row,
-    keyed,
+    kept_rows,
+    gains,
+    w_qkv,
     queries,
     queries_beyond,
     w_proj,
@@ -266,7 +272,9 @@
     points,
     *refs,
 ):
-    *points_beyond, outgoing, attended, points_held, first_held, outgoing_held, sems = refs
+    late, refs = refs[: len(late_rows)], refs[len(late_rows) :]
+    *points_beyond, outgoing, keyed, attended, points_held, first_held, outgoing_held = refs[:-3]
+    late_held, sems, late_sems = refs[-3:]
     rows, channels = points.shape
     devices, capacity, _ = outgoing_held.shape
     row_tiles = channels // LANES * capacity
@@ -274,6 +282,11 @@
     chosen = pattern.shape[0]
     me = lax.axis_index(GROUP)
     part = rows // len(points_beyond)
+    late_part = late_held.shape[1]
+    landing = started(
+        [(piece.at[pl.ds(0, late_part), :], late_held.at[i]) for i, piece in enumerate(late)],
+        late_sems,
+    )
     copies = started(
         [(tail, outgoing.at[:, pl.ds(row_tiles, TAIL), :]), (points, points_held.at[:rows])]
         + [
@@ -282,6 +295,13 @@
         ],
         sems.at[0],
     )
+    for i, first in enumerate(late_rows):
+        landing[i].wait()
+        keyed[first : first + late_part, :] = jnp.dot(
+            layer_norm(late_held[i], gains[0:1, :]),
+            w_qkv[:, channels:],
+            preferred_element_type=F32,
+        ).astype(BF16)
     blocks = ((pattern, queries, 0), (pattern_beyond, queries_beyond, ring_chips or 1))
     loaded = []
     for b, (picked, asking, own_slot) in enumerate(blocks):
@@ -360,17 +380,7 @@
         [(tail, tail_held), (gains, gains_held), (w_head, head_held)], sems.at[0]
     )
     landing = started(lane_tiles(incoming, incoming_held), sems.at[1])
-    copies = started(
-        [
-            (w_up.at[0], first_up_held),
-            (w_down.at[0], first_down_held),
-            (w_qkv.at[1], qkv_held),
-            (w_proj.at[1], proj_held),
-            (w_up.at[1], up_held),
-            (w_down.at[1], down_held),
-        ],
-        sems.at[2],
-    )
+    copies = started([(w_up.at[0], first_up_held)], sems.at[2])
     for copy in small:
         copy.wait()
     per_row = LANES // capacity
@@ -385,12 +395,17 @@
     places = jnp.concatenate(pieces, axis=1).astype(jnp.int32) - 1
     place = one_hot_rows(places, rows)
     sides = []
+    later = (
+        [(w_down.at[0], first_down_held), (w_qkv.at[1], qkv_held)],
+        [(w_proj.at[1], proj_held), (w_up.at[1], up_held), (w_down.at[1], down_held)],
+    )
     for at in range(0, len(landing), 2):
         for copy in landing[at : at + 2]:
             copy.wait()
         moved = incoming_held[:, :, at * LANES : (at + 2) * LANES]
         moved = moved.reshape(devices * capacity, 2 * LANES)
         sides.append(jnp.dot(place, moved, preferred_element_type=F32).astype(BF16))
+        copies += started(later[at // 2], sems.at[3 + at // 2])
     first = jnp.concatenate(sides, axis=1)
     second = feed(first, gains_held[1:2, :], first_up_held, first_down_held, copies[:2])
     normed = layer_norm(second, gains_held[2:3, :])
@@ -550,13 +565,10 @@
                 column[0], slot_index = lax.optimization_barrier((column[0], slot_index))
             beside = [lax.ppermute(rows, GROUP, swap) for rows in column]
             waiting = [(2 * step, 0, column), (2 * step + 1, 0, beside)]
-        for i in range(RING_PARTS):
-            halves = [(slot, i * part, block[i : i + 1]) for slot, _, block in waiting]
-            if i + 1 < RING_PARTS:
-                (keyed,) = project(keyed, halves)
-            else:
-                for half in halves:
-                    (keyed,) = project(keyed, [half])
+        early = [(slot, 0, block[:-1]) for slot, _, block in waiting]
+        (keyed,) = project(keyed, early)
+        late_rows = [(slot + 1) * rows_here - part for slot, _, _ in waiting]
+        late = [block[-1] for _, _, block in waiting]
     else:
         group = lax.all_gather(points, GROUP, axis=0, tiled=True)
         partner = lax.rem(lax.axis_index(GROUP) + chips, shards_in_group)
@@ -571,24 +583,30 @@
         keyed, queries_beyond = project(keyed, [(1, 0, points_beyond)], ask=True, rows=rows_here)
         (keyed,) = project(keyed, [(2, 0, [picked[0]])], rows=wide)
         (keyed,) = project(keyed, [(2 + chosen, 0, [picked[1]])], rows=wide)
+        late_rows, late = [], []
 
     held_weights = [pltpu.VMEM(w.shape[1:], BF16) for w in weights]
     held_rows = pltpu.VMEM((rows_here, channels), BF16)
     held_slots = pltpu.VMEM((devices, pair_slots, channels), BF16)
     held_both = pltpu.VMEM((2 * rows_here, channels), BF16)
     pair_rows = channels // LANES * pair_slots + TAIL
-    outgoing = pl.pallas_call(
-        functools.partial(first_kernel, chips if ring else 0),
-        out_shape=jax.ShapeDtypeStruct((devices, pair_rows, LANES), BF16),
-        in_specs=[SMEM_SPEC] * 2 + [VMEM_SPEC] * 5 + [ANY_SPEC] * (2 + len(points_beyond)),
-        out_specs=ANY_SPEC,
+    outgoing, _ = pl.pallas_call(
+        functools.partial(first_kernel, chips if ring else 0, late_rows),
+        out_shape=[jax.ShapeDtypeStruct((devices, pair_rows, LANES), BF16), kv_shape],
+        in_specs=[SMEM_SPEC] * 2
+        + [VMEM_SPEC] * 7
+        + [ANY_SPEC] * (2 + len(late) + len(points_beyond)),
+        out_specs=[ANY_SPEC, VMEM_SPEC],
         scratch_shapes=[
             held_both,
             held_both,
             held_both,
             held_slots,
+            pltpu.VMEM((max(len(late), 1), part, channels), BF16),
             pltpu.SemaphoreType.DMA((1 + SEND_PARTS, 4)),
+            pltpu.SemaphoreType.DMA((max(len(late), 1),)),
         ],
+        input_output_aliases={3: 1},
         compiler_params=pltpu.CompilerParams(vmem_limit_bytes=FIRST_BYTES),
         name="block_first",
     )(
@@ -596,11 +614,14 @@
         pattern_beyond,
         slot_index,
         keyed,
+        gains_kept,
+        qkv_kept,
         queries,
         queries_beyond,
         proj_kept,
         tail,
         points,
+        *late,
         *points_beyond,
     )
     incoming = lax.all_to_all(outgoing, ("grp", "seq"), split_axis=0, concat_axis=0, tiled=True)
@@ -624,7 +645,7 @@
             pltpu.VMEM(norm_gains.shape, F32),
             pltpu.VMEM(tail.shape, BF16),
             pltpu.VMEM(w_head.shape, BF16),
-            pltpu.SemaphoreType.DMA((3, 6)),
+            pltpu.SemaphoreType.DMA((5, 4)),
         ],
         compiler_params=pltpu.CompilerParams(vmem_limit_bytes=SECOND_BYTES),
         name="block_second",

time: 85.3 us -> 85.7 us (level)
    pallas_call x8 -> x6, Pallas kernels: 11.1 us -> 9.77 us  [project(): pl.pallas_call(functools.partial(project_kernel, first_rows, new, ask), o...]
    pallas_call x1, Pallas kernels: 6.28 us -> 7.57 us  [shards(): pl.pallas_call(functools.partial(first_kernel, chips if ring else 0, late...]
    unnamed x24 -> x22, local copies, waits for them, and re-layouts: 6.04 us -> 5.75 us
  transfers between devices with their start and end apart: 14 -> 14, of which waited for: 6 -> 6; matrix products, arithmetic and copies ran while one was open for 0% -> 0% of each run, Pallas kernels for 13% -> 12%
where the time goes in v13:
time: 85.7 us; the launch traced here: 85.4 us
  Pallas kernels  32.8 us (38%)
  blocking collectives  20.4 us (24%)
  waiting for transfers between devices  18.4 us (21%)
  starting transfers between devices  7.08 us (8%)
  local copies, waits for them, and re-layouts  5.75 us (7%)
  between operations  0.99 us (1%)
    all_to_all x1, blocking collectives, shards(): lax.all_to_all(outgoing, ('grp', 'seq'), split_axis=0, concat_axis=0, til...  20.4 us
    ppermute x6, waiting for transfers between devices, shards(): column = [lax.ppermute(rows, GROUP, onward) for rows in column]  18.2 us
    pallas_call x1, Pallas kernels, shards(): pl.pallas_call(second_kernel, out_shape=(jax.ShapeDtypeStruct((rows_here,...  12.8 us
    pallas_call x6, Pallas kernels, project(): pl.pallas_call(functools.partial(project_kernel, first_rows, new, ask), o...  9.77 us
    pallas_call x1, Pallas kernels, shards(): pl.pallas_call(functools.partial(first_kernel, chips if ring else 0, late...  7.57 us
    ppermute x6, starting transfers between devices, shards(): column = [lax.ppermute(rows, GROUP, onward) for rows in column]  6.03 us
    unnamed x22, local copies, waits for them, and re-layouts  5.75 us
    pallas_call x1, Pallas kernels, shards(): pl.pallas_call(split_kernel, out_shape=[jax.ShapeDtypeStruct((rows, chann...  1.89 us
  transfers between devices with their start and end apart: 14, of which 6 were waited for; matrix products, arithmetic and copies ran while one was open for 0% of the time, Pallas kernels for 12%

profile of v13, /device:TPU:0, one launch (start us, length us, event | category | flops | bytes accessed | tf_op | source)
XLA Modules:
  0.0 85.4 jit_solution(15949356938501742733)
XLA Ops:
  0.6 1.9 %split.1 = (bf16[264,512]{1,0:T(8,128)(2,1)}, bf16[256,512]{1,0:T(8,128)(2,1)}) custom-call(bf16[512,512]{1,0:T(8,128)(2,1)} %points.3, s32[1,512]{1,0:T(1,128)} %bitcast.3, s32[3,8]{1,0:T(4,128)} %bitcast.5), custom_call_target="tpu_custom_call" | custom-call | tf_op jit(solution)/shard_map/split/pallas_call | solution.py:467
  2.5 3.1 %collective-permute-start = (bf16[264,512]{1,0:T(8,128)(2,1)}, bf16[264,512]{1,0:T(8,128)(2,1)S(1)}, u32[]{:S(2)}, u32[]{:S(2)}) collective-permute-start(bf16[264,512]{1,0:T(8,128)(2,1)} %get-tuple-element.29.refs_0_), channel_id=1, source_target_pairs={{0,2},{1,3},{2,4},{3,5},{4,6},{5,7},{6,0},{7,1},{8,10},{9,11},{10,... | collective-permute-start | bytes 811016 | tf_op jit(solution)/shard_map/ppermute | solution.py:549
  5.6 0.0 collective-permute-start.3
  5.6 0.5 collective-permute-start.4
  6.1 1.6 %collective-permute-start.2 = (bf16[256,512]{1,0:T(8,128)(2,1)}, bf16[256,512]{1,0:T(8,128)(2,1)S(1)}, u32[]{:S(2)}, u32[]{:S(2)}) collective-permute-start(bf16[256,512]{1,0:T(8,128)(2,1)} %get-tuple-element.32.refs_1_), channel_id=1, source_target_pairs={{0,2},{1,3},{2,4},{3,5},{4,6},{5,7},{6,0},{7,1},{8,10},{9,11},{10,... | collective-permute-start | bytes 786440 | tf_op jit(solution)/shard_map/ppermute | solution.py:549
  7.7 1.9 %copy-done = bf16[2,512,1536]{2,1,0:T(8,128)(2,1)S(1)} copy-done((bf16[2,512,1536]{2,1,0:T(8,128)(2,1)S(1)}, bf16[2,512,1536]{2,1,0:T(8,128)(2,1)}, u32[]{:S(2)}) %copy-start) | copy-done | bytes 3145752
  9.6 1.2 %copy-done.1 = bf16[2,512,512]{2,1,0:T(8,128)(2,1)S(1)} copy-done((bf16[2,512,512]{2,1,0:T(8,128)(2,1)S(1)}, bf16[2,512,512]{2,1,0:T(8,128)(2,1)}, u32[]{:S(2)}) %copy-start.1) | copy-done | bytes 1048600
  10.8 0.7 copy-done.4
  11.5 0.2 keep.1
  11.7 3.5 %collective-permute-done.refs_0_ = bf16[264,512]{1,0:T(8,128)(2,1)S(1)} collective-permute-done((bf16[264,512]{1,0:T(8,128)(2,1)}, bf16[264,512]{1,0:T(8,128)(2,1)S(1)}, u32[]{:S(2)}, u32[]{:S(2)}) %collective-permute-start) | collective-permute-done | bytes 270368 | tf_op jit(solution)/shard_map/ppermute | solution.py:549
  15.1 0.0 collective-permute-start.7
  15.2 0.0 collective-permute-start.1
  15.2 0.0 collective-permute-done.4.refs_3_
  15.2 0.0 collective-permute-done.3.refs_2_
  15.2 0.9 %copy-done.9 = bf16[264,512]{1,0:T(8,128)(2,1)S(1)} copy-done((bf16[264,512]{1,0:T(8,128)(2,1)S(1)}, bf16[264,512]{1,0:T(8,128)(2,1)}, u32[]{:S(2)}) %copy-start.9) | copy-done | bytes 270360
  16.2 0.9 %copy-done.10 = bf16[256,512]{1,0:T(8,128)(2,1)S(1)} copy-done((bf16[256,512]{1,0:T(8,128)(2,1)S(1)}, bf16[256,512]{1,0:T(8,128)(2,1)}, u32[]{:S(2)}) %copy-start.10) | copy-done | bytes 262168
  17.1 2.9 %project_own.1 = (bf16[4096,1024]{1,0:T(8,128)(2,1)S(1)}, bf16[512,512]{1,0:T(8,128)(2,1)S(1)}) custom-call(bf16[264,512]{1,0:T(8,128)(2,1)S(1)} %copy-done.9, bf16[256,512]{1,0:T(8,128)(2,1)S(1)} %copy-done.10, bf16[264,512]{1,0:T(8,128)(2,1)S(1)} %collective-permute-done.3.refs_2_, bf16[256,512]{1,0:T(8,128)(2,1)S(1)} %collective-permute-done.4.refs_3_, ...), custom_call_target="tpu_custom_call" | custom-call | flops 1073741824 | bytes 4718592 | tf_op jit(solution)/shard_map/project_own/pallas_call | solution.py:526
  20.0 0.0 collective-permute-done.2.refs_1_
  20.0 0.5 collective-permute-start.8
  20.6 1.3 %collective-permute-start.6 = (bf16[256,512]{1,0:T(8,128)(2,1)S(1)}, bf16[256,512]{1,0:T(8,128)(2,1)S(1)}, u32[]{:S(2)}, u32[]{:S(2)}) collective-permute-start(bf16[256,512]{1,0:T(8,128)(2,1)S(1)} %collective-permute-done.2.refs_1_), channel_id=1, source_target_pairs={{0,2},{1,3},{2,4},{3,5},{4,6},{5,7},{6,0},{7,1},{8,10},{9,11},{10,... | collective-permute-start | bytes 786440 | tf_op jit(solution)/shard_map/ppermute | solution.py:549
  21.9 1.3 %project.5.refs_4_ = bf16[4096,1024]{1,0:T(8,128)(2,1)S(1)} custom-call(bf16[264,512]{1,0:T(8,128)(2,1)S(1)} %collective-permute-done.refs_0_, bf16[256,512]{1,0:T(8,128)(2,1)S(1)} %collective-permute-done.2.refs_1_, f32[4,512]{1,0:T(4,128)S(1)} %get-tuple-element.33.refs_4_.refs_2_.gains, ...), custom_call_target="tpu_custom_call", output_to_operand_aliasing={{}: (4, {})} | custom-call | flops 536870912 | bytes 3145728 | tf_op jit(solution)/shard_map/project/pallas_call | solution.py:526
  23.2 0.0 copy-start.5
  23.2 3.0 %collective-permute-done.1.beyond.refs_0_.refs_2_ = bf16[264,512]{1,0:T(8,128)(2,1)S(1)} collective-permute-done((bf16[264,512]{1,0:T(8,128)(2,1)S(1)}, bf16[264,512]{1,0:T(8,128)(2,1)S(1)}, u32[]{:S(2)}, u32[]{:S(2)}) %collective-permute-start.1) | collective-permute-done | bytes 270368 | tf_op jit(solution)/shard_map/ppermute | solution.py:549
  26.2 0.0 collective-permute-start.11
  26.2 0.0 collective-permute-start.5
  26.2 0.0 collective-permute-done.8.refs_1_
  26.3 1.3 %project.6.refs_4_ = bf16[4096,1024]{1,0:T(8,128)(2,1)S(1)} custom-call(bf16[264,512]{1,0:T(8,128)(2,1)S(1)} %collective-permute-done.7.refs_0_, bf16[256,512]{1,0:T(8,128)(2,1)S(1)} %collective-permute-done.8.refs_1_, f32[4,512]{1,0:T(4,128)S(1)} %get-tuple-element.33.refs_4_.refs_2_.gains, ...), custom_call_target="tpu_custom_call", output_to_operand_aliasing={{}: (4, {})} | custom-call | flops 536870912 | bytes 3145728 | tf_op jit(solution)/shard_map/project/pallas_call | solution.py:526
  27.6 4.2 %collective-permute-done.6.refs_1_.refs_3_ = bf16[256,512]{1,0:T(8,128)(2,1)S(1)} collective-permute-done((bf16[256,512]{1,0:T(8,128)(2,1)S(1)}, bf16[256,512]{1,0:T(8,128)(2,1)S(1)}, u32[]{:S(2)}, u32[]{:S(2)}) %collective-permute-start.6) | collective-permute-done | bytes 262176 | tf_op jit(solution)/shard_map/ppermute | solution.py:549
  31.7 0.0 collective-permute-start.10
  31.7 0.6 index.1
  32.4 1.6 %project.7 = (bf16[4096,1024]{1,0:T(8,128)(2,1)S(1)}, bf16[512,512]{1,0:T(8,128)(2,1)S(1)}) custom-call(bf16[264,512]{1,0:T(8,128)(2,1)S(1)} %collective-permute-done.1.beyond.refs_0_.refs_2_, bf16[256,512]{1,0:T(8,128)(2,1)S(1)} %collective-permute-done.6.refs_1_.refs_3_, ...), custom_call_target="tpu_custom_call", output_to_operand_aliasing={{0}: (4, {})} | custom-call | flops 536870912 | bytes 3145728 | tf_op jit(solution)/shard_map/project/pallas_call | solution.py:526
  34.0 3.6 %collective-permute-done.5.refs_0_ = bf16[264,512]{1,0:T(8,128)(2,1)S(1)} collective-permute-done((bf16[264,512]{1,0:T(8,128)(2,1)S(1)}, bf16[264,512]{1,0:T(8,128)(2,1)S(1)}, u32[]{:S(2)}, u32[]{:S(2)}) %collective-permute-start.5) | collective-permute-done | bytes 270368 | tf_op jit(solution)/shard_map/ppermute | solution.py:549
  37.5 0.0 collective-permute-start.9
  37.5 0.0 collective-permute-done.12.refs_1_
  37.5 0.0 collective-permute-done.11.refs_0_
  37.5 1.3 %project.8.refs_4_ = bf16[4096,1024]{1,0:T(8,128)(2,1)S(1)} custom-call(bf16[264,512]{1,0:T(8,128)(2,1)S(1)} %collective-permute-done.11.refs_0_, bf16[256,512]{1,0:T(8,128)(2,1)S(1)} %collective-permute-done.12.refs_1_, f32[4,512]{1,0:T(4,128)S(1)} %get-tuple-element.33.refs_4_.refs_2_.gains, ...), custom_call_target="tpu_custom_call", output_to_operand_aliasing={{}: (4, {})} | custom-call | flops 536870912 | bytes 3145728 | tf_op jit(solution)/shard_map/project/pallas_call | solution.py:526
  38.9 0.0 copy-start.3
  38.9 0.0 copy-start.6
  38.9 4.0 %collective-permute-done.10.refs_0_ = bf16[256,512]{1,0:T(8,128)(2,1)S(1)} collective-permute-done((bf16[256,512]{1,0:T(8,128)(2,1)S(1)}, bf16[256,512]{1,0:T(8,128)(2,1)S(1)}, u32[]{:S(2)}, u32[]{:S(2)}) %collective-permute-start.10) | collective-permute-done | bytes 262176 | tf_op jit(solution)/shard_map/ppermute | solution.py:549
  42.9 0.0 collective-permute-start.13
  42.9 1.3 %project.9.kept_rows = bf16[4096,1024]{1,0:T(8,128)(2,1)S(1)} custom-call(bf16[264,512]{1,0:T(8,128)(2,1)S(1)} %collective-permute-done.5.refs_0_, bf16[264,512]{1,0:T(8,128)(2,1)S(1)} %collective-permute-done.9.refs_1_, f32[4,512]{1,0:T(4,128)S(1)} %get-tuple-element.33.refs_4_.refs_2_.gains, ...), custom_call_target="tpu_custom_call", output_to_operand_aliasing={{}: (4, {})} | custom-call | flops 536870912 | bytes 3145728 | tf_op jit(solution)/shard_map/project/pallas_call | solution.py:526
  44.2 0.0 copy-start.2
  44.2 0.0 copy-start.7
  44.2 0.0 copy-start.8
  44.2 0.2 collective-permute-done.13.refs_1_
  44.4 7.6 %block_first.1 = (bf16[16,264,128]{2,1,0:T(8,128)(2,1)S(1)}, bf16[4096,1024]{1,0:T(8,128)(2,1)S(1)}) custom-call(s32[3,8]{1,0:T(4,128)S(1)} %bitcast.6, s32[3,8]{1,0:T(4,128)S(1)} %get-tuple-element.39.pattern_beyond, s32[1,1024]{1,0:T(1,128)S(1)} %get-tuple-element.46.slot_of_row, ...), custom_call_target="tpu_custom_call", output_to_operand_aliasing={{1}: (3, {})} | custom-call | tf_op jit(solution)/shard_map/block_first/pallas_call | solution.py:593
  52.0 20.4 %all_to_all.5.incoming = bf16[16,264,128]{2,1,0:T(8,128)(2,1)S(1)} all-to-all(bf16[16,264,128]{2,1,0:T(8,128)(2,1)S(1)} %get-tuple-element.55), channel_id=1, replica_groups=mesh['grp'=4,'half'=2,'seq'=4] {'grp','seq'}, dimensions={0} | all-to-all | bytes 2162688 | tf_op jit(solution)/shard_map/all_to_all | solution.py:627
  72.4 12.8 %block_second.1 = (bf16[512,512]{1,0:T(8,128)(2,1)}, f32[3,512]{1,0:T(4,128)}) custom-call(s32[3,8]{1,0:T(4,128)S(1)} %bitcast.7, f32[4,512]{1,0:T(4,128)S(1)} %copy-done.4, bf16[16,264,128]{2,1,0:T(8,128)(2,1)S(1)} %all_to_all.5.incoming, bf16[2,512,1536]{2,1,0:T(8,128)(2,1)} %w_qkv.1, bf16[2,512,512]{2,1,0:T(8,128)(2,1)S(1)} %copy-done.2, ...), custom_call_target="tpu_custom_call" | custom-call | tf_op jit(solution)/shard_map/block_second/pallas_call | solution.py:629
  (14 shorter events, 0.0 us)
Async XLA Ops:
  2.5 12.6 %collective-permute-start = (bf16[264,512]{1,0:T(8,128)(2,1)}, bf16[264,512]{1,0:T(8,128)(2,1)S(1)}, u32[]{:S(2)}, u32[]{:S(2)}) collective-permute-start(bf16[264,512]{1,0:T(8,128)(2,1)} %get-tuple-element.29.refs_0_), channel_id=1, source_target_pairs={{0,2},{1,3},{2,4},{3,5},{4,6},{5,7},{6,0},{7,1},{8,10},{9,11},{10,... | collective-permute-start | bytes 811016 | tf_op jit(solution)/shard_map/ppermute | solution.py:549
  5.6 9.6 %collective-permute-start.3 = (bf16[264,512]{1,0:T(8,128)(2,1)}, bf16[264,512]{1,0:T(8,128)(2,1)S(1)}, u32[]{:S(2)}, u32[]{:S(2)}) collective-permute-start(bf16[264,512]{1,0:T(8,128)(2,1)} %get-tuple-element.29.refs_0_), channel_id=1, source_target_pairs={{0,1},{1,0},{2,3},{3,2},{4,5},{5,4},{6,7},{7,6},{8,9},{9,8},{10,11... | collective-permute-start | bytes 811016 | tf_op jit(solution)/shard_map/ppermute | solution.py:546
  5.6 9.6 %collective-permute-start.4 = (bf16[256,512]{1,0:T(8,128)(2,1)}, bf16[256,512]{1,0:T(8,128)(2,1)S(1)}, u32[]{:S(2)}, u32[]{:S(2)}) collective-permute-start(bf16[256,512]{1,0:T(8,128)(2,1)} %get-tuple-element.32.refs_1_), channel_id=1, source_target_pairs={{0,1},{1,0},{2,3},{3,2},{4,5},{5,4},{6,7},{7,6},{8,9},{9,8},{10,11... | collective-permute-start | bytes 786440 | tf_op jit(solution)/shard_map/ppermute | solution.py:546
  6.1 13.9 %collective-permute-start.2 = (bf16[256,512]{1,0:T(8,128)(2,1)}, bf16[256,512]{1,0:T(8,128)(2,1)S(1)}, u32[]{:S(2)}, u32[]{:S(2)}) collective-permute-start(bf16[256,512]{1,0:T(8,128)(2,1)} %get-tuple-element.32.refs_1_), channel_id=1, source_target_pairs={{0,2},{1,3},{2,4},{3,5},{4,6},{5,7},{6,0},{7,1},{8,10},{9,11},{10,... | collective-permute-start | bytes 786440 | tf_op jit(solution)/shard_map/ppermute | solution.py:549
  7.7 1.9 %copy-start = (bf16[2,512,1536]{2,1,0:T(8,128)(2,1)S(1)}, bf16[2,512,1536]{2,1,0:T(8,128)(2,1)}, u32[]{:S(2)}) copy-start(bf16[2,512,1536]{2,1,0:T(8,128)(2,1)} %w_qkv.1) | copy-start | bytes 9437188
  9.6 1.2 %copy-start.1 = (bf16[2,512,512]{2,1,0:T(8,128)(2,1)S(1)}, bf16[2,512,512]{2,1,0:T(8,128)(2,1)}, u32[]{:S(2)}) copy-start(bf16[2,512,512]{2,1,0:T(8,128)(2,1)} %w_proj.1) | copy-start | bytes 3145732
  10.8 0.7 copy-start.4
  15.1 11.1 %collective-permute-start.7 = (bf16[264,512]{1,0:T(8,128)(2,1)S(1)}, bf16[264,512]{1,0:T(8,128)(2,1)S(1)}, u32[]{:S(2)}, u32[]{:S(2)}) collective-permute-start(bf16[264,512]{1,0:T(8,128)(2,1)S(1)} %collective-permute-done.refs_0_), channel_id=1, source_target_pairs={{0,1},{1,0},{2,3},{3,2},{4,5},{5,4},{6,7},{7,6},{8,9},{9,8},{10,11... | collective-permute-start | bytes 811016 | tf_op jit(solution)/shard_map/ppermute | solution.py:566
  15.2 11.1 %collective-permute-start.1 = (bf16[264,512]{1,0:T(8,128)(2,1)S(1)}, bf16[264,512]{1,0:T(8,128)(2,1)S(1)}, u32[]{:S(2)}, u32[]{:S(2)}) collective-permute-start(bf16[264,512]{1,0:T(8,128)(2,1)S(1)} %collective-permute-done.refs_0_), channel_id=1, source_target_pairs={{0,2},{1,3},{2,4},{3,5},{4,6},{5,7},{6,0},{7,1},{8,10},{9,11},{10,... | collective-permute-start | bytes 811016 | tf_op jit(solution)/shard_map/ppermute | solution.py:549
  15.2 1.0 %copy-start.9 = (bf16[264,512]{1,0:T(8,128)(2,1)S(1)}, bf16[264,512]{1,0:T(8,128)(2,1)}, u32[]{:S(2)}) copy-start(bf16[264,512]{1,0:T(8,128)(2,1)} %get-tuple-element.29.refs_0_) | copy-start | bytes 811012
  16.1 0.9 %copy-start.10 = (bf16[256,512]{1,0:T(8,128)(2,1)S(1)}, bf16[256,512]{1,0:T(8,128)(2,1)}, u32[]{:S(2)}) copy-start(bf16[256,512]{1,0:T(8,128)(2,1)} %get-tuple-element.32.refs_1_) | copy-start | bytes 786436
  20.0 6.2 %collective-permute-start.8 = (bf16[256,512]{1,0:T(8,128)(2,1)S(1)}, bf16[256,512]{1,0:T(8,128)(2,1)S(1)}, u32[]{:S(2)}, u32[]{:S(2)}) collective-permute-start(bf16[256,512]{1,0:T(8,128)(2,1)S(1)} %collective-permute-done.2.refs_1_), channel_id=1, source_target_pairs={{0,1},{1,0},{2,3},{3,2},{4,5},{5,4},{6,7},{7,6},{8,9},{9,8},{10,11... | collective-permute-start | bytes 786440 | tf_op jit(solution)/shard_map/ppermute | solution.py:566
  20.6 11.2 %collective-permute-start.6 = (bf16[256,512]{1,0:T(8,128)(2,1)S(1)}, bf16[256,512]{1,0:T(8,128)(2,1)S(1)}, u32[]{:S(2)}, u32[]{:S(2)}) collective-permute-start(bf16[256,512]{1,0:T(8,128)(2,1)S(1)} %collective-permute-done.2.refs_1_), channel_id=1, source_target_pairs={{0,2},{1,3},{2,4},{3,5},{4,6},{5,7},{6,0},{7,1},{8,10},{9,11},{10,... | collective-permute-start | bytes 786440 | tf_op jit(solution)/shard_map/ppermute | solution.py:549
  23.2 8.5 %copy-start.5 = (s32[512]{0:T(512)S(1)}, s32[512]{0:T(512)}, u32[]{:S(2)}) copy-start(s32[512]{0:T(512)} %param.13) | copy-start | bytes 6148
  26.2 11.3 %collective-permute-start.11 = (bf16[264,512]{1,0:T(8,128)(2,1)S(1)}, bf16[264,512]{1,0:T(8,128)(2,1)S(1)}, u32[]{:S(2)}, u32[]{:S(2)}) collective-permute-start(bf16[264,512]{1,0:T(8,128)(2,1)S(1)} %collective-permute-done.1.beyond.refs_0_.refs_2_), channel_id=1, source_target_pairs={{0,1},{1,0},{2,3},{3,2},{4,5},{5,4},{6,7},{7,6},{8,9},{9,8},{10,11... | collective-permute-start | bytes 811016 | tf_op jit(solution)/shard_map/ppermute | solution.py:566
  26.2 11.3 %collective-permute-start.5 = (bf16[264,512]{1,0:T(8,128)(2,1)S(1)}, bf16[264,512]{1,0:T(8,128)(2,1)S(1)}, u32[]{:S(2)}, u32[]{:S(2)}) collective-permute-start(bf16[264,512]{1,0:T(8,128)(2,1)S(1)} %collective-permute-done.1.beyond.refs_0_.refs_2_), channel_id=1, source_target_pairs={{0,2},{1,3},{2,4},{3,5},{4,6},{5,7},{6,0},{7,1},{8,10},{9,11},{10,... | collective-permute-start | bytes 811016 | tf_op jit(solution)/shard_map/ppermute | solution.py:549
  31.7 5.8 %collective-permute-start.12 = (bf16[256,512]{1,0:T(8,128)(2,1)S(1)}, bf16[256,512]{1,0:T(8,128)(2,1)S(1)}, u32[]{:S(2)}, u32[]{:S(2)}) collective-permute-start(bf16[256,512]{1,0:T(8,128)(2,1)S(1)} %collective-permute-done.6.refs_1_.refs_3_), channel_id=1, source_target_pairs={{0,1},{1,0},{2,3},{3,2},{4,5},{5,4},{6,7},{7,6},{8,9},{9,8},{10,11... | collective-permute-start | bytes 786440 | tf_op jit(solution)/shard_map/ppermute | solution.py:566
  31.7 11.1 %collective-permute-start.10 = (bf16[256,512]{1,0:T(8,128)(2,1)S(1)}, bf16[256,512]{1,0:T(8,128)(2,1)S(1)}, u32[]{:S(2)}, u32[]{:S(2)}) collective-permute-start(bf16[256,512]{1,0:T(8,128)(2,1)S(1)} %collective-permute-done.6.refs_1_.refs_3_), channel_id=1, source_target_pairs={{0,2},{1,3},{2,4},{3,5},{4,6},{5,7},{6,0},{7,1},{8,10},{9,11},{10,... | collective-permute-start | bytes 786440 | tf_op jit(solution)/shard_map/ppermute | solution.py:549
  37.5 5.4 %collective-permute-start.9 = (bf16[264,512]{1,0:T(8,128)(2,1)S(1)}, bf16[264,512]{1,0:T(8,128)(2,1)S(1)}, u32[]{:S(2)}, u32[]{:S(2)}) collective-permute-start(bf16[264,512]{1,0:T(8,128)(2,1)S(1)} %collective-permute-done.5.refs_0_), channel_id=1, source_target_pairs={{0,1},{1,0},{2,3},{3,2},{4,5},{5,4},{6,7},{7,6},{8,9},{9,8},{10,11... | collective-permute-start | bytes 811016 | tf_op jit(solution)/shard_map/ppermute | solution.py:566
  38.9 5.6 %copy-start.3 = (bf16[512,512]{1,0:T(8,128)(2,1)S(1)}, bf16[512,512]{1,0:T(8,128)(2,1)}, u32[]{:S(2)}) copy-start(bf16[512,512]{1,0:T(8,128)(2,1)} %points.3) | copy-start | bytes 1572868
  38.9 5.5 %copy-start.6 = (s32[8,3]{0,1:T(4,128)S(1)}, s32[8,3]{0,1:T(4,128)}, u32[]{:S(2)}) copy-start(s32[8,3]{0,1:T(4,128)} %param.11) | copy-start | bytes 292
  42.9 1.5 %collective-permute-start.13 = (bf16[256,512]{1,0:T(8,128)(2,1)S(1)}, bf16[256,512]{1,0:T(8,128)(2,1)S(1)}, u32[]{:S(2)}, u32[]{:S(2)}) collective-permute-start(bf16[256,512]{1,0:T(8,128)(2,1)S(1)} %collective-permute-done.10.refs_0_), channel_id=1, source_target_pairs={{0,1},{1,0},{2,3},{3,2},{4,5},{5,4},{6,7},{7,6},{8,9},{9,8},{10,11... | collective-permute-start | bytes 786440 | tf_op jit(solution)/shard_map/ppermute | solution.py:566
  44.2 28.2 %copy-start.2 = (bf16[2,512,512]{2,1,0:T(8,128)(2,1)S(1)}, bf16[2,512,512]{2,1,0:T(8,128)(2,1)}, u32[]{:S(2)}) copy-start(bf16[2,512,512]{2,1,0:T(8,128)(2,1)} %w_proj.1) | copy-start | bytes 3145732
  44.2 28.2 %copy-start.7 = (bf16[3,512]{1,0:T(4,128)(2,1)S(1)}, bf16[3,512]{1,0:T(4,128)(2,1)}, u32[]{:S(2)}) copy-start(bf16[3,512]{1,0:T(4,128)(2,1)} %w_head.1) | copy-start | bytes 9220
  44.2 28.2 %copy-start.8 = (s32[8,3]{0,1:T(4,128)S(1)}, s32[8,3]{0,1:T(4,128)}, u32[]{:S(2)}) copy-start(s32[8,3]{0,1:T(4,128)} %param.12) | copy-start | bytes 292

commit v14 on v13

--- a/solution.py
+++ b/solution.py
@@ -51,34 +51,43 @@
     width = HEADS_TOGETHER * head_dim
     heads_per_tile = LANES // head_dim
     lane = lax.broadcasted_iota(jnp.int32, (PATCH, LANES), 1)
-    steps = [(p, g) for p in range(len(patches)) for g in range(HEADS // HEADS_TOGETHER)]
-
-    def scores_of(step):
-        p, g = step
-        queries, keys, _ = patches[p]
-        q = queries(g * width, width)
-        stacked = jnp.concatenate([q * mask for mask in masks], axis=0)
-        return lax.dot_general(
-            stacked, keys(g * width, width), (((1,), (1,)), ((), ())), preferred_element_type=F32
-        )
-
-    scores = scores_of(steps[0])
-    for i, (p, g) in enumerate(steps):
-        later = scores_of(steps[i + 1]) if i + 1 < len(steps) else None
-        grown = jnp.exp(scores - jnp.max(scores, axis=-1, keepdims=True))
-        scale = 1.0 / jnp.sum(grown, axis=-1, keepdims=True)
-        values = patches[p][2](g * width, width)
-        mixed = jnp.dot(grown.astype(BF16), values, preferred_element_type=F32)
-        tiles = []
-        for t in range(width // LANES):
-            tile = None
-            for h in range(heads_per_tile):
-                rows = slice((t * heads_per_tile + h) * PATCH, (t * heads_per_tile + h + 1) * PATCH)
-                head = mixed[rows, t * LANES : (t + 1) * LANES] * scale[rows]
-                tile = head if tile is None else jnp.where(lane < h * head_dim, tile, head)
-            tiles.append(tile)
-        yield p, g * width, jnp.concatenate(tiles, axis=1).astype(BF16)
-        scores = later
+    firsts = range(0, HEADS * head_dim, width)
+
+    def scores_of(patch):
+        queries, keys, _ = patch
+        every = []
+        for at in firsts:
+            q = queries(at, width)
+            stacked = jnp.concatenate([q * mask for mask in masks], axis=0)
+            every.append(
+                lax.dot_general(
+                    stacked, keys(at, width), (((1,), (1,)), ((), ())), preferred_element_type=F32
+                )
+            )
+        return every
+
+    every = scores_of(patches[0])
+    for p, (_, _, values) in enumerate(patches):
+        later = scores_of(patches[p + 1]) if p + 1 < len(patches) else None
+        grown = [jnp.exp(scores - jnp.max(scores, axis=-1, keepdims=True)) for scores in every]
+        sides = []
+        for at, weights in zip(firsts, grown):
+            mixed = jnp.dot(
+                weights.astype(BF16), values(at, width), preferred_element_type=F32
+            )
+            scale = 1.0 / jnp.sum(weights, axis=-1, keepdims=True)
+            tiles = []
+            for t in range(width // LANES):
+                tile = None
+                for h in range(heads_per_tile):
+                    head = t * heads_per_tile + h
+                    rows = slice(head * PATCH, (head + 1) * PATCH)
+                    side = mixed[rows, t * LANES : (t + 1) * LANES] * scale[rows]
+                    tile = side if tile is None else jnp.where(lane < h * head_dim, tile, side)
+                tiles.append(tile)
+            sides += tiles
+        yield p, jnp.concatenate(sides, axis=1).astype(BF16)
+        every = later
 
 
 def one_hot_rows(places, rows):
@@ -317,8 +326,8 @@
                 else:
                     starts.append((2 * patches + (b * patches + p) * chosen + j) * PATCH)
             loaded.append(loads(asking, p, keyed, starts))
-    for p, at, rows_done in attend(loaded, channels // HEADS):
-        attended[p * PATCH : (p + 1) * PATCH, at : at + rows_done.shape[1]] = rows_done
+    for p, done in attend(loaded, channels // HEADS):
+        attended[p * PATCH : (p + 1) * PATCH, :] = done
     for copy in copies[1:]:
         copy.wait()
 
@@ -380,7 +389,17 @@
         [(tail, tail_held), (gains, gains_held), (w_head, head_held)], sems.at[0]
     )
     landing = started(lane_tiles(incoming, incoming_held), sems.at[1])
-    copies = started([(w_up.at[0], first_up_held)], sems.at[2])
+    copies = started(
+        [
+            (w_up.at[0], first_up_held),
+            (w_down.at[0], first_down_held),
+            (w_qkv.at[1], qkv_held),
+            (w_proj.at[1], proj_held),
+            (w_up.at[1], up_held),
+            (w_down.at[1], down_held),
+        ],
+        sems.at[2],
+    )
     for copy in small:
         copy.wait()
     per_row = LANES // capacity
@@ -395,17 +414,12 @@
     places = jnp.concatenate(pieces, axis=1).astype(jnp.int32) - 1
     place = one_hot_rows(places, rows)
     sides = []
-    later = (
-        [(w_down.at[0], first_down_held), (w_qkv.at[1], qkv_held)],
-        [(w_proj.at[1], proj_held), (w_up.at[1], up_held), (w_down.at[1], down_held)],
-    )
     for at in range(0, len(landing), 2):
         for copy in landing[at : at + 2]:
             copy.wait()
         moved = incoming_held[:, :, at * LANES : (at + 2) * LANES]
         moved = moved.reshape(devices * capacity, 2 * LANES)
         sides.append(jnp.dot(place, moved, preferred_element_type=F32).astype(BF16))
-        copies += started(later[at // 2], sems.at[3 + at // 2])
     first = jnp.concatenate(sides, axis=1)
     second = feed(first, gains_held[1:2, :], first_up_held, first_down_held, copies[:2])
     normed = layer_norm(second, gains_held[2:3, :])
@@ -418,8 +432,8 @@
     for p in range(patches):
         starts = [pl.multiple_of(pattern[j, p] * PATCH, PATCH) for j in range(chosen)]
         loaded.append(loads(queries, p, kv, [p * PATCH] + starts))
-    for p, at, rows_done in attend(loaded, channels // HEADS):
-        attended[p * PATCH : (p + 1) * PATCH, at : at + rows_done.shape[1]] = rows_done
+    for p, done in attend(loaded, channels // HEADS):
+        attended[p * PATCH : (p + 1) * PATCH, :] = done
     copies[3].wait()
     mixed = mix(second, attended[...], proj_held)
     done = feed(mixed, gains_held[3:4, :], up_held, down_held, copies[4:])
@@ -645,7 +659,7 @@
             pltpu.VMEM(norm_gains.shape, F32),
             pltpu.VMEM(tail.shape, BF16),
             pltpu.VMEM(w_head.shape, BF16),
-            pltpu.SemaphoreType.DMA((5, 4)),
+            pltpu.SemaphoreType.DMA((3, 6)),
         ],
         compiler_params=pltpu.CompilerParams(vmem_limit_bytes=SECOND_BYTES),
         name="block_second",

time: 85.7 us -> 85.9 us (level)
  no operation moved by 1% of the time
where the time goes in v14:
time: 85.9 us; the launch traced here: 85.6 us
  Pallas kernels  33 us (38%)
  blocking collectives  20.4 us (24%)
  waiting for transfers between devices  18.4 us (21%)
  starting transfers between devices  7.08 us (8%)
  local copies, waits for them, and re-layouts  5.75 us (7%)
  between operations  0.99 us (1%)
    all_to_all x1, blocking collectives, shards(): lax.all_to_all(outgoing, ('grp', 'seq'), split_axis=0, concat_axis=0, til...  20.4 us
    ppermute x6, waiting for transfers between devices, shards(): column = [lax.ppermute(rows, GROUP, onward) for rows in column]  18.2 us
    pallas_call x1, Pallas kernels, shards(): pl.pallas_call(second_kernel, out_shape=(jax.ShapeDtypeStruct((rows_here,...  12.7 us
    pallas_call x6, Pallas kernels, project(): pl.pallas_call(functools.partial(project_kernel, first_rows, new, ask), o...  9.77 us
    pallas_call x1, Pallas kernels, shards(): pl.pallas_call(functools.partial(first_kernel, chips if ring else 0, late...  7.79 us
    ppermute x6, starting transfers between devices, shards(): column = [lax.ppermute(rows, GROUP, onward) for rows in column]  6.03 us
    unnamed x22, local copies, waits for them, and re-layouts  5.75 us
    pallas_call x1, Pallas kernels, shards(): pl.pallas_call(split_kernel, out_shape=[jax.ShapeDtypeStruct((rows, chann...  1.89 us
  transfers between devices with their start and end apart: 14, of which 6 were waited for; matrix products, arithmetic and copies ran while one was open for 0% of the time, Pallas kernels for 12%

profile of v14, /device:TPU:0, one launch (start us, length us, event | category | flops | bytes accessed | tf_op | source)
XLA Modules:
  0.0 85.6 jit_solution(15255850001562714042)
XLA Ops:
  0.6 1.9 %split.1 = (bf16[264,512]{1,0:T(8,128)(2,1)}, bf16[256,512]{1,0:T(8,128)(2,1)}) custom-call(bf16[512,512]{1,0:T(8,128)(2,1)} %points.3, s32[1,512]{1,0:T(1,128)} %bitcast.3, s32[3,8]{1,0:T(4,128)} %bitcast.5), custom_call_target="tpu_custom_call" | custom-call | tf_op jit(solution)/shard_map/split/pallas_call | solution.py:481
  2.5 3.1 %collective-permute-start = (bf16[264,512]{1,0:T(8,128)(2,1)}, bf16[264,512]{1,0:T(8,128)(2,1)S(1)}, u32[]{:S(2)}, u32[]{:S(2)}) collective-permute-start(bf16[264,512]{1,0:T(8,128)(2,1)} %get-tuple-element.29.refs_0_), channel_id=1, source_target_pairs={{0,2},{1,3},{2,4},{3,5},{4,6},{5,7},{6,0},{7,1},{8,10},{9,11},{10,... | collective-permute-start | bytes 811016 | tf_op jit(solution)/shard_map/ppermute | solution.py:563
  5.6 0.0 collective-permute-start.3
  5.6 0.5 collective-permute-start.4
  6.1 1.6 %collective-permute-start.2 = (bf16[256,512]{1,0:T(8,128)(2,1)}, bf16[256,512]{1,0:T(8,128)(2,1)S(1)}, u32[]{:S(2)}, u32[]{:S(2)}) collective-permute-start(bf16[256,512]{1,0:T(8,128)(2,1)} %get-tuple-element.32.refs_1_), channel_id=1, source_target_pairs={{0,2},{1,3},{2,4},{3,5},{4,6},{5,7},{6,0},{7,1},{8,10},{9,11},{10,... | collective-permute-start | bytes 786440 | tf_op jit(solution)/shard_map/ppermute | solution.py:563
  7.7 1.9 %copy-done = bf16[2,512,1536]{2,1,0:T(8,128)(2,1)S(1)} copy-done((bf16[2,512,1536]{2,1,0:T(8,128)(2,1)S(1)}, bf16[2,512,1536]{2,1,0:T(8,128)(2,1)}, u32[]{:S(2)}) %copy-start) | copy-done | bytes 3145752
  9.6 1.2 %copy-done.1 = bf16[2,512,512]{2,1,0:T(8,128)(2,1)S(1)} copy-done((bf16[2,512,512]{2,1,0:T(8,128)(2,1)S(1)}, bf16[2,512,512]{2,1,0:T(8,128)(2,1)}, u32[]{:S(2)}) %copy-start.1) | copy-done | bytes 1048600
  10.8 0.7 copy-done.4
  11.5 0.2 keep.1
  11.7 3.5 %collective-permute-done.refs_0_ = bf16[264,512]{1,0:T(8,128)(2,1)S(1)} collective-permute-done((bf16[264,512]{1,0:T(8,128)(2,1)}, bf16[264,512]{1,0:T(8,128)(2,1)S(1)}, u32[]{:S(2)}, u32[]{:S(2)}) %collective-permute-start) | collective-permute-done | bytes 270368 | tf_op jit(solution)/shard_map/ppermute | solution.py:563
  15.1 0.0 collective-permute-start.7
  15.2 0.0 collective-permute-start.1
  15.2 0.0 collective-permute-done.4.refs_3_
  15.2 0.0 collective-permute-done.3.refs_2_
  15.2 0.9 %copy-done.9 = bf16[264,512]{1,0:T(8,128)(2,1)S(1)} copy-done((bf16[264,512]{1,0:T(8,128)(2,1)S(1)}, bf16[264,512]{1,0:T(8,128)(2,1)}, u32[]{:S(2)}) %copy-start.9) | copy-done | bytes 270360
  16.2 0.9 %copy-done.10 = bf16[256,512]{1,0:T(8,128)(2,1)S(1)} copy-done((bf16[256,512]{1,0:T(8,128)(2,1)S(1)}, bf16[256,512]{1,0:T(8,128)(2,1)}, u32[]{:S(2)}) %copy-start.10) | copy-done | bytes 262168
  17.1 2.9 %project_own.1 = (bf16[4096,1024]{1,0:T(8,128)(2,1)S(1)}, bf16[512,512]{1,0:T(8,128)(2,1)S(1)}) custom-call(bf16[264,512]{1,0:T(8,128)(2,1)S(1)} %copy-done.9, bf16[256,512]{1,0:T(8,128)(2,1)S(1)} %copy-done.10, bf16[264,512]{1,0:T(8,128)(2,1)S(1)} %collective-permute-done.3.refs_2_, bf16[256,512]{1,0:T(8,128)(2,1)S(1)} %collective-permute-done.4.refs_3_, ...), custom_call_target="tpu_custom_call" | custom-call | flops 1073741824 | bytes 4718592 | tf_op jit(solution)/shard_map/project_own/pallas_call | solution.py:540
  20.0 0.0 collective-permute-done.2.refs_1_
  20.0 0.5 collective-permute-start.8
  20.6 1.3 %collective-permute-start.6 = (bf16[256,512]{1,0:T(8,128)(2,1)S(1)}, bf16[256,512]{1,0:T(8,128)(2,1)S(1)}, u32[]{:S(2)}, u32[]{:S(2)}) collective-permute-start(bf16[256,512]{1,0:T(8,128)(2,1)S(1)} %collective-permute-done.2.refs_1_), channel_id=1, source_target_pairs={{0,2},{1,3},{2,4},{3,5},{4,6},{5,7},{6,0},{7,1},{8,10},{9,11},{10,... | collective-permute-start | bytes 786440 | tf_op jit(solution)/shard_map/ppermute | solution.py:563
  21.9 1.3 %project.5.refs_4_ = bf16[4096,1024]{1,0:T(8,128)(2,1)S(1)} custom-call(bf16[264,512]{1,0:T(8,128)(2,1)S(1)} %collective-permute-done.refs_0_, bf16[256,512]{1,0:T(8,128)(2,1)S(1)} %collective-permute-done.2.refs_1_, f32[4,512]{1,0:T(4,128)S(1)} %get-tuple-element.33.refs_4_.refs_2_.gains, ...), custom_call_target="tpu_custom_call", output_to_operand_aliasing={{}: (4, {})} | custom-call | flops 536870912 | bytes 3145728 | tf_op jit(solution)/shard_map/project/pallas_call | solution.py:540
  23.2 0.0 copy-start.5
  23.2 3.0 %collective-permute-done.1.beyond.refs_0_.refs_2_ = bf16[264,512]{1,0:T(8,128)(2,1)S(1)} collective-permute-done((bf16[264,512]{1,0:T(8,128)(2,1)S(1)}, bf16[264,512]{1,0:T(8,128)(2,1)S(1)}, u32[]{:S(2)}, u32[]{:S(2)}) %collective-permute-start.1) | collective-permute-done | bytes 270368 | tf_op jit(solution)/shard_map/ppermute | solution.py:563
  26.2 0.0 collective-permute-start.11
  26.2 0.0 collective-permute-start.5
  26.2 0.0 collective-permute-done.8.refs_1_
  26.3 1.3 %project.6.refs_4_ = bf16[4096,1024]{1,0:T(8,128)(2,1)S(1)} custom-call(bf16[264,512]{1,0:T(8,128)(2,1)S(1)} %collective-permute-done.7.refs_0_, bf16[256,512]{1,0:T(8,128)(2,1)S(1)} %collective-permute-done.8.refs_1_, f32[4,512]{1,0:T(4,128)S(1)} %get-tuple-element.33.refs_4_.refs_2_.gains, ...), custom_call_target="tpu_custom_call", output_to_operand_aliasing={{}: (4, {})} | custom-call | flops 536870912 | bytes 3145728 | tf_op jit(solution)/shard_map/project/pallas_call | solution.py:540
  27.6 4.2 %collective-permute-done.6.refs_1_.refs_3_ = bf16[256,512]{1,0:T(8,128)(2,1)S(1)} collective-permute-done((bf16[256,512]{1,0:T(8,128)(2,1)S(1)}, bf16[256,512]{1,0:T(8,128)(2,1)S(1)}, u32[]{:S(2)}, u32[]{:S(2)}) %collective-permute-start.6) | collective-permute-done | bytes 262176 | tf_op jit(solution)/shard_map/ppermute | solution.py:563
  31.7 0.0 collective-permute-start.10
  31.7 0.6 index.1
  32.4 1.6 %project.7 = (bf16[4096,1024]{1,0:T(8,128)(2,1)S(1)}, bf16[512,512]{1,0:T(8,128)(2,1)S(1)}) custom-call(bf16[264,512]{1,0:T(8,128)(2,1)S(1)} %collective-permute-done.1.beyond.refs_0_.refs_2_, bf16[256,512]{1,0:T(8,128)(2,1)S(1)} %collective-permute-done.6.refs_1_.refs_3_, ...), custom_call_target="tpu_custom_call", output_to_operand_aliasing={{0}: (4, {})} | custom-call | flops 536870912 | bytes 3145728 | tf_op jit(solution)/shard_map/project/pallas_call | solution.py:540
  34.0 3.6 %collective-permute-done.5.refs_0_ = bf16[264,512]{1,0:T(8,128)(2,1)S(1)} collective-permute-done((bf16[264,512]{1,0:T(8,128)(2,1)S(1)}, bf16[264,512]{1,0:T(8,128)(2,1)S(1)}, u32[]{:S(2)}, u32[]{:S(2)}) %collective-permute-start.5) | collective-permute-done | bytes 270368 | tf_op jit(solution)/shard_map/ppermute | solution.py:563
  37.5 0.0 collective-permute-start.9
  37.5 0.0 collective-permute-done.12.refs_1_
  37.5 0.0 collective-permute-done.11.refs_0_
  37.5 1.3 %project.8.refs_4_ = bf16[4096,1024]{1,0:T(8,128)(2,1)S(1)} custom-call(bf16[264,512]{1,0:T(8,128)(2,1)S(1)} %collective-permute-done.11.refs_0_, bf16[256,512]{1,0:T(8,128)(2,1)S(1)} %collective-permute-done.12.refs_1_, f32[4,512]{1,0:T(4,128)S(1)} %get-tuple-element.33.refs_4_.refs_2_.gains, ...), custom_call_target="tpu_custom_call", output_to_operand_aliasing={{}: (4, {})} | custom-call | flops 536870912 | bytes 3145728 | tf_op jit(solution)/shard_map/project/pallas_call | solution.py:540
  38.9 0.0 copy-start.3
  38.9 0.0 copy-start.6
  38.9 4.0 %collective-permute-done.10.refs_0_ = bf16[256,512]{1,0:T(8,128)(2,1)S(1)} collective-permute-done((bf16[256,512]{1,0:T(8,128)(2,1)S(1)}, bf16[256,512]{1,0:T(8,128)(2,1)S(1)}, u32[]{:S(2)}, u32[]{:S(2)}) %collective-permute-start.10) | collective-permute-done | bytes 262176 | tf_op jit(solution)/shard_map/ppermute | solution.py:563
  42.9 0.0 collective-permute-start.13
  42.9 1.3 %project.9.kept_rows = bf16[4096,1024]{1,0:T(8,128)(2,1)S(1)} custom-call(bf16[264,512]{1,0:T(8,128)(2,1)S(1)} %collective-permute-done.5.refs_0_, bf16[264,512]{1,0:T(8,128)(2,1)S(1)} %collective-permute-done.9.refs_1_, f32[4,512]{1,0:T(4,128)S(1)} %get-tuple-element.33.refs_4_.refs_2_.gains, ...), custom_call_target="tpu_custom_call", output_to_operand_aliasing={{}: (4, {})} | custom-call | flops 536870912 | bytes 3145728 | tf_op jit(solution)/shard_map/project/pallas_call | solution.py:540
  44.2 0.0 copy-start.2
  44.2 0.0 copy-start.7
  44.2 0.0 copy-start.8
  44.2 0.2 collective-permute-done.13.refs_1_
  44.4 7.8 %block_first.1 = (bf16[16,264,128]{2,1,0:T(8,128)(2,1)S(1)}, bf16[4096,1024]{1,0:T(8,128)(2,1)S(1)}) custom-call(s32[3,8]{1,0:T(4,128)S(1)} %bitcast.6, s32[3,8]{1,0:T(4,128)S(1)} %get-tuple-element.39.pattern_beyond, s32[1,1024]{1,0:T(1,128)S(1)} %get-tuple-element.46.slot_of_row, ...), custom_call_target="tpu_custom_call", output_to_operand_aliasing={{1}: (3, {})} | custom-call | tf_op jit(solution)/shard_map/block_first/pallas_call | solution.py:607
  52.2 20.4 %all_to_all.5.incoming = bf16[16,264,128]{2,1,0:T(8,128)(2,1)S(1)} all-to-all(bf16[16,264,128]{2,1,0:T(8,128)(2,1)S(1)} %get-tuple-element.55), channel_id=1, replica_groups=mesh['grp'=4,'half'=2,'seq'=4] {'grp','seq'}, dimensions={0} | all-to-all | bytes 2162688 | tf_op jit(solution)/shard_map/all_to_all | solution.py:641
  72.6 12.7 %block_second.1 = (bf16[512,512]{1,0:T(8,128)(2,1)}, f32[3,512]{1,0:T(4,128)}) custom-call(s32[3,8]{1,0:T(4,128)S(1)} %bitcast.7, f32[4,512]{1,0:T(4,128)S(1)} %copy-done.4, bf16[16,264,128]{2,1,0:T(8,128)(2,1)S(1)} %all_to_all.5.incoming, bf16[2,512,1536]{2,1,0:T(8,128)(2,1)} %w_qkv.1, bf16[2,512,512]{2,1,0:T(8,128)(2,1)S(1)} %copy-done.2, ...), custom_call_target="tpu_custom_call" | custom-call | tf_op jit(solution)/shard_map/block_second/pallas_call | solution.py:643
  (14 shorter events, 0.0 us)
Async XLA Ops:
  2.5 12.6 %collective-permute-start = (bf16[264,512]{1,0:T(8,128)(2,1)}, bf16[264,512]{1,0:T(8,128)(2,1)S(1)}, u32[]{:S(2)}, u32[]{:S(2)}) collective-permute-start(bf16[264,512]{1,0:T(8,128)(2,1)} %get-tuple-element.29.refs_0_), channel_id=1, source_target_pairs={{0,2},{1,3},{2,4},{3,5},{4,6},{5,7},{6,0},{7,1},{8,10},{9,11},{10,... | collective-permute-start | bytes 811016 | tf_op jit(solution)/shard_map/ppermute | solution.py:563
  5.6 9.6 %collective-permute-start.3 = (bf16[264,512]{1,0:T(8,128)(2,1)}, bf16[264,512]{1,0:T(8,128)(2,1)S(1)}, u32[]{:S(2)}, u32[]{:S(2)}) collective-permute-start(bf16[264,512]{1,0:T(8,128)(2,1)} %get-tuple-element.29.refs_0_), channel_id=1, source_target_pairs={{0,1},{1,0},{2,3},{3,2},{4,5},{5,4},{6,7},{7,6},{8,9},{9,8},{10,11... | collective-permute-start | bytes 811016 | tf_op jit(solution)/shard_map/ppermute | solution.py:560
  5.6 9.6 %collective-permute-start.4 = (bf16[256,512]{1,0:T(8,128)(2,1)}, bf16[256,512]{1,0:T(8,128)(2,1)S(1)}, u32[]{:S(2)}, u32[]{:S(2)}) collective-permute-start(bf16[256,512]{1,0:T(8,128)(2,1)} %get-tuple-element.32.refs_1_), channel_id=1, source_target_pairs={{0,1},{1,0},{2,3},{3,2},{4,5},{5,4},{6,7},{7,6},{8,9},{9,8},{10,11... | collective-permute-start | bytes 786440 | tf_op jit(solution)/shard_map/ppermute | solution.py:560
  6.1 13.9 %collective-permute-start.2 = (bf16[256,512]{1,0:T(8,128)(2,1)}, bf16[256,512]{1,0:T(8,128)(2,1)S(1)}, u32[]{:S(2)}, u32[]{:S(2)}) collective-permute-start(bf16[256,512]{1,0:T(8,128)(2,1)} %get-tuple-element.32.refs_1_), channel_id=1, source_target_pairs={{0,2},{1,3},{2,4},{3,5},{4,6},{5,7},{6,0},{7,1},{8,10},{9,11},{10,... | collective-permute-start | bytes 786440 | tf_op jit(solution)/shard_map/ppermute | solution.py:563
  7.7 1.9 %copy-start = (bf16[2,512,1536]{2,1,0:T(8,128)(2,1)S(1)}, bf16[2,512,1536]{2,1,0:T(8,128)(2,1)}, u32[]{:S(2)}) copy-start(bf16[2,512,1536]{2,1,0:T(8,128)(2,1)} %w_qkv.1) | copy-start | bytes 9437188
  9.6 1.2 %copy-start.1 = (bf16[2,512,512]{2,1,0:T(8,128)(2,1)S(1)}, bf16[2,512,512]{2,1,0:T(8,128)(2,1)}, u32[]{:S(2)}) copy-start(bf16[2,512,512]{2,1,0:T(8,128)(2,1)} %w_proj.1) | copy-start | bytes 3145732
  10.8 0.7 copy-start.4
  15.1 11.1 %collective-permute-start.7 = (bf16[264,512]{1,0:T(8,128)(2,1)S(1)}, bf16[264,512]{1,0:T(8,128)(2,1)S(1)}, u32[]{:S(2)}, u32[]{:S(2)}) collective-permute-start(bf16[264,512]{1,0:T(8,128)(2,1)S(1)} %collective-permute-done.refs_0_), channel_id=1, source_target_pairs={{0,1},{1,0},{2,3},{3,2},{4,5},{5,4},{6,7},{7,6},{8,9},{9,8},{10,11... | collective-permute-start | bytes 811016 | tf_op jit(solution)/shard_map/ppermute | solution.py:580
  15.2 11.1 %collective-permute-start.1 = (bf16[264,512]{1,0:T(8,128)(2,1)S(1)}, bf16[264,512]{1,0:T(8,128)(2,1)S(1)}, u32[]{:S(2)}, u32[]{:S(2)}) collective-permute-start(bf16[264,512]{1,0:T(8,128)(2,1)S(1)} %collective-permute-done.refs_0_), channel_id=1, source_target_pairs={{0,2},{1,3},{2,4},{3,5},{4,6},{5,7},{6,0},{7,1},{8,10},{9,11},{10,... | collective-permute-start | bytes 811016 | tf_op jit(solution)/shard_map/ppermute | solution.py:563
  15.2 1.0 %copy-start.9 = (bf16[264,512]{1,0:T(8,128)(2,1)S(1)}, bf16[264,512]{1,0:T(8,128)(2,1)}, u32[]{:S(2)}) copy-start(bf16[264,512]{1,0:T(8,128)(2,1)} %get-tuple-element.29.refs_0_) | copy-start | bytes 811012
  16.1 0.9 %copy-start.10 = (bf16[256,512]{1,0:T(8,128)(2,1)S(1)}, bf16[256,512]{1,0:T(8,128)(2,1)}, u32[]{:S(2)}) copy-start(bf16[256,512]{1,0:T(8,128)(2,1)} %get-tuple-element.32.refs_1_) | copy-start | bytes 786436
  20.0 6.2 %collective-permute-start.8 = (bf16[256,512]{1,0:T(8,128)(2,1)S(1)}, bf16[256,512]{1,0:T(8,128)(2,1)S(1)}, u32[]{:S(2)}, u32[]{:S(2)}) collective-permute-start(bf16[256,512]{1,0:T(8,128)(2,1)S(1)} %collective-permute-done.2.refs_1_), channel_id=1, source_target_pairs={{0,1},{1,0},{2,3},{3,2},{4,5},{5,4},{6,7},{7,6},{8,9},{9,8},{10,11... | collective-permute-start | bytes 786440 | tf_op jit(solution)/shard_map/ppermute | solution.py:580
  20.6 11.2 %collective-permute-start.6 = (bf16[256,512]{1,0:T(8,128)(2,1)S(1)}, bf16[256,512]{1,0:T(8,128)(2,1)S(1)}, u32[]{:S(2)}, u32[]{:S(2)}) collective-permute-start(bf16[256,512]{1,0:T(8,128)(2,1)S(1)} %collective-permute-done.2.refs_1_), channel_id=1, source_target_pairs={{0,2},{1,3},{2,4},{3,5},{4,6},{5,7},{6,0},{7,1},{8,10},{9,11},{10,... | collective-permute-start | bytes 786440 | tf_op jit(solution)/shard_map/ppermute | solution.py:563
  23.2 8.5 %copy-start.5 = (s32[512]{0:T(512)S(1)}, s32[512]{0:T(512)}, u32[]{:S(2)}) copy-start(s32[512]{0:T(512)} %param.13) | copy-start | bytes 6148
  26.2 11.3 %collective-permute-start.11 = (bf16[264,512]{1,0:T(8,128)(2,1)S(1)}, bf16[264,512]{1,0:T(8,128)(2,1)S(1)}, u32[]{:S(2)}, u32[]{:S(2)}) collective-permute-start(bf16[264,512]{1,0:T(8,128)(2,1)S(1)} %collective-permute-done.1.beyond.refs_0_.refs_2_), channel_id=1, source_target_pairs={{0,1},{1,0},{2,3},{3,2},{4,5},{5,4},{6,7},{7,6},{8,9},{9,8},{10,11... | collective-permute-start | bytes 811016 | tf_op jit(solution)/shard_map/ppermute | solution.py:580
  26.2 11.3 %collective-permute-start.5 = (bf16[264,512]{1,0:T(8,128)(2,1)S(1)}, bf16[264,512]{1,0:T(8,128)(2,1)S(1)}, u32[]{:S(2)}, u32[]{:S(2)}) collective-permute-start(bf16[264,512]{1,0:T(8,128)(2,1)S(1)} %collective-permute-done.1.beyond.refs_0_.refs_2_), channel_id=1, source_target_pairs={{0,2},{1,3},{2,4},{3,5},{4,6},{5,7},{6,0},{7,1},{8,10},{9,11},{10,... | collective-permute-start | bytes 811016 | tf_op jit(solution)/shard_map/ppermute | solution.py:563
  31.7 5.8 %collective-permute-start.12 = (bf16[256,512]{1,0:T(8,128)(2,1)S(1)}, bf16[256,512]{1,0:T(8,128)(2,1)S(1)}, u32[]{:S(2)}, u32[]{:S(2)}) collective-permute-start(bf16[256,512]{1,0:T(8,128)(2,1)S(1)} %collective-permute-done.6.refs_1_.refs_3_), channel_id=1, source_target_pairs={{0,1},{1,0},{2,3},{3,2},{4,5},{5,4},{6,7},{7,6},{8,9},{9,8},{10,11... | collective-permute-start | bytes 786440 | tf_op jit(solution)/shard_map/ppermute | solution.py:580
  31.7 11.1 %collective-permute-start.10 = (bf16[256,512]{1,0:T(8,128)(2,1)S(1)}, bf16[256,512]{1,0:T(8,128)(2,1)S(1)}, u32[]{:S(2)}, u32[]{:S(2)}) collective-permute-start(bf16[256,512]{1,0:T(8,128)(2,1)S(1)} %collective-permute-done.6.refs_1_.refs_3_), channel_id=1, source_target_pairs={{0,2},{1,3},{2,4},{3,5},{4,6},{5,7},{6,0},{7,1},{8,10},{9,11},{10,... | collective-permute-start | bytes 786440 | tf_op jit(solution)/shard_map/ppermute | solution.py:563
  37.5 5.4 %collective-permute-start.9 = (bf16[264,512]{1,0:T(8,128)(2,1)S(1)}, bf16[264,512]{1,0:T(8,128)(2,1)S(1)}, u32[]{:S(2)}, u32[]{:S(2)}) collective-permute-start(bf16[264,512]{1,0:T(8,128)(2,1)S(1)} %collective-permute-done.5.refs_0_), channel_id=1, source_target_pairs={{0,1},{1,0},{2,3},{3,2},{4,5},{5,4},{6,7},{7,6},{8,9},{9,8},{10,11... | collective-permute-start | bytes 811016 | tf_op jit(solution)/shard_map/ppermute | solution.py:580
  38.9 5.6 %copy-start.3 = (bf16[512,512]{1,0:T(8,128)(2,1)S(1)}, bf16[512,512]{1,0:T(8,128)(2,1)}, u32[]{:S(2)}) copy-start(bf16[512,512]{1,0:T(8,128)(2,1)} %points.3) | copy-start | bytes 1572868
  38.9 5.5 %copy-start.6 = (s32[8,3]{0,1:T(4,128)S(1)}, s32[8,3]{0,1:T(4,128)}, u32[]{:S(2)}) copy-start(s32[8,3]{0,1:T(4,128)} %param.11) | copy-start | bytes 292
  42.9 1.5 %collective-permute-start.13 = (bf16[256,512]{1,0:T(8,128)(2,1)S(1)}, bf16[256,512]{1,0:T(8,128)(2,1)S(1)}, u32[]{:S(2)}, u32[]{:S(2)}) collective-permute-start(bf16[256,512]{1,0:T(8,128)(2,1)S(1)} %collective-permute-done.10.refs_0_), channel_id=1, source_target_pairs={{0,1},{1,0},{2,3},{3,2},{4,5},{5,4},{6,7},{7,6},{8,9},{9,8},{10,11... | collective-permute-start | bytes 786440 | tf_op jit(solution)/shard_map/ppermute | solution.py:580
  44.2 28.4 %copy-start.2 = (bf16[2,512,512]{2,1,0:T(8,128)(2,1)S(1)}, bf16[2,512,512]{2,1,0:T(8,128)(2,1)}, u32[]{:S(2)}) copy-start(bf16[2,512,512]{2,1,0:T(8,128)(2,1)} %w_proj.1) | copy-start | bytes 3145732
  44.2 28.4 %copy-start.7 = (bf16[3,512]{1,0:T(4,128)(2,1)S(1)}, bf16[3,512]{1,0:T(4,128)(2,1)}, u32[]{:S(2)}) copy-start(bf16[3,512]{1,0:T(4,128)(2,1)} %w_head.1) | copy-start | bytes 9220
  44.2 28.4 %copy-start.8 = (s32[8,3]{0,1:T(4,128)S(1)}, s32[8,3]{0,1:T(4,128)}, u32[]{:S(2)}) copy-start(s32[8,3]{0,1:T(4,128)} %param.12) | copy-start | bytes 292

commit v15 on v13

--- a/solution.py
+++ b/solution.py
@@ -311,7 +311,9 @@
                 if ring_chips:
                     patch = picked[j, p]
                     owner, local = lax.div(patch, patches), lax.rem(patch, patches)
-                    chip = lax.rem(lax.div(me, 2) - lax.div(owner, 2) + ring_chips, ring_chips)
+                    chip = lax.div(me, 2) - lax.div(owner, 2)
+                    chip = jnp.where(local * RING_PARTS < patches, chip, -chip)
+                    chip = lax.rem(chip + ring_chips, ring_chips)
                     slot = 2 * chip + jnp.where(lax.rem(me, 2) == lax.rem(owner, 2), 0, 1)
                     starts.append(pl.multiple_of((slot * patches + local) * PATCH, PATCH))
                 else:
@@ -380,7 +382,17 @@
         [(tail, tail_held), (gains, gains_held), (w_head, head_held)], sems.at[0]
     )
     landing = started(lane_tiles(incoming, incoming_held), sems.at[1])
-    copies = started([(w_up.at[0], first_up_held)], sems.at[2])
+    copies = started(
+        [
+            (w_up.at[0], first_up_held),
+            (w_down.at[0], first_down_held),
+            (w_qkv.at[1], qkv_held),
+            (w_proj.at[1], proj_held),
+            (w_up.at[1], up_held),
+            (w_down.at[1], down_held),
+        ],
+        sems.at[2],
+    )
     for copy in small:
         copy.wait()
     per_row = LANES // capacity
@@ -395,17 +407,12 @@
     places = jnp.concatenate(pieces, axis=1).astype(jnp.int32) - 1
     place = one_hot_rows(places, rows)
     sides = []
-    later = (
-        [(w_down.at[0], first_down_held), (w_qkv.at[1], qkv_held)],
-        [(w_proj.at[1], proj_held), (w_up.at[1], up_held), (w_down.at[1], down_held)],
-    )
     for at in range(0, len(landing), 2):
         for copy in landing[at : at + 2]:
             copy.wait()
         moved = incoming_held[:, :, at * LANES : (at + 2) * LANES]
         moved = moved.reshape(devices * capacity, 2 * LANES)
         sides.append(jnp.dot(place, moved, preferred_element_type=F32).astype(BF16))
-        copies += started(later[at // 2], sems.at[3 + at // 2])
     first = jnp.concatenate(sides, axis=1)
     second = feed(first, gains_held[1:2, :], first_up_held, first_down_held, copies[:2])
     normed = layer_norm(second, gains_held[2:3, :])
@@ -454,7 +461,7 @@
 
     shards_in_group = lax.axis_size(GROUP)
     chips = shards_in_group // 2
-    onward = [(i, (i + 2) % shards_in_group) for i in range(shards_in_group)]
+    ways = [[(i, (i + by) % shards_in_group) for i in range(shards_in_group)] for by in (2, -2)]
     swap = [(i, i ^ 1) for i in range(shards_in_group)]
     across = [(i, (i + chips) % shards_in_group) for i in range(shards_in_group)]
     ring = shards_in_group * rows_here * 2 * channels * 2 <= RING_BYTES
@@ -546,7 +553,7 @@
         beside = [lax.ppermute(rows, GROUP, swap) for rows in column]
         waiting = [(0, 0, column), (1, 0, beside)]
         for step in range(1, chips):
-            column = [lax.ppermute(rows, GROUP, onward) for rows in column]
+            column = [lax.ppermute(rows, GROUP, way) for rows, way in zip(column, ways)]
             if step == 1:
                 column[0], gains_kept = lax.optimization_barrier((column[0], gains_kept))
                 keyed, queries = project(None, waiting, ask=True)
@@ -645,7 +652,7 @@
             pltpu.VMEM(norm_gains.shape, F32),
             pltpu.VMEM(tail.shape, BF16),
             pltpu.VMEM(w_head.shape, BF16),
-            pltpu.SemaphoreType.DMA((5, 4)),
+            pltpu.SemaphoreType.DMA((3, 6)),
         ],
         compiler_params=pltpu.CompilerParams(vmem_limit_bytes=SECOND_BYTES),
         name="block_second",

time: 85.7 us -> 88.5 us (1.033)
  starting transfers between devices: 7.08 us -> 15.6 us
  waiting for transfers between devices: 18.4 us -> 12.8 us
    ppermute x6, starting transfers between devices: 6.03 us -> 14.4 us  [shards(): column = [lax.ppermute(rows, GROUP, way) for rows, way in zip(column, ways)]]
    ppermute x6, waiting for transfers between devices: 18.2 us -> 12.7 us  [shards(): column = [lax.ppermute(rows, GROUP, way) for rows, way in zip(column, ways)]]
where the time goes in v15:
time: 88.5 us; the launch traced here: 88.2 us
  Pallas kernels  32.6 us (37%)
  blocking collectives  20.4 us (23%)
  starting transfers between devices  15.6 us (18%)
  waiting for transfers between devices  12.8 us (14%)
  local copies, waits for them, and re-layouts  5.74 us (6%)
  between operations  1 us (1%)
    all_to_all x1, blocking collectives, shards(): lax.all_to_all(outgoing, ('grp', 'seq'), split_axis=0, concat_axis=0, til...  20.4 us
    ppermute x6, starting transfers between devices, shards(): column = [lax.ppermute(rows, GROUP, way) for rows, way in zip(column, ways)]  14.4 us
    ppermute x6, waiting for transfers between devices, shards(): column = [lax.ppermute(rows, GROUP, way) for rows, way in zip(column, ways)]  12.7 us
    pallas_call x1, Pallas kernels, shards(): pl.pallas_call(second_kernel, out_shape=(jax.ShapeDtypeStruct((rows_here,...  12.6 us
    pallas_call x6, Pallas kernels, project(): pl.pallas_call(functools.partial(project_kernel, first_rows, new, ask), o...  9.79 us
    pallas_call x1, Pallas kernels, shards(): pl.pallas_call(functools.partial(first_kernel, chips if ring else 0, late...  7.56 us
    unnamed x22, local copies, waits for them, and re-layouts  5.74 us
    pallas_call x1, Pallas kernels, shards(): pl.pallas_call(split_kernel, out_shape=[jax.ShapeDtypeStruct((rows, chann...  1.89 us
  transfers between devices with their start and end apart: 14, of which 6 were waited for; matrix products, arithmetic and copies ran while one was open for 0% of the time, Pallas kernels for 12%

profile of v15, /device:TPU:0, one launch (start us, length us, event | category | flops | bytes accessed | tf_op | source)
XLA Modules:
  0.0 88.2 jit_solution(213026730150755897)
XLA Ops:
  0.6 1.9 %split.1 = (bf16[264,512]{1,0:T(8,128)(2,1)}, bf16[256,512]{1,0:T(8,128)(2,1)}) custom-call(bf16[512,512]{1,0:T(8,128)(2,1)} %points.3, s32[1,512]{1,0:T(1,128)} %bitcast.3, s32[3,8]{1,0:T(4,128)} %bitcast.5), custom_call_target="tpu_custom_call" | custom-call | tf_op jit(solution)/shard_map/split/pallas_call | solution.py:474
  2.5 3.1 %collective-permute-start = (bf16[264,512]{1,0:T(8,128)(2,1)}, bf16[264,512]{1,0:T(8,128)(2,1)S(1)}, u32[]{:S(2)}, u32[]{:S(2)}) collective-permute-start(bf16[264,512]{1,0:T(8,128)(2,1)} %get-tuple-element.29.refs_0_), channel_id=1, source_target_pairs={{0,2},{1,3},{2,4},{3,5},{4,6},{5,7},{6,0},{7,1},{8,10},{9,11},{10,... | collective-permute-start | bytes 811016 | tf_op jit(solution)/shard_map/ppermute | solution.py:556
  5.6 0.0 collective-permute-start.3
  5.6 0.5 collective-permute-start.4
  6.1 2.1 %collective-permute-start.2 = (bf16[256,512]{1,0:T(8,128)(2,1)}, bf16[256,512]{1,0:T(8,128)(2,1)S(1)}, u32[]{:S(2)}, u32[]{:S(2)}) collective-permute-start(bf16[256,512]{1,0:T(8,128)(2,1)} %get-tuple-element.32.refs_1_), channel_id=1, source_target_pairs={{0,6},{1,7},{2,0},{3,1},{4,2},{5,3},{6,4},{7,5},{8,14},{9,15},{10,... | collective-permute-start | bytes 786440 | tf_op jit(solution)/shard_map/ppermute | solution.py:556
  8.2 1.9 %copy-done = bf16[2,512,1536]{2,1,0:T(8,128)(2,1)S(1)} copy-done((bf16[2,512,1536]{2,1,0:T(8,128)(2,1)S(1)}, bf16[2,512,1536]{2,1,0:T(8,128)(2,1)}, u32[]{:S(2)}) %copy-start) | copy-done | bytes 3145752
  10.1 1.2 %copy-done.1 = bf16[2,512,512]{2,1,0:T(8,128)(2,1)S(1)} copy-done((bf16[2,512,512]{2,1,0:T(8,128)(2,1)S(1)}, bf16[2,512,512]{2,1,0:T(8,128)(2,1)}, u32[]{:S(2)}) %copy-start.1) | copy-done | bytes 1048600
  11.3 0.7 copy-done.4
  12.0 0.2 keep.1
  12.2 3.0 %collective-permute-done.refs_0_ = bf16[264,512]{1,0:T(8,128)(2,1)S(1)} collective-permute-done((bf16[264,512]{1,0:T(8,128)(2,1)}, bf16[264,512]{1,0:T(8,128)(2,1)S(1)}, u32[]{:S(2)}, u32[]{:S(2)}) %collective-permute-start) | collective-permute-done | bytes 270368 | tf_op jit(solution)/shard_map/ppermute | solution.py:556
  15.2 0.0 collective-permute-start.7
  15.2 0.0 collective-permute-start.1
  15.2 0.0 collective-permute-done.4.refs_3_
  15.2 0.0 collective-permute-done.3.refs_2_
  15.2 0.0 copy-start.9
  15.2 0.9 %copy-done.9 = bf16[264,512]{1,0:T(8,128)(2,1)S(1)} copy-done((bf16[264,512]{1,0:T(8,128)(2,1)S(1)}, bf16[264,512]{1,0:T(8,128)(2,1)}, u32[]{:S(2)}) %copy-start.9) | copy-done | bytes 270360
  16.2 0.9 %copy-done.10 = bf16[256,512]{1,0:T(8,128)(2,1)S(1)} copy-done((bf16[256,512]{1,0:T(8,128)(2,1)S(1)}, bf16[256,512]{1,0:T(8,128)(2,1)}, u32[]{:S(2)}) %copy-start.10) | copy-done | bytes 262168
  17.1 2.9 %project_own.1 = (bf16[4096,1024]{1,0:T(8,128)(2,1)S(1)}, bf16[512,512]{1,0:T(8,128)(2,1)S(1)}) custom-call(bf16[264,512]{1,0:T(8,128)(2,1)S(1)} %copy-done.9, bf16[256,512]{1,0:T(8,128)(2,1)S(1)} %copy-done.10, bf16[264,512]{1,0:T(8,128)(2,1)S(1)} %collective-permute-done.3.refs_2_, bf16[256,512]{1,0:T(8,128)(2,1)S(1)} %collective-permute-done.4.refs_3_, ...), custom_call_target="tpu_custom_call" | custom-call | flops 1073741824 | bytes 4718592 | tf_op jit(solution)/shard_map/project_own/pallas_call | solution.py:533
  20.0 0.0 collective-permute-done.2.refs_1_
  20.0 0.6 collective-permute-start.8
  20.6 5.6 %collective-permute-start.6 = (bf16[256,512]{1,0:T(8,128)(2,1)S(1)}, bf16[256,512]{1,0:T(8,128)(2,1)S(1)}, u32[]{:S(2)}, u32[]{:S(2)}) collective-permute-start(bf16[256,512]{1,0:T(8,128)(2,1)S(1)} %collective-permute-done.2.refs_1_), channel_id=1, source_target_pairs={{0,6},{1,7},{2,0},{3,1},{4,2},{5,3},{6,4},{7,5},{8,14},{9,15},{10,... | collective-permute-start | bytes 786440 | tf_op jit(solution)/shard_map/ppermute | solution.py:556
  26.2 1.3 %project.5.refs_4_ = bf16[4096,1024]{1,0:T(8,128)(2,1)S(1)} custom-call(bf16[264,512]{1,0:T(8,128)(2,1)S(1)} %collective-permute-done.refs_0_, bf16[256,512]{1,0:T(8,128)(2,1)S(1)} %collective-permute-done.2.refs_1_, f32[4,512]{1,0:T(4,128)S(1)} %get-tuple-element.33.refs_4_.refs_2_.gains, ...), custom_call_target="tpu_custom_call", output_to_operand_aliasing={{}: (4, {})} | custom-call | flops 536870912 | bytes 3145728 | tf_op jit(solution)/shard_map/project/pallas_call | solution.py:533
  27.5 0.0 copy-start.5
  27.5 0.5 collective-permute-done.1.beyond.refs_0_.refs_2_
  28.1 0.0 collective-permute-start.11
  28.1 0.0 collective-permute-start.5
  28.1 0.0 collective-permute-done.8.refs_1_
  28.1 1.3 %project.6.refs_4_ = bf16[4096,1024]{1,0:T(8,128)(2,1)S(1)} custom-call(bf16[264,512]{1,0:T(8,128)(2,1)S(1)} %collective-permute-done.7.refs_0_, bf16[256,512]{1,0:T(8,128)(2,1)S(1)} %collective-permute-done.8.refs_1_, f32[4,512]{1,0:T(4,128)S(1)} %get-tuple-element.33.refs_4_.refs_2_.gains, ...), custom_call_target="tpu_custom_call", output_to_operand_aliasing={{}: (4, {})} | custom-call | flops 536870912 | bytes 3145728 | tf_op jit(solution)/shard_map/project/pallas_call | solution.py:533
  29.4 4.2 %collective-permute-done.6.refs_1_.refs_3_ = bf16[256,512]{1,0:T(8,128)(2,1)S(1)} collective-permute-done((bf16[256,512]{1,0:T(8,128)(2,1)S(1)}, bf16[256,512]{1,0:T(8,128)(2,1)S(1)}, u32[]{:S(2)}, u32[]{:S(2)}) %collective-permute-start.6) | collective-permute-done | bytes 262176 | tf_op jit(solution)/shard_map/ppermute | solution.py:556
  33.6 0.1 collective-permute-start.12
  33.6 3.6 %collective-permute-start.10 = (bf16[256,512]{1,0:T(8,128)(2,1)S(1)}, bf16[256,512]{1,0:T(8,128)(2,1)S(1)}, u32[]{:S(2)}, u32[]{:S(2)}) collective-permute-start(bf16[256,512]{1,0:T(8,128)(2,1)S(1)} %collective-permute-done.6.refs_1_.refs_3_), channel_id=1, source_target_pairs={{0,6},{1,7},{2,0},{3,1},{4,2},{5,3},{6,4},{7,5},{8,14},{9,15},{10,... | collective-permute-start | bytes 786440 | tf_op jit(solution)/shard_map/ppermute | solution.py:556
  37.2 0.6 index.1
  37.8 1.6 %project.7 = (bf16[4096,1024]{1,0:T(8,128)(2,1)S(1)}, bf16[512,512]{1,0:T(8,128)(2,1)S(1)}) custom-call(bf16[264,512]{1,0:T(8,128)(2,1)S(1)} %collective-permute-done.1.beyond.refs_0_.refs_2_, bf16[256,512]{1,0:T(8,128)(2,1)S(1)} %collective-permute-done.6.refs_1_.refs_3_, ...), custom_call_target="tpu_custom_call", output_to_operand_aliasing={{0}: (4, {})} | custom-call | flops 536870912 | bytes 3145728 | tf_op jit(solution)/shard_map/project/pallas_call | solution.py:533
  39.4 1.5 %collective-permute-done.5.refs_0_ = bf16[264,512]{1,0:T(8,128)(2,1)S(1)} collective-permute-done((bf16[264,512]{1,0:T(8,128)(2,1)S(1)}, bf16[264,512]{1,0:T(8,128)(2,1)S(1)}, u32[]{:S(2)}, u32[]{:S(2)}) %collective-permute-start.5) | collective-permute-done | bytes 270368 | tf_op jit(solution)/shard_map/ppermute | solution.py:556
  40.9 0.0 collective-permute-done.12.refs_1_
  40.9 1.3 %project.8.refs_4_ = bf16[4096,1024]{1,0:T(8,128)(2,1)S(1)} custom-call(bf16[264,512]{1,0:T(8,128)(2,1)S(1)} %collective-permute-done.11.refs_0_, bf16[256,512]{1,0:T(8,128)(2,1)S(1)} %collective-permute-done.12.refs_1_, f32[4,512]{1,0:T(4,128)S(1)} %get-tuple-element.33.refs_4_.refs_2_.gains, ...), custom_call_target="tpu_custom_call", output_to_operand_aliasing={{}: (4, {})} | custom-call | flops 536870912 | bytes 3145728 | tf_op jit(solution)/shard_map/project/pallas_call | solution.py:533
  42.2 0.0 copy-start.3
  42.2 0.0 copy-start.6
  42.3 3.6 %collective-permute-done.10.refs_0_ = bf16[256,512]{1,0:T(8,128)(2,1)S(1)} collective-permute-done((bf16[256,512]{1,0:T(8,128)(2,1)S(1)}, bf16[256,512]{1,0:T(8,128)(2,1)S(1)}, u32[]{:S(2)}, u32[]{:S(2)}) %collective-permute-start.10) | collective-permute-done | bytes 262176 | tf_op jit(solution)/shard_map/ppermute | solution.py:556
  45.8 0.1 collective-permute-start.13
  45.9 1.3 %project.9.kept_rows = bf16[4096,1024]{1,0:T(8,128)(2,1)S(1)} custom-call(bf16[264,512]{1,0:T(8,128)(2,1)S(1)} %collective-permute-done.5.refs_0_, bf16[264,512]{1,0:T(8,128)(2,1)S(1)} %collective-permute-done.9.refs_1_, f32[4,512]{1,0:T(4,128)S(1)} %get-tuple-element.33.refs_4_.refs_2_.gains, ...), custom_call_target="tpu_custom_call", output_to_operand_aliasing={{}: (4, {})} | custom-call | flops 536870912 | bytes 3145728 | tf_op jit(solution)/shard_map/project/pallas_call | solution.py:533
  47.2 0.0 copy-start.2
  47.3 0.0 copy-start.7
  47.3 0.0 copy-start.8
  47.3 0.1 collective-permute-done.13.refs_1_
  47.4 7.6 %block_first.1 = (bf16[16,264,128]{2,1,0:T(8,128)(2,1)S(1)}, bf16[4096,1024]{1,0:T(8,128)(2,1)S(1)}) custom-call(s32[3,8]{1,0:T(4,128)S(1)} %bitcast.6, s32[3,8]{1,0:T(4,128)S(1)} %get-tuple-element.39.pattern_beyond, s32[1,1024]{1,0:T(1,128)S(1)} %get-tuple-element.46.slot_of_row, ...), custom_call_target="tpu_custom_call", output_to_operand_aliasing={{1}: (3, {})} | custom-call | tf_op jit(solution)/shard_map/block_first/pallas_call | solution.py:600
  54.9 20.4 %all_to_all.5.incoming = bf16[16,264,128]{2,1,0:T(8,128)(2,1)S(1)} all-to-all(bf16[16,264,128]{2,1,0:T(8,128)(2,1)S(1)} %get-tuple-element.55), channel_id=1, replica_groups=mesh['grp'=4,'half'=2,'seq'=4] {'grp','seq'}, dimensions={0} | all-to-all | bytes 2162688 | tf_op jit(solution)/shard_map/all_to_all | solution.py:634
  75.4 12.6 %block_second.1 = (bf16[512,512]{1,0:T(8,128)(2,1)}, f32[3,512]{1,0:T(4,128)}) custom-call(s32[3,8]{1,0:T(4,128)S(1)} %bitcast.7, f32[4,512]{1,0:T(4,128)S(1)} %copy-done.4, bf16[16,264,128]{2,1,0:T(8,128)(2,1)S(1)} %all_to_all.5.incoming, bf16[2,512,1536]{2,1,0:T(8,128)(2,1)} %w_qkv.1, bf16[2,512,512]{2,1,0:T(8,128)(2,1)S(1)} %copy-done.2, ...), custom_call_target="tpu_custom_call" | custom-call | tf_op jit(solution)/shard_map/block_second/pallas_call | solution.py:636
  (14 shorter events, 0.0 us)
Async XLA Ops:
  2.5 12.7 %collective-permute-start = (bf16[264,512]{1,0:T(8,128)(2,1)}, bf16[264,512]{1,0:T(8,128)(2,1)S(1)}, u32[]{:S(2)}, u32[]{:S(2)}) collective-permute-start(bf16[264,512]{1,0:T(8,128)(2,1)} %get-tuple-element.29.refs_0_), channel_id=1, source_target_pairs={{0,2},{1,3},{2,4},{3,5},{4,6},{5,7},{6,0},{7,1},{8,10},{9,11},{10,... | collective-permute-start | bytes 811016 | tf_op jit(solution)/shard_map/ppermute | solution.py:556
  5.6 9.6 %collective-permute-start.3 = (bf16[264,512]{1,0:T(8,128)(2,1)}, bf16[264,512]{1,0:T(8,128)(2,1)S(1)}, u32[]{:S(2)}, u32[]{:S(2)}) collective-permute-start(bf16[264,512]{1,0:T(8,128)(2,1)} %get-tuple-element.29.refs_0_), channel_id=1, source_target_pairs={{0,1},{1,0},{2,3},{3,2},{4,5},{5,4},{6,7},{7,6},{8,9},{9,8},{10,11... | collective-permute-start | bytes 811016 | tf_op jit(solution)/shard_map/ppermute | solution.py:553
  5.6 9.6 %collective-permute-start.4 = (bf16[256,512]{1,0:T(8,128)(2,1)}, bf16[256,512]{1,0:T(8,128)(2,1)S(1)}, u32[]{:S(2)}, u32[]{:S(2)}) collective-permute-start(bf16[256,512]{1,0:T(8,128)(2,1)} %get-tuple-element.32.refs_1_), channel_id=1, source_target_pairs={{0,1},{1,0},{2,3},{3,2},{4,5},{5,4},{6,7},{7,6},{8,9},{9,8},{10,11... | collective-permute-start | bytes 786440 | tf_op jit(solution)/shard_map/ppermute | solution.py:553
  6.1 13.9 %collective-permute-start.2 = (bf16[256,512]{1,0:T(8,128)(2,1)}, bf16[256,512]{1,0:T(8,128)(2,1)S(1)}, u32[]{:S(2)}, u32[]{:S(2)}) collective-permute-start(bf16[256,512]{1,0:T(8,128)(2,1)} %get-tuple-element.32.refs_1_), channel_id=1, source_target_pairs={{0,6},{1,7},{2,0},{3,1},{4,2},{5,3},{6,4},{7,5},{8,14},{9,15},{10,... | collective-permute-start | bytes 786440 | tf_op jit(solution)/shard_map/ppermute | solution.py:556
  8.2 1.9 %copy-start = (bf16[2,512,1536]{2,1,0:T(8,128)(2,1)S(1)}, bf16[2,512,1536]{2,1,0:T(8,128)(2,1)}, u32[]{:S(2)}) copy-start(bf16[2,512,1536]{2,1,0:T(8,128)(2,1)} %w_qkv.1) | copy-start | bytes 9437188
  10.1 1.2 %copy-start.1 = (bf16[2,512,512]{2,1,0:T(8,128)(2,1)S(1)}, bf16[2,512,512]{2,1,0:T(8,128)(2,1)}, u32[]{:S(2)}) copy-start(bf16[2,512,512]{2,1,0:T(8,128)(2,1)} %w_proj.1) | copy-start | bytes 3145732
  11.3 0.7 copy-start.4
  15.2 12.9 %collective-permute-start.7 = (bf16[264,512]{1,0:T(8,128)(2,1)S(1)}, bf16[264,512]{1,0:T(8,128)(2,1)S(1)}, u32[]{:S(2)}, u32[]{:S(2)}) collective-permute-start(bf16[264,512]{1,0:T(8,128)(2,1)S(1)} %collective-permute-done.refs_0_), channel_id=1, source_target_pairs={{0,1},{1,0},{2,3},{3,2},{4,5},{5,4},{6,7},{7,6},{8,9},{9,8},{10,11... | collective-permute-start | bytes 811016 | tf_op jit(solution)/shard_map/ppermute | solution.py:573
  15.2 12.9 %collective-permute-start.1 = (bf16[264,512]{1,0:T(8,128)(2,1)S(1)}, bf16[264,512]{1,0:T(8,128)(2,1)S(1)}, u32[]{:S(2)}, u32[]{:S(2)}) collective-permute-start(bf16[264,512]{1,0:T(8,128)(2,1)S(1)} %collective-permute-done.refs_0_), channel_id=1, source_target_pairs={{0,2},{1,3},{2,4},{3,5},{4,6},{5,7},{6,0},{7,1},{8,10},{9,11},{10,... | collective-permute-start | bytes 811016 | tf_op jit(solution)/shard_map/ppermute | solution.py:556
  15.2 1.0 %copy-start.9 = (bf16[264,512]{1,0:T(8,128)(2,1)S(1)}, bf16[264,512]{1,0:T(8,128)(2,1)}, u32[]{:S(2)}) copy-start(bf16[264,512]{1,0:T(8,128)(2,1)} %get-tuple-element.29.refs_0_) | copy-start | bytes 811012
  16.2 0.9 %copy-start.10 = (bf16[256,512]{1,0:T(8,128)(2,1)S(1)}, bf16[256,512]{1,0:T(8,128)(2,1)}, u32[]{:S(2)}) copy-start(bf16[256,512]{1,0:T(8,128)(2,1)} %get-tuple-element.32.refs_1_) | copy-start | bytes 786436
  20.0 8.0 %collective-permute-start.8 = (bf16[256,512]{1,0:T(8,128)(2,1)S(1)}, bf16[256,512]{1,0:T(8,128)(2,1)S(1)}, u32[]{:S(2)}, u32[]{:S(2)}) collective-permute-start(bf16[256,512]{1,0:T(8,128)(2,1)S(1)} %collective-permute-done.2.refs_1_), channel_id=1, source_target_pairs={{0,1},{1,0},{2,3},{3,2},{4,5},{5,4},{6,7},{7,6},{8,9},{9,8},{10,11... | collective-permute-start | bytes 786440 | tf_op jit(solution)/shard_map/ppermute | solution.py:573
  20.6 13.0 %collective-permute-start.6 = (bf16[256,512]{1,0:T(8,128)(2,1)S(1)}, bf16[256,512]{1,0:T(8,128)(2,1)S(1)}, u32[]{:S(2)}, u32[]{:S(2)}) collective-permute-start(bf16[256,512]{1,0:T(8,128)(2,1)S(1)} %collective-permute-done.2.refs_1_), channel_id=1, source_target_pairs={{0,6},{1,7},{2,0},{3,1},{4,2},{5,3},{6,4},{7,5},{8,14},{9,15},{10,... | collective-permute-start | bytes 786440 | tf_op jit(solution)/shard_map/ppermute | solution.py:556
  27.5 9.7 %copy-start.5 = (s32[512]{0:T(512)S(1)}, s32[512]{0:T(512)}, u32[]{:S(2)}) copy-start(s32[512]{0:T(512)} %param.13) | copy-start | bytes 6148
  28.1 12.8 %collective-permute-start.11 = (bf16[264,512]{1,0:T(8,128)(2,1)S(1)}, bf16[264,512]{1,0:T(8,128)(2,1)S(1)}, u32[]{:S(2)}, u32[]{:S(2)}) collective-permute-start(bf16[264,512]{1,0:T(8,128)(2,1)S(1)} %collective-permute-done.1.beyond.refs_0_.refs_2_), channel_id=1, source_target_pairs={{0,1},{1,0},{2,3},{3,2},{4,5},{5,4},{6,7},{7,6},{8,9},{9,8},{10,11... | collective-permute-start | bytes 811016 | tf_op jit(solution)/shard_map/ppermute | solution.py:573
  28.1 12.8 %collective-permute-start.5 = (bf16[264,512]{1,0:T(8,128)(2,1)S(1)}, bf16[264,512]{1,0:T(8,128)(2,1)S(1)}, u32[]{:S(2)}, u32[]{:S(2)}) collective-permute-start(bf16[264,512]{1,0:T(8,128)(2,1)S(1)} %collective-permute-done.1.beyond.refs_0_.refs_2_), channel_id=1, source_target_pairs={{0,2},{1,3},{2,4},{3,5},{4,6},{5,7},{6,0},{7,1},{8,10},{9,11},{10,... | collective-permute-start | bytes 811016 | tf_op jit(solution)/shard_map/ppermute | solution.py:556
  33.6 7.3 %collective-permute-start.12 = (bf16[256,512]{1,0:T(8,128)(2,1)S(1)}, bf16[256,512]{1,0:T(8,128)(2,1)S(1)}, u32[]{:S(2)}, u32[]{:S(2)}) collective-permute-start(bf16[256,512]{1,0:T(8,128)(2,1)S(1)} %collective-permute-done.6.refs_1_.refs_3_), channel_id=1, source_target_pairs={{0,1},{1,0},{2,3},{3,2},{4,5},{5,4},{6,7},{7,6},{8,9},{9,8},{10,11... | collective-permute-start | bytes 786440 | tf_op jit(solution)/shard_map/ppermute | solution.py:573
  33.6 12.2 %collective-permute-start.10 = (bf16[256,512]{1,0:T(8,128)(2,1)S(1)}, bf16[256,512]{1,0:T(8,128)(2,1)S(1)}, u32[]{:S(2)}, u32[]{:S(2)}) collective-permute-start(bf16[256,512]{1,0:T(8,128)(2,1)S(1)} %collective-permute-done.6.refs_1_.refs_3_), channel_id=1, source_target_pairs={{0,6},{1,7},{2,0},{3,1},{4,2},{5,3},{6,4},{7,5},{8,14},{9,15},{10,... | collective-permute-start | bytes 786440 | tf_op jit(solution)/shard_map/ppermute | solution.py:556
  40.9 5.0 %collective-permute-start.9 = (bf16[264,512]{1,0:T(8,128)(2,1)S(1)}, bf16[264,512]{1,0:T(8,128)(2,1)S(1)}, u32[]{:S(2)}, u32[]{:S(2)}) collective-permute-start(bf16[264,512]{1,0:T(8,128)(2,1)S(1)} %collective-permute-done.5.refs_0_), channel_id=1, source_target_pairs={{0,1},{1,0},{2,3},{3,2},{4,5},{5,4},{6,7},{7,6},{8,9},{9,8},{10,11... | collective-permute-start | bytes 811016 | tf_op jit(solution)/shard_map/ppermute | solution.py:573
  42.2 5.1 %copy-start.3 = (bf16[512,512]{1,0:T(8,128)(2,1)S(1)}, bf16[512,512]{1,0:T(8,128)(2,1)}, u32[]{:S(2)}) copy-start(bf16[512,512]{1,0:T(8,128)(2,1)} %points.3) | copy-start | bytes 1572868
  42.2 5.1 %copy-start.6 = (s32[8,3]{0,1:T(4,128)S(1)}, s32[8,3]{0,1:T(4,128)}, u32[]{:S(2)}) copy-start(s32[8,3]{0,1:T(4,128)} %param.11) | copy-start | bytes 292
  45.8 1.5 %collective-permute-start.13 = (bf16[256,512]{1,0:T(8,128)(2,1)S(1)}, bf16[256,512]{1,0:T(8,128)(2,1)S(1)}, u32[]{:S(2)}, u32[]{:S(2)}) collective-permute-start(bf16[256,512]{1,0:T(8,128)(2,1)S(1)} %collective-permute-done.10.refs_0_), channel_id=1, source_target_pairs={{0,1},{1,0},{2,3},{3,2},{4,5},{5,4},{6,7},{7,6},{8,9},{9,8},{10,11... | collective-permute-start | bytes 786440 | tf_op jit(solution)/shard_map/ppermute | solution.py:573
  47.2 28.1 %copy-start.2 = (bf16[2,512,512]{2,1,0:T(8,128)(2,1)S(1)}, bf16[2,512,512]{2,1,0:T(8,128)(2,1)}, u32[]{:S(2)}) copy-start(bf16[2,512,512]{2,1,0:T(8,128)(2,1)} %w_proj.1) | copy-start | bytes 3145732
  47.3 28.1 %copy-start.7 = (bf16[3,512]{1,0:T(4,128)(2,1)S(1)}, bf16[3,512]{1,0:T(4,128)(2,1)}, u32[]{:S(2)}) copy-start(bf16[3,512]{1,0:T(4,128)(2,1)} %w_head.1) | copy-start | bytes 9220
  47.3 28.1 %copy-start.8 = (s32[8,3]{0,1:T(4,128)S(1)}, s32[8,3]{0,1:T(4,128)}, u32[]{:S(2)}) copy-start(s32[8,3]{0,1:T(4,128)} %param.12) | copy-start | bytes 292

commit v16 on v15

--- a/solution.py
+++ b/solution.py
@@ -101,11 +101,9 @@
     return (rows.astype(F32) + mixed).astype(BF16)
 
 
-def feed(first, gain, w_up, w_down, copies=()):
+def feed(first, gain, w_up, w_down):
     hidden = layer_norm(first, gain)
     total = first.astype(F32)
-    for copy in copies[:1]:
-        copy.wait()
     piece = 512
     pieces = range(0, w_up.shape[1], piece)
     upper = jnp.dot(hidden, w_up[:, :piece], preferred_element_type=F32)
@@ -116,9 +114,6 @@
                 hidden, w_up[:, at + piece : at + 2 * piece], preferred_element_type=F32
             )
         act = gelu(upper).astype(BF16)
-        if at == 0:
-            for copy in copies[1:]:
-                copy.wait()
         total = total + jnp.dot(act, w_down[at : at + piece, :], preferred_element_type=F32)
         upper = later
     return total.astype(BF16)
@@ -295,8 +290,9 @@
         ],
         sems.at[0],
     )
+    for copy in landing + copies[1:]:
+        copy.wait()
     for i, first in enumerate(late_rows):
-        landing[i].wait()
         keyed[first : first + late_part, :] = jnp.dot(
             layer_norm(late_held[i], gains[0:1, :]),
             w_qkv[:, channels:],
@@ -311,9 +307,7 @@
                 if ring_chips:
                     patch = picked[j, p]
                     owner, local = lax.div(patch, patches), lax.rem(patch, patches)
-                    chip = lax.div(me, 2) - lax.div(owner, 2)
-                    chip = jnp.where(local * RING_PARTS < patches, chip, -chip)
-                    chip = lax.rem(chip + ring_chips, ring_chips)
+                    chip = lax.rem(lax.div(me, 2) - lax.div(owner, 2) + ring_chips, ring_chips)
                     slot = 2 * chip + jnp.where(lax.rem(me, 2) == lax.rem(owner, 2), 0, 1)
                     starts.append(pl.multiple_of((slot * patches + local) * PATCH, PATCH))
                 else:
@@ -321,11 +315,8 @@
             loaded.append(loads(asking, p, keyed, starts))
     for p, at, rows_done in attend(loaded, channels // HEADS):
         attended[p * PATCH : (p + 1) * PATCH, at : at + rows_done.shape[1]] = rows_done
-    for copy in copies[1:]:
-        copy.wait()
 
     first_held[...] = mix(points_held[...], attended[...], w_proj)
-    copies[0].wait()
     targets = devices // SEND_PARTS
     block_slots = capacity // 2
     leaving = []
@@ -343,7 +334,7 @@
             )
         pairs = lane_tiles(outgoing.at[here], outgoing_held.at[here])
         leaving += started([(source, place) for place, source in pairs], sems.at[1 + i])
-    for copy in leaving:
+    for copy in copies[:1] + leaving:
         copy.wait()
 
 
@@ -414,10 +405,13 @@
         moved = moved.reshape(devices * capacity, 2 * LANES)
         sides.append(jnp.dot(place, moved, preferred_element_type=F32).astype(BF16))
     first = jnp.concatenate(sides, axis=1)
-    second = feed(first, gains_held[1:2, :], first_up_held, first_down_held, copies[:2])
+    for copy in copies[:2]:
+        copy.wait()
+    second = feed(first, gains_held[1:2, :], first_up_held, first_down_held)
+    for copy in copies[2:]:
+        copy.wait()
     normed = layer_norm(second, gains_held[2:3, :])
     scale = (channels // HEADS) ** (-0.5)
-    copies[2].wait()
     asked = jnp.dot(normed, qkv_held[:, :channels], preferred_element_type=F32).astype(BF16)
     queries[...] = (asked * BF16(scale)).astype(BF16)
     kv[...] = jnp.dot(normed, qkv_held[:, channels:], preferred_element_type=F32).astype(BF16)
@@ -427,9 +421,8 @@
         loaded.append(loads(queries, p, kv, [p * PATCH] + starts))
     for p, at, rows_done in attend(loaded, channels // HEADS):
         attended[p * PATCH : (p + 1) * PATCH, at : at + rows_done.shape[1]] = rows_done
-    copies[3].wait()
     mixed = mix(second, attended[...], proj_held)
-    done = feed(mixed, gains_held[3:4, :], up_held, down_held, copies[4:])
+    done = feed(mixed, gains_held[3:4, :], up_held, down_held)
     features[...] = done
     normals[...] = lax.dot_general(
         head_held[...], done, (((1,), (1,)), ((), ())), preferred_element_type=F32
@@ -461,7 +454,7 @@
 
     shards_in_group = lax.axis_size(GROUP)
     chips = shards_in_group // 2
-    ways = [[(i, (i + by) % shards_in_group) for i in range(shards_in_group)] for by in (2, -2)]
+    onward = [(i, (i + 2) % shards_in_group) for i in range(shards_in_group)]
     swap = [(i, i ^ 1) for i in range(shards_in_group)]
     across = [(i, (i + chips) % shards_in_group) for i in range(shards_in_group)]
     ring = shards_in_group * rows_here * 2 * channels * 2 <= RING_BYTES
@@ -553,7 +546,7 @@
         beside = [lax.ppermute(rows, GROUP, swap) for rows in column]
         waiting = [(0, 0, column), (1, 0, beside)]
         for step in range(1, chips):
-            column = [lax.ppermute(rows, GROUP, way) for rows, way in zip(column, ways)]
+            column = [lax.ppermute(rows, GROUP, onward) for rows in column]
             if step == 1:
                 column[0], gains_kept = lax.optimization_barrier((column[0], gains_kept))
                 keyed, queries = project(None, waiting, ask=True)

time: 88.5 us -> 84.2 us (0.951)
  starting transfers between devices: 15.6 us -> 7.08 us
  waiting for transfers between devices: 12.8 us -> 18.4 us
  Pallas kernels: 32.6 us -> 31.3 us
    ppermute x6, starting transfers between devices: 14.4 us -> 6.03 us  [shards(): column = [lax.ppermute(rows, GROUP, onward) for rows in column]]
    ppermute x6, waiting for transfers between devices: 12.7 us -> 18.2 us  [shards(): column = [lax.ppermute(rows, GROUP, onward) for rows in column]]
  transfers between devices with their start and end apart: 14 -> 14, of which waited for: 6 -> 6; matrix products, arithmetic and copies ran while one was open for 0% -> 0% of each run, Pallas kernels for 12% -> 13%
where the time goes in v16:
time: 84.2 us; the launch traced here: 83.9 us
  Pallas kernels  31.3 us (37%)
  blocking collectives  20.4 us (24%)
  waiting for transfers between devices  18.4 us (22%)
  starting transfers between devices  7.08 us (8%)
  local copies, waits for them, and re-layouts  5.75 us (7%)
  between operations  0.99 us (1%)
    all_to_all x1, blocking collectives, shards(): lax.all_to_all(outgoing, ('grp', 'seq'), split_axis=0, concat_axis=0, til...  20.4 us
    ppermute x6, waiting for transfers between devices, shards(): column = [lax.ppermute(rows, GROUP, onward) for rows in column]  18.2 us
    pallas_call x1, Pallas kernels, shards(): pl.pallas_call(second_kernel, out_shape=(jax.ShapeDtypeStruct((rows_here,...  12.2 us
    pallas_call x6, Pallas kernels, project(): pl.pallas_call(functools.partial(project_kernel, first_rows, new, ask), o...  9.77 us
    pallas_call x1, Pallas kernels, shards(): pl.pallas_call(functools.partial(first_kernel, chips if ring else 0, late...  6.69 us
    ppermute x6, starting transfers between devices, shards(): column = [lax.ppermute(rows, GROUP, onward) for rows in column]  6.03 us
    unnamed x22, local copies, waits for them, and re-layouts  5.75 us
    pallas_call x1, Pallas kernels, shards(): pl.pallas_call(split_kernel, out_shape=[jax.ShapeDtypeStruct((rows, chann...  1.89 us
  transfers between devices with their start and end apart: 14, of which 6 were waited for; matrix products, arithmetic and copies ran while one was open for 0% of the time, Pallas kernels for 13%

profile of v16, /device:TPU:0, one launch (start us, length us, event | category | flops | bytes accessed | tf_op | source)
XLA Modules:
  0.0 83.9 jit_solution(5349601360337614750)
XLA Ops:
  0.6 1.9 %split.1 = (bf16[264,512]{1,0:T(8,128)(2,1)}, bf16[256,512]{1,0:T(8,128)(2,1)}) custom-call(bf16[512,512]{1,0:T(8,128)(2,1)} %points.3, s32[1,512]{1,0:T(1,128)} %bitcast.3, s32[3,8]{1,0:T(4,128)} %bitcast.5), custom_call_target="tpu_custom_call" | custom-call | tf_op jit(solution)/shard_map/split/pallas_call | solution.py:467
  2.5 3.1 %collective-permute-start = (bf16[264,512]{1,0:T(8,128)(2,1)}, bf16[264,512]{1,0:T(8,128)(2,1)S(1)}, u32[]{:S(2)}, u32[]{:S(2)}) collective-permute-start(bf16[264,512]{1,0:T(8,128)(2,1)} %get-tuple-element.29.refs_0_), channel_id=1, source_target_pairs={{0,2},{1,3},{2,4},{3,5},{4,6},{5,7},{6,0},{7,1},{8,10},{9,11},{10,... | collective-permute-start | bytes 811016 | tf_op jit(solution)/shard_map/ppermute | solution.py:549
  5.6 0.0 collective-permute-start.3
  5.6 0.5 collective-permute-start.4
  6.1 1.6 %collective-permute-start.2 = (bf16[256,512]{1,0:T(8,128)(2,1)}, bf16[256,512]{1,0:T(8,128)(2,1)S(1)}, u32[]{:S(2)}, u32[]{:S(2)}) collective-permute-start(bf16[256,512]{1,0:T(8,128)(2,1)} %get-tuple-element.32.refs_1_), channel_id=1, source_target_pairs={{0,2},{1,3},{2,4},{3,5},{4,6},{5,7},{6,0},{7,1},{8,10},{9,11},{10,... | collective-permute-start | bytes 786440 | tf_op jit(solution)/shard_map/ppermute | solution.py:549
  7.7 1.9 %copy-done = bf16[2,512,1536]{2,1,0:T(8,128)(2,1)S(1)} copy-done((bf16[2,512,1536]{2,1,0:T(8,128)(2,1)S(1)}, bf16[2,512,1536]{2,1,0:T(8,128)(2,1)}, u32[]{:S(2)}) %copy-start) | copy-done | bytes 3145752
  9.6 1.2 %copy-done.1 = bf16[2,512,512]{2,1,0:T(8,128)(2,1)S(1)} copy-done((bf16[2,512,512]{2,1,0:T(8,128)(2,1)S(1)}, bf16[2,512,512]{2,1,0:T(8,128)(2,1)}, u32[]{:S(2)}) %copy-start.1) | copy-done | bytes 1048600
  10.8 0.7 copy-done.4
  11.5 0.2 keep.1
  11.7 3.5 %collective-permute-done.refs_0_ = bf16[264,512]{1,0:T(8,128)(2,1)S(1)} collective-permute-done((bf16[264,512]{1,0:T(8,128)(2,1)}, bf16[264,512]{1,0:T(8,128)(2,1)S(1)}, u32[]{:S(2)}, u32[]{:S(2)}) %collective-permute-start) | collective-permute-done | bytes 270368 | tf_op jit(solution)/shard_map/ppermute | solution.py:549
  15.1 0.0 collective-permute-start.7
  15.2 0.0 collective-permute-start.1
  15.2 0.0 collective-permute-done.4.refs_3_
  15.2 0.0 collective-permute-done.3.refs_2_
  15.2 0.9 %copy-done.9 = bf16[264,512]{1,0:T(8,128)(2,1)S(1)} copy-done((bf16[264,512]{1,0:T(8,128)(2,1)S(1)}, bf16[264,512]{1,0:T(8,128)(2,1)}, u32[]{:S(2)}) %copy-start.9) | copy-done | bytes 270360
  16.2 0.9 %copy-done.10 = bf16[256,512]{1,0:T(8,128)(2,1)S(1)} copy-done((bf16[256,512]{1,0:T(8,128)(2,1)S(1)}, bf16[256,512]{1,0:T(8,128)(2,1)}, u32[]{:S(2)}) %copy-start.10) | copy-done | bytes 262168
  17.1 2.9 %project_own.1 = (bf16[4096,1024]{1,0:T(8,128)(2,1)S(1)}, bf16[512,512]{1,0:T(8,128)(2,1)S(1)}) custom-call(bf16[264,512]{1,0:T(8,128)(2,1)S(1)} %copy-done.9, bf16[256,512]{1,0:T(8,128)(2,1)S(1)} %copy-done.10, bf16[264,512]{1,0:T(8,128)(2,1)S(1)} %collective-permute-done.3.refs_2_, bf16[256,512]{1,0:T(8,128)(2,1)S(1)} %collective-permute-done.4.refs_3_, ...), custom_call_target="tpu_custom_call" | custom-call | flops 1073741824 | bytes 4718592 | tf_op jit(solution)/shard_map/project_own/pallas_call | solution.py:526
  20.0 0.0 collective-permute-done.2.refs_1_
  20.0 0.5 collective-permute-start.8
  20.6 1.3 %collective-permute-start.6 = (bf16[256,512]{1,0:T(8,128)(2,1)S(1)}, bf16[256,512]{1,0:T(8,128)(2,1)S(1)}, u32[]{:S(2)}, u32[]{:S(2)}) collective-permute-start(bf16[256,512]{1,0:T(8,128)(2,1)S(1)} %collective-permute-done.2.refs_1_), channel_id=1, source_target_pairs={{0,2},{1,3},{2,4},{3,5},{4,6},{5,7},{6,0},{7,1},{8,10},{9,11},{10,... | collective-permute-start | bytes 786440 | tf_op jit(solution)/shard_map/ppermute | solution.py:549
  21.9 1.3 %project.5.refs_4_ = bf16[4096,1024]{1,0:T(8,128)(2,1)S(1)} custom-call(bf16[264,512]{1,0:T(8,128)(2,1)S(1)} %collective-permute-done.refs_0_, bf16[256,512]{1,0:T(8,128)(2,1)S(1)} %collective-permute-done.2.refs_1_, f32[4,512]{1,0:T(4,128)S(1)} %get-tuple-element.33.refs_4_.refs_2_.gains, ...), custom_call_target="tpu_custom_call", output_to_operand_aliasing={{}: (4, {})} | custom-call | flops 536870912 | bytes 3145728 | tf_op jit(solution)/shard_map/project/pallas_call | solution.py:526
  23.2 0.0 copy-start.5
  23.2 3.0 %collective-permute-done.1.beyond.refs_0_.refs_2_ = bf16[264,512]{1,0:T(8,128)(2,1)S(1)} collective-permute-done((bf16[264,512]{1,0:T(8,128)(2,1)S(1)}, bf16[264,512]{1,0:T(8,128)(2,1)S(1)}, u32[]{:S(2)}, u32[]{:S(2)}) %collective-permute-start.1) | collective-permute-done | bytes 270368 | tf_op jit(solution)/shard_map/ppermute | solution.py:549
  26.2 0.0 collective-permute-start.11
  26.2 0.0 collective-permute-start.5
  26.2 0.0 collective-permute-done.8.refs_1_
  26.3 1.3 %project.6.refs_4_ = bf16[4096,1024]{1,0:T(8,128)(2,1)S(1)} custom-call(bf16[264,512]{1,0:T(8,128)(2,1)S(1)} %collective-permute-done.7.refs_0_, bf16[256,512]{1,0:T(8,128)(2,1)S(1)} %collective-permute-done.8.refs_1_, f32[4,512]{1,0:T(4,128)S(1)} %get-tuple-element.33.refs_4_.refs_2_.gains, ...), custom_call_target="tpu_custom_call", output_to_operand_aliasing={{}: (4, {})} | custom-call | flops 536870912 | bytes 3145728 | tf_op jit(solution)/shard_map/project/pallas_call | solution.py:526
  27.6 4.2 %collective-permute-done.6.refs_1_.refs_3_ = bf16[256,512]{1,0:T(8,128)(2,1)S(1)} collective-permute-done((bf16[256,512]{1,0:T(8,128)(2,1)S(1)}, bf16[256,512]{1,0:T(8,128)(2,1)S(1)}, u32[]{:S(2)}, u32[]{:S(2)}) %collective-permute-start.6) | collective-permute-done | bytes 262176 | tf_op jit(solution)/shard_map/ppermute | solution.py:549
  31.7 0.0 collective-permute-start.10
  31.7 0.6 index.1
  32.4 1.6 %project.7 = (bf16[4096,1024]{1,0:T(8,128)(2,1)S(1)}, bf16[512,512]{1,0:T(8,128)(2,1)S(1)}) custom-call(bf16[264,512]{1,0:T(8,128)(2,1)S(1)} %collective-permute-done.1.beyond.refs_0_.refs_2_, bf16[256,512]{1,0:T(8,128)(2,1)S(1)} %collective-permute-done.6.refs_1_.refs_3_, ...), custom_call_target="tpu_custom_call", output_to_operand_aliasing={{0}: (4, {})} | custom-call | flops 536870912 | bytes 3145728 | tf_op jit(solution)/shard_map/project/pallas_call | solution.py:526
  34.0 3.6 %collective-permute-done.5.refs_0_ = bf16[264,512]{1,0:T(8,128)(2,1)S(1)} collective-permute-done((bf16[264,512]{1,0:T(8,128)(2,1)S(1)}, bf16[264,512]{1,0:T(8,128)(2,1)S(1)}, u32[]{:S(2)}, u32[]{:S(2)}) %collective-permute-start.5) | collective-permute-done | bytes 270368 | tf_op jit(solution)/shard_map/ppermute | solution.py:549
  37.5 0.0 collective-permute-start.9
  37.5 0.0 collective-permute-done.12.refs_1_
  37.5 0.0 collective-permute-done.11.refs_0_
  37.5 1.3 %project.8.refs_4_ = bf16[4096,1024]{1,0:T(8,128)(2,1)S(1)} custom-call(bf16[264,512]{1,0:T(8,128)(2,1)S(1)} %collective-permute-done.11.refs_0_, bf16[256,512]{1,0:T(8,128)(2,1)S(1)} %collective-permute-done.12.refs_1_, f32[4,512]{1,0:T(4,128)S(1)} %get-tuple-element.33.refs_4_.refs_2_.gains, ...), custom_call_target="tpu_custom_call", output_to_operand_aliasing={{}: (4, {})} | custom-call | flops 536870912 | bytes 3145728 | tf_op jit(solution)/shard_map/project/pallas_call | solution.py:526
  38.9 0.0 copy-start.3
  38.9 0.0 copy-start.6
  38.9 4.0 %collective-permute-done.10.refs_0_ = bf16[256,512]{1,0:T(8,128)(2,1)S(1)} collective-permute-done((bf16[256,512]{1,0:T(8,128)(2,1)S(1)}, bf16[256,512]{1,0:T(8,128)(2,1)S(1)}, u32[]{:S(2)}, u32[]{:S(2)}) %collective-permute-start.10) | collective-permute-done | bytes 262176 | tf_op jit(solution)/shard_map/ppermute | solution.py:549
  42.9 0.0 collective-permute-start.13
  42.9 1.3 %project.9.kept_rows = bf16[4096,1024]{1,0:T(8,128)(2,1)S(1)} custom-call(bf16[264,512]{1,0:T(8,128)(2,1)S(1)} %collective-permute-done.5.refs_0_, bf16[264,512]{1,0:T(8,128)(2,1)S(1)} %collective-permute-done.9.refs_1_, f32[4,512]{1,0:T(4,128)S(1)} %get-tuple-element.33.refs_4_.refs_2_.gains, ...), custom_call_target="tpu_custom_call", output_to_operand_aliasing={{}: (4, {})} | custom-call | flops 536870912 | bytes 3145728 | tf_op jit(solution)/shard_map/project/pallas_call | solution.py:526
  44.2 0.0 copy-start.2
  44.2 0.0 copy-start.7
  44.2 0.0 copy-start.8
  44.2 0.2 collective-permute-done.13.refs_1_
  44.4 6.7 %block_first.1 = (bf16[16,264,128]{2,1,0:T(8,128)(2,1)S(1)}, bf16[4096,1024]{1,0:T(8,128)(2,1)S(1)}) custom-call(s32[3,8]{1,0:T(4,128)S(1)} %bitcast.6, s32[3,8]{1,0:T(4,128)S(1)} %get-tuple-element.39.pattern_beyond, s32[1,1024]{1,0:T(1,128)S(1)} %get-tuple-element.46.slot_of_row, ...), custom_call_target="tpu_custom_call", output_to_operand_aliasing={{1}: (3, {})} | custom-call | tf_op jit(solution)/shard_map/block_first/pallas_call | solution.py:593
  51.1 20.4 %all_to_all.5.incoming = bf16[16,264,128]{2,1,0:T(8,128)(2,1)S(1)} all-to-all(bf16[16,264,128]{2,1,0:T(8,128)(2,1)S(1)} %get-tuple-element.55), channel_id=1, replica_groups=mesh['grp'=4,'half'=2,'seq'=4] {'grp','seq'}, dimensions={0} | all-to-all | bytes 2162688 | tf_op jit(solution)/shard_map/all_to_all | solution.py:627
  71.5 12.2 %block_second.1 = (bf16[512,512]{1,0:T(8,128)(2,1)}, f32[3,512]{1,0:T(4,128)}) custom-call(s32[3,8]{1,0:T(4,128)S(1)} %bitcast.7, f32[4,512]{1,0:T(4,128)S(1)} %copy-done.4, bf16[16,264,128]{2,1,0:T(8,128)(2,1)S(1)} %all_to_all.5.incoming, bf16[2,512,1536]{2,1,0:T(8,128)(2,1)} %w_qkv.1, bf16[2,512,512]{2,1,0:T(8,128)(2,1)S(1)} %copy-done.2, ...), custom_call_target="tpu_custom_call" | custom-call | tf_op jit(solution)/shard_map/block_second/pallas_call | solution.py:629
  (14 shorter events, 0.0 us)
Async XLA Ops:
  2.5 12.6 %collective-permute-start = (bf16[264,512]{1,0:T(8,128)(2,1)}, bf16[264,512]{1,0:T(8,128)(2,1)S(1)}, u32[]{:S(2)}, u32[]{:S(2)}) collective-permute-start(bf16[264,512]{1,0:T(8,128)(2,1)} %get-tuple-element.29.refs_0_), channel_id=1, source_target_pairs={{0,2},{1,3},{2,4},{3,5},{4,6},{5,7},{6,0},{7,1},{8,10},{9,11},{10,... | collective-permute-start | bytes 811016 | tf_op jit(solution)/shard_map/ppermute | solution.py:549
  5.6 9.6 %collective-permute-start.3 = (bf16[264,512]{1,0:T(8,128)(2,1)}, bf16[264,512]{1,0:T(8,128)(2,1)S(1)}, u32[]{:S(2)}, u32[]{:S(2)}) collective-permute-start(bf16[264,512]{1,0:T(8,128)(2,1)} %get-tuple-element.29.refs_0_), channel_id=1, source_target_pairs={{0,1},{1,0},{2,3},{3,2},{4,5},{5,4},{6,7},{7,6},{8,9},{9,8},{10,11... | collective-permute-start | bytes 811016 | tf_op jit(solution)/shard_map/ppermute | solution.py:546
  5.6 9.6 %collective-permute-start.4 = (bf16[256,512]{1,0:T(8,128)(2,1)}, bf16[256,512]{1,0:T(8,128)(2,1)S(1)}, u32[]{:S(2)}, u32[]{:S(2)}) collective-permute-start(bf16[256,512]{1,0:T(8,128)(2,1)} %get-tuple-element.32.refs_1_), channel_id=1, source_target_pairs={{0,1},{1,0},{2,3},{3,2},{4,5},{5,4},{6,7},{7,6},{8,9},{9,8},{10,11... | collective-permute-start | bytes 786440 | tf_op jit(solution)/shard_map/ppermute | solution.py:546
  6.1 13.9 %collective-permute-start.2 = (bf16[256,512]{1,0:T(8,128)(2,1)}, bf16[256,512]{1,0:T(8,128)(2,1)S(1)}, u32[]{:S(2)}, u32[]{:S(2)}) collective-permute-start(bf16[256,512]{1,0:T(8,128)(2,1)} %get-tuple-element.32.refs_1_), channel_id=1, source_target_pairs={{0,2},{1,3},{2,4},{3,5},{4,6},{5,7},{6,0},{7,1},{8,10},{9,11},{10,... | collective-permute-start | bytes 786440 | tf_op jit(solution)/shard_map/ppermute | solution.py:549
  7.7 1.9 %copy-start = (bf16[2,512,1536]{2,1,0:T(8,128)(2,1)S(1)}, bf16[2,512,1536]{2,1,0:T(8,128)(2,1)}, u32[]{:S(2)}) copy-start(bf16[2,512,1536]{2,1,0:T(8,128)(2,1)} %w_qkv.1) | copy-start | bytes 9437188
  9.6 1.2 %copy-start.1 = (bf16[2,512,512]{2,1,0:T(8,128)(2,1)S(1)}, bf16[2,512,512]{2,1,0:T(8,128)(2,1)}, u32[]{:S(2)}) copy-start(bf16[2,512,512]{2,1,0:T(8,128)(2,1)} %w_proj.1) | copy-start | bytes 3145732
  10.8 0.7 copy-start.4
  15.1 11.1 %collective-permute-start.7 = (bf16[264,512]{1,0:T(8,128)(2,1)S(1)}, bf16[264,512]{1,0:T(8,128)(2,1)S(1)}, u32[]{:S(2)}, u32[]{:S(2)}) collective-permute-start(bf16[264,512]{1,0:T(8,128)(2,1)S(1)} %collective-permute-done.refs_0_), channel_id=1, source_target_pairs={{0,1},{1,0},{2,3},{3,2},{4,5},{5,4},{6,7},{7,6},{8,9},{9,8},{10,11... | collective-permute-start | bytes 811016 | tf_op jit(solution)/shard_map/ppermute | solution.py:566
  15.2 11.1 %collective-permute-start.1 = (bf16[264,512]{1,0:T(8,128)(2,1)S(1)}, bf16[264,512]{1,0:T(8,128)(2,1)S(1)}, u32[]{:S(2)}, u32[]{:S(2)}) collective-permute-start(bf16[264,512]{1,0:T(8,128)(2,1)S(1)} %collective-permute-done.refs_0_), channel_id=1, source_target_pairs={{0,2},{1,3},{2,4},{3,5},{4,6},{5,7},{6,0},{7,1},{8,10},{9,11},{10,... | collective-permute-start | bytes 811016 | tf_op jit(solution)/shard_map/ppermute | solution.py:549
  15.2 1.0 %copy-start.9 = (bf16[264,512]{1,0:T(8,128)(2,1)S(1)}, bf16[264,512]{1,0:T(8,128)(2,1)}, u32[]{:S(2)}) copy-start(bf16[264,512]{1,0:T(8,128)(2,1)} %get-tuple-element.29.refs_0_) | copy-start | bytes 811012
  16.1 0.9 %copy-start.10 = (bf16[256,512]{1,0:T(8,128)(2,1)S(1)}, bf16[256,512]{1,0:T(8,128)(2,1)}, u32[]{:S(2)}) copy-start(bf16[256,512]{1,0:T(8,128)(2,1)} %get-tuple-element.32.refs_1_) | copy-start | bytes 786436
  20.0 6.2 %collective-permute-start.8 = (bf16[256,512]{1,0:T(8,128)(2,1)S(1)}, bf16[256,512]{1,0:T(8,128)(2,1)S(1)}, u32[]{:S(2)}, u32[]{:S(2)}) collective-permute-start(bf16[256,512]{1,0:T(8,128)(2,1)S(1)} %collective-permute-done.2.refs_1_), channel_id=1, source_target_pairs={{0,1},{1,0},{2,3},{3,2},{4,5},{5,4},{6,7},{7,6},{8,9},{9,8},{10,11... | collective-permute-start | bytes 786440 | tf_op jit(solution)/shard_map/ppermute | solution.py:566
  20.6 11.2 %collective-permute-start.6 = (bf16[256,512]{1,0:T(8,128)(2,1)S(1)}, bf16[256,512]{1,0:T(8,128)(2,1)S(1)}, u32[]{:S(2)}, u32[]{:S(2)}) collective-permute-start(bf16[256,512]{1,0:T(8,128)(2,1)S(1)} %collective-permute-done.2.refs_1_), channel_id=1, source_target_pairs={{0,2},{1,3},{2,4},{3,5},{4,6},{5,7},{6,0},{7,1},{8,10},{9,11},{10,... | collective-permute-start | bytes 786440 | tf_op jit(solution)/shard_map/ppermute | solution.py:549
  23.2 8.5 %copy-start.5 = (s32[512]{0:T(512)S(1)}, s32[512]{0:T(512)}, u32[]{:S(2)}) copy-start(s32[512]{0:T(512)} %param.13) | copy-start | bytes 6148
  26.2 11.3 %collective-permute-start.11 = (bf16[264,512]{1,0:T(8,128)(2,1)S(1)}, bf16[264,512]{1,0:T(8,128)(2,1)S(1)}, u32[]{:S(2)}, u32[]{:S(2)}) collective-permute-start(bf16[264,512]{1,0:T(8,128)(2,1)S(1)} %collective-permute-done.1.beyond.refs_0_.refs_2_), channel_id=1, source_target_pairs={{0,1},{1,0},{2,3},{3,2},{4,5},{5,4},{6,7},{7,6},{8,9},{9,8},{10,11... | collective-permute-start | bytes 811016 | tf_op jit(solution)/shard_map/ppermute | solution.py:566
  26.2 11.3 %collective-permute-start.5 = (bf16[264,512]{1,0:T(8,128)(2,1)S(1)}, bf16[264,512]{1,0:T(8,128)(2,1)S(1)}, u32[]{:S(2)}, u32[]{:S(2)}) collective-permute-start(bf16[264,512]{1,0:T(8,128)(2,1)S(1)} %collective-permute-done.1.beyond.refs_0_.refs_2_), channel_id=1, source_target_pairs={{0,2},{1,3},{2,4},{3,5},{4,6},{5,7},{6,0},{7,1},{8,10},{9,11},{10,... | collective-permute-start | bytes 811016 | tf_op jit(solution)/shard_map/ppermute | solution.py:549
  31.7 5.8 %collective-permute-start.12 = (bf16[256,512]{1,0:T(8,128)(2,1)S(1)}, bf16[256,512]{1,0:T(8,128)(2,1)S(1)}, u32[]{:S(2)}, u32[]{:S(2)}) collective-permute-start(bf16[256,512]{1,0:T(8,128)(2,1)S(1)} %collective-permute-done.6.refs_1_.refs_3_), channel_id=1, source_target_pairs={{0,1},{1,0},{2,3},{3,2},{4,5},{5,4},{6,7},{7,6},{8,9},{9,8},{10,11... | collective-permute-start | bytes 786440 | tf_op jit(solution)/shard_map/ppermute | solution.py:566
  31.7 11.1 %collective-permute-start.10 = (bf16[256,512]{1,0:T(8,128)(2,1)S(1)}, bf16[256,512]{1,0:T(8,128)(2,1)S(1)}, u32[]{:S(2)}, u32[]{:S(2)}) collective-permute-start(bf16[256,512]{1,0:T(8,128)(2,1)S(1)} %collective-permute-done.6.refs_1_.refs_3_), channel_id=1, source_target_pairs={{0,2},{1,3},{2,4},{3,5},{4,6},{5,7},{6,0},{7,1},{8,10},{9,11},{10,... | collective-permute-start | bytes 786440 | tf_op jit(solution)/shard_map/ppermute | solution.py:549
  37.5 5.4 %collective-permute-start.9 = (bf16[264,512]{1,0:T(8,128)(2,1)S(1)}, bf16[264,512]{1,0:T(8,128)(2,1)S(1)}, u32[]{:S(2)}, u32[]{:S(2)}) collective-permute-start(bf16[264,512]{1,0:T(8,128)(2,1)S(1)} %collective-permute-done.5.refs_0_), channel_id=1, source_target_pairs={{0,1},{1,0},{2,3},{3,2},{4,5},{5,4},{6,7},{7,6},{8,9},{9,8},{10,11... | collective-permute-start | bytes 811016 | tf_op jit(solution)/shard_map/ppermute | solution.py:566
  38.9 5.6 %copy-start.3 = (bf16[512,512]{1,0:T(8,128)(2,1)S(1)}, bf16[512,512]{1,0:T(8,128)(2,1)}, u32[]{:S(2)}) copy-start(bf16[512,512]{1,0:T(8,128)(2,1)} %points.3) | copy-start | bytes 1572868
  38.9 5.5 %copy-start.6 = (s32[8,3]{0,1:T(4,128)S(1)}, s32[8,3]{0,1:T(4,128)}, u32[]{:S(2)}) copy-start(s32[8,3]{0,1:T(4,128)} %param.11) | copy-start | bytes 292
  42.9 1.5 %collective-permute-start.13 = (bf16[256,512]{1,0:T(8,128)(2,1)S(1)}, bf16[256,512]{1,0:T(8,128)(2,1)S(1)}, u32[]{:S(2)}, u32[]{:S(2)}) collective-permute-start(bf16[256,512]{1,0:T(8,128)(2,1)S(1)} %collective-permute-done.10.refs_0_), channel_id=1, source_target_pairs={{0,1},{1,0},{2,3},{3,2},{4,5},{5,4},{6,7},{7,6},{8,9},{9,8},{10,11... | collective-permute-start | bytes 786440 | tf_op jit(solution)/shard_map/ppermute | solution.py:566
  44.2 27.3 %copy-start.2 = (bf16[2,512,512]{2,1,0:T(8,128)(2,1)S(1)}, bf16[2,512,512]{2,1,0:T(8,128)(2,1)}, u32[]{:S(2)}) copy-start(bf16[2,512,512]{2,1,0:T(8,128)(2,1)} %w_proj.1) | copy-start | bytes 3145732
  44.2 27.3 %copy-start.7 = (bf16[3,512]{1,0:T(4,128)(2,1)S(1)}, bf16[3,512]{1,0:T(4,128)(2,1)}, u32[]{:S(2)}) copy-start(bf16[3,512]{1,0:T(4,128)(2,1)} %w_head.1) | copy-start | bytes 9220
  44.2 27.3 %copy-start.8 = (s32[8,3]{0,1:T(4,128)S(1)}, s32[8,3]{0,1:T(4,128)}, u32[]{:S(2)}) copy-start(s32[8,3]{0,1:T(4,128)} %param.12) | copy-start | bytes 292

commit v17 on v16

--- a/solution.py
+++ b/solution.py
@@ -12,7 +12,7 @@
 HEADS_TOGETHER = 4
 GROUP = ("half", "seq")
 RING_PARTS = 2
-SEND_PARTS = 4
+SEND_PARTS = 2
 LANES = 128
 TAIL = 8
 DIGIT = 256
@@ -104,7 +104,7 @@
 def feed(first, gain, w_up, w_down):
     hidden = layer_norm(first, gain)
     total = first.astype(F32)
-    piece = 512
+    piece = 1024
     pieces = range(0, w_up.shape[1], piece)
     upper = jnp.dot(hidden, w_up[:, :piece], preferred_element_type=F32)
     for at in pieces:

time: 84.2 us -> 83.8 us (level)
  no operation moved by 1% of the time
where the time goes in v17:
time: 83.8 us; the launch traced here: 83.5 us
  Pallas kernels  30.9 us (37%)
  blocking collectives  20.4 us (24%)
  waiting for transfers between devices  18.4 us (22%)
  starting transfers between devices  7.08 us (8%)
  local copies, waits for them, and re-layouts  5.75 us (7%)
  between operations  0.99 us (1%)
    all_to_all x1, blocking collectives, shards(): lax.all_to_all(outgoing, ('grp', 'seq'), split_axis=0, concat_axis=0, til...  20.4 us
    ppermute x6, waiting for transfers between devices, shards(): column = [lax.ppermute(rows, GROUP, onward) for rows in column]  18.2 us
    pallas_call x1, Pallas kernels, shards(): pl.pallas_call(second_kernel, out_shape=(jax.ShapeDtypeStruct((rows_here,...  12.2 us
    pallas_call x6, Pallas kernels, project(): pl.pallas_call(functools.partial(project_kernel, first_rows, new, ask), o...  9.77 us
    pallas_call x1, Pallas kernels, shards(): pl.pallas_call(functools.partial(first_kernel, chips if ring else 0, late...  6.27 us
    ppermute x6, starting transfers between devices, shards(): column = [lax.ppermute(rows, GROUP, onward) for rows in column]  6.03 us
    unnamed x22, local copies, waits for them, and re-layouts  5.75 us
    pallas_call x1, Pallas kernels, shards(): pl.pallas_call(split_kernel, out_shape=[jax.ShapeDtypeStruct((rows, chann...  1.89 us
  transfers between devices with their start and end apart: 14, of which 6 were waited for; matrix products, arithmetic and copies ran while one was open for 0% of the time, Pallas kernels for 13%

profile of v17, /device:TPU:0, one launch (start us, length us, event | category | flops | bytes accessed | tf_op | source)
XLA Modules:
  0.0 83.5 jit_solution(3701520172817119443)
XLA Ops:
  0.6 1.9 %split.1 = (bf16[264,512]{1,0:T(8,128)(2,1)}, bf16[256,512]{1,0:T(8,128)(2,1)}) custom-call(bf16[512,512]{1,0:T(8,128)(2,1)} %points.3, s32[1,512]{1,0:T(1,128)} %bitcast.3, s32[3,8]{1,0:T(4,128)} %bitcast.5), custom_call_target="tpu_custom_call" | custom-call | tf_op jit(solution)/shard_map/split/pallas_call | solution.py:467
  2.5 3.1 %collective-permute-start = (bf16[264,512]{1,0:T(8,128)(2,1)}, bf16[264,512]{1,0:T(8,128)(2,1)S(1)}, u32[]{:S(2)}, u32[]{:S(2)}) collective-permute-start(bf16[264,512]{1,0:T(8,128)(2,1)} %get-tuple-element.29.refs_0_), channel_id=1, source_target_pairs={{0,2},{1,3},{2,4},{3,5},{4,6},{5,7},{6,0},{7,1},{8,10},{9,11},{10,... | collective-permute-start | bytes 811016 | tf_op jit(solution)/shard_map/ppermute | solution.py:549
  5.6 0.0 collective-permute-start.3
  5.6 0.5 collective-permute-start.4
  6.1 1.6 %collective-permute-start.2 = (bf16[256,512]{1,0:T(8,128)(2,1)}, bf16[256,512]{1,0:T(8,128)(2,1)S(1)}, u32[]{:S(2)}, u32[]{:S(2)}) collective-permute-start(bf16[256,512]{1,0:T(8,128)(2,1)} %get-tuple-element.32.refs_1_), channel_id=1, source_target_pairs={{0,2},{1,3},{2,4},{3,5},{4,6},{5,7},{6,0},{7,1},{8,10},{9,11},{10,... | collective-permute-start | bytes 786440 | tf_op jit(solution)/shard_map/ppermute | solution.py:549
  7.7 1.9 %copy-done = bf16[2,512,1536]{2,1,0:T(8,128)(2,1)S(1)} copy-done((bf16[2,512,1536]{2,1,0:T(8,128)(2,1)S(1)}, bf16[2,512,1536]{2,1,0:T(8,128)(2,1)}, u32[]{:S(2)}) %copy-start) | copy-done | bytes 3145752
  9.6 1.2 %copy-done.1 = bf16[2,512,512]{2,1,0:T(8,128)(2,1)S(1)} copy-done((bf16[2,512,512]{2,1,0:T(8,128)(2,1)S(1)}, bf16[2,512,512]{2,1,0:T(8,128)(2,1)}, u32[]{:S(2)}) %copy-start.1) | copy-done | bytes 1048600
  10.8 0.7 copy-done.4
  11.5 0.2 keep.1
  11.7 3.5 %collective-permute-done.refs_0_ = bf16[264,512]{1,0:T(8,128)(2,1)S(1)} collective-permute-done((bf16[264,512]{1,0:T(8,128)(2,1)}, bf16[264,512]{1,0:T(8,128)(2,1)S(1)}, u32[]{:S(2)}, u32[]{:S(2)}) %collective-permute-start) | collective-permute-done | bytes 270368 | tf_op jit(solution)/shard_map/ppermute | solution.py:549
  15.1 0.0 collective-permute-start.7
  15.2 0.0 collective-permute-start.1
  15.2 0.0 collective-permute-done.4.refs_3_
  15.2 0.0 collective-permute-done.3.refs_2_
  15.2 0.9 %copy-done.9 = bf16[264,512]{1,0:T(8,128)(2,1)S(1)} copy-done((bf16[264,512]{1,0:T(8,128)(2,1)S(1)}, bf16[264,512]{1,0:T(8,128)(2,1)}, u32[]{:S(2)}) %copy-start.9) | copy-done | bytes 270360
  16.2 0.9 %copy-done.10 = bf16[256,512]{1,0:T(8,128)(2,1)S(1)} copy-done((bf16[256,512]{1,0:T(8,128)(2,1)S(1)}, bf16[256,512]{1,0:T(8,128)(2,1)}, u32[]{:S(2)}) %copy-start.10) | copy-done | bytes 262168
  17.1 2.9 %project_own.1 = (bf16[4096,1024]{1,0:T(8,128)(2,1)S(1)}, bf16[512,512]{1,0:T(8,128)(2,1)S(1)}) custom-call(bf16[264,512]{1,0:T(8,128)(2,1)S(1)} %copy-done.9, bf16[256,512]{1,0:T(8,128)(2,1)S(1)} %copy-done.10, bf16[264,512]{1,0:T(8,128)(2,1)S(1)} %collective-permute-done.3.refs_2_, bf16[256,512]{1,0:T(8,128)(2,1)S(1)} %collective-permute-done.4.refs_3_, ...), custom_call_target="tpu_custom_call" | custom-call | flops 1073741824 | bytes 4718592 | tf_op jit(solution)/shard_map/project_own/pallas_call | solution.py:526
  20.0 0.0 collective-permute-done.2.refs_1_
  20.0 0.5 collective-permute-start.8
  20.6 1.3 %collective-permute-start.6 = (bf16[256,512]{1,0:T(8,128)(2,1)S(1)}, bf16[256,512]{1,0:T(8,128)(2,1)S(1)}, u32[]{:S(2)}, u32[]{:S(2)}) collective-permute-start(bf16[256,512]{1,0:T(8,128)(2,1)S(1)} %collective-permute-done.2.refs_1_), channel_id=1, source_target_pairs={{0,2},{1,3},{2,4},{3,5},{4,6},{5,7},{6,0},{7,1},{8,10},{9,11},{10,... | collective-permute-start | bytes 786440 | tf_op jit(solution)/shard_map/ppermute | solution.py:549
  21.9 1.3 %project.5.refs_4_ = bf16[4096,1024]{1,0:T(8,128)(2,1)S(1)} custom-call(bf16[264,512]{1,0:T(8,128)(2,1)S(1)} %collective-permute-done.refs_0_, bf16[256,512]{1,0:T(8,128)(2,1)S(1)} %collective-permute-done.2.refs_1_, f32[4,512]{1,0:T(4,128)S(1)} %get-tuple-element.33.refs_4_.refs_2_.gains, ...), custom_call_target="tpu_custom_call", output_to_operand_aliasing={{}: (4, {})} | custom-call | flops 536870912 | bytes 3145728 | tf_op jit(solution)/shard_map/project/pallas_call | solution.py:526
  23.2 0.0 copy-start.5
  23.2 3.0 %collective-permute-done.1.beyond.refs_0_.refs_2_ = bf16[264,512]{1,0:T(8,128)(2,1)S(1)} collective-permute-done((bf16[264,512]{1,0:T(8,128)(2,1)S(1)}, bf16[264,512]{1,0:T(8,128)(2,1)S(1)}, u32[]{:S(2)}, u32[]{:S(2)}) %collective-permute-start.1) | collective-permute-done | bytes 270368 | tf_op jit(solution)/shard_map/ppermute | solution.py:549
  26.2 0.0 collective-permute-start.11
  26.2 0.0 collective-permute-start.5
  26.2 0.0 collective-permute-done.8.refs_1_
  26.3 1.3 %project.6.refs_4_ = bf16[4096,1024]{1,0:T(8,128)(2,1)S(1)} custom-call(bf16[264,512]{1,0:T(8,128)(2,1)S(1)} %collective-permute-done.7.refs_0_, bf16[256,512]{1,0:T(8,128)(2,1)S(1)} %collective-permute-done.8.refs_1_, f32[4,512]{1,0:T(4,128)S(1)} %get-tuple-element.33.refs_4_.refs_2_.gains, ...), custom_call_target="tpu_custom_call", output_to_operand_aliasing={{}: (4, {})} | custom-call | flops 536870912 | bytes 3145728 | tf_op jit(solution)/shard_map/project/pallas_call | solution.py:526
  27.6 4.2 %collective-permute-done.6.refs_1_.refs_3_ = bf16[256,512]{1,0:T(8,128)(2,1)S(1)} collective-permute-done((bf16[256,512]{1,0:T(8,128)(2,1)S(1)}, bf16[256,512]{1,0:T(8,128)(2,1)S(1)}, u32[]{:S(2)}, u32[]{:S(2)}) %collective-permute-start.6) | collective-permute-done | bytes 262176 | tf_op jit(solution)/shard_map/ppermute | solution.py:549
  31.7 0.0 collective-permute-start.10
  31.7 0.6 index.1
  32.4 1.6 %project.7 = (bf16[4096,1024]{1,0:T(8,128)(2,1)S(1)}, bf16[512,512]{1,0:T(8,128)(2,1)S(1)}) custom-call(bf16[264,512]{1,0:T(8,128)(2,1)S(1)} %collective-permute-done.1.beyond.refs_0_.refs_2_, bf16[256,512]{1,0:T(8,128)(2,1)S(1)} %collective-permute-done.6.refs_1_.refs_3_, ...), custom_call_target="tpu_custom_call", output_to_operand_aliasing={{0}: (4, {})} | custom-call | flops 536870912 | bytes 3145728 | tf_op jit(solution)/shard_map/project/pallas_call | solution.py:526
  34.0 3.6 %collective-permute-done.5.refs_0_ = bf16[264,512]{1,0:T(8,128)(2,1)S(1)} collective-permute-done((bf16[264,512]{1,0:T(8,128)(2,1)S(1)}, bf16[264,512]{1,0:T(8,128)(2,1)S(1)}, u32[]{:S(2)}, u32[]{:S(2)}) %collective-permute-start.5) | collective-permute-done | bytes 270368 | tf_op jit(solution)/shard_map/ppermute | solution.py:549
  37.5 0.0 collective-permute-start.9
  37.5 0.0 collective-permute-done.12.refs_1_
  37.5 0.0 collective-permute-done.11.refs_0_
  37.5 1.3 %project.8.refs_4_ = bf16[4096,1024]{1,0:T(8,128)(2,1)S(1)} custom-call(bf16[264,512]{1,0:T(8,128)(2,1)S(1)} %collective-permute-done.11.refs_0_, bf16[256,512]{1,0:T(8,128)(2,1)S(1)} %collective-permute-done.12.refs_1_, f32[4,512]{1,0:T(4,128)S(1)} %get-tuple-element.33.refs_4_.refs_2_.gains, ...), custom_call_target="tpu_custom_call", output_to_operand_aliasing={{}: (4, {})} | custom-call | flops 536870912 | bytes 3145728 | tf_op jit(solution)/shard_map/project/pallas_call | solution.py:526
  38.9 0.0 copy-start.3
  38.9 0.0 copy-start.6
  38.9 4.0 %collective-permute-done.10.refs_0_ = bf16[256,512]{1,0:T(8,128)(2,1)S(1)} collective-permute-done((bf16[256,512]{1,0:T(8,128)(2,1)S(1)}, bf16[256,512]{1,0:T(8,128)(2,1)S(1)}, u32[]{:S(2)}, u32[]{:S(2)}) %collective-permute-start.10) | collective-permute-done | bytes 262176 | tf_op jit(solution)/shard_map/ppermute | solution.py:549
  42.9 0.0 collective-permute-start.13
  42.9 1.3 %project.9.kept_rows = bf16[4096,1024]{1,0:T(8,128)(2,1)S(1)} custom-call(bf16[264,512]{1,0:T(8,128)(2,1)S(1)} %collective-permute-done.5.refs_0_, bf16[264,512]{1,0:T(8,128)(2,1)S(1)} %collective-permute-done.9.refs_1_, f32[4,512]{1,0:T(4,128)S(1)} %get-tuple-element.33.refs_4_.refs_2_.gains, ...), custom_call_target="tpu_custom_call", output_to_operand_aliasing={{}: (4, {})} | custom-call | flops 536870912 | bytes 3145728 | tf_op jit(solution)/shard_map/project/pallas_call | solution.py:526
  44.2 0.0 copy-start.2
  44.2 0.0 copy-start.7
  44.2 0.0 copy-start.8
  44.2 0.2 collective-permute-done.13.refs_1_
  44.4 6.3 %block_first.1 = (bf16[16,264,128]{2,1,0:T(8,128)(2,1)S(1)}, bf16[4096,1024]{1,0:T(8,128)(2,1)S(1)}) custom-call(s32[3,8]{1,0:T(4,128)S(1)} %bitcast.6, s32[3,8]{1,0:T(4,128)S(1)} %get-tuple-element.39.pattern_beyond, s32[1,1024]{1,0:T(1,128)S(1)} %get-tuple-element.46.slot_of_row, ...), custom_call_target="tpu_custom_call", output_to_operand_aliasing={{1}: (3, {})} | custom-call | tf_op jit(solution)/shard_map/block_first/pallas_call | solution.py:593
  50.7 20.4 %all_to_all.5.incoming = bf16[16,264,128]{2,1,0:T(8,128)(2,1)S(1)} all-to-all(bf16[16,264,128]{2,1,0:T(8,128)(2,1)S(1)} %get-tuple-element.55), channel_id=1, replica_groups=mesh['grp'=4,'half'=2,'seq'=4] {'grp','seq'}, dimensions={0} | all-to-all | bytes 2162688 | tf_op jit(solution)/shard_map/all_to_all | solution.py:627
  71.1 12.2 %block_second.1 = (bf16[512,512]{1,0:T(8,128)(2,1)}, f32[3,512]{1,0:T(4,128)}) custom-call(s32[3,8]{1,0:T(4,128)S(1)} %bitcast.7, f32[4,512]{1,0:T(4,128)S(1)} %copy-done.4, bf16[16,264,128]{2,1,0:T(8,128)(2,1)S(1)} %all_to_all.5.incoming, bf16[2,512,1536]{2,1,0:T(8,128)(2,1)} %w_qkv.1, bf16[2,512,512]{2,1,0:T(8,128)(2,1)S(1)} %copy-done.2, ...), custom_call_target="tpu_custom_call" | custom-call | tf_op jit(solution)/shard_map/block_second/pallas_call | solution.py:629
  (14 shorter events, 0.0 us)
Async XLA Ops:
  2.5 12.6 %collective-permute-start = (bf16[264,512]{1,0:T(8,128)(2,1)}, bf16[264,512]{1,0:T(8,128)(2,1)S(1)}, u32[]{:S(2)}, u32[]{:S(2)}) collective-permute-start(bf16[264,512]{1,0:T(8,128)(2,1)} %get-tuple-element.29.refs_0_), channel_id=1, source_target_pairs={{0,2},{1,3},{2,4},{3,5},{4,6},{5,7},{6,0},{7,1},{8,10},{9,11},{10,... | collective-permute-start | bytes 811016 | tf_op jit(solution)/shard_map/ppermute | solution.py:549
  5.6 9.6 %collective-permute-start.3 = (bf16[264,512]{1,0:T(8,128)(2,1)}, bf16[264,512]{1,0:T(8,128)(2,1)S(1)}, u32[]{:S(2)}, u32[]{:S(2)}) collective-permute-start(bf16[264,512]{1,0:T(8,128)(2,1)} %get-tuple-element.29.refs_0_), channel_id=1, source_target_pairs={{0,1},{1,0},{2,3},{3,2},{4,5},{5,4},{6,7},{7,6},{8,9},{9,8},{10,11... | collective-permute-start | bytes 811016 | tf_op jit(solution)/shard_map/ppermute | solution.py:546
  5.6 9.6 %collective-permute-start.4 = (bf16[256,512]{1,0:T(8,128)(2,1)}, bf16[256,512]{1,0:T(8,128)(2,1)S(1)}, u32[]{:S(2)}, u32[]{:S(2)}) collective-permute-start(bf16[256,512]{1,0:T(8,128)(2,1)} %get-tuple-element.32.refs_1_), channel_id=1, source_target_pairs={{0,1},{1,0},{2,3},{3,2},{4,5},{5,4},{6,7},{7,6},{8,9},{9,8},{10,11... | collective-permute-start | bytes 786440 | tf_op jit(solution)/shard_map/ppermute | solution.py:546
  6.1 13.9 %collective-permute-start.2 = (bf16[256,512]{1,0:T(8,128)(2,1)}, bf16[256,512]{1,0:T(8,128)(2,1)S(1)}, u32[]{:S(2)}, u32[]{:S(2)}) collective-permute-start(bf16[256,512]{1,0:T(8,128)(2,1)} %get-tuple-element.32.refs_1_), channel_id=1, source_target_pairs={{0,2},{1,3},{2,4},{3,5},{4,6},{5,7},{6,0},{7,1},{8,10},{9,11},{10,... | collective-permute-start | bytes 786440 | tf_op jit(solution)/shard_map/ppermute | solution.py:549
  7.7 1.9 %copy-start = (bf16[2,512,1536]{2,1,0:T(8,128)(2,1)S(1)}, bf16[2,512,1536]{2,1,0:T(8,128)(2,1)}, u32[]{:S(2)}) copy-start(bf16[2,512,1536]{2,1,0:T(8,128)(2,1)} %w_qkv.1) | copy-start | bytes 9437188
  9.6 1.2 %copy-start.1 = (bf16[2,512,512]{2,1,0:T(8,128)(2,1)S(1)}, bf16[2,512,512]{2,1,0:T(8,128)(2,1)}, u32[]{:S(2)}) copy-start(bf16[2,512,512]{2,1,0:T(8,128)(2,1)} %w_proj.1) | copy-start | bytes 3145732
  10.8 0.7 copy-start.4
  15.1 11.1 %collective-permute-start.7 = (bf16[264,512]{1,0:T(8,128)(2,1)S(1)}, bf16[264,512]{1,0:T(8,128)(2,1)S(1)}, u32[]{:S(2)}, u32[]{:S(2)}) collective-permute-start(bf16[264,512]{1,0:T(8,128)(2,1)S(1)} %collective-permute-done.refs_0_), channel_id=1, source_target_pairs={{0,1},{1,0},{2,3},{3,2},{4,5},{5,4},{6,7},{7,6},{8,9},{9,8},{10,11... | collective-permute-start | bytes 811016 | tf_op jit(solution)/shard_map/ppermute | solution.py:566
  15.2 11.1 %collective-permute-start.1 = (bf16[264,512]{1,0:T(8,128)(2,1)S(1)}, bf16[264,512]{1,0:T(8,128)(2,1)S(1)}, u32[]{:S(2)}, u32[]{:S(2)}) collective-permute-start(bf16[264,512]{1,0:T(8,128)(2,1)S(1)} %collective-permute-done.refs_0_), channel_id=1, source_target_pairs={{0,2},{1,3},{2,4},{3,5},{4,6},{5,7},{6,0},{7,1},{8,10},{9,11},{10,... | collective-permute-start | bytes 811016 | tf_op jit(solution)/shard_map/ppermute | solution.py:549
  15.2 1.0 %copy-start.9 = (bf16[264,512]{1,0:T(8,128)(2,1)S(1)}, bf16[264,512]{1,0:T(8,128)(2,1)}, u32[]{:S(2)}) copy-start(bf16[264,512]{1,0:T(8,128)(2,1)} %get-tuple-element.29.refs_0_) | copy-start | bytes 811012
  16.1 0.9 %copy-start.10 = (bf16[256,512]{1,0:T(8,128)(2,1)S(1)}, bf16[256,512]{1,0:T(8,128)(2,1)}, u32[]{:S(2)}) copy-start(bf16[256,512]{1,0:T(8,128)(2,1)} %get-tuple-element.32.refs_1_) | copy-start | bytes 786436
  20.0 6.2 %collective-permute-start.8 = (bf16[256,512]{1,0:T(8,128)(2,1)S(1)}, bf16[256,512]{1,0:T(8,128)(2,1)S(1)}, u32[]{:S(2)}, u32[]{:S(2)}) collective-permute-start(bf16[256,512]{1,0:T(8,128)(2,1)S(1)} %collective-permute-done.2.refs_1_), channel_id=1, source_target_pairs={{0,1},{1,0},{2,3},{3,2},{4,5},{5,4},{6,7},{7,6},{8,9},{9,8},{10,11... | collective-permute-start | bytes 786440 | tf_op jit(solution)/shard_map/ppermute | solution.py:566
  20.6 11.2 %collective-permute-start.6 = (bf16[256,512]{1,0:T(8,128)(2,1)S(1)}, bf16[256,512]{1,0:T(8,128)(2,1)S(1)}, u32[]{:S(2)}, u32[]{:S(2)}) collective-permute-start(bf16[256,512]{1,0:T(8,128)(2,1)S(1)} %collective-permute-done.2.refs_1_), channel_id=1, source_target_pairs={{0,2},{1,3},{2,4},{3,5},{4,6},{5,7},{6,0},{7,1},{8,10},{9,11},{10,... | collective-permute-start | bytes 786440 | tf_op jit(solution)/shard_map/ppermute | solution.py:549
  23.2 8.5 %copy-start.5 = (s32[512]{0:T(512)S(1)}, s32[512]{0:T(512)}, u32[]{:S(2)}) copy-start(s32[512]{0:T(512)} %param.13) | copy-start | bytes 6148
  26.2 11.3 %collective-permute-start.11 = (bf16[264,512]{1,0:T(8,128)(2,1)S(1)}, bf16[264,512]{1,0:T(8,128)(2,1)S(1)}, u32[]{:S(2)}, u32[]{:S(2)}) collective-permute-start(bf16[264,512]{1,0:T(8,128)(2,1)S(1)} %collective-permute-done.1.beyond.refs_0_.refs_2_), channel_id=1, source_target_pairs={{0,1},{1,0},{2,3},{3,2},{4,5},{5,4},{6,7},{7,6},{8,9},{9,8},{10,11... | collective-permute-start | bytes 811016 | tf_op jit(solution)/shard_map/ppermute | solution.py:566
  26.2 11.3 %collective-permute-start.5 = (bf16[264,512]{1,0:T(8,128)(2,1)S(1)}, bf16[264,512]{1,0:T(8,128)(2,1)S(1)}, u32[]{:S(2)}, u32[]{:S(2)}) collective-permute-start(bf16[264,512]{1,0:T(8,128)(2,1)S(1)} %collective-permute-done.1.beyond.refs_0_.refs_2_), channel_id=1, source_target_pairs={{0,2},{1,3},{2,4},{3,5},{4,6},{5,7},{6,0},{7,1},{8,10},{9,11},{10,... | collective-permute-start | bytes 811016 | tf_op jit(solution)/shard_map/ppermute | solution.py:549
  31.7 5.8 %collective-permute-start.12 = (bf16[256,512]{1,0:T(8,128)(2,1)S(1)}, bf16[256,512]{1,0:T(8,128)(2,1)S(1)}, u32[]{:S(2)}, u32[]{:S(2)}) collective-permute-start(bf16[256,512]{1,0:T(8,128)(2,1)S(1)} %collective-permute-done.6.refs_1_.refs_3_), channel_id=1, source_target_pairs={{0,1},{1,0},{2,3},{3,2},{4,5},{5,4},{6,7},{7,6},{8,9},{9,8},{10,11... | collective-permute-start | bytes 786440 | tf_op jit(solution)/shard_map/ppermute | solution.py:566
  31.7 11.1 %collective-permute-start.10 = (bf16[256,512]{1,0:T(8,128)(2,1)S(1)}, bf16[256,512]{1,0:T(8,128)(2,1)S(1)}, u32[]{:S(2)}, u32[]{:S(2)}) collective-permute-start(bf16[256,512]{1,0:T(8,128)(2,1)S(1)} %collective-permute-done.6.refs_1_.refs_3_), channel_id=1, source_target_pairs={{0,2},{1,3},{2,4},{3,5},{4,6},{5,7},{6,0},{7,1},{8,10},{9,11},{10,... | collective-permute-start | bytes 786440 | tf_op jit(solution)/shard_map/ppermute | solution.py:549
  37.5 5.4 %collective-permute-start.9 = (bf16[264,512]{1,0:T(8,128)(2,1)S(1)}, bf16[264,512]{1,0:T(8,128)(2,1)S(1)}, u32[]{:S(2)}, u32[]{:S(2)}) collective-permute-start(bf16[264,512]{1,0:T(8,128)(2,1)S(1)} %collective-permute-done.5.refs_0_), channel_id=1, source_target_pairs={{0,1},{1,0},{2,3},{3,2},{4,5},{5,4},{6,7},{7,6},{8,9},{9,8},{10,11... | collective-permute-start | bytes 811016 | tf_op jit(solution)/shard_map/ppermute | solution.py:566
  38.9 5.6 %copy-start.3 = (bf16[512,512]{1,0:T(8,128)(2,1)S(1)}, bf16[512,512]{1,0:T(8,128)(2,1)}, u32[]{:S(2)}) copy-start(bf16[512,512]{1,0:T(8,128)(2,1)} %points.3) | copy-start | bytes 1572868
  38.9 5.5 %copy-start.6 = (s32[8,3]{0,1:T(4,128)S(1)}, s32[8,3]{0,1:T(4,128)}, u32[]{:S(2)}) copy-start(s32[8,3]{0,1:T(4,128)} %param.11) | copy-start | bytes 292
  42.9 1.5 %collective-permute-start.13 = (bf16[256,512]{1,0:T(8,128)(2,1)S(1)}, bf16[256,512]{1,0:T(8,128)(2,1)S(1)}, u32[]{:S(2)}, u32[]{:S(2)}) collective-permute-start(bf16[256,512]{1,0:T(8,128)(2,1)S(1)} %collective-permute-done.10.refs_0_), channel_id=1, source_target_pairs={{0,1},{1,0},{2,3},{3,2},{4,5},{5,4},{6,7},{7,6},{8,9},{9,8},{10,11... | collective-permute-start | bytes 786440 | tf_op jit(solution)/shard_map/ppermute | solution.py:566
  44.2 26.9 %copy-start.2 = (bf16[2,512,512]{2,1,0:T(8,128)(2,1)S(1)}, bf16[2,512,512]{2,1,0:T(8,128)(2,1)}, u32[]{:S(2)}) copy-start(bf16[2,512,512]{2,1,0:T(8,128)(2,1)} %w_proj.1) | copy-start | bytes 3145732
  44.2 26.9 %copy-start.7 = (bf16[3,512]{1,0:T(4,128)(2,1)S(1)}, bf16[3,512]{1,0:T(4,128)(2,1)}, u32[]{:S(2)}) copy-start(bf16[3,512]{1,0:T(4,128)(2,1)} %w_head.1) | copy-start | bytes 9220
  44.2 26.9 %copy-start.8 = (s32[8,3]{0,1:T(4,128)S(1)}, s32[8,3]{0,1:T(4,128)}, u32[]{:S(2)}) copy-start(s32[8,3]{0,1:T(4,128)} %param.12) | copy-start | bytes 292

commit v18 on v17

--- a/solution.py
+++ b/solution.py
@@ -12,7 +12,7 @@
 HEADS_TOGETHER = 4
 GROUP = ("half", "seq")
 RING_PARTS = 2
-SEND_PARTS = 2
+SEND_PARTS = 1
 LANES = 128
 TAIL = 8
 DIGIT = 256
@@ -397,14 +397,10 @@
         pieces.append(code)
     places = jnp.concatenate(pieces, axis=1).astype(jnp.int32) - 1
     place = one_hot_rows(places, rows)
-    sides = []
-    for at in range(0, len(landing), 2):
-        for copy in landing[at : at + 2]:
-            copy.wait()
-        moved = incoming_held[:, :, at * LANES : (at + 2) * LANES]
-        moved = moved.reshape(devices * capacity, 2 * LANES)
-        sides.append(jnp.dot(place, moved, preferred_element_type=F32).astype(BF16))
-    first = jnp.concatenate(sides, axis=1)
+    for copy in landing:
+        copy.wait()
+    moved = incoming_held[...].reshape(devices * capacity, channels)
+    first = jnp.dot(place, moved, preferred_element_type=F32).astype(BF16)
     for copy in copies[:2]:
         copy.wait()
     second = feed(first, gains_held[1:2, :], first_up_held, first_down_held)

time: 83.8 us -> 83.7 us (level)
  no operation moved by 1% of the time
where the time goes in v18:
time: 83.7 us; the launch traced here: 83.3 us
  Pallas kernels  30.8 us (37%)
  blocking collectives  20.4 us (24%)
  waiting for transfers between devices  18.4 us (22%)
  starting transfers between devices  7.08 us (8%)
  local copies, waits for them, and re-layouts  5.75 us (7%)
  between operations  0.99 us (1%)
    all_to_all x1, blocking collectives, shards(): lax.all_to_all(outgoing, ('grp', 'seq'), split_axis=0, concat_axis=0, til...  20.4 us
    ppermute x6, waiting for transfers between devices, shards(): column = [lax.ppermute(rows, GROUP, onward) for rows in column]  18.2 us
    pallas_call x1, Pallas kernels, shards(): pl.pallas_call(second_kernel, out_shape=(jax.ShapeDtypeStruct((rows_here,...  12.2 us
    pallas_call x6, Pallas kernels, project(): pl.pallas_call(functools.partial(project_kernel, first_rows, new, ask), o...  9.77 us
    pallas_call x1, Pallas kernels, shards(): pl.pallas_call(functools.partial(first_kernel, chips if ring else 0, late...  6.15 us
    ppermute x6, starting transfers between devices, shards(): column = [lax.ppermute(rows, GROUP, onward) for rows in column]  6.03 us
    unnamed x22, local copies, waits for them, and re-layouts  5.75 us
    pallas_call x1, Pallas kernels, shards(): pl.pallas_call(split_kernel, out_shape=[jax.ShapeDtypeStruct((rows, chann...  1.89 us
  transfers between devices with their start and end apart: 14, of which 6 were waited for; matrix products, arithmetic and copies ran while one was open for 0% of the time, Pallas kernels for 13%

profile of v18, /device:TPU:0, one launch (start us, length us, event | category | flops | bytes accessed | tf_op | source)
XLA Modules:
  0.0 83.3 jit_solution(11635827668306316385)
XLA Ops:
  0.6 1.9 %split.1 = (bf16[264,512]{1,0:T(8,128)(2,1)}, bf16[256,512]{1,0:T(8,128)(2,1)}) custom-call(bf16[512,512]{1,0:T(8,128)(2,1)} %points.3, s32[1,512]{1,0:T(1,128)} %bitcast.3, s32[3,8]{1,0:T(4,128)} %bitcast.5), custom_call_target="tpu_custom_call" | custom-call | tf_op jit(solution)/shard_map/split/pallas_call | solution.py:463
  2.5 3.1 %collective-permute-start = (bf16[264,512]{1,0:T(8,128)(2,1)}, bf16[264,512]{1,0:T(8,128)(2,1)S(1)}, u32[]{:S(2)}, u32[]{:S(2)}) collective-permute-start(bf16[264,512]{1,0:T(8,128)(2,1)} %get-tuple-element.29.refs_0_), channel_id=1, source_target_pairs={{0,2},{1,3},{2,4},{3,5},{4,6},{5,7},{6,0},{7,1},{8,10},{9,11},{10,... | collective-permute-start | bytes 811016 | tf_op jit(solution)/shard_map/ppermute | solution.py:545
  5.6 0.0 collective-permute-start.3
  5.6 0.5 collective-permute-start.4
  6.1 1.6 %collective-permute-start.2 = (bf16[256,512]{1,0:T(8,128)(2,1)}, bf16[256,512]{1,0:T(8,128)(2,1)S(1)}, u32[]{:S(2)}, u32[]{:S(2)}) collective-permute-start(bf16[256,512]{1,0:T(8,128)(2,1)} %get-tuple-element.32.refs_1_), channel_id=1, source_target_pairs={{0,2},{1,3},{2,4},{3,5},{4,6},{5,7},{6,0},{7,1},{8,10},{9,11},{10,... | collective-permute-start | bytes 786440 | tf_op jit(solution)/shard_map/ppermute | solution.py:545
  7.7 1.9 %copy-done = bf16[2,512,1536]{2,1,0:T(8,128)(2,1)S(1)} copy-done((bf16[2,512,1536]{2,1,0:T(8,128)(2,1)S(1)}, bf16[2,512,1536]{2,1,0:T(8,128)(2,1)}, u32[]{:S(2)}) %copy-start) | copy-done | bytes 3145752
  9.6 1.2 %copy-done.1 = bf16[2,512,512]{2,1,0:T(8,128)(2,1)S(1)} copy-done((bf16[2,512,512]{2,1,0:T(8,128)(2,1)S(1)}, bf16[2,512,512]{2,1,0:T(8,128)(2,1)}, u32[]{:S(2)}) %copy-start.1) | copy-done | bytes 1048600
  10.8 0.7 copy-done.4
  11.5 0.2 keep.1
  11.7 3.5 %collective-permute-done.refs_0_ = bf16[264,512]{1,0:T(8,128)(2,1)S(1)} collective-permute-done((bf16[264,512]{1,0:T(8,128)(2,1)}, bf16[264,512]{1,0:T(8,128)(2,1)S(1)}, u32[]{:S(2)}, u32[]{:S(2)}) %collective-permute-start) | collective-permute-done | bytes 270368 | tf_op jit(solution)/shard_map/ppermute | solution.py:545
  15.1 0.0 collective-permute-start.7
  15.2 0.0 collective-permute-start.1
  15.2 0.0 collective-permute-done.4.refs_3_
  15.2 0.0 collective-permute-done.3.refs_2_
  15.2 0.9 %copy-done.9 = bf16[264,512]{1,0:T(8,128)(2,1)S(1)} copy-done((bf16[264,512]{1,0:T(8,128)(2,1)S(1)}, bf16[264,512]{1,0:T(8,128)(2,1)}, u32[]{:S(2)}) %copy-start.9) | copy-done | bytes 270360
  16.2 0.9 %copy-done.10 = bf16[256,512]{1,0:T(8,128)(2,1)S(1)} copy-done((bf16[256,512]{1,0:T(8,128)(2,1)S(1)}, bf16[256,512]{1,0:T(8,128)(2,1)}, u32[]{:S(2)}) %copy-start.10) | copy-done | bytes 262168
  17.1 2.9 %project_own.1 = (bf16[4096,1024]{1,0:T(8,128)(2,1)S(1)}, bf16[512,512]{1,0:T(8,128)(2,1)S(1)}) custom-call(bf16[264,512]{1,0:T(8,128)(2,1)S(1)} %copy-done.9, bf16[256,512]{1,0:T(8,128)(2,1)S(1)} %copy-done.10, bf16[264,512]{1,0:T(8,128)(2,1)S(1)} %collective-permute-done.3.refs_2_, bf16[256,512]{1,0:T(8,128)(2,1)S(1)} %collective-permute-done.4.refs_3_, ...), custom_call_target="tpu_custom_call" | custom-call | flops 1073741824 | bytes 4718592 | tf_op jit(solution)/shard_map/project_own/pallas_call | solution.py:522
  20.0 0.0 collective-permute-done.2.refs_1_
  20.0 0.5 collective-permute-start.8
  20.6 1.3 %collective-permute-start.6 = (bf16[256,512]{1,0:T(8,128)(2,1)S(1)}, bf16[256,512]{1,0:T(8,128)(2,1)S(1)}, u32[]{:S(2)}, u32[]{:S(2)}) collective-permute-start(bf16[256,512]{1,0:T(8,128)(2,1)S(1)} %collective-permute-done.2.refs_1_), channel_id=1, source_target_pairs={{0,2},{1,3},{2,4},{3,5},{4,6},{5,7},{6,0},{7,1},{8,10},{9,11},{10,... | collective-permute-start | bytes 786440 | tf_op jit(solution)/shard_map/ppermute | solution.py:545
  21.9 1.3 %project.5.refs_4_ = bf16[4096,1024]{1,0:T(8,128)(2,1)S(1)} custom-call(bf16[264,512]{1,0:T(8,128)(2,1)S(1)} %collective-permute-done.refs_0_, bf16[256,512]{1,0:T(8,128)(2,1)S(1)} %collective-permute-done.2.refs_1_, f32[4,512]{1,0:T(4,128)S(1)} %get-tuple-element.33.refs_4_.refs_2_.gains, ...), custom_call_target="tpu_custom_call", output_to_operand_aliasing={{}: (4, {})} | custom-call | flops 536870912 | bytes 3145728 | tf_op jit(solution)/shard_map/project/pallas_call | solution.py:522
  23.2 0.0 copy-start.5
  23.2 3.0 %collective-permute-done.1.beyond.refs_0_.refs_2_ = bf16[264,512]{1,0:T(8,128)(2,1)S(1)} collective-permute-done((bf16[264,512]{1,0:T(8,128)(2,1)S(1)}, bf16[264,512]{1,0:T(8,128)(2,1)S(1)}, u32[]{:S(2)}, u32[]{:S(2)}) %collective-permute-start.1) | collective-permute-done | bytes 270368 | tf_op jit(solution)/shard_map/ppermute | solution.py:545
  26.2 0.0 collective-permute-start.11
  26.2 0.0 collective-permute-start.5
  26.2 0.0 collective-permute-done.8.refs_1_
  26.3 1.3 %project.6.refs_4_ = bf16[4096,1024]{1,0:T(8,128)(2,1)S(1)} custom-call(bf16[264,512]{1,0:T(8,128)(2,1)S(1)} %collective-permute-done.7.refs_0_, bf16[256,512]{1,0:T(8,128)(2,1)S(1)} %collective-permute-done.8.refs_1_, f32[4,512]{1,0:T(4,128)S(1)} %get-tuple-element.33.refs_4_.refs_2_.gains, ...), custom_call_target="tpu_custom_call", output_to_operand_aliasing={{}: (4, {})} | custom-call | flops 536870912 | bytes 3145728 | tf_op jit(solution)/shard_map/project/pallas_call | solution.py:522
  27.6 4.2 %collective-permute-done.6.refs_1_.refs_3_ = bf16[256,512]{1,0:T(8,128)(2,1)S(1)} collective-permute-done((bf16[256,512]{1,0:T(8,128)(2,1)S(1)}, bf16[256,512]{1,0:T(8,128)(2,1)S(1)}, u32[]{:S(2)}, u32[]{:S(2)}) %collective-permute-start.6) | collective-permute-done | bytes 262176 | tf_op jit(solution)/shard_map/ppermute | solution.py:545
  31.7 0.0 collective-permute-start.10
  31.7 0.6 index.1
  32.4 1.6 %project.7 = (bf16[4096,1024]{1,0:T(8,128)(2,1)S(1)}, bf16[512,512]{1,0:T(8,128)(2,1)S(1)}) custom-call(bf16[264,512]{1,0:T(8,128)(2,1)S(1)} %collective-permute-done.1.beyond.refs_0_.refs_2_, bf16[256,512]{1,0:T(8,128)(2,1)S(1)} %collective-permute-done.6.refs_1_.refs_3_, ...), custom_call_target="tpu_custom_call", output_to_operand_aliasing={{0}: (4, {})} | custom-call | flops 536870912 | bytes 3145728 | tf_op jit(solution)/shard_map/project/pallas_call | solution.py:522
  34.0 3.6 %collective-permute-done.5.refs_0_ = bf16[264,512]{1,0:T(8,128)(2,1)S(1)} collective-permute-done((bf16[264,512]{1,0:T(8,128)(2,1)S(1)}, bf16[264,512]{1,0:T(8,128)(2,1)S(1)}, u32[]{:S(2)}, u32[]{:S(2)}) %collective-permute-start.5) | collective-permute-done | bytes 270368 | tf_op jit(solution)/shard_map/ppermute | solution.py:545
  37.5 0.0 collective-permute-start.9
  37.5 0.0 collective-permute-done.12.refs_1_
  37.5 0.0 collective-permute-done.11.refs_0_
  37.5 1.3 %project.8.refs_4_ = bf16[4096,1024]{1,0:T(8,128)(2,1)S(1)} custom-call(bf16[264,512]{1,0:T(8,128)(2,1)S(1)} %collective-permute-done.11.refs_0_, bf16[256,512]{1,0:T(8,128)(2,1)S(1)} %collective-permute-done.12.refs_1_, f32[4,512]{1,0:T(4,128)S(1)} %get-tuple-element.33.refs_4_.refs_2_.gains, ...), custom_call_target="tpu_custom_call", output_to_operand_aliasing={{}: (4, {})} | custom-call | flops 536870912 | bytes 3145728 | tf_op jit(solution)/shard_map/project/pallas_call | solution.py:522
  38.9 0.0 copy-start.3
  38.9 0.0 copy-start.6
  38.9 4.0 %collective-permute-done.10.refs_0_ = bf16[256,512]{1,0:T(8,128)(2,1)S(1)} collective-permute-done((bf16[256,512]{1,0:T(8,128)(2,1)S(1)}, bf16[256,512]{1,0:T(8,128)(2,1)S(1)}, u32[]{:S(2)}, u32[]{:S(2)}) %collective-permute-start.10) | collective-permute-done | bytes 262176 | tf_op jit(solution)/shard_map/ppermute | solution.py:545
  42.9 0.0 collective-permute-start.13
  42.9 1.3 %project.9.kept_rows = bf16[4096,1024]{1,0:T(8,128)(2,1)S(1)} custom-call(bf16[264,512]{1,0:T(8,128)(2,1)S(1)} %collective-permute-done.5.refs_0_, bf16[264,512]{1,0:T(8,128)(2,1)S(1)} %collective-permute-done.9.refs_1_, f32[4,512]{1,0:T(4,128)S(1)} %get-tuple-element.33.refs_4_.refs_2_.gains, ...), custom_call_target="tpu_custom_call", output_to_operand_aliasing={{}: (4, {})} | custom-call | flops 536870912 | bytes 3145728 | tf_op jit(solution)/shard_map/project/pallas_call | solution.py:522
  44.2 0.0 copy-start.2
  44.2 0.0 copy-start.7
  44.2 0.0 copy-start.8
  44.2 0.2 collective-permute-done.13.refs_1_
  44.4 6.1 %block_first.1 = (bf16[16,264,128]{2,1,0:T(8,128)(2,1)S(1)}, bf16[4096,1024]{1,0:T(8,128)(2,1)S(1)}) custom-call(s32[3,8]{1,0:T(4,128)S(1)} %bitcast.6, s32[3,8]{1,0:T(4,128)S(1)} %get-tuple-element.39.pattern_beyond, s32[1,1024]{1,0:T(1,128)S(1)} %get-tuple-element.46.slot_of_row, ...), custom_call_target="tpu_custom_call", output_to_operand_aliasing={{1}: (3, {})} | custom-call | tf_op jit(solution)/shard_map/block_first/pallas_call | solution.py:589
  50.6 20.4 %all_to_all.5.incoming = bf16[16,264,128]{2,1,0:T(8,128)(2,1)S(1)} all-to-all(bf16[16,264,128]{2,1,0:T(8,128)(2,1)S(1)} %get-tuple-element.55), channel_id=1, replica_groups=mesh['grp'=4,'half'=2,'seq'=4] {'grp','seq'}, dimensions={0} | all-to-all | bytes 2162688 | tf_op jit(solution)/shard_map/all_to_all | solution.py:623
  71.0 12.2 %block_second.1 = (bf16[512,512]{1,0:T(8,128)(2,1)}, f32[3,512]{1,0:T(4,128)}) custom-call(s32[3,8]{1,0:T(4,128)S(1)} %bitcast.7, f32[4,512]{1,0:T(4,128)S(1)} %copy-done.4, bf16[16,264,128]{2,1,0:T(8,128)(2,1)S(1)} %all_to_all.5.incoming, bf16[2,512,1536]{2,1,0:T(8,128)(2,1)} %w_qkv.1, bf16[2,512,512]{2,1,0:T(8,128)(2,1)S(1)} %copy-done.2, ...), custom_call_target="tpu_custom_call" | custom-call | tf_op jit(solution)/shard_map/block_second/pallas_call | solution.py:625
  (14 shorter events, 0.0 us)
Async XLA Ops:
  2.5 12.6 %collective-permute-start = (bf16[264,512]{1,0:T(8,128)(2,1)}, bf16[264,512]{1,0:T(8,128)(2,1)S(1)}, u32[]{:S(2)}, u32[]{:S(2)}) collective-permute-start(bf16[264,512]{1,0:T(8,128)(2,1)} %get-tuple-element.29.refs_0_), channel_id=1, source_target_pairs={{0,2},{1,3},{2,4},{3,5},{4,6},{5,7},{6,0},{7,1},{8,10},{9,11},{10,... | collective-permute-start | bytes 811016 | tf_op jit(solution)/shard_map/ppermute | solution.py:545
  5.6 9.6 %collective-permute-start.3 = (bf16[264,512]{1,0:T(8,128)(2,1)}, bf16[264,512]{1,0:T(8,128)(2,1)S(1)}, u32[]{:S(2)}, u32[]{:S(2)}) collective-permute-start(bf16[264,512]{1,0:T(8,128)(2,1)} %get-tuple-element.29.refs_0_), channel_id=1, source_target_pairs={{0,1},{1,0},{2,3},{3,2},{4,5},{5,4},{6,7},{7,6},{8,9},{9,8},{10,11... | collective-permute-start | bytes 811016 | tf_op jit(solution)/shard_map/ppermute | solution.py:542
  5.6 9.6 %collective-permute-start.4 = (bf16[256,512]{1,0:T(8,128)(2,1)}, bf16[256,512]{1,0:T(8,128)(2,1)S(1)}, u32[]{:S(2)}, u32[]{:S(2)}) collective-permute-start(bf16[256,512]{1,0:T(8,128)(2,1)} %get-tuple-element.32.refs_1_), channel_id=1, source_target_pairs={{0,1},{1,0},{2,3},{3,2},{4,5},{5,4},{6,7},{7,6},{8,9},{9,8},{10,11... | collective-permute-start | bytes 786440 | tf_op jit(solution)/shard_map/ppermute | solution.py:542
  6.1 13.9 %collective-permute-start.2 = (bf16[256,512]{1,0:T(8,128)(2,1)}, bf16[256,512]{1,0:T(8,128)(2,1)S(1)}, u32[]{:S(2)}, u32[]{:S(2)}) collective-permute-start(bf16[256,512]{1,0:T(8,128)(2,1)} %get-tuple-element.32.refs_1_), channel_id=1, source_target_pairs={{0,2},{1,3},{2,4},{3,5},{4,6},{5,7},{6,0},{7,1},{8,10},{9,11},{10,... | collective-permute-start | bytes 786440 | tf_op jit(solution)/shard_map/ppermute | solution.py:545
  7.7 1.9 %copy-start = (bf16[2,512,1536]{2,1,0:T(8,128)(2,1)S(1)}, bf16[2,512,1536]{2,1,0:T(8,128)(2,1)}, u32[]{:S(2)}) copy-start(bf16[2,512,1536]{2,1,0:T(8,128)(2,1)} %w_qkv.1) | copy-start | bytes 9437188
  9.6 1.2 %copy-start.1 = (bf16[2,512,512]{2,1,0:T(8,128)(2,1)S(1)}, bf16[2,512,512]{2,1,0:T(8,128)(2,1)}, u32[]{:S(2)}) copy-start(bf16[2,512,512]{2,1,0:T(8,128)(2,1)} %w_proj.1) | copy-start | bytes 3145732
  10.8 0.7 copy-start.4
  15.1 11.1 %collective-permute-start.7 = (bf16[264,512]{1,0:T(8,128)(2,1)S(1)}, bf16[264,512]{1,0:T(8,128)(2,1)S(1)}, u32[]{:S(2)}, u32[]{:S(2)}) collective-permute-start(bf16[264,512]{1,0:T(8,128)(2,1)S(1)} %collective-permute-done.refs_0_), channel_id=1, source_target_pairs={{0,1},{1,0},{2,3},{3,2},{4,5},{5,4},{6,7},{7,6},{8,9},{9,8},{10,11... | collective-permute-start | bytes 811016 | tf_op jit(solution)/shard_map/ppermute | solution.py:562
  15.2 11.1 %collective-permute-start.1 = (bf16[264,512]{1,0:T(8,128)(2,1)S(1)}, bf16[264,512]{1,0:T(8,128)(2,1)S(1)}, u32[]{:S(2)}, u32[]{:S(2)}) collective-permute-start(bf16[264,512]{1,0:T(8,128)(2,1)S(1)} %collective-permute-done.refs_0_), channel_id=1, source_target_pairs={{0,2},{1,3},{2,4},{3,5},{4,6},{5,7},{6,0},{7,1},{8,10},{9,11},{10,... | collective-permute-start | bytes 811016 | tf_op jit(solution)/shard_map/ppermute | solution.py:545
  15.2 1.0 %copy-start.9 = (bf16[264,512]{1,0:T(8,128)(2,1)S(1)}, bf16[264,512]{1,0:T(8,128)(2,1)}, u32[]{:S(2)}) copy-start(bf16[264,512]{1,0:T(8,128)(2,1)} %get-tuple-element.29.refs_0_) | copy-start | bytes 811012
  16.1 0.9 %copy-start.10 = (bf16[256,512]{1,0:T(8,128)(2,1)S(1)}, bf16[256,512]{1,0:T(8,128)(2,1)}, u32[]{:S(2)}) copy-start(bf16[256,512]{1,0:T(8,128)(2,1)} %get-tuple-element.32.refs_1_) | copy-start | bytes 786436
  20.0 6.2 %collective-permute-start.8 = (bf16[256,512]{1,0:T(8,128)(2,1)S(1)}, bf16[256,512]{1,0:T(8,128)(2,1)S(1)}, u32[]{:S(2)}, u32[]{:S(2)}) collective-permute-start(bf16[256,512]{1,0:T(8,128)(2,1)S(1)} %collective-permute-done.2.refs_1_), channel_id=1, source_target_pairs={{0,1},{1,0},{2,3},{3,2},{4,5},{5,4},{6,7},{7,6},{8,9},{9,8},{10,11... | collective-permute-start | bytes 786440 | tf_op jit(solution)/shard_map/ppermute | solution.py:562
  20.6 11.2 %collective-permute-start.6 = (bf16[256,512]{1,0:T(8,128)(2,1)S(1)}, bf16[256,512]{1,0:T(8,128)(2,1)S(1)}, u32[]{:S(2)}, u32[]{:S(2)}) collective-permute-start(bf16[256,512]{1,0:T(8,128)(2,1)S(1)} %collective-permute-done.2.refs_1_), channel_id=1, source_target_pairs={{0,2},{1,3},{2,4},{3,5},{4,6},{5,7},{6,0},{7,1},{8,10},{9,11},{10,... | collective-permute-start | bytes 786440 | tf_op jit(solution)/shard_map/ppermute | solution.py:545
  23.2 8.5 %copy-start.5 = (s32[512]{0:T(512)S(1)}, s32[512]{0:T(512)}, u32[]{:S(2)}) copy-start(s32[512]{0:T(512)} %param.13) | copy-start | bytes 6148
  26.2 11.3 %collective-permute-start.11 = (bf16[264,512]{1,0:T(8,128)(2,1)S(1)}, bf16[264,512]{1,0:T(8,128)(2,1)S(1)}, u32[]{:S(2)}, u32[]{:S(2)}) collective-permute-start(bf16[264,512]{1,0:T(8,128)(2,1)S(1)} %collective-permute-done.1.beyond.refs_0_.refs_2_), channel_id=1, source_target_pairs={{0,1},{1,0},{2,3},{3,2},{4,5},{5,4},{6,7},{7,6},{8,9},{9,8},{10,11... | collective-permute-start | bytes 811016 | tf_op jit(solution)/shard_map/ppermute | solution.py:562
  26.2 11.3 %collective-permute-start.5 = (bf16[264,512]{1,0:T(8,128)(2,1)S(1)}, bf16[264,512]{1,0:T(8,128)(2,1)S(1)}, u32[]{:S(2)}, u32[]{:S(2)}) collective-permute-start(bf16[264,512]{1,0:T(8,128)(2,1)S(1)} %collective-permute-done.1.beyond.refs_0_.refs_2_), channel_id=1, source_target_pairs={{0,2},{1,3},{2,4},{3,5},{4,6},{5,7},{6,0},{7,1},{8,10},{9,11},{10,... | collective-permute-start | bytes 811016 | tf_op jit(solution)/shard_map/ppermute | solution.py:545
  31.7 5.8 %collective-permute-start.12 = (bf16[256,512]{1,0:T(8,128)(2,1)S(1)}, bf16[256,512]{1,0:T(8,128)(2,1)S(1)}, u32[]{:S(2)}, u32[]{:S(2)}) collective-permute-start(bf16[256,512]{1,0:T(8,128)(2,1)S(1)} %collective-permute-done.6.refs_1_.refs_3_), channel_id=1, source_target_pairs={{0,1},{1,0},{2,3},{3,2},{4,5},{5,4},{6,7},{7,6},{8,9},{9,8},{10,11... | collective-permute-start | bytes 786440 | tf_op jit(solution)/shard_map/ppermute | solution.py:562
  31.7 11.1 %collective-permute-start.10 = (bf16[256,512]{1,0:T(8,128)(2,1)S(1)}, bf16[256,512]{1,0:T(8,128)(2,1)S(1)}, u32[]{:S(2)}, u32[]{:S(2)}) collective-permute-start(bf16[256,512]{1,0:T(8,128)(2,1)S(1)} %collective-permute-done.6.refs_1_.refs_3_), channel_id=1, source_target_pairs={{0,2},{1,3},{2,4},{3,5},{4,6},{5,7},{6,0},{7,1},{8,10},{9,11},{10,... | collective-permute-start | bytes 786440 | tf_op jit(solution)/shard_map/ppermute | solution.py:545
  37.5 5.4 %collective-permute-start.9 = (bf16[264,512]{1,0:T(8,128)(2,1)S(1)}, bf16[264,512]{1,0:T(8,128)(2,1)S(1)}, u32[]{:S(2)}, u32[]{:S(2)}) collective-permute-start(bf16[264,512]{1,0:T(8,128)(2,1)S(1)} %collective-permute-done.5.refs_0_), channel_id=1, source_target_pairs={{0,1},{1,0},{2,3},{3,2},{4,5},{5,4},{6,7},{7,6},{8,9},{9,8},{10,11... | collective-permute-start | bytes 811016 | tf_op jit(solution)/shard_map/ppermute | solution.py:562
  38.9 5.6 %copy-start.3 = (bf16[512,512]{1,0:T(8,128)(2,1)S(1)}, bf16[512,512]{1,0:T(8,128)(2,1)}, u32[]{:S(2)}) copy-start(bf16[512,512]{1,0:T(8,128)(2,1)} %points.3) | copy-start | bytes 1572868
  38.9 5.5 %copy-start.6 = (s32[8,3]{0,1:T(4,128)S(1)}, s32[8,3]{0,1:T(4,128)}, u32[]{:S(2)}) copy-start(s32[8,3]{0,1:T(4,128)} %param.11) | copy-start | bytes 292
  42.9 1.5 %collective-permute-start.13 = (bf16[256,512]{1,0:T(8,128)(2,1)S(1)}, bf16[256,512]{1,0:T(8,128)(2,1)S(1)}, u32[]{:S(2)}, u32[]{:S(2)}) collective-permute-start(bf16[256,512]{1,0:T(8,128)(2,1)S(1)} %collective-permute-done.10.refs_0_), channel_id=1, source_target_pairs={{0,1},{1,0},{2,3},{3,2},{4,5},{5,4},{6,7},{7,6},{8,9},{9,8},{10,11... | collective-permute-start | bytes 786440 | tf_op jit(solution)/shard_map/ppermute | solution.py:562
  44.2 26.8 %copy-start.2 = (bf16[2,512,512]{2,1,0:T(8,128)(2,1)S(1)}, bf16[2,512,512]{2,1,0:T(8,128)(2,1)}, u32[]{:S(2)}) copy-start(bf16[2,512,512]{2,1,0:T(8,128)(2,1)} %w_proj.1) | copy-start | bytes 3145732
  44.2 26.8 %copy-start.7 = (bf16[3,512]{1,0:T(4,128)(2,1)S(1)}, bf16[3,512]{1,0:T(4,128)(2,1)}, u32[]{:S(2)}) copy-start(bf16[3,512]{1,0:T(4,128)(2,1)} %w_head.1) | copy-start | bytes 9220
  44.2 26.8 %copy-start.8 = (s32[8,3]{0,1:T(4,128)S(1)}, s32[8,3]{0,1:T(4,128)}, u32[]{:S(2)}) copy-start(s32[8,3]{0,1:T(4,128)} %param.12) | copy-start | bytes 292

commit v19 on v18

--- a/solution.py
+++ b/solution.py
@@ -120,13 +120,13 @@
 
 
 def split_kernel(points, destination, pattern, *refs):
-    *parts, destination_held, pattern_held, notes, sems = refs
+    *parts, held, destination_held, pattern_held, notes, sems = refs
     rows = points.shape[0] // len(parts)
     fetches = started([(destination, destination_held), (pattern, pattern_held)], sems.at[0])
     copies = started(
         [
-            (points.at[pl.ds(i * rows, rows), :], part.at[pl.ds(0, rows), :])
-            for i, part in enumerate(parts)
+            (points.at[pl.ds(i * rows, rows), :], held.at[i, pl.ds(0, rows), :])
+            for i in range(len(parts))
         ],
         sems.at[1],
     )
@@ -139,8 +139,12 @@
     values = jnp.where(row == chosen, low, jnp.where(row == chosen + 1, high, 0))
     notes[...] = values.astype(F32)
     notes[0:chosen, 0:patches] = pattern_held[...].astype(F32)
-    parts[0][rows : rows + TAIL, :] = notes[...].astype(BF16)
-    for copy in copies:
+    held[0, rows : rows + TAIL, :] = notes[...].astype(BF16)
+    leaving = []
+    for i, part in enumerate(parts):
+        copies[i].wait()
+        leaving += started([(held.at[i, pl.ds(0, part.shape[0]), :], part)], sems.at[2 + i])
+    for copy in leaving:
         copy.wait()
 
 
@@ -464,12 +468,13 @@
         split_kernel,
         out_shape=[jax.ShapeDtypeStruct((rows, channels), BF16) for rows in part_rows],
         in_specs=[ANY_SPEC] * 3,
-        out_specs=[VMEM_SPEC] * RING_PARTS,
+        out_specs=[ANY_SPEC] * RING_PARTS,
         scratch_shapes=[
+            pltpu.VMEM((RING_PARTS, part + TAIL, channels), BF16),
             pltpu.VMEM((1, rows_here), jnp.int32),
             pltpu.VMEM(pattern_first.shape, jnp.int32),
             pltpu.VMEM((TAIL, channels), F32),
-            pltpu.SemaphoreType.DMA((2, RING_PARTS)),
+            pltpu.SemaphoreType.DMA((2 + RING_PARTS, 2)),
         ],
         compiler_params=pltpu.CompilerParams(vmem_limit_bytes=SPLIT_BYTES),
         name="split",

time: 83.7 us -> 83.7 us (level)
  no operation moved by 1% of the time
where the time goes in v19:
time: 83.7 us; the launch traced here: 83.3 us
  Pallas kernels  30.7 us (37%)
  blocking collectives  20.4 us (24%)
  waiting for transfers between devices  18.3 us (22%)
  starting transfers between devices  7.09 us (8%)
  local copies, waits for them, and re-layouts  5.75 us (7%)
  between operations  0.99 us (1%)
    all_to_all x1, blocking collectives, shards(): lax.all_to_all(outgoing, ('grp', 'seq'), split_axis=0, concat_axis=0, til...  20.4 us
    ppermute x6, waiting for transfers between devices, shards(): column = [lax.ppermute(rows, GROUP, onward) for rows in column]  18.1 us
    pallas_call x1, Pallas kernels, shards(): pl.pallas_call(second_kernel, out_shape=(jax.ShapeDtypeStruct((rows_here,...  12.2 us
    pallas_call x6, Pallas kernels, project(): pl.pallas_call(functools.partial(project_kernel, first_rows, new, ask), o...  9.79 us
    pallas_call x1, Pallas kernels, shards(): pl.pallas_call(functools.partial(first_kernel, chips if ring else 0, late...  6.15 us
    ppermute x6, starting transfers between devices, shards(): column = [lax.ppermute(rows, GROUP, onward) for rows in column]  6.02 us
    unnamed x22, local copies, waits for them, and re-layouts  5.75 us
    pallas_call x1, Pallas kernels, shards(): pl.pallas_call(split_kernel, out_shape=[jax.ShapeDtypeStruct((rows, chann...  1.85 us
  transfers between devices with their start and end apart: 14, of which 6 were waited for; matrix products, arithmetic and copies ran while one was open for 0% of the time, Pallas kernels for 13%

profile of v19, /device:TPU:0, one launch (start us, length us, event | category | flops | bytes accessed | tf_op | source)
XLA Modules:
  0.0 83.3 jit_solution(5765942141006994786)
XLA Ops:
  0.6 1.8 %split.1 = (bf16[264,512]{1,0:T(8,128)(2,1)}, bf16[256,512]{1,0:T(8,128)(2,1)}) custom-call(bf16[512,512]{1,0:T(8,128)(2,1)} %points.3, s32[1,512]{1,0:T(1,128)} %bitcast.3, s32[3,8]{1,0:T(4,128)} %bitcast.5), custom_call_target="tpu_custom_call" | custom-call | tf_op jit(solution)/shard_map/split/pallas_call | solution.py:467
  2.5 3.1 %collective-permute-start = (bf16[264,512]{1,0:T(8,128)(2,1)}, bf16[264,512]{1,0:T(8,128)(2,1)S(1)}, u32[]{:S(2)}, u32[]{:S(2)}) collective-permute-start(bf16[264,512]{1,0:T(8,128)(2,1)} %get-tuple-element.29.refs_0_), channel_id=1, source_target_pairs={{0,2},{1,3},{2,4},{3,5},{4,6},{5,7},{6,0},{7,1},{8,10},{9,11},{10,... | collective-permute-start | bytes 811016 | tf_op jit(solution)/shard_map/ppermute | solution.py:550
  5.6 0.0 collective-permute-start.3
  5.6 0.5 collective-permute-start.4
  6.1 1.6 %collective-permute-start.2 = (bf16[256,512]{1,0:T(8,128)(2,1)}, bf16[256,512]{1,0:T(8,128)(2,1)S(1)}, u32[]{:S(2)}, u32[]{:S(2)}) collective-permute-start(bf16[256,512]{1,0:T(8,128)(2,1)} %get-tuple-element.32.refs_1_), channel_id=1, source_target_pairs={{0,2},{1,3},{2,4},{3,5},{4,6},{5,7},{6,0},{7,1},{8,10},{9,11},{10,... | collective-permute-start | bytes 786440 | tf_op jit(solution)/shard_map/ppermute | solution.py:550
  7.7 1.9 %copy-done = bf16[2,512,1536]{2,1,0:T(8,128)(2,1)S(1)} copy-done((bf16[2,512,1536]{2,1,0:T(8,128)(2,1)S(1)}, bf16[2,512,1536]{2,1,0:T(8,128)(2,1)}, u32[]{:S(2)}) %copy-start) | copy-done | bytes 3145752
  9.5 1.2 %copy-done.1 = bf16[2,512,512]{2,1,0:T(8,128)(2,1)S(1)} copy-done((bf16[2,512,512]{2,1,0:T(8,128)(2,1)S(1)}, bf16[2,512,512]{2,1,0:T(8,128)(2,1)}, u32[]{:S(2)}) %copy-start.1) | copy-done | bytes 1048600
  10.8 0.7 copy-done.4
  11.5 0.2 keep.1
  11.6 3.5 %collective-permute-done.refs_0_ = bf16[264,512]{1,0:T(8,128)(2,1)S(1)} collective-permute-done((bf16[264,512]{1,0:T(8,128)(2,1)}, bf16[264,512]{1,0:T(8,128)(2,1)S(1)}, u32[]{:S(2)}, u32[]{:S(2)}) %collective-permute-start) | collective-permute-done | bytes 270368 | tf_op jit(solution)/shard_map/ppermute | solution.py:550
  15.1 0.0 collective-permute-start.7
  15.1 0.0 collective-permute-start.1
  15.1 0.0 collective-permute-done.4.refs_3_
  15.1 0.0 collective-permute-done.3.refs_2_
  15.2 0.9 %copy-done.9 = bf16[264,512]{1,0:T(8,128)(2,1)S(1)} copy-done((bf16[264,512]{1,0:T(8,128)(2,1)S(1)}, bf16[264,512]{1,0:T(8,128)(2,1)}, u32[]{:S(2)}) %copy-start.9) | copy-done | bytes 270360
  16.1 0.9 %copy-done.10 = bf16[256,512]{1,0:T(8,128)(2,1)S(1)} copy-done((bf16[256,512]{1,0:T(8,128)(2,1)S(1)}, bf16[256,512]{1,0:T(8,128)(2,1)}, u32[]{:S(2)}) %copy-start.10) | copy-done | bytes 262168
  17.1 2.9 %project_own.1 = (bf16[4096,1024]{1,0:T(8,128)(2,1)S(1)}, bf16[512,512]{1,0:T(8,128)(2,1)S(1)}) custom-call(bf16[264,512]{1,0:T(8,128)(2,1)S(1)} %copy-done.9, bf16[256,512]{1,0:T(8,128)(2,1)S(1)} %copy-done.10, bf16[264,512]{1,0:T(8,128)(2,1)S(1)} %collective-permute-done.3.refs_2_, bf16[256,512]{1,0:T(8,128)(2,1)S(1)} %collective-permute-done.4.refs_3_, ...), custom_call_target="tpu_custom_call" | custom-call | flops 1073741824 | bytes 4718592 | tf_op jit(solution)/shard_map/project_own/pallas_call | solution.py:527
  20.0 0.0 collective-permute-done.2.refs_1_
  20.0 0.5 collective-permute-start.8
  20.5 1.3 %collective-permute-start.6 = (bf16[256,512]{1,0:T(8,128)(2,1)S(1)}, bf16[256,512]{1,0:T(8,128)(2,1)S(1)}, u32[]{:S(2)}, u32[]{:S(2)}) collective-permute-start(bf16[256,512]{1,0:T(8,128)(2,1)S(1)} %collective-permute-done.2.refs_1_), channel_id=1, source_target_pairs={{0,2},{1,3},{2,4},{3,5},{4,6},{5,7},{6,0},{7,1},{8,10},{9,11},{10,... | collective-permute-start | bytes 786440 | tf_op jit(solution)/shard_map/ppermute | solution.py:550
  21.9 1.3 %project.5.refs_4_ = bf16[4096,1024]{1,0:T(8,128)(2,1)S(1)} custom-call(bf16[264,512]{1,0:T(8,128)(2,1)S(1)} %collective-permute-done.refs_0_, bf16[256,512]{1,0:T(8,128)(2,1)S(1)} %collective-permute-done.2.refs_1_, f32[4,512]{1,0:T(4,128)S(1)} %get-tuple-element.33.refs_4_.refs_2_.gains, ...), custom_call_target="tpu_custom_call", output_to_operand_aliasing={{}: (4, {})} | custom-call | flops 536870912 | bytes 3145728 | tf_op jit(solution)/shard_map/project/pallas_call | solution.py:527
  23.2 0.0 copy-start.5
  23.2 3.0 %collective-permute-done.1.beyond.refs_0_.refs_2_ = bf16[264,512]{1,0:T(8,128)(2,1)S(1)} collective-permute-done((bf16[264,512]{1,0:T(8,128)(2,1)S(1)}, bf16[264,512]{1,0:T(8,128)(2,1)S(1)}, u32[]{:S(2)}, u32[]{:S(2)}) %collective-permute-start.1) | collective-permute-done | bytes 270368 | tf_op jit(solution)/shard_map/ppermute | solution.py:550
  26.2 0.0 collective-permute-start.11
  26.2 0.0 collective-permute-start.5
  26.2 0.0 collective-permute-done.7.refs_0_
  26.2 1.3 %project.6.refs_4_ = bf16[4096,1024]{1,0:T(8,128)(2,1)S(1)} custom-call(bf16[264,512]{1,0:T(8,128)(2,1)S(1)} %collective-permute-done.7.refs_0_, bf16[256,512]{1,0:T(8,128)(2,1)S(1)} %collective-permute-done.8.refs_1_, f32[4,512]{1,0:T(4,128)S(1)} %get-tuple-element.33.refs_4_.refs_2_.gains, ...), custom_call_target="tpu_custom_call", output_to_operand_aliasing={{}: (4, {})} | custom-call | flops 536870912 | bytes 3145728 | tf_op jit(solution)/shard_map/project/pallas_call | solution.py:527
  27.5 4.1 %collective-permute-done.6.refs_1_.refs_3_ = bf16[256,512]{1,0:T(8,128)(2,1)S(1)} collective-permute-done((bf16[256,512]{1,0:T(8,128)(2,1)S(1)}, bf16[256,512]{1,0:T(8,128)(2,1)S(1)}, u32[]{:S(2)}, u32[]{:S(2)}) %collective-permute-start.6) | collective-permute-done | bytes 262176 | tf_op jit(solution)/shard_map/ppermute | solution.py:550
  31.7 0.0 collective-permute-start.12
  31.7 0.0 collective-permute-start.10
  31.7 0.6 index.1
  32.3 1.6 %project.7 = (bf16[4096,1024]{1,0:T(8,128)(2,1)S(1)}, bf16[512,512]{1,0:T(8,128)(2,1)S(1)}) custom-call(bf16[264,512]{1,0:T(8,128)(2,1)S(1)} %collective-permute-done.1.beyond.refs_0_.refs_2_, bf16[256,512]{1,0:T(8,128)(2,1)S(1)} %collective-permute-done.6.refs_1_.refs_3_, ...), custom_call_target="tpu_custom_call", output_to_operand_aliasing={{0}: (4, {})} | custom-call | flops 536870912 | bytes 3145728 | tf_op jit(solution)/shard_map/project/pallas_call | solution.py:527
  33.9 3.6 %collective-permute-done.5.refs_0_ = bf16[264,512]{1,0:T(8,128)(2,1)S(1)} collective-permute-done((bf16[264,512]{1,0:T(8,128)(2,1)S(1)}, bf16[264,512]{1,0:T(8,128)(2,1)S(1)}, u32[]{:S(2)}, u32[]{:S(2)}) %collective-permute-start.5) | collective-permute-done | bytes 270368 | tf_op jit(solution)/shard_map/ppermute | solution.py:550
  37.5 0.0 collective-permute-start.9
  37.5 0.0 collective-permute-done.12.refs_1_
  37.5 0.0 collective-permute-done.11.refs_0_
  37.5 1.3 %project.8.refs_4_ = bf16[4096,1024]{1,0:T(8,128)(2,1)S(1)} custom-call(bf16[264,512]{1,0:T(8,128)(2,1)S(1)} %collective-permute-done.11.refs_0_, bf16[256,512]{1,0:T(8,128)(2,1)S(1)} %collective-permute-done.12.refs_1_, f32[4,512]{1,0:T(4,128)S(1)} %get-tuple-element.33.refs_4_.refs_2_.gains, ...), custom_call_target="tpu_custom_call", output_to_operand_aliasing={{}: (4, {})} | custom-call | flops 536870912 | bytes 3145728 | tf_op jit(solution)/shard_map/project/pallas_call | solution.py:527
  38.8 0.0 copy-start.3
  38.8 0.0 copy-start.6
  38.8 4.0 %collective-permute-done.10.refs_0_ = bf16[256,512]{1,0:T(8,128)(2,1)S(1)} collective-permute-done((bf16[256,512]{1,0:T(8,128)(2,1)S(1)}, bf16[256,512]{1,0:T(8,128)(2,1)S(1)}, u32[]{:S(2)}, u32[]{:S(2)}) %collective-permute-start.10) | collective-permute-done | bytes 262176 | tf_op jit(solution)/shard_map/ppermute | solution.py:550
  42.8 1.3 %project.9.kept_rows = bf16[4096,1024]{1,0:T(8,128)(2,1)S(1)} custom-call(bf16[264,512]{1,0:T(8,128)(2,1)S(1)} %collective-permute-done.5.refs_0_, bf16[264,512]{1,0:T(8,128)(2,1)S(1)} %collective-permute-done.9.refs_1_, f32[4,512]{1,0:T(4,128)S(1)} %get-tuple-element.33.refs_4_.refs_2_.gains, ...), custom_call_target="tpu_custom_call", output_to_operand_aliasing={{}: (4, {})} | custom-call | flops 536870912 | bytes 3145728 | tf_op jit(solution)/shard_map/project/pallas_call | solution.py:527
  44.2 0.0 copy-start.2
  44.2 0.0 copy-start.7
  44.2 0.0 copy-start.8
  44.2 0.2 collective-permute-done.13.refs_1_
  44.4 6.1 %block_first.1 = (bf16[16,264,128]{2,1,0:T(8,128)(2,1)S(1)}, bf16[4096,1024]{1,0:T(8,128)(2,1)S(1)}) custom-call(s32[3,8]{1,0:T(4,128)S(1)} %bitcast.6, s32[3,8]{1,0:T(4,128)S(1)} %get-tuple-element.39.pattern_beyond, s32[1,1024]{1,0:T(1,128)S(1)} %get-tuple-element.46.slot_of_row, ...), custom_call_target="tpu_custom_call", output_to_operand_aliasing={{1}: (3, {})} | custom-call | tf_op jit(solution)/shard_map/block_first/pallas_call | solution.py:594
  50.5 20.4 %all_to_all.5.incoming = bf16[16,264,128]{2,1,0:T(8,128)(2,1)S(1)} all-to-all(bf16[16,264,128]{2,1,0:T(8,128)(2,1)S(1)} %get-tuple-element.55), channel_id=1, replica_groups=mesh['grp'=4,'half'=2,'seq'=4] {'grp','seq'}, dimensions={0} | all-to-all | bytes 2162688 | tf_op jit(solution)/shard_map/all_to_all | solution.py:628
  70.9 12.2 %block_second.1 = (bf16[512,512]{1,0:T(8,128)(2,1)}, f32[3,512]{1,0:T(4,128)}) custom-call(s32[3,8]{1,0:T(4,128)S(1)} %bitcast.7, f32[4,512]{1,0:T(4,128)S(1)} %copy-done.4, bf16[16,264,128]{2,1,0:T(8,128)(2,1)S(1)} %all_to_all.5.incoming, bf16[2,512,1536]{2,1,0:T(8,128)(2,1)} %w_qkv.1, bf16[2,512,512]{2,1,0:T(8,128)(2,1)S(1)} %copy-done.2, ...), custom_call_target="tpu_custom_call" | custom-call | tf_op jit(solution)/shard_map/block_second/pallas_call | solution.py:630
  (14 shorter events, 0.0 us)
Async XLA Ops:
  2.5 12.6 %collective-permute-start = (bf16[264,512]{1,0:T(8,128)(2,1)}, bf16[264,512]{1,0:T(8,128)(2,1)S(1)}, u32[]{:S(2)}, u32[]{:S(2)}) collective-permute-start(bf16[264,512]{1,0:T(8,128)(2,1)} %get-tuple-element.29.refs_0_), channel_id=1, source_target_pairs={{0,2},{1,3},{2,4},{3,5},{4,6},{5,7},{6,0},{7,1},{8,10},{9,11},{10,... | collective-permute-start | bytes 811016 | tf_op jit(solution)/shard_map/ppermute | solution.py:550
  5.6 9.6 %collective-permute-start.3 = (bf16[264,512]{1,0:T(8,128)(2,1)}, bf16[264,512]{1,0:T(8,128)(2,1)S(1)}, u32[]{:S(2)}, u32[]{:S(2)}) collective-permute-start(bf16[264,512]{1,0:T(8,128)(2,1)} %get-tuple-element.29.refs_0_), channel_id=1, source_target_pairs={{0,1},{1,0},{2,3},{3,2},{4,5},{5,4},{6,7},{7,6},{8,9},{9,8},{10,11... | collective-permute-start | bytes 811016 | tf_op jit(solution)/shard_map/ppermute | solution.py:547
  5.6 9.6 %collective-permute-start.4 = (bf16[256,512]{1,0:T(8,128)(2,1)}, bf16[256,512]{1,0:T(8,128)(2,1)S(1)}, u32[]{:S(2)}, u32[]{:S(2)}) collective-permute-start(bf16[256,512]{1,0:T(8,128)(2,1)} %get-tuple-element.32.refs_1_), channel_id=1, source_target_pairs={{0,1},{1,0},{2,3},{3,2},{4,5},{5,4},{6,7},{7,6},{8,9},{9,8},{10,11... | collective-permute-start | bytes 786440 | tf_op jit(solution)/shard_map/ppermute | solution.py:547
  6.1 13.9 %collective-permute-start.2 = (bf16[256,512]{1,0:T(8,128)(2,1)}, bf16[256,512]{1,0:T(8,128)(2,1)S(1)}, u32[]{:S(2)}, u32[]{:S(2)}) collective-permute-start(bf16[256,512]{1,0:T(8,128)(2,1)} %get-tuple-element.32.refs_1_), channel_id=1, source_target_pairs={{0,2},{1,3},{2,4},{3,5},{4,6},{5,7},{6,0},{7,1},{8,10},{9,11},{10,... | collective-permute-start | bytes 786440 | tf_op jit(solution)/shard_map/ppermute | solution.py:550
  7.6 1.9 %copy-start = (bf16[2,512,1536]{2,1,0:T(8,128)(2,1)S(1)}, bf16[2,512,1536]{2,1,0:T(8,128)(2,1)}, u32[]{:S(2)}) copy-start(bf16[2,512,1536]{2,1,0:T(8,128)(2,1)} %w_qkv.1) | copy-start | bytes 9437188
  9.5 1.2 %copy-start.1 = (bf16[2,512,512]{2,1,0:T(8,128)(2,1)S(1)}, bf16[2,512,512]{2,1,0:T(8,128)(2,1)}, u32[]{:S(2)}) copy-start(bf16[2,512,512]{2,1,0:T(8,128)(2,1)} %w_proj.1) | copy-start | bytes 3145732
  10.8 0.7 copy-start.4
  15.1 11.1 %collective-permute-start.7 = (bf16[264,512]{1,0:T(8,128)(2,1)S(1)}, bf16[264,512]{1,0:T(8,128)(2,1)S(1)}, u32[]{:S(2)}, u32[]{:S(2)}) collective-permute-start(bf16[264,512]{1,0:T(8,128)(2,1)S(1)} %collective-permute-done.refs_0_), channel_id=1, source_target_pairs={{0,1},{1,0},{2,3},{3,2},{4,5},{5,4},{6,7},{7,6},{8,9},{9,8},{10,11... | collective-permute-start | bytes 811016 | tf_op jit(solution)/shard_map/ppermute | solution.py:567
  15.1 11.1 %collective-permute-start.1 = (bf16[264,512]{1,0:T(8,128)(2,1)S(1)}, bf16[264,512]{1,0:T(8,128)(2,1)S(1)}, u32[]{:S(2)}, u32[]{:S(2)}) collective-permute-start(bf16[264,512]{1,0:T(8,128)(2,1)S(1)} %collective-permute-done.refs_0_), channel_id=1, source_target_pairs={{0,2},{1,3},{2,4},{3,5},{4,6},{5,7},{6,0},{7,1},{8,10},{9,11},{10,... | collective-permute-start | bytes 811016 | tf_op jit(solution)/shard_map/ppermute | solution.py:550
  15.1 1.0 %copy-start.9 = (bf16[264,512]{1,0:T(8,128)(2,1)S(1)}, bf16[264,512]{1,0:T(8,128)(2,1)}, u32[]{:S(2)}) copy-start(bf16[264,512]{1,0:T(8,128)(2,1)} %get-tuple-element.29.refs_0_) | copy-start | bytes 811012
  16.1 0.9 %copy-start.10 = (bf16[256,512]{1,0:T(8,128)(2,1)S(1)}, bf16[256,512]{1,0:T(8,128)(2,1)}, u32[]{:S(2)}) copy-start(bf16[256,512]{1,0:T(8,128)(2,1)} %get-tuple-element.32.refs_1_) | copy-start | bytes 786436
  20.0 6.2 %collective-permute-start.8 = (bf16[256,512]{1,0:T(8,128)(2,1)S(1)}, bf16[256,512]{1,0:T(8,128)(2,1)S(1)}, u32[]{:S(2)}, u32[]{:S(2)}) collective-permute-start(bf16[256,512]{1,0:T(8,128)(2,1)S(1)} %collective-permute-done.2.refs_1_), channel_id=1, source_target_pairs={{0,1},{1,0},{2,3},{3,2},{4,5},{5,4},{6,7},{7,6},{8,9},{9,8},{10,11... | collective-permute-start | bytes 786440 | tf_op jit(solution)/shard_map/ppermute | solution.py:567
  20.5 11.2 %collective-permute-start.6 = (bf16[256,512]{1,0:T(8,128)(2,1)S(1)}, bf16[256,512]{1,0:T(8,128)(2,1)S(1)}, u32[]{:S(2)}, u32[]{:S(2)}) collective-permute-start(bf16[256,512]{1,0:T(8,128)(2,1)S(1)} %collective-permute-done.2.refs_1_), channel_id=1, source_target_pairs={{0,2},{1,3},{2,4},{3,5},{4,6},{5,7},{6,0},{7,1},{8,10},{9,11},{10,... | collective-permute-start | bytes 786440 | tf_op jit(solution)/shard_map/ppermute | solution.py:550
  23.2 8.5 %copy-start.5 = (s32[512]{0:T(512)S(1)}, s32[512]{0:T(512)}, u32[]{:S(2)}) copy-start(s32[512]{0:T(512)} %param.13) | copy-start | bytes 6148
  26.2 11.3 %collective-permute-start.11 = (bf16[264,512]{1,0:T(8,128)(2,1)S(1)}, bf16[264,512]{1,0:T(8,128)(2,1)S(1)}, u32[]{:S(2)}, u32[]{:S(2)}) collective-permute-start(bf16[264,512]{1,0:T(8,128)(2,1)S(1)} %collective-permute-done.1.beyond.refs_0_.refs_2_), channel_id=1, source_target_pairs={{0,1},{1,0},{2,3},{3,2},{4,5},{5,4},{6,7},{7,6},{8,9},{9,8},{10,11... | collective-permute-start | bytes 811016 | tf_op jit(solution)/shard_map/ppermute | solution.py:567
  26.2 11.3 %collective-permute-start.5 = (bf16[264,512]{1,0:T(8,128)(2,1)S(1)}, bf16[264,512]{1,0:T(8,128)(2,1)S(1)}, u32[]{:S(2)}, u32[]{:S(2)}) collective-permute-start(bf16[264,512]{1,0:T(8,128)(2,1)S(1)} %collective-permute-done.1.beyond.refs_0_.refs_2_), channel_id=1, source_target_pairs={{0,2},{1,3},{2,4},{3,5},{4,6},{5,7},{6,0},{7,1},{8,10},{9,11},{10,... | collective-permute-start | bytes 811016 | tf_op jit(solution)/shard_map/ppermute | solution.py:550
  31.7 5.8 %collective-permute-start.12 = (bf16[256,512]{1,0:T(8,128)(2,1)S(1)}, bf16[256,512]{1,0:T(8,128)(2,1)S(1)}, u32[]{:S(2)}, u32[]{:S(2)}) collective-permute-start(bf16[256,512]{1,0:T(8,128)(2,1)S(1)} %collective-permute-done.6.refs_1_.refs_3_), channel_id=1, source_target_pairs={{0,1},{1,0},{2,3},{3,2},{4,5},{5,4},{6,7},{7,6},{8,9},{9,8},{10,11... | collective-permute-start | bytes 786440 | tf_op jit(solution)/shard_map/ppermute | solution.py:567
  31.7 11.1 %collective-permute-start.10 = (bf16[256,512]{1,0:T(8,128)(2,1)S(1)}, bf16[256,512]{1,0:T(8,128)(2,1)S(1)}, u32[]{:S(2)}, u32[]{:S(2)}) collective-permute-start(bf16[256,512]{1,0:T(8,128)(2,1)S(1)} %collective-permute-done.6.refs_1_.refs_3_), channel_id=1, source_target_pairs={{0,2},{1,3},{2,4},{3,5},{4,6},{5,7},{6,0},{7,1},{8,10},{9,11},{10,... | collective-permute-start | bytes 786440 | tf_op jit(solution)/shard_map/ppermute | solution.py:550
  37.5 5.4 %collective-permute-start.9 = (bf16[264,512]{1,0:T(8,128)(2,1)S(1)}, bf16[264,512]{1,0:T(8,128)(2,1)S(1)}, u32[]{:S(2)}, u32[]{:S(2)}) collective-permute-start(bf16[264,512]{1,0:T(8,128)(2,1)S(1)} %collective-permute-done.5.refs_0_), channel_id=1, source_target_pairs={{0,1},{1,0},{2,3},{3,2},{4,5},{5,4},{6,7},{7,6},{8,9},{9,8},{10,11... | collective-permute-start | bytes 811016 | tf_op jit(solution)/shard_map/ppermute | solution.py:567
  38.8 5.6 %copy-start.3 = (bf16[512,512]{1,0:T(8,128)(2,1)S(1)}, bf16[512,512]{1,0:T(8,128)(2,1)}, u32[]{:S(2)}) copy-start(bf16[512,512]{1,0:T(8,128)(2,1)} %points.3) | copy-start | bytes 1572868
  38.8 5.5 %copy-start.6 = (s32[8,3]{0,1:T(4,128)S(1)}, s32[8,3]{0,1:T(4,128)}, u32[]{:S(2)}) copy-start(s32[8,3]{0,1:T(4,128)} %param.11) | copy-start | bytes 292
  42.8 1.5 %collective-permute-start.13 = (bf16[256,512]{1,0:T(8,128)(2,1)S(1)}, bf16[256,512]{1,0:T(8,128)(2,1)S(1)}, u32[]{:S(2)}, u32[]{:S(2)}) collective-permute-start(bf16[256,512]{1,0:T(8,128)(2,1)S(1)} %collective-permute-done.10.refs_0_), channel_id=1, source_target_pairs={{0,1},{1,0},{2,3},{3,2},{4,5},{5,4},{6,7},{7,6},{8,9},{9,8},{10,11... | collective-permute-start | bytes 786440 | tf_op jit(solution)/shard_map/ppermute | solution.py:567
  44.2 26.8 %copy-start.2 = (bf16[2,512,512]{2,1,0:T(8,128)(2,1)S(1)}, bf16[2,512,512]{2,1,0:T(8,128)(2,1)}, u32[]{:S(2)}) copy-start(bf16[2,512,512]{2,1,0:T(8,128)(2,1)} %w_proj.1) | copy-start | bytes 3145732
  44.2 26.8 %copy-start.7 = (bf16[3,512]{1,0:T(4,128)(2,1)S(1)}, bf16[3,512]{1,0:T(4,128)(2,1)}, u32[]{:S(2)}) copy-start(bf16[3,512]{1,0:T(4,128)(2,1)} %w_head.1) | copy-start | bytes 9220
  44.2 26.8 %copy-start.8 = (s32[8,3]{0,1:T(4,128)S(1)}, s32[8,3]{0,1:T(4,128)}, u32[]{:S(2)}) copy-start(s32[8,3]{0,1:T(4,128)} %param.12) | copy-start | bytes 292

commit v20 on v18

--- a/solution.py
+++ b/solution.py
@@ -408,9 +408,9 @@
         copy.wait()
     normed = layer_norm(second, gains_held[2:3, :])
     scale = (channels // HEADS) ** (-0.5)
-    asked = jnp.dot(normed, qkv_held[:, :channels], preferred_element_type=F32).astype(BF16)
-    queries[...] = (asked * BF16(scale)).astype(BF16)
-    kv[...] = jnp.dot(normed, qkv_held[:, channels:], preferred_element_type=F32).astype(BF16)
+    every = jnp.dot(normed, qkv_held[...], preferred_element_type=F32).astype(BF16)
+    queries[...] = (every[:, :channels] * BF16(scale)).astype(BF16)
+    kv[...] = every[:, channels:]
     loaded = []
     for p in range(patches):
         starts = [pl.multiple_of(pattern[j, p] * PATCH, PATCH) for j in range(chosen)]

time: 83.7 us -> 83.7 us (level)
  no operation moved by 1% of the time
where the time goes in v20:
time: 83.7 us; the launch traced here: 83.4 us
  Pallas kernels  30.8 us (37%)
  blocking collectives  20.4 us (24%)
  waiting for transfers between devices  18.4 us (22%)
  starting transfers between devices  7.08 us (8%)
  local copies, waits for them, and re-layouts  5.75 us (7%)
  between operations  0.99 us (1%)
    all_to_all x1, blocking collectives, shards(): lax.all_to_all(outgoing, ('grp', 'seq'), split_axis=0, concat_axis=0, til...  20.4 us
    ppermute x6, waiting for transfers between devices, shards(): column = [lax.ppermute(rows, GROUP, onward) for rows in column]  18.2 us
    pallas_call x1, Pallas kernels, shards(): pl.pallas_call(second_kernel, out_shape=(jax.ShapeDtypeStruct((rows_here,...  12.2 us
    pallas_call x6, Pallas kernels, project(): pl.pallas_call(functools.partial(project_kernel, first_rows, new, ask), o...  9.77 us
    pallas_call x1, Pallas kernels, shards(): pl.pallas_call(functools.partial(first_kernel, chips if ring else 0, late...  6.15 us
    ppermute x6, starting transfers between devices, shards(): column = [lax.ppermute(rows, GROUP, onward) for rows in column]  6.03 us
    unnamed x22, local copies, waits for them, and re-layouts  5.75 us
    pallas_call x1, Pallas kernels, shards(): pl.pallas_call(split_kernel, out_shape=[jax.ShapeDtypeStruct((rows, chann...  1.89 us
  transfers between devices with their start and end apart: 14, of which 6 were waited for; matrix products, arithmetic and copies ran while one was open for 0% of the time, Pallas kernels for 13%

profile of v20, /device:TPU:0, one launch (start us, length us, event | category | flops | bytes accessed | tf_op | source)
XLA Modules:
  0.0 83.4 jit_solution(4775707333055040793)
XLA Ops:
  0.6 1.9 %split.1 = (bf16[264,512]{1,0:T(8,128)(2,1)}, bf16[256,512]{1,0:T(8,128)(2,1)}) custom-call(bf16[512,512]{1,0:T(8,128)(2,1)} %points.3, s32[1,512]{1,0:T(1,128)} %bitcast.3, s32[3,8]{1,0:T(4,128)} %bitcast.5), custom_call_target="tpu_custom_call" | custom-call | tf_op jit(solution)/shard_map/split/pallas_call | solution.py:463
  2.5 3.1 %collective-permute-start = (bf16[264,512]{1,0:T(8,128)(2,1)}, bf16[264,512]{1,0:T(8,128)(2,1)S(1)}, u32[]{:S(2)}, u32[]{:S(2)}) collective-permute-start(bf16[264,512]{1,0:T(8,128)(2,1)} %get-tuple-element.29.refs_0_), channel_id=1, source_target_pairs={{0,2},{1,3},{2,4},{3,5},{4,6},{5,7},{6,0},{7,1},{8,10},{9,11},{10,... | collective-permute-start | bytes 811016 | tf_op jit(solution)/shard_map/ppermute | solution.py:545
  5.6 0.0 collective-permute-start.3
  5.6 0.5 collective-permute-start.4
  6.1 1.6 %collective-permute-start.2 = (bf16[256,512]{1,0:T(8,128)(2,1)}, bf16[256,512]{1,0:T(8,128)(2,1)S(1)}, u32[]{:S(2)}, u32[]{:S(2)}) collective-permute-start(bf16[256,512]{1,0:T(8,128)(2,1)} %get-tuple-element.32.refs_1_), channel_id=1, source_target_pairs={{0,2},{1,3},{2,4},{3,5},{4,6},{5,7},{6,0},{7,1},{8,10},{9,11},{10,... | collective-permute-start | bytes 786440 | tf_op jit(solution)/shard_map/ppermute | solution.py:545
  7.7 1.9 %copy-done = bf16[2,512,1536]{2,1,0:T(8,128)(2,1)S(1)} copy-done((bf16[2,512,1536]{2,1,0:T(8,128)(2,1)S(1)}, bf16[2,512,1536]{2,1,0:T(8,128)(2,1)}, u32[]{:S(2)}) %copy-start) | copy-done | bytes 3145752
  9.6 1.2 %copy-done.1 = bf16[2,512,512]{2,1,0:T(8,128)(2,1)S(1)} copy-done((bf16[2,512,512]{2,1,0:T(8,128)(2,1)S(1)}, bf16[2,512,512]{2,1,0:T(8,128)(2,1)}, u32[]{:S(2)}) %copy-start.1) | copy-done | bytes 1048600
  10.8 0.7 copy-done.4
  11.5 0.2 keep.1
  11.7 3.5 %collective-permute-done.refs_0_ = bf16[264,512]{1,0:T(8,128)(2,1)S(1)} collective-permute-done((bf16[264,512]{1,0:T(8,128)(2,1)}, bf16[264,512]{1,0:T(8,128)(2,1)S(1)}, u32[]{:S(2)}, u32[]{:S(2)}) %collective-permute-start) | collective-permute-done | bytes 270368 | tf_op jit(solution)/shard_map/ppermute | solution.py:545
  15.1 0.0 collective-permute-start.7
  15.2 0.0 collective-permute-start.1
  15.2 0.0 collective-permute-done.4.refs_3_
  15.2 0.0 collective-permute-done.3.refs_2_
  15.2 0.9 %copy-done.9 = bf16[264,512]{1,0:T(8,128)(2,1)S(1)} copy-done((bf16[264,512]{1,0:T(8,128)(2,1)S(1)}, bf16[264,512]{1,0:T(8,128)(2,1)}, u32[]{:S(2)}) %copy-start.9) | copy-done | bytes 270360
  16.2 0.9 %copy-done.10 = bf16[256,512]{1,0:T(8,128)(2,1)S(1)} copy-done((bf16[256,512]{1,0:T(8,128)(2,1)S(1)}, bf16[256,512]{1,0:T(8,128)(2,1)}, u32[]{:S(2)}) %copy-start.10) | copy-done | bytes 262168
  17.1 2.9 %project_own.1 = (bf16[4096,1024]{1,0:T(8,128)(2,1)S(1)}, bf16[512,512]{1,0:T(8,128)(2,1)S(1)}) custom-call(bf16[264,512]{1,0:T(8,128)(2,1)S(1)} %copy-done.9, bf16[256,512]{1,0:T(8,128)(2,1)S(1)} %copy-done.10, bf16[264,512]{1,0:T(8,128)(2,1)S(1)} %collective-permute-done.3.refs_2_, bf16[256,512]{1,0:T(8,128)(2,1)S(1)} %collective-permute-done.4.refs_3_, ...), custom_call_target="tpu_custom_call" | custom-call | flops 1073741824 | bytes 4718592 | tf_op jit(solution)/shard_map/project_own/pallas_call | solution.py:522
  20.0 0.0 collective-permute-done.2.refs_1_
  20.0 0.5 collective-permute-start.8
  20.6 1.3 %collective-permute-start.6 = (bf16[256,512]{1,0:T(8,128)(2,1)S(1)}, bf16[256,512]{1,0:T(8,128)(2,1)S(1)}, u32[]{:S(2)}, u32[]{:S(2)}) collective-permute-start(bf16[256,512]{1,0:T(8,128)(2,1)S(1)} %collective-permute-done.2.refs_1_), channel_id=1, source_target_pairs={{0,2},{1,3},{2,4},{3,5},{4,6},{5,7},{6,0},{7,1},{8,10},{9,11},{10,... | collective-permute-start | bytes 786440 | tf_op jit(solution)/shard_map/ppermute | solution.py:545
  21.9 1.3 %project.5.refs_4_ = bf16[4096,1024]{1,0:T(8,128)(2,1)S(1)} custom-call(bf16[264,512]{1,0:T(8,128)(2,1)S(1)} %collective-permute-done.refs_0_, bf16[256,512]{1,0:T(8,128)(2,1)S(1)} %collective-permute-done.2.refs_1_, f32[4,512]{1,0:T(4,128)S(1)} %get-tuple-element.33.refs_4_.refs_2_.gains, ...), custom_call_target="tpu_custom_call", output_to_operand_aliasing={{}: (4, {})} | custom-call | flops 536870912 | bytes 3145728 | tf_op jit(solution)/shard_map/project/pallas_call | solution.py:522
  23.2 0.0 copy-start.5
  23.2 3.0 %collective-permute-done.1.beyond.refs_0_.refs_2_ = bf16[264,512]{1,0:T(8,128)(2,1)S(1)} collective-permute-done((bf16[264,512]{1,0:T(8,128)(2,1)S(1)}, bf16[264,512]{1,0:T(8,128)(2,1)S(1)}, u32[]{:S(2)}, u32[]{:S(2)}) %collective-permute-start.1) | collective-permute-done | bytes 270368 | tf_op jit(solution)/shard_map/ppermute | solution.py:545
  26.2 0.0 collective-permute-start.11
  26.2 0.0 collective-permute-start.5
  26.2 0.0 collective-permute-done.8.refs_1_
  26.3 1.3 %project.6.refs_4_ = bf16[4096,1024]{1,0:T(8,128)(2,1)S(1)} custom-call(bf16[264,512]{1,0:T(8,128)(2,1)S(1)} %collective-permute-done.7.refs_0_, bf16[256,512]{1,0:T(8,128)(2,1)S(1)} %collective-permute-done.8.refs_1_, f32[4,512]{1,0:T(4,128)S(1)} %get-tuple-element.33.refs_4_.refs_2_.gains, ...), custom_call_target="tpu_custom_call", output_to_operand_aliasing={{}: (4, {})} | custom-call | flops 536870912 | bytes 3145728 | tf_op jit(solution)/shard_map/project/pallas_call | solution.py:522
  27.6 4.2 %collective-permute-done.6.refs_1_.refs_3_ = bf16[256,512]{1,0:T(8,128)(2,1)S(1)} collective-permute-done((bf16[256,512]{1,0:T(8,128)(2,1)S(1)}, bf16[256,512]{1,0:T(8,128)(2,1)S(1)}, u32[]{:S(2)}, u32[]{:S(2)}) %collective-permute-start.6) | collective-permute-done | bytes 262176 | tf_op jit(solution)/shard_map/ppermute | solution.py:545
  31.7 0.0 collective-permute-start.10
  31.7 0.6 index.1
  32.4 1.6 %project.7 = (bf16[4096,1024]{1,0:T(8,128)(2,1)S(1)}, bf16[512,512]{1,0:T(8,128)(2,1)S(1)}) custom-call(bf16[264,512]{1,0:T(8,128)(2,1)S(1)} %collective-permute-done.1.beyond.refs_0_.refs_2_, bf16[256,512]{1,0:T(8,128)(2,1)S(1)} %collective-permute-done.6.refs_1_.refs_3_, ...), custom_call_target="tpu_custom_call", output_to_operand_aliasing={{0}: (4, {})} | custom-call | flops 536870912 | bytes 3145728 | tf_op jit(solution)/shard_map/project/pallas_call | solution.py:522
  34.0 3.6 %collective-permute-done.5.refs_0_ = bf16[264,512]{1,0:T(8,128)(2,1)S(1)} collective-permute-done((bf16[264,512]{1,0:T(8,128)(2,1)S(1)}, bf16[264,512]{1,0:T(8,128)(2,1)S(1)}, u32[]{:S(2)}, u32[]{:S(2)}) %collective-permute-start.5) | collective-permute-done | bytes 270368 | tf_op jit(solution)/shard_map/ppermute | solution.py:545
  37.5 0.0 collective-permute-start.9
  37.5 0.0 collective-permute-done.12.refs_1_
  37.5 0.0 collective-permute-done.11.refs_0_
  37.5 1.3 %project.8.refs_4_ = bf16[4096,1024]{1,0:T(8,128)(2,1)S(1)} custom-call(bf16[264,512]{1,0:T(8,128)(2,1)S(1)} %collective-permute-done.11.refs_0_, bf16[256,512]{1,0:T(8,128)(2,1)S(1)} %collective-permute-done.12.refs_1_, f32[4,512]{1,0:T(4,128)S(1)} %get-tuple-element.33.refs_4_.refs_2_.gains, ...), custom_call_target="tpu_custom_call", output_to_operand_aliasing={{}: (4, {})} | custom-call | flops 536870912 | bytes 3145728 | tf_op jit(solution)/shard_map/project/pallas_call | solution.py:522
  38.9 0.0 copy-start.3
  38.9 0.0 copy-start.6
  38.9 4.0 %collective-permute-done.10.refs_0_ = bf16[256,512]{1,0:T(8,128)(2,1)S(1)} collective-permute-done((bf16[256,512]{1,0:T(8,128)(2,1)S(1)}, bf16[256,512]{1,0:T(8,128)(2,1)S(1)}, u32[]{:S(2)}, u32[]{:S(2)}) %collective-permute-start.10) | collective-permute-done | bytes 262176 | tf_op jit(solution)/shard_map/ppermute | solution.py:545
  42.9 0.0 collective-permute-start.13
  42.9 1.3 %project.9.kept_rows = bf16[4096,1024]{1,0:T(8,128)(2,1)S(1)} custom-call(bf16[264,512]{1,0:T(8,128)(2,1)S(1)} %collective-permute-done.5.refs_0_, bf16[264,512]{1,0:T(8,128)(2,1)S(1)} %collective-permute-done.9.refs_1_, f32[4,512]{1,0:T(4,128)S(1)} %get-tuple-element.33.refs_4_.refs_2_.gains, ...), custom_call_target="tpu_custom_call", output_to_operand_aliasing={{}: (4, {})} | custom-call | flops 536870912 | bytes 3145728 | tf_op jit(solution)/shard_map/project/pallas_call | solution.py:522
  44.2 0.0 copy-start.2
  44.2 0.0 copy-start.7
  44.2 0.0 copy-start.8
  44.2 0.2 collective-permute-done.13.refs_1_
  44.4 6.1 %block_first.1 = (bf16[16,264,128]{2,1,0:T(8,128)(2,1)S(1)}, bf16[4096,1024]{1,0:T(8,128)(2,1)S(1)}) custom-call(s32[3,8]{1,0:T(4,128)S(1)} %bitcast.6, s32[3,8]{1,0:T(4,128)S(1)} %get-tuple-element.39.pattern_beyond, s32[1,1024]{1,0:T(1,128)S(1)} %get-tuple-element.46.slot_of_row, ...), custom_call_target="tpu_custom_call", output_to_operand_aliasing={{1}: (3, {})} | custom-call | tf_op jit(solution)/shard_map/block_first/pallas_call | solution.py:589
  50.6 20.4 %all_to_all.5.incoming = bf16[16,264,128]{2,1,0:T(8,128)(2,1)S(1)} all-to-all(bf16[16,264,128]{2,1,0:T(8,128)(2,1)S(1)} %get-tuple-element.55), channel_id=1, replica_groups=mesh['grp'=4,'half'=2,'seq'=4] {'grp','seq'}, dimensions={0} | all-to-all | bytes 2162688 | tf_op jit(solution)/shard_map/all_to_all | solution.py:623
  71.0 12.2 %block_second.1 = (bf16[512,512]{1,0:T(8,128)(2,1)}, f32[3,512]{1,0:T(4,128)}) custom-call(s32[3,8]{1,0:T(4,128)S(1)} %bitcast.7, f32[4,512]{1,0:T(4,128)S(1)} %copy-done.4, bf16[16,264,128]{2,1,0:T(8,128)(2,1)S(1)} %all_to_all.5.incoming, bf16[2,512,1536]{2,1,0:T(8,128)(2,1)} %w_qkv.1, bf16[2,512,512]{2,1,0:T(8,128)(2,1)S(1)} %copy-done.2, ...), custom_call_target="tpu_custom_call" | custom-call | tf_op jit(solution)/shard_map/block_second/pallas_call | solution.py:625
  (14 shorter events, 0.0 us)
Async XLA Ops:
  2.5 12.6 %collective-permute-start = (bf16[264,512]{1,0:T(8,128)(2,1)}, bf16[264,512]{1,0:T(8,128)(2,1)S(1)}, u32[]{:S(2)}, u32[]{:S(2)}) collective-permute-start(bf16[264,512]{1,0:T(8,128)(2,1)} %get-tuple-element.29.refs_0_), channel_id=1, source_target_pairs={{0,2},{1,3},{2,4},{3,5},{4,6},{5,7},{6,0},{7,1},{8,10},{9,11},{10,... | collective-permute-start | bytes 811016 | tf_op jit(solution)/shard_map/ppermute | solution.py:545
  5.6 9.6 %collective-permute-start.3 = (bf16[264,512]{1,0:T(8,128)(2,1)}, bf16[264,512]{1,0:T(8,128)(2,1)S(1)}, u32[]{:S(2)}, u32[]{:S(2)}) collective-permute-start(bf16[264,512]{1,0:T(8,128)(2,1)} %get-tuple-element.29.refs_0_), channel_id=1, source_target_pairs={{0,1},{1,0},{2,3},{3,2},{4,5},{5,4},{6,7},{7,6},{8,9},{9,8},{10,11... | collective-permute-start | bytes 811016 | tf_op jit(solution)/shard_map/ppermute | solution.py:542
  5.6 9.6 %collective-permute-start.4 = (bf16[256,512]{1,0:T(8,128)(2,1)}, bf16[256,512]{1,0:T(8,128)(2,1)S(1)}, u32[]{:S(2)}, u32[]{:S(2)}) collective-permute-start(bf16[256,512]{1,0:T(8,128)(2,1)} %get-tuple-element.32.refs_1_), channel_id=1, source_target_pairs={{0,1},{1,0},{2,3},{3,2},{4,5},{5,4},{6,7},{7,6},{8,9},{9,8},{10,11... | collective-permute-start | bytes 786440 | tf_op jit(solution)/shard_map/ppermute | solution.py:542
  6.1 13.9 %collective-permute-start.2 = (bf16[256,512]{1,0:T(8,128)(2,1)}, bf16[256,512]{1,0:T(8,128)(2,1)S(1)}, u32[]{:S(2)}, u32[]{:S(2)}) collective-permute-start(bf16[256,512]{1,0:T(8,128)(2,1)} %get-tuple-element.32.refs_1_), channel_id=1, source_target_pairs={{0,2},{1,3},{2,4},{3,5},{4,6},{5,7},{6,0},{7,1},{8,10},{9,11},{10,... | collective-permute-start | bytes 786440 | tf_op jit(solution)/shard_map/ppermute | solution.py:545
  7.7 1.9 %copy-start = (bf16[2,512,1536]{2,1,0:T(8,128)(2,1)S(1)}, bf16[2,512,1536]{2,1,0:T(8,128)(2,1)}, u32[]{:S(2)}) copy-start(bf16[2,512,1536]{2,1,0:T(8,128)(2,1)} %w_qkv.1) | copy-start | bytes 9437188
  9.6 1.2 %copy-start.1 = (bf16[2,512,512]{2,1,0:T(8,128)(2,1)S(1)}, bf16[2,512,512]{2,1,0:T(8,128)(2,1)}, u32[]{:S(2)}) copy-start(bf16[2,512,512]{2,1,0:T(8,128)(2,1)} %w_proj.1) | copy-start | bytes 3145732
  10.8 0.7 copy-start.4
  15.1 11.1 %collective-permute-start.7 = (bf16[264,512]{1,0:T(8,128)(2,1)S(1)}, bf16[264,512]{1,0:T(8,128)(2,1)S(1)}, u32[]{:S(2)}, u32[]{:S(2)}) collective-permute-start(bf16[264,512]{1,0:T(8,128)(2,1)S(1)} %collective-permute-done.refs_0_), channel_id=1, source_target_pairs={{0,1},{1,0},{2,3},{3,2},{4,5},{5,4},{6,7},{7,6},{8,9},{9,8},{10,11... | collective-permute-start | bytes 811016 | tf_op jit(solution)/shard_map/ppermute | solution.py:562
  15.2 11.1 %collective-permute-start.1 = (bf16[264,512]{1,0:T(8,128)(2,1)S(1)}, bf16[264,512]{1,0:T(8,128)(2,1)S(1)}, u32[]{:S(2)}, u32[]{:S(2)}) collective-permute-start(bf16[264,512]{1,0:T(8,128)(2,1)S(1)} %collective-permute-done.refs_0_), channel_id=1, source_target_pairs={{0,2},{1,3},{2,4},{3,5},{4,6},{5,7},{6,0},{7,1},{8,10},{9,11},{10,... | collective-permute-start | bytes 811016 | tf_op jit(solution)/shard_map/ppermute | solution.py:545
  15.2 1.0 %copy-start.9 = (bf16[264,512]{1,0:T(8,128)(2,1)S(1)}, bf16[264,512]{1,0:T(8,128)(2,1)}, u32[]{:S(2)}) copy-start(bf16[264,512]{1,0:T(8,128)(2,1)} %get-tuple-element.29.refs_0_) | copy-start | bytes 811012
  16.1 0.9 %copy-start.10 = (bf16[256,512]{1,0:T(8,128)(2,1)S(1)}, bf16[256,512]{1,0:T(8,128)(2,1)}, u32[]{:S(2)}) copy-start(bf16[256,512]{1,0:T(8,128)(2,1)} %get-tuple-element.32.refs_1_) | copy-start | bytes 786436
  20.0 6.2 %collective-permute-start.8 = (bf16[256,512]{1,0:T(8,128)(2,1)S(1)}, bf16[256,512]{1,0:T(8,128)(2,1)S(1)}, u32[]{:S(2)}, u32[]{:S(2)}) collective-permute-start(bf16[256,512]{1,0:T(8,128)(2,1)S(1)} %collective-permute-done.2.refs_1_), channel_id=1, source_target_pairs={{0,1},{1,0},{2,3},{3,2},{4,5},{5,4},{6,7},{7,6},{8,9},{9,8},{10,11... | collective-permute-start | bytes 786440 | tf_op jit(solution)/shard_map/ppermute | solution.py:562
  20.6 11.2 %collective-permute-start.6 = (bf16[256,512]{1,0:T(8,128)(2,1)S(1)}, bf16[256,512]{1,0:T(8,128)(2,1)S(1)}, u32[]{:S(2)}, u32[]{:S(2)}) collective-permute-start(bf16[256,512]{1,0:T(8,128)(2,1)S(1)} %collective-permute-done.2.refs_1_), channel_id=1, source_target_pairs={{0,2},{1,3},{2,4},{3,5},{4,6},{5,7},{6,0},{7,1},{8,10},{9,11},{10,... | collective-permute-start | bytes 786440 | tf_op jit(solution)/shard_map/ppermute | solution.py:545
  23.2 8.5 %copy-start.5 = (s32[512]{0:T(512)S(1)}, s32[512]{0:T(512)}, u32[]{:S(2)}) copy-start(s32[512]{0:T(512)} %param.13) | copy-start | bytes 6148
  26.2 11.3 %collective-permute-start.11 = (bf16[264,512]{1,0:T(8,128)(2,1)S(1)}, bf16[264,512]{1,0:T(8,128)(2,1)S(1)}, u32[]{:S(2)}, u32[]{:S(2)}) collective-permute-start(bf16[264,512]{1,0:T(8,128)(2,1)S(1)} %collective-permute-done.1.beyond.refs_0_.refs_2_), channel_id=1, source_target_pairs={{0,1},{1,0},{2,3},{3,2},{4,5},{5,4},{6,7},{7,6},{8,9},{9,8},{10,11... | collective-permute-start | bytes 811016 | tf_op jit(solution)/shard_map/ppermute | solution.py:562
  26.2 11.3 %collective-permute-start.5 = (bf16[264,512]{1,0:T(8,128)(2,1)S(1)}, bf16[264,512]{1,0:T(8,128)(2,1)S(1)}, u32[]{:S(2)}, u32[]{:S(2)}) collective-permute-start(bf16[264,512]{1,0:T(8,128)(2,1)S(1)} %collective-permute-done.1.beyond.refs_0_.refs_2_), channel_id=1, source_target_pairs={{0,2},{1,3},{2,4},{3,5},{4,6},{5,7},{6,0},{7,1},{8,10},{9,11},{10,... | collective-permute-start | bytes 811016 | tf_op jit(solution)/shard_map/ppermute | solution.py:545
  31.7 5.8 %collective-permute-start.12 = (bf16[256,512]{1,0:T(8,128)(2,1)S(1)}, bf16[256,512]{1,0:T(8,128)(2,1)S(1)}, u32[]{:S(2)}, u32[]{:S(2)}) collective-permute-start(bf16[256,512]{1,0:T(8,128)(2,1)S(1)} %collective-permute-done.6.refs_1_.refs_3_), channel_id=1, source_target_pairs={{0,1},{1,0},{2,3},{3,2},{4,5},{5,4},{6,7},{7,6},{8,9},{9,8},{10,11... | collective-permute-start | bytes 786440 | tf_op jit(solution)/shard_map/ppermute | solution.py:562
  31.7 11.1 %collective-permute-start.10 = (bf16[256,512]{1,0:T(8,128)(2,1)S(1)}, bf16[256,512]{1,0:T(8,128)(2,1)S(1)}, u32[]{:S(2)}, u32[]{:S(2)}) collective-permute-start(bf16[256,512]{1,0:T(8,128)(2,1)S(1)} %collective-permute-done.6.refs_1_.refs_3_), channel_id=1, source_target_pairs={{0,2},{1,3},{2,4},{3,5},{4,6},{5,7},{6,0},{7,1},{8,10},{9,11},{10,... | collective-permute-start | bytes 786440 | tf_op jit(solution)/shard_map/ppermute | solution.py:545
  37.5 5.4 %collective-permute-start.9 = (bf16[264,512]{1,0:T(8,128)(2,1)S(1)}, bf16[264,512]{1,0:T(8,128)(2,1)S(1)}, u32[]{:S(2)}, u32[]{:S(2)}) collective-permute-start(bf16[264,512]{1,0:T(8,128)(2,1)S(1)} %collective-permute-done.5.refs_0_), channel_id=1, source_target_pairs={{0,1},{1,0},{2,3},{3,2},{4,5},{5,4},{6,7},{7,6},{8,9},{9,8},{10,11... | collective-permute-start | bytes 811016 | tf_op jit(solution)/shard_map/ppermute | solution.py:562
  38.9 5.6 %copy-start.3 = (bf16[512,512]{1,0:T(8,128)(2,1)S(1)}, bf16[512,512]{1,0:T(8,128)(2,1)}, u32[]{:S(2)}) copy-start(bf16[512,512]{1,0:T(8,128)(2,1)} %points.3) | copy-start | bytes 1572868
  38.9 5.5 %copy-start.6 = (s32[8,3]{0,1:T(4,128)S(1)}, s32[8,3]{0,1:T(4,128)}, u32[]{:S(2)}) copy-start(s32[8,3]{0,1:T(4,128)} %param.11) | copy-start | bytes 292
  42.9 1.5 %collective-permute-start.13 = (bf16[256,512]{1,0:T(8,128)(2,1)S(1)}, bf16[256,512]{1,0:T(8,128)(2,1)S(1)}, u32[]{:S(2)}, u32[]{:S(2)}) collective-permute-start(bf16[256,512]{1,0:T(8,128)(2,1)S(1)} %collective-permute-done.10.refs_0_), channel_id=1, source_target_pairs={{0,1},{1,0},{2,3},{3,2},{4,5},{5,4},{6,7},{7,6},{8,9},{9,8},{10,11... | collective-permute-start | bytes 786440 | tf_op jit(solution)/shard_map/ppermute | solution.py:562
  44.2 26.8 %copy-start.2 = (bf16[2,512,512]{2,1,0:T(8,128)(2,1)S(1)}, bf16[2,512,512]{2,1,0:T(8,128)(2,1)}, u32[]{:S(2)}) copy-start(bf16[2,512,512]{2,1,0:T(8,128)(2,1)} %w_proj.1) | copy-start | bytes 3145732
  44.2 26.8 %copy-start.7 = (bf16[3,512]{1,0:T(4,128)(2,1)S(1)}, bf16[3,512]{1,0:T(4,128)(2,1)}, u32[]{:S(2)}) copy-start(bf16[3,512]{1,0:T(4,128)(2,1)} %w_head.1) | copy-start | bytes 9220
  44.2 26.8 %copy-start.8 = (s32[8,3]{0,1:T(4,128)S(1)}, s32[8,3]{0,1:T(4,128)}, u32[]{:S(2)}) copy-start(s32[8,3]{0,1:T(4,128)} %param.12) | copy-start | bytes 292
